TPU v7x, 32 devices: a whole 2x2x4 slice. The times are simulated.
32 devices in a mesh: bank: 2 (over x), tmpl: 16 (over z, y, core).
Axes of the slice: x: 2, y: 2, z: 4, core: 2. Of those that a mesh axis runs over, the one named last changes fastest.
Arguments:
- strain_fast: bfloat16 [9216], replicated, may hold values from -6 to 6
- strain_half: bfloat16 [8704], replicated, may hold values from -6 to 6
- strain_quarter: bfloat16 [8448], replicated, may hold values from -6 to 6
- strain_eighth: bfloat16 [8320], replicated, may hold values from -6 to 6
- basis_taps: bfloat16 [8, 512, 8192], P('bank', 'tmpl'), parts along dimension 0, may hold values from -0.0625 to 0.0625
- recon_coeffs: bfloat16 [8, 4096, 512], P('bank', 'tmpl'), parts along dimension 0, may hold values from -0.25 to 0.25
Outputs:
- snr_series: bfloat16 [8192, 1024], P(('bank', 'tmpl')), parts along dimension 0
- peak_snr: float32 [2048], P('bank'), parts along dimension 0
There are 2 independent parts, one for each index of `bank`. A program takes and returns all parts, laid end to end along the dimension named above; an argument that names none is the same for every part. Nothing has to cross between parts.
All inputs are finite; a program needn't handle non-finite values.
Results may differ from a plain program's by a relative error of at most 0.0049.
Values may be sent and summed in bfloat16 or wider, within the bound.
No kernel may reach another device: no remote copies, remote signals or barrier semaphores. Data moves between devices by JAX's collectives and lax.ppermute only.
A program may use at most 128 MiB of HBM per device.

v0:
```python
import functools

import jax
import jax.numpy as jnp
from jax import lax
from jax.experimental import pallas as pl
from jax.experimental.pallas import tpu as pltpu
from jax.sharding import PartitionSpec as P

LANE = 128
CHUNK = 8
SUB = 16


def shifted_rows(x_ref, start, tiles):
    width = (tiles + 1) * LANE
    wide = jnp.broadcast_to(x_ref[:, pl.ds(start, width)], (SUB, width))
    row = lax.broadcasted_iota(jnp.int32, (SUB, width), 0)
    step = 1
    while step < SUB:
        moved = pltpu.roll(wide, width - step, axis=1)
        wide = jnp.where((row & step) != 0, moved, wide)
        step *= 2
    return wide


def build_frames(x_ref, frames_ref, start, tiles):
    wide = shifted_rows(x_ref, start, tiles)
    width = wide.shape[1]
    for q in range(LANE // SUB):
        moved = wide if q == 0 else pltpu.roll(wide, width - SUB * q, axis=1)
        for tile in range(tiles):
            frames_ref[pl.ds(start + tile * LANE + SUB * q, SUB), :] = moved[
                :, tile * LANE : (tile + 1) * LANE
            ]


def correlate_kernel(x0, x1, x2, x3, taps_ref, out_ref, f0, f1, f2, f3):
    streams, frames = (x0, x1, x2, x3), (f0, f1, f2, f3)
    rows, taps = taps_ref.shape[1], taps_ref.shape[2]
    blocks = [(x.shape[1] - taps) // LANE for x in streams]
    offsets = [sum(blocks[:s]) * LANE for s in range(len(blocks))]
    span = CHUNK * LANE
    chunks = taps // span

    def build(section, start, tiles=CHUNK):
        build_frames(streams[section], frames[section], start, tiles)

    def head(section):
        pieces = []
        for u in range(blocks[section]):
            part = taps_ref[section, :, 0 : span - u * LANE]
            if u:
                part = jnp.concatenate([jnp.zeros((rows, u * LANE), part.dtype), part], axis=1)
            pieces.append(part)
        return jnp.concatenate(pieces, axis=0)

    def middle(section, start):
        pieces = []
        for u in range(blocks[section]):
            first = pl.multiple_of(start - u * LANE, LANE)
            pieces.append(taps_ref[section, :, pl.ds(first, span)])
        return jnp.concatenate(pieces, axis=0)

    def tail(section):
        width = (blocks[section] - 1) * LANE
        pieces = []
        for u in range(blocks[section]):
            parts = []
            if u:
                parts.append(taps_ref[section, :, taps - u * LANE : taps])
            if width > u * LANE:
                parts.append(jnp.zeros((rows, width - u * LANE), taps_ref.dtype))
            pieces.append(jnp.concatenate(parts, axis=1))
        return jnp.concatenate(pieces, axis=0)

    def product(section, left, start):
        right = frames[section][pl.ds(start, left.shape[1]), :]
        return jnp.dot(left, right, preferred_element_type=jnp.float32)

    def build_all(section):
        def step(number, carry):
            build(section, pl.multiple_of(number * span, span))
            return carry

        lax.fori_loop(0, chunks, step, 0)
        if blocks[section] > 1:
            build(section, taps, blocks[section] - 1)

    build_all(0)
    for section in range(len(blocks)):
        following = section + 1 if section + 1 < len(blocks) else None
        total = product(section, head(section), 0)
        if following is not None:
            build(following, 0)

        def step(number, total, section=section, following=following):
            start = pl.multiple_of(number * span, span)
            total = total + product(section, middle(section, start), start)
            if following is not None:
                build(following, start)
            return total

        total = lax.fori_loop(1, chunks, step, total)
        if blocks[section] > 1:
            total = total + product(section, tail(section), taps)
        if following is not None and blocks[following] > 1:
            build(following, taps, blocks[following] - 1)
        for u in range(blocks[section]):
            place = offsets[section] + u * LANE
            out_ref[:, place : place + LANE] = total[u * rows : (u + 1) * rows].astype(out_ref.dtype)


def correlate(streams, basis_taps):
    sections, rows, taps = basis_taps.shape
    padded = -(-rows // SUB) * SUB
    if padded != rows:
        basis_taps = jnp.pad(basis_taps, ((0, 0), (0, padded - rows), (0, 0)))
    samples = [x.shape[0] - taps for x in streams]
    out = pl.pallas_call(
        correlate_kernel,
        out_shape=jax.ShapeDtypeStruct((padded, sum(samples)), jnp.bfloat16),
        in_specs=[pl.BlockSpec(memory_space=pltpu.VMEM)] * 5,
        out_specs=pl.BlockSpec(memory_space=pltpu.VMEM),
        scratch_shapes=[
            pltpu.VMEM((taps + count - LANE, LANE), jnp.bfloat16) for count in samples
        ],
        compiler_params=pltpu.CompilerParams(vmem_limit_bytes=24 * 2**20),
        name="correlate",
    )(*[x.reshape(1, -1) for x in streams], basis_taps)
    return out[:rows]


def recon_kernel(coeffs_ref, basis_ref, snr_ref, peak_ref):
    samples = snr_ref.shape[1]
    source = lax.broadcasted_iota(jnp.int32, (2 * LANE, 2 * LANE), 0) % LANE
    target = lax.broadcasted_iota(jnp.int32, (2 * LANE, 2 * LANE), 1) // 2
    repeat = jnp.where(source == target, 1.0, 0.0).astype(jnp.bfloat16)
    running = None
    for section in (3, 2, 1, 0):
        width = samples >> section
        offset = sum(samples >> s for s in range(section))
        summed = []
        for place in range(0, width, 2 * LANE):
            size = min(2 * LANE, width)
            part = jnp.dot(
                coeffs_ref[section],
                basis_ref[:, offset + place : offset + place + size],
                preferred_element_type=jnp.float32,
            )
            if running is not None:
                coarse = running[place // (2 * LANE)]
                high = coarse.astype(jnp.bfloat16)
                low = (coarse - high.astype(jnp.float32)).astype(jnp.bfloat16)
                part = part + jnp.dot(
                    jnp.concatenate([high, low], axis=1),
                    repeat,
                    preferred_element_type=jnp.float32,
                )
            summed.append(part)
        running = []
        for part in summed:
            running += [part[:, at : at + LANE] for at in range(0, part.shape[1], LANE)]
        if section == 0:
            for number, part in enumerate(summed):
                place = number * 2 * LANE
                snr_ref[:, place : place + 2 * LANE] = part.astype(snr_ref.dtype)
                peak_ref[:, place : place + 2 * LANE] = jnp.max(
                    jnp.abs(part), axis=0, keepdims=True
                )


def reconstruct(coeffs, basis, samples):
    return pl.pallas_call(
        recon_kernel,
        out_shape=(
            jax.ShapeDtypeStruct((coeffs.shape[1], samples), jnp.bfloat16),
            jax.ShapeDtypeStruct((1, samples), jnp.float32),
        ),
        in_specs=[pl.BlockSpec(memory_space=pltpu.VMEM)] * 2,
        out_specs=(pl.BlockSpec(memory_space=pltpu.VMEM),) * 2,
        compiler_params=pltpu.CompilerParams(vmem_limit_bytes=24 * 2**20),
        name="reconstruct",
    )(coeffs, basis)


def per_device(strain_fast, strain_half, strain_quarter, strain_eighth, basis_taps, recon_coeffs):
    streams = (strain_fast, strain_half, strain_quarter, strain_eighth)
    samples = strain_fast.shape[0] - basis_taps.shape[2]
    own = correlate(streams, basis_taps)
    basis = lax.all_gather(own, "tmpl", axis=0, tiled=True)
    snr_series, local_peak = reconstruct(recon_coeffs, basis, samples)
    peak_snr = lax.pmax(local_peak.reshape(samples), "tmpl")
    return (snr_series, peak_snr)


def solution(mesh):
    in_specs = (P(), P(), P(), P(), P("bank", "tmpl", None), P("bank", "tmpl", None))
    out_specs = (P(("bank", "tmpl"), None), P("bank"))
    return jax.shard_map(
        per_device, mesh=mesh, in_specs=in_specs, out_specs=out_specs, check_vma=False
    )
```

profile of v0, /device:TPU:0, one launch (start us, length us, event | category | flops | bytes accessed | tf_op | source)
XLA Modules:
  0.0 114.6 jit_solution(3488175039154950995)
XLA Ops:
  7.2 0.0 all-gather.2.cloned.1.call-start
  7.2 0.7 reshape.22.x3
  8.0 0.7 reshape.21.x2
  8.7 0.7 reshape.20.x1
  9.5 0.7 reshape.19.x0
  10.2 0.0 copy-start
  10.2 1.6 %copy-done = bf16[4,32,8192]{2,1,0:T(8,128)(2,1)S(1)} copy-done((bf16[4,32,8192]{2,1,0:T(8,128)(2,1)S(1)}, bf16[4,32,8192]{2,1,0:T(8,128)(2,1)}, u32[]{:S(2)}) %copy-start) | copy-done | bytes 2097176
  11.8 0.0 copy-start.2
  11.8 16.6 %correlate.1 = bf16[32,1920]{1,0:T(8,128)(2,1)} custom-call(bf16[1,9216]{1,0:T(2,128)(2,1)S(1)} %reshape.19.x0, bf16[1,8704]{1,0:T(2,128)(2,1)S(1)} %reshape.20.x1, bf16[1,8448]{1,0:T(2,128)(2,1)S(1)} %reshape.21.x2, bf16[1,8320]{1,0:T(2,128)(2,1)S(1)} %reshape.22.x3, bf16[4,32,8192]{2,1,0:T(8,128)(2,1)S(1)} %copy-done), custom_call_target="tpu_custom_call" | custom-call | tf_op jit(solution)/shard_map/correlate/pallas_call | solution.py:120
  28.4 0.0 all-gather.2.cloned.1.call-update
  28.4 43.7 %all-gather.2.cloned.1.call-done.basis_ref = bf16[512,1920]{1,0:T(8,128)(2,1)} async-done(((bf16[32,1920]{1,0:T(8,128)(2,1)}), bf16[512,1920]{1,0:T(8,128)(2,1)}) %all-gather.2.cloned.1.call-update) | async-done | bytes 1966096 | tf_op jit(solution)/shard_map/all_gather | solution.py:191
  72.1 0.0 copy-done.2
  72.1 0.0 copy-start.1
  72.1 1.5 %copy-done.1 = bf16[512,1920]{1,0:T(8,128)(2,1)S(1)} copy-done((bf16[512,1920]{1,0:T(8,128)(2,1)S(1)}, bf16[512,1920]{1,0:T(8,128)(2,1)}, u32[]{:S(2)}) %copy-start.1) | copy-done | bytes 1966104
  73.6 1.9 %reconstruct.1 = (bf16[256,1024]{1,0:T(8,128)(2,1)}, f32[1,1024]{1,0:T(1,128)S(1)}) custom-call(bf16[4,256,512]{2,1,0:T(8,128)(2,1)S(1)} %copy-done.2, bf16[512,1920]{1,0:T(8,128)(2,1)S(1)} %copy-done.1), custom_call_target="tpu_custom_call" | custom-call | tf_op jit(solution)/shard_map/reconstruct/pallas_call | solution.py:174
  75.6 32.2 %pmax.7 = f32[1024]{0:T(1024)} all-reduce(f32[1024]{0:T(1024)S(1)} %bitcast.1), channel_id=1, replica_groups=mesh['bank'=2,'tmpl'=16] {'tmpl'}, use_global_device_ids=true, to_apply=%region_0.0 | all-reduce | flops 1024 | bytes 8192 | tf_op jit(solution)/shard_map/pmax | solution.py:193
Async XLA Ops:
  7.2 64.9 %all-gather.2.cloned.1.call-start = ((), (), s32[]{:S(2)}) async-start(), calls=%async_computation | async-start | bytes 2088960 | tf_op jit(solution)/shard_map/all_gather | solution.py:191
  10.2 1.6 %copy-start = (bf16[4,32,8192]{2,1,0:T(8,128)(2,1)S(1)}, bf16[4,32,8192]{2,1,0:T(8,128)(2,1)}, u32[]{:S(2)}) copy-start(bf16[4,32,8192]{2,1,0:T(8,128)(2,1)} %taps_ref.1) | copy-start | bytes 6291460
  11.8 60.3 %copy-start.2 = (bf16[4,256,512]{2,1,0:T(8,128)(2,1)S(1)}, bf16[4,256,512]{2,1,0:T(8,128)(2,1)}, u32[]{:S(2)}) copy-start(bf16[4,256,512]{2,1,0:T(8,128)(2,1)} %coeffs_ref.1) | copy-start | bytes 3145732
  72.1 1.5 %copy-start.1 = (bf16[512,1920]{1,0:T(8,128)(2,1)S(1)}, bf16[512,1920]{1,0:T(8,128)(2,1)}, u32[]{:S(2)}) copy-start(bf16[512,1920]{1,0:T(8,128)(2,1)} %all-gather.2.cloned.1.call-done.basis_ref) | copy-start | bytes 5898244
Sparse Core Ops, SparseCore 0:
  28.5 43.5 all-gather.1
where the time goes:
time: 115 us
  waiting for transfers between devices  43.7 us (38%)
  blocking collectives  32.2 us (28%)
  Pallas kernels  18.5 us (16%)
  between operations  14 us (12%)
  local copies, waits for them, and re-layouts  6.11 us (5%)
    all_gather x1, waiting for transfers between devices, per_device(): basis = lax.all_gather(own, 'tmpl', axis=0, tiled=True)  43.7 us
    pmax x1, blocking collectives, per_device(): peak_snr = lax.pmax(local_peak.reshape(samples), 'tmpl')  32.2 us
    pallas_call x1, Pallas kernels, correlate(): pl.pallas_call(correlate_kernel, out_shape=jax.ShapeDtypeStruct((padded,...  16.6 us
    unnamed x6, local copies, waits for them, and re-layouts  3.14 us
    reshape x4, local copies, waits for them, and re-layouts, correlate(): x.reshape(1, -1)  2.98 us
  transfers between devices with their start and end apart: 1, of which 1 were waited for; matrix products, arithmetic and copies ran while one was open for 0% of the time, Pallas kernels for 0%

commit v1 on v0

v1 whole, which is shorter than its diff:
```python
import functools

import jax
import jax.numpy as jnp
from jax import lax
from jax.experimental import pallas as pl
from jax.experimental.pallas import tpu as pltpu
from jax.sharding import PartitionSpec as P

LANE = 128
CHUNK = 8
SUB = 16


def shifted_rows(x_ref, start, tiles):
    width = (tiles + 1) * LANE
    wide = jnp.broadcast_to(x_ref[pl.ds(start, width)].reshape(1, width), (SUB, width))
    row = lax.broadcasted_iota(jnp.int32, (SUB, width), 0)
    step = 1
    while step < SUB:
        moved = pltpu.roll(wide, width - step, axis=1)
        wide = jnp.where((row & step) != 0, moved, wide)
        step *= 2
    return wide


def build_frames(x_ref, start, tiles):
    wide = shifted_rows(x_ref, start, tiles)
    width = wide.shape[1]
    moved = [wide]
    for q in range(1, LANE // SUB):
        moved.append(pltpu.roll(wide, width - SUB * q, axis=1))
    pieces = []
    for tile in range(tiles):
        pieces += [part[:, tile * LANE : (tile + 1) * LANE] for part in moved]
    return jnp.concatenate(pieces, axis=0)


def shifted_taps(taps_ref, start, width, u):
    rows, taps = taps_ref.shape
    first, last = start - u * LANE, start - u * LANE + width
    parts = []
    if first < 0:
        parts.append(jnp.zeros((rows, -first), taps_ref.dtype))
    if last > 0 and first < taps:
        parts.append(taps_ref[:, max(first, 0) : min(last, taps)])
    if last > taps:
        parts.append(jnp.zeros((rows, last - taps), taps_ref.dtype))
    return parts[0] if len(parts) == 1 else jnp.concatenate(parts, axis=1)


def correlate_kernel(sections, *refs):
    count = len(sections)
    streams, taps_ref, out_ref = refs[:count], refs[count], refs[count + 1]
    held_ref, sems = refs[count + 2], refs[count + 3]
    rows, taps = taps_ref.shape[1], taps_ref.shape[2]
    copies = [
        pltpu.make_async_copy(taps_ref.at[section], held_ref.at[number], sems.at[number])
        for number, section in enumerate(sections)
    ]
    for copy in copies:
        copy.start()
    place = 0
    for number in range(count):
        blocks = (streams[number].shape[0] - taps) // LANE
        tiles = taps // LANE + blocks - 1
        total = None
        for tile in range(0, tiles, CHUNK):
            size = min(CHUNK, tiles - tile)
            frames = build_frames(streams[number], tile * LANE, size)
            if tile == 0:
                copies[number].wait()
            held = held_ref.at[number]
            left = jnp.concatenate(
                [shifted_taps(held, tile * LANE, size * LANE, u) for u in range(blocks)], axis=0
            )
            part = jnp.dot(left, frames, preferred_element_type=jnp.float32)
            total = part if total is None else total + part
        for u in range(blocks):
            out_ref[:, place : place + LANE] = total[u * rows : (u + 1) * rows].astype(out_ref.dtype)
            place += LANE


def correlate(streams, basis_taps, sections):
    _, rows, taps = basis_taps.shape
    padded = -(-rows // SUB) * SUB
    if padded != rows:
        basis_taps = jnp.pad(basis_taps, ((0, 0), (0, padded - rows), (0, 0)))
    used = [streams[section] for section in sections]
    samples = sum(x.shape[0] - taps for x in used)
    out = pl.pallas_call(
        functools.partial(correlate_kernel, sections),
        out_shape=jax.ShapeDtypeStruct((padded, samples), jnp.bfloat16),
        in_specs=[pl.BlockSpec(memory_space=pltpu.VMEM)] * len(used)
        + [pl.BlockSpec(memory_space=pl.ANY)],
        out_specs=pl.BlockSpec(memory_space=pltpu.VMEM),
        scratch_shapes=[
            pltpu.VMEM((len(used), padded, taps), jnp.bfloat16),
            pltpu.SemaphoreType.DMA((len(used),)),
        ],
        compiler_params=pltpu.CompilerParams(vmem_limit_bytes=16 * 2**20),
        cost_estimate=pl.CostEstimate(
            flops=2 * padded * taps * samples,
            bytes_accessed=2 * len(used) * padded * taps,
            transcendentals=0,
        ),
        name="correlate",
    )(*used, basis_taps)
    return out[:rows]


def exchange(block, distance):
    size = lax.axis_size("tmpl")
    return lax.ppermute(block, "tmpl", [(i, i ^ distance) for i in range(size)])


def gather_blocks(block):
    size = lax.axis_size("tmpl")
    merge = block.shape[0] % SUB != 0
    held = {0: block}
    top = size
    while top > 1:
        radix = 4 if top > 4 and top % 4 == 0 else 2
        stride = top // radix
        for place, own in list(held.items()):
            for step in range(1, radix):
                held[place + step * stride] = exchange(own, step * stride)
        top = stride
    blocks = [held[place] for place in range(size)]
    return [jnp.concatenate(blocks, axis=0)] if merge else blocks


def maximum_over_group(values):
    size = lax.axis_size("tmpl")
    stride = 1
    while stride < size:
        radix = 4 if size // stride >= 4 else 2
        others = [exchange(values, step * stride) for step in range(1, radix)]
        values = functools.reduce(jnp.maximum, others, values)
        stride *= radix
    return values


def arrange_kernel(offset_ref, coeffs_ref, out_ref):
    bases = coeffs_ref.shape[2]
    source = lax.broadcasted_iota(jnp.int32, (bases, bases), 0)
    target = lax.broadcasted_iota(jnp.int32, (bases, bases), 1) ^ offset_ref[0]
    select = jnp.where(source == target, 1.0, 0.0).astype(jnp.bfloat16)
    for section in range(coeffs_ref.shape[0]):
        out_ref[section] = jnp.dot(
            coeffs_ref[section], select, preferred_element_type=jnp.float32
        ).astype(out_ref.dtype)


def arrange(coeffs, offset):
    return pl.pallas_call(
        arrange_kernel,
        out_shape=jax.ShapeDtypeStruct(coeffs.shape, coeffs.dtype),
        in_specs=[
            pl.BlockSpec(memory_space=pltpu.SMEM),
            pl.BlockSpec(memory_space=pltpu.VMEM),
        ],
        out_specs=pl.BlockSpec(memory_space=pltpu.VMEM),
        compiler_params=pltpu.CompilerParams(vmem_limit_bytes=16 * 2**20),
        cost_estimate=pl.CostEstimate(
            flops=2 * coeffs.size * coeffs.shape[2],
            bytes_accessed=4 * coeffs.size,
            transcendentals=0,
        ),
        name="arrange",
    )(offset, coeffs)


def recon_kernel(fast_count, *refs):
    coeffs_ref, snr_ref, peak_ref = refs[0], refs[-2], refs[-1]
    fast_refs, slow_refs = refs[1 : 1 + fast_count], refs[1 + fast_count : -2]
    samples = snr_ref.shape[1]
    source = lax.broadcasted_iota(jnp.int32, (2 * LANE, 2 * LANE), 0) % LANE
    target = lax.broadcasted_iota(jnp.int32, (2 * LANE, 2 * LANE), 1) // 2
    repeat = jnp.where(source == target, 1.0, 0.0).astype(jnp.bfloat16)
    running = None
    for section in (3, 2, 1, 0):
        width = samples >> section
        offset = sum(samples >> s for s in range(1, section))
        pieces = slow_refs if section else fast_refs
        summed = []
        for place in range(0, width, 2 * LANE):
            size = min(2 * LANE, width)
            first = offset + place
            basis = jnp.concatenate([ref[:, first : first + size] for ref in pieces], axis=0)
            part = jnp.dot(coeffs_ref[section], basis, preferred_element_type=jnp.float32)
            if running is not None:
                coarse = running[place // (2 * LANE)]
                high = coarse.astype(jnp.bfloat16)
                low = (coarse - high.astype(jnp.float32)).astype(jnp.bfloat16)
                part = part + jnp.dot(
                    jnp.concatenate([high, low], axis=1),
                    repeat,
                    preferred_element_type=jnp.float32,
                )
            summed.append(part)
        running = []
        for part in summed:
            running += [part[:, at : at + LANE] for at in range(0, part.shape[1], LANE)]
        if section == 0:
            for number, part in enumerate(summed):
                place = number * 2 * LANE
                snr_ref[:, place : place + 2 * LANE] = part.astype(snr_ref.dtype)
                peak_ref[:, place : place + 2 * LANE] = jnp.max(
                    jnp.abs(part), axis=0, keepdims=True
                )


def reconstruct(coeffs, fast, slow, samples):
    return pl.pallas_call(
        functools.partial(recon_kernel, len(fast)),
        out_shape=(
            jax.ShapeDtypeStruct((coeffs.shape[1], samples), jnp.bfloat16),
            jax.ShapeDtypeStruct((1, samples), jnp.float32),
        ),
        in_specs=[pl.BlockSpec(memory_space=pltpu.VMEM)] * (1 + len(fast) + len(slow)),
        out_specs=(pl.BlockSpec(memory_space=pltpu.VMEM),) * 2,
        compiler_params=pltpu.CompilerParams(vmem_limit_bytes=16 * 2**20),
        name="reconstruct",
    )(coeffs, *fast, *slow)


def per_device(strain_fast, strain_half, strain_quarter, strain_eighth, basis_taps, recon_coeffs):
    streams = (strain_fast, strain_half, strain_quarter, strain_eighth)
    samples = strain_fast.shape[0] - basis_taps.shape[2]
    offset = (lax.axis_index("tmpl") * basis_taps.shape[1]).astype(jnp.int32).reshape(1)
    fast = gather_blocks(correlate(streams, basis_taps, (0,)))
    slow = gather_blocks(correlate(streams, basis_taps, (1, 2, 3)))
    coeffs = arrange(recon_coeffs, offset)
    snr_series, local_peak = reconstruct(coeffs, fast, slow, samples)
    peak_snr = maximum_over_group(local_peak.reshape(samples))
    return (snr_series, peak_snr)


def solution(mesh):
    in_specs = (P(), P(), P(), P(), P("bank", "tmpl", None), P("bank", "tmpl", None))
    out_specs = (P(("bank", "tmpl"), None), P("bank"))
    return jax.shard_map(
        per_device, mesh=mesh, in_specs=in_specs, out_specs=out_specs, check_vma=False
    )
```

time: 115 us -> 59.3 us (0.52)
  blocking collectives: 32.2 us -> 0 us
  waiting for transfers between devices: 43.7 us -> 14.9 us
  starting transfers between devices: 0.04 us -> 26.5 us
  between operations: 14 us -> 0.73 us
  Pallas kernels: 18.5 us -> 11.7 us
  local copies, waits for them, and re-layouts: 6.11 us -> 4.48 us
    all_gather x1 -> x0, waiting for transfers between devices: 43.7 us -> none  [per_device(): basis = lax.all_gather(own, 'tmpl', axis=0, tiled=True)]
    pmax x1 -> x0, blocking collectives: 32.2 us -> none  [per_device(): peak_snr = lax.pmax(local_peak.reshape(samples), 'tmpl')]
    ppermute x0 -> x36, starting transfers between devices: none -> 26.5 us  [exchange(): return lax.ppermute(block, 'tmpl', [(i, i ^ distance) for i in range(size)])]
    ppermute x0 -> x36, waiting for transfers between devices: none -> 14.9 us  [exchange(): return lax.ppermute(block, 'tmpl', [(i, i ^ distance) for i in range(size)])]
    pallas_call x2 -> x4, Pallas kernels: 18.5 us -> 11.7 us  [the longest x2 8.95 us: correlate(): pl.pallas_call(functools.partial(correlate_kernel, sections), out_shape=j...]
    reshape x4 -> x0, local copies, waits for them, and re-layouts: 2.98 us -> none  [correlate(): x.reshape(1, -1)]
    unnamed x6 -> x14, local copies, waits for them, and re-layouts: 3.14 us -> 4.48 us
  transfers between devices with their start and end apart: 1 -> 36, of which waited for: 1 -> 11; matrix products, arithmetic and copies ran while one was open for 0% -> 0% of each run, Pallas kernels for 0% -> 6%
where the time goes in v1:
time: 59.3 us; the launch traced here: 58.9 us
  starting transfers between devices  26.5 us (45%)
  waiting for transfers between devices  14.9 us (25%)
  Pallas kernels  11.7 us (20%)
  local copies, waits for them, and re-layouts  4.48 us (8%)
  between operations  0.73 us (1%)
  other arithmetic  0.6 us (1%)
    ppermute x36, starting transfers between devices, exchange(): return lax.ppermute(block, 'tmpl', [(i, i ^ distance) for i in range(size)])  26.5 us
    ppermute x36, waiting for transfers between devices, exchange(): return lax.ppermute(block, 'tmpl', [(i, i ^ distance) for i in range(size)])  14.9 us
    pallas_call x2, Pallas kernels, correlate(): pl.pallas_call(functools.partial(correlate_kernel, sections), out_shape=j...  8.95 us
    unnamed x14, local copies, waits for them, and re-layouts  4.48 us
    pallas_call x1, Pallas kernels, reconstruct(): pl.pallas_call(functools.partial(recon_kernel, len(fast)), out_shape=(jax...  2.02 us
  transfers between devices with their start and end apart: 36, of which 11 were waited for; matrix products, arithmetic and copies ran while one was open for 0% of the time, Pallas kernels for 6%

profile of v1, /device:TPU:0, one launch (start us, length us, event | category | flops | bytes accessed | tf_op | source)
XLA Modules:
  0.0 58.9 jit_solution(17296709660638697646)
XLA Ops:
  0.6 1.6 %copy-done = bf16[4,32,8192]{2,1,0:T(8,128)(2,1)S(1)} copy-done((bf16[4,32,8192]{2,1,0:T(8,128)(2,1)S(1)}, bf16[4,32,8192]{2,1,0:T(8,128)(2,1)}, u32[]{:S(2)}) %copy-start) | copy-done | bytes 2097176
  2.2 0.7 %copy-done.3 = bf16[8704]{0:T(1024)(128)(2,1)S(1)} copy-done((bf16[8704]{0:T(1024)(128)(2,1)S(1)}, bf16[8704]{0:T(1024)(128)(2,1)}, u32[]{:S(2)}) %copy-start.3) | copy-done | bytes 17432
  2.9 0.7 %copy-done.4 = bf16[8448]{0:T(1024)(128)(2,1)S(1)} copy-done((bf16[8448]{0:T(1024)(128)(2,1)S(1)}, bf16[8448]{0:T(1024)(128)(2,1)}, u32[]{:S(2)}) %copy-start.4) | copy-done | bytes 16920
  3.7 0.7 %copy-done.5 = bf16[8320]{0:T(1024)(128)(2,1)S(1)} copy-done((bf16[8320]{0:T(1024)(128)(2,1)S(1)}, bf16[8320]{0:T(1024)(128)(2,1)}, u32[]{:S(2)}) %copy-start.5) | copy-done | bytes 16664
  4.4 6.0 %correlate.3.refs_17_ = bf16[32,896]{1,0:T(8,128)(2,1)S(1)} custom-call(bf16[8704]{0:T(1024)(128)(2,1)S(1)} %copy-done.3, bf16[8448]{0:T(1024)(128)(2,1)S(1)} %copy-done.4, bf16[8320]{0:T(1024)(128)(2,1)S(1)} %copy-done.5, bf16[4,32,8192]{2,1,0:T(8,128)(2,1)S(1)} %copy-done), custom_call_target="tpu_custom_call" | custom-call | flops 469762048 | bytes 1572864 | tf_op jit(solution)/shard_map/correlate/pallas_call | solution.py:91
  10.4 5.1 %collective-permute-start.26 = (bf16[32,896]{1,0:T(8,128)(2,1)S(1)}, bf16[32,896]{1,0:T(8,128)(2,1)S(1)}, u32[]{:S(2)}, u32[]{:S(2)}) collective-permute-start(bf16[32,896]{1,0:T(8,128)(2,1)S(1)} %correlate.3.refs_17_), channel_id=1, source_target_pairs={{0,12},{1,13},{2,14},{3,15},{4,8},{5,9},{6,10},{7,11},{8,4},{9,5},... | collective-permute-start | bytes 172040 | tf_op jit(solution)/shard_map/ppermute | solution.py:114
  15.5 0.0 collective-permute-start.22
  15.5 0.6 %collective-permute-start.18 = (bf16[32,896]{1,0:T(8,128)(2,1)S(1)}, bf16[32,896]{1,0:T(8,128)(2,1)S(1)}, u32[]{:S(2)}, u32[]{:S(2)}) collective-permute-start(bf16[32,896]{1,0:T(8,128)(2,1)S(1)} %correlate.3.refs_17_), channel_id=1, source_target_pairs={{0,4},{1,5},{2,6},{3,7},{4,0},{5,1},{6,2},{7,3},{8,12},{9,13},{10,... | collective-permute-start | bytes 172040 | tf_op jit(solution)/shard_map/ppermute | solution.py:114
  16.1 1.7 %collective-permute-start.16 = (bf16[32,896]{1,0:T(8,128)(2,1)S(1)}, bf16[32,896]{1,0:T(8,128)(2,1)S(1)}, u32[]{:S(2)}, u32[]{:S(2)}) collective-permute-start(bf16[32,896]{1,0:T(8,128)(2,1)S(1)} %correlate.3.refs_17_), channel_id=1, source_target_pairs={{0,2},{1,3},{2,0},{3,1},{4,6},{5,7},{6,4},{7,5},{8,10},{9,11},{10,... | collective-permute-start | bytes 172040 | tf_op jit(solution)/shard_map/ppermute | solution.py:114
  17.8 0.0 collective-permute-start.15
  17.8 0.7 %copy-done.6 = bf16[9216]{0:T(1024)(128)(2,1)S(1)} copy-done((bf16[9216]{0:T(1024)(128)(2,1)S(1)}, bf16[9216]{0:T(1024)(128)(2,1)}, u32[]{:S(2)}) %copy-start.6) | copy-done | bytes 18456
  18.5 3.0 %correlate.2.refs_1_ = bf16[32,1024]{1,0:T(8,128)(2,1)S(1)} custom-call(bf16[9216]{0:T(1024)(128)(2,1)S(1)} %copy-done.6, bf16[4,32,8192]{2,1,0:T(8,128)(2,1)S(1)} %copy-done.1), custom_call_target="tpu_custom_call" | custom-call | flops 536870912 | bytes 524288 | tf_op jit(solution)/shard_map/correlate/pallas_call | solution.py:91
  21.5 3.7 %collective-permute-start.11 = (bf16[32,1024]{1,0:T(8,128)(2,1)S(1)}, bf16[32,1024]{1,0:T(8,128)(2,1)S(1)}, u32[]{:S(2)}, u32[]{:S(2)}) collective-permute-start(bf16[32,1024]{1,0:T(8,128)(2,1)S(1)} %correlate.2.refs_1_), channel_id=1, source_target_pairs={{0,12},{1,13},{2,14},{3,15},{4,8},{5,9},{6,10},{7,11},{8,4},{9,5},... | collective-permute-start | bytes 196616 | tf_op jit(solution)/shard_map/ppermute | solution.py:114
  25.2 0.8 %collective-permute-start.3 = (bf16[32,1024]{1,0:T(8,128)(2,1)S(1)}, bf16[32,1024]{1,0:T(8,128)(2,1)S(1)}, u32[]{:S(2)}, u32[]{:S(2)}) collective-permute-start(bf16[32,1024]{1,0:T(8,128)(2,1)S(1)} %correlate.2.refs_1_), channel_id=1, source_target_pairs={{0,4},{1,5},{2,6},{3,7},{4,0},{5,1},{6,2},{7,3},{8,12},{9,13},{10,... | collective-permute-start | bytes 196616 | tf_op jit(solution)/shard_map/ppermute | solution.py:114
  26.0 0.4 collective-permute-start.1
  26.4 2.0 %collective-permute-done.11.refs_13_ = bf16[32,1024]{1,0:T(8,128)(2,1)S(1)} collective-permute-done((bf16[32,1024]{1,0:T(8,128)(2,1)S(1)}, bf16[32,1024]{1,0:T(8,128)(2,1)S(1)}, u32[]{:S(2)}, u32[]{:S(2)}) %collective-permute-start.11) | collective-permute-done | bytes 65568 | tf_op jit(solution)/shard_map/ppermute | solution.py:114
  28.4 0.4 collective-permute-start.28
  28.8 2.2 %collective-permute-done.7.refs_9_ = bf16[32,1024]{1,0:T(8,128)(2,1)S(1)} collective-permute-done((bf16[32,1024]{1,0:T(8,128)(2,1)S(1)}, bf16[32,1024]{1,0:T(8,128)(2,1)S(1)}, u32[]{:S(2)}, u32[]{:S(2)}) %collective-permute-start.7) | collective-permute-done | bytes 65568 | tf_op jit(solution)/shard_map/ppermute | solution.py:114
  31.0 0.5 collective-permute-start.24
  31.5 0.2 collective-permute-start.23
  31.8 1.6 %collective-permute-start.20 = (bf16[32,896]{1,0:T(8,128)(2,1)S(1)}, bf16[32,896]{1,0:T(8,128)(2,1)S(1)}, u32[]{:S(2)}, u32[]{:S(2)}) collective-permute-start(bf16[32,896]{1,0:T(8,128)(2,1)S(1)} %collective-permute-done.18.refs_21_), channel_id=1, source_target_pairs={{0,2},{1,3},{2,0},{3,1},{4,6},{5,7},{6,4},{7,5},{8,10},{9,11},{10,... | collective-permute-start | bytes 172040 | tf_op jit(solution)/shard_map/ppermute | solution.py:114
  33.3 0.5 collective-permute-start.13
  33.8 2.0 %collective-permute-done.24.refs_27_ = bf16[32,896]{1,0:T(8,128)(2,1)S(1)} collective-permute-done((bf16[32,896]{1,0:T(8,128)(2,1)S(1)}, bf16[32,896]{1,0:T(8,128)(2,1)S(1)}, u32[]{:S(2)}, u32[]{:S(2)}) %collective-permute-start.24) | collective-permute-done | bytes 57376 | tf_op jit(solution)/shard_map/ppermute | solution.py:114
  35.8 0.5 collective-permute-start.17
  36.3 0.7 %collective-permute-done.20.refs_23_ = bf16[32,896]{1,0:T(8,128)(2,1)S(1)} collective-permute-done((bf16[32,896]{1,0:T(8,128)(2,1)S(1)}, bf16[32,896]{1,0:T(8,128)(2,1)S(1)}, u32[]{:S(2)}, u32[]{:S(2)}) %collective-permute-start.20) | collective-permute-done | bytes 57376 | tf_op jit(solution)/shard_map/ppermute | solution.py:114
  37.0 1.1 %collective-permute-start.9 = (bf16[32,1024]{1,0:T(8,128)(2,1)S(1)}, bf16[32,1024]{1,0:T(8,128)(2,1)S(1)}, u32[]{:S(2)}, u32[]{:S(2)}) collective-permute-start(bf16[32,1024]{1,0:T(8,128)(2,1)S(1)} %collective-permute-done.7.refs_9_), channel_id=1, source_target_pairs={{0,2},{1,3},{2,0},{3,1},{4,6},{5,7},{6,4},{7,5},{8,10},{9,11},{10,... | collective-permute-start | bytes 196616 | tf_op jit(solution)/shard_map/ppermute | solution.py:114
  38.1 1.0 %collective-permute-start.5 = (bf16[32,1024]{1,0:T(8,128)(2,1)S(1)}, bf16[32,1024]{1,0:T(8,128)(2,1)S(1)}, u32[]{:S(2)}, u32[]{:S(2)}) collective-permute-start(bf16[32,1024]{1,0:T(8,128)(2,1)S(1)} %collective-permute-done.3.refs_5_), channel_id=1, source_target_pairs={{0,2},{1,3},{2,0},{3,1},{4,6},{5,7},{6,4},{7,5},{8,10},{9,11},{10,... | collective-permute-start | bytes 196616 | tf_op jit(solution)/shard_map/ppermute | solution.py:114
  39.1 0.2 collective-permute-start.4
  39.3 0.3 collective-permute-start.2
  39.6 1.8 %collective-permute-done.9.refs_11_ = bf16[32,1024]{1,0:T(8,128)(2,1)S(1)} collective-permute-done((bf16[32,1024]{1,0:T(8,128)(2,1)S(1)}, bf16[32,1024]{1,0:T(8,128)(2,1)S(1)}, u32[]{:S(2)}, u32[]{:S(2)}) %collective-permute-start.9) | collective-permute-done | bytes 65568 | tf_op jit(solution)/shard_map/ppermute | solution.py:114
  41.4 0.5 collective-permute-start.14
  41.9 0.8 %collective-permute-done.5.refs_7_ = bf16[32,1024]{1,0:T(8,128)(2,1)S(1)} collective-permute-done((bf16[32,1024]{1,0:T(8,128)(2,1)S(1)}, bf16[32,1024]{1,0:T(8,128)(2,1)S(1)}, u32[]{:S(2)}, u32[]{:S(2)}) %collective-permute-start.5) | collective-permute-done | bytes 65568 | tf_op jit(solution)/shard_map/ppermute | solution.py:114
  42.7 0.5 collective-permute-start.6
  43.2 0.1 collective-permute-start.25
  43.3 0.4 collective-permute-start.21
  43.7 0.7 %arrange.1.refs_0_ = bf16[4,256,512]{2,1,0:T(8,128)(2,1)S(1)} custom-call(s32[1]{0:T(128)} %bitcast.offset_ref, bf16[4,256,512]{2,1,0:T(8,128)(2,1)S(1)} %copy-done.2), custom_call_target="tpu_custom_call" | custom-call | flops 536870912 | bytes 2097152 | tf_op jit(solution)/shard_map/arrange/pallas_call | solution.py:156
  44.4 0.1 collective-permute-done.21.refs_24_
  44.6 2.0 %reconstruct.1 = (bf16[256,1024]{1,0:T(8,128)(2,1)}, f32[1,1024]{1,0:T(1,128)S(1)}) custom-call(bf16[4,256,512]{2,1,0:T(8,128)(2,1)S(1)} %arrange.1.refs_0_, bf16[32,1024]{1,0:T(8,128)(2,1)S(1)} %correlate.2.refs_1_, bf16[32,1024]{1,0:T(8,128)(2,1)S(1)} %collective-permute-done.refs_2_, bf16[32,1024]{1,0:T(8,128)(2,1)S(1)} %collective-permute-done.1.refs_3_, ...), custom_call_target="tpu_custom_call" | custom-call | tf_op jit(solution)/shard_map/reconstruct/pallas_call | solution.py:215
  46.6 1.0 %collective-permute-start.32 = (f32[1024]{0:T(1024)S(1)}, f32[1024]{0:T(1024)S(1)}, u32[]{:S(2)}, u32[]{:S(2)}) collective-permute-start(f32[1024]{0:T(1024)S(1)} %bitcast.2), channel_id=1, source_target_pairs={{0,3},{1,2},{2,1},{3,0},{4,7},{5,6},{6,5},{7,4},{8,11},{9,10},{10,... | collective-permute-start | bytes 12296 | tf_op jit(solution)/shard_map/ppermute | solution.py:114
  47.6 1.0 %collective-permute-start.31 = (f32[1024]{0:T(1024)S(1)}, f32[1024]{0:T(1024)S(1)}, u32[]{:S(2)}, u32[]{:S(2)}) collective-permute-start(f32[1024]{0:T(1024)S(1)} %bitcast.3), channel_id=1, source_target_pairs={{0,2},{1,3},{2,0},{3,1},{4,6},{5,7},{6,4},{7,5},{8,10},{9,11},{10,... | collective-permute-start | bytes 12296 | tf_op jit(solution)/shard_map/ppermute | solution.py:114
  48.6 1.0 %collective-permute-done.32 = f32[1024]{0:T(1024)S(1)} collective-permute-done((f32[1024]{0:T(1024)S(1)}, f32[1024]{0:T(1024)S(1)}, u32[]{:S(2)}, u32[]{:S(2)}) %collective-permute-start.32) | collective-permute-done | bytes 4128 | tf_op jit(solution)/shard_map/ppermute | solution.py:114
  49.7 1.6 %collective-permute-done.31 = f32[1024]{0:T(1024)S(1)} collective-permute-done((f32[1024]{0:T(1024)S(1)}, f32[1024]{0:T(1024)S(1)}, u32[]{:S(2)}, u32[]{:S(2)}) %collective-permute-start.31) | collective-permute-done | bytes 4128 | tf_op jit(solution)/shard_map/ppermute | solution.py:114
  51.2 2.5 %collective-permute-start.35 = (f32[1024]{0:T(1024)S(1)}, f32[1024]{0:T(1024)S(1)}, u32[]{:S(2)}, u32[]{:S(2)}) collective-permute-start(f32[1024]{0:T(1024)S(1)} %maximum_maximum_fusion.1), channel_id=1, source_target_pairs={{0,12},{1,13},{2,14},{3,15},{4,8},{5,9},{6,10},{7,11},{8,4},{9,5},... | collective-permute-start | bytes 12296 | tf_op jit(solution)/shard_map/ppermute | solution.py:114
  53.8 0.3 collective-permute-start.34
  54.1 1.6 %collective-permute-start.33 = (f32[1024]{0:T(1024)S(1)}, f32[1024]{0:T(1024)S(1)}, u32[]{:S(2)}, u32[]{:S(2)}) collective-permute-start(f32[1024]{0:T(1024)S(1)} %maximum_maximum_fusion.1), channel_id=1, source_target_pairs={{0,4},{1,5},{2,6},{3,7},{4,0},{5,1},{6,2},{7,3},{8,12},{9,13},{10,... | collective-permute-start | bytes 12296 | tf_op jit(solution)/shard_map/ppermute | solution.py:114
  55.7 1.0 %collective-permute-done.35 = f32[1024]{0:T(1024)S(1)} collective-permute-done((f32[1024]{0:T(1024)S(1)}, f32[1024]{0:T(1024)S(1)}, u32[]{:S(2)}, u32[]{:S(2)}) %collective-permute-start.35) | collective-permute-done | bytes 4128 | tf_op jit(solution)/shard_map/ppermute | solution.py:114
  56.7 1.6 %collective-permute-done.34 = f32[1024]{0:T(1024)S(1)} collective-permute-done((f32[1024]{0:T(1024)S(1)}, f32[1024]{0:T(1024)S(1)}, u32[]{:S(2)}, u32[]{:S(2)}) %collective-permute-start.34) | collective-permute-done | bytes 4128 | tf_op jit(solution)/shard_map/ppermute | solution.py:114
  58.3 0.6 %maximum_maximum_fusion = f32[1024]{0:T(1024)} fusion(f32[1024]{0:T(1024)S(1)} %collective-permute-done.35, f32[1024]{0:T(1024)S(1)} %collective-permute-done.34, f32[1024]{0:T(1024)S(1)} %maximum_maximum_fusion.1, f32[1024]{0:T(1024)S(1)} %collective-permute-done.33), kind=kLoop, calls=%fused_computation | loop fusion | flops 3072 | bytes 20480 | tf_op jit(solution)/shard_map/max | solution.py:139
  (44 shorter events, 0.1 us)
Async XLA Ops:
  0.6 1.6 %copy-start = (bf16[4,32,8192]{2,1,0:T(8,128)(2,1)S(1)}, bf16[4,32,8192]{2,1,0:T(8,128)(2,1)}, u32[]{:S(2)}) copy-start(bf16[4,32,8192]{2,1,0:T(8,128)(2,1)} %refs_3_.1) | copy-start | bytes 6291460
  2.2 0.7 %copy-start.3 = (bf16[8704]{0:T(1024)(128)(2,1)S(1)}, bf16[8704]{0:T(1024)(128)(2,1)}, u32[]{:S(2)}) copy-start(bf16[8704]{0:T(1024)(128)(2,1)} %refs_0_.3) | copy-start | bytes 52228
  2.9 0.7 %copy-start.4 = (bf16[8448]{0:T(1024)(128)(2,1)S(1)}, bf16[8448]{0:T(1024)(128)(2,1)}, u32[]{:S(2)}) copy-start(bf16[8448]{0:T(1024)(128)(2,1)} %refs_1_.3) | copy-start | bytes 50692
  3.7 0.7 %copy-start.5 = (bf16[8320]{0:T(1024)(128)(2,1)S(1)}, bf16[8320]{0:T(1024)(128)(2,1)}, u32[]{:S(2)}) copy-start(bf16[8320]{0:T(1024)(128)(2,1)} %refs_2_.1) | copy-start | bytes 49924
  4.4 13.4 %copy-start.1 = (bf16[4,32,8192]{2,1,0:T(8,128)(2,1)S(1)}, bf16[4,32,8192]{2,1,0:T(8,128)(2,1)}, u32[]{:S(2)}) copy-start(bf16[4,32,8192]{2,1,0:T(8,128)(2,1)} %refs_3_.1) | copy-start | bytes 6291460
  4.4 39.3 %copy-start.2 = (bf16[4,256,512]{2,1,0:T(8,128)(2,1)S(1)}, bf16[4,256,512]{2,1,0:T(8,128)(2,1)}, u32[]{:S(2)}) copy-start(bf16[4,256,512]{2,1,0:T(8,128)(2,1)} %coeffs_ref.1) | copy-start | bytes 3145732
  10.4 11.2 %collective-permute-start.26 = (bf16[32,896]{1,0:T(8,128)(2,1)S(1)}, bf16[32,896]{1,0:T(8,128)(2,1)S(1)}, u32[]{:S(2)}, u32[]{:S(2)}) collective-permute-start(bf16[32,896]{1,0:T(8,128)(2,1)S(1)} %correlate.3.refs_17_), channel_id=1, source_target_pairs={{0,12},{1,13},{2,14},{3,15},{4,8},{5,9},{6,10},{7,11},{8,4},{9,5},... | collective-permute-start | bytes 172040 | tf_op jit(solution)/shard_map/ppermute | solution.py:114
  15.5 9.7 %collective-permute-start.22 = (bf16[32,896]{1,0:T(8,128)(2,1)S(1)}, bf16[32,896]{1,0:T(8,128)(2,1)S(1)}, u32[]{:S(2)}, u32[]{:S(2)}) collective-permute-start(bf16[32,896]{1,0:T(8,128)(2,1)S(1)} %correlate.3.refs_17_), channel_id=1, source_target_pairs={{0,8},{1,9},{2,10},{3,11},{4,12},{5,13},{6,14},{7,15},{8,0},{9,1},... | collective-permute-start | bytes 172040 | tf_op jit(solution)/shard_map/ppermute | solution.py:114
  15.5 9.7 %collective-permute-start.18 = (bf16[32,896]{1,0:T(8,128)(2,1)S(1)}, bf16[32,896]{1,0:T(8,128)(2,1)S(1)}, u32[]{:S(2)}, u32[]{:S(2)}) collective-permute-start(bf16[32,896]{1,0:T(8,128)(2,1)S(1)} %correlate.3.refs_17_), channel_id=1, source_target_pairs={{0,4},{1,5},{2,6},{3,7},{4,0},{5,1},{6,2},{7,3},{8,12},{9,13},{10,... | collective-permute-start | bytes 172040 | tf_op jit(solution)/shard_map/ppermute | solution.py:114
  16.1 9.9 %collective-permute-start.16 = (bf16[32,896]{1,0:T(8,128)(2,1)S(1)}, bf16[32,896]{1,0:T(8,128)(2,1)S(1)}, u32[]{:S(2)}, u32[]{:S(2)}) collective-permute-start(bf16[32,896]{1,0:T(8,128)(2,1)S(1)} %correlate.3.refs_17_), channel_id=1, source_target_pairs={{0,2},{1,3},{2,0},{3,1},{4,6},{5,7},{6,4},{7,5},{8,10},{9,11},{10,... | collective-permute-start | bytes 172040 | tf_op jit(solution)/shard_map/ppermute | solution.py:114
  17.8 8.6 %collective-permute-start.15 = (bf16[32,896]{1,0:T(8,128)(2,1)S(1)}, bf16[32,896]{1,0:T(8,128)(2,1)S(1)}, u32[]{:S(2)}, u32[]{:S(2)}) collective-permute-start(bf16[32,896]{1,0:T(8,128)(2,1)S(1)} %correlate.3.refs_17_), channel_id=1, source_target_pairs={{0,1},{1,0},{2,3},{3,2},{4,5},{5,4},{6,7},{7,6},{8,9},{9,8},{10,11... | collective-permute-start | bytes 172040 | tf_op jit(solution)/shard_map/ppermute | solution.py:114
  17.8 0.7 %copy-start.6 = (bf16[9216]{0:T(1024)(128)(2,1)S(1)}, bf16[9216]{0:T(1024)(128)(2,1)}, u32[]{:S(2)}) copy-start(bf16[9216]{0:T(1024)(128)(2,1)} %refs_0_.2) | copy-start | bytes 55300
  21.5 6.8 %collective-permute-start.11 = (bf16[32,1024]{1,0:T(8,128)(2,1)S(1)}, bf16[32,1024]{1,0:T(8,128)(2,1)S(1)}, u32[]{:S(2)}, u32[]{:S(2)}) collective-permute-start(bf16[32,1024]{1,0:T(8,128)(2,1)S(1)} %correlate.2.refs_1_), channel_id=1, source_target_pairs={{0,12},{1,13},{2,14},{3,15},{4,8},{5,9},{6,10},{7,11},{8,4},{9,5},... | collective-permute-start | bytes 196616 | tf_op jit(solution)/shard_map/ppermute | solution.py:114
  25.2 5.8 %collective-permute-start.7 = (bf16[32,1024]{1,0:T(8,128)(2,1)S(1)}, bf16[32,1024]{1,0:T(8,128)(2,1)S(1)}, u32[]{:S(2)}, u32[]{:S(2)}) collective-permute-start(bf16[32,1024]{1,0:T(8,128)(2,1)S(1)} %correlate.2.refs_1_), channel_id=1, source_target_pairs={{0,8},{1,9},{2,10},{3,11},{4,12},{5,13},{6,14},{7,15},{8,0},{9,1},... | collective-permute-start | bytes 196616 | tf_op jit(solution)/shard_map/ppermute | solution.py:114
  25.2 5.8 %collective-permute-start.3 = (bf16[32,1024]{1,0:T(8,128)(2,1)S(1)}, bf16[32,1024]{1,0:T(8,128)(2,1)S(1)}, u32[]{:S(2)}, u32[]{:S(2)}) collective-permute-start(bf16[32,1024]{1,0:T(8,128)(2,1)S(1)} %correlate.2.refs_1_), channel_id=1, source_target_pairs={{0,4},{1,5},{2,6},{3,7},{4,0},{5,1},{6,2},{7,3},{8,12},{9,13},{10,... | collective-permute-start | bytes 196616 | tf_op jit(solution)/shard_map/ppermute | solution.py:114
  26.0 5.5 %collective-permute-start.1 = (bf16[32,1024]{1,0:T(8,128)(2,1)S(1)}, bf16[32,1024]{1,0:T(8,128)(2,1)S(1)}, u32[]{:S(2)}, u32[]{:S(2)}) collective-permute-start(bf16[32,1024]{1,0:T(8,128)(2,1)S(1)} %correlate.2.refs_1_), channel_id=1, source_target_pairs={{0,2},{1,3},{2,0},{3,1},{4,6},{5,7},{6,4},{7,5},{8,10},{9,11},{10,... | collective-permute-start | bytes 196616 | tf_op jit(solution)/shard_map/ppermute | solution.py:114
  26.4 5.4 %collective-permute-start = (bf16[32,1024]{1,0:T(8,128)(2,1)S(1)}, bf16[32,1024]{1,0:T(8,128)(2,1)S(1)}, u32[]{:S(2)}, u32[]{:S(2)}) collective-permute-start(bf16[32,1024]{1,0:T(8,128)(2,1)S(1)} %correlate.2.refs_1_), channel_id=1, source_target_pairs={{0,1},{1,0},{2,3},{3,2},{4,5},{5,4},{6,7},{7,6},{8,9},{9,8},{10,11... | collective-permute-start | bytes 196616 | tf_op jit(solution)/shard_map/ppermute | solution.py:114
  28.4 4.9 %collective-permute-start.28 = (bf16[32,896]{1,0:T(8,128)(2,1)S(1)}, bf16[32,896]{1,0:T(8,128)(2,1)S(1)}, u32[]{:S(2)}, u32[]{:S(2)}) collective-permute-start(bf16[32,896]{1,0:T(8,128)(2,1)S(1)} %collective-permute-done.26.refs_29_), channel_id=1, source_target_pairs={{0,2},{1,3},{2,0},{3,1},{4,6},{5,7},{6,4},{7,5},{8,10},{9,11},{10,... | collective-permute-start | bytes 172040 | tf_op jit(solution)/shard_map/ppermute | solution.py:114
  31.0 2.7 %collective-permute-start.27 = (bf16[32,896]{1,0:T(8,128)(2,1)S(1)}, bf16[32,896]{1,0:T(8,128)(2,1)S(1)}, u32[]{:S(2)}, u32[]{:S(2)}) collective-permute-start(bf16[32,896]{1,0:T(8,128)(2,1)S(1)} %collective-permute-done.26.refs_29_), channel_id=1, source_target_pairs={{0,1},{1,0},{2,3},{3,2},{4,5},{5,4},{6,7},{7,6},{8,9},{9,8},{10,11... | collective-permute-start | bytes 172040 | tf_op jit(solution)/shard_map/ppermute | solution.py:114
  31.0 4.7 %collective-permute-start.24 = (bf16[32,896]{1,0:T(8,128)(2,1)S(1)}, bf16[32,896]{1,0:T(8,128)(2,1)S(1)}, u32[]{:S(2)}, u32[]{:S(2)}) collective-permute-start(bf16[32,896]{1,0:T(8,128)(2,1)S(1)} %collective-permute-done.22.refs_25_), channel_id=1, source_target_pairs={{0,2},{1,3},{2,0},{3,1},{4,6},{5,7},{6,4},{7,5},{8,10},{9,11},{10,... | collective-permute-start | bytes 172040 | tf_op jit(solution)/shard_map/ppermute | solution.py:114
  31.5 4.2 %collective-permute-start.23 = (bf16[32,896]{1,0:T(8,128)(2,1)S(1)}, bf16[32,896]{1,0:T(8,128)(2,1)S(1)}, u32[]{:S(2)}, u32[]{:S(2)}) collective-permute-start(bf16[32,896]{1,0:T(8,128)(2,1)S(1)} %collective-permute-done.22.refs_25_), channel_id=1, source_target_pairs={{0,1},{1,0},{2,3},{3,2},{4,5},{5,4},{6,7},{7,6},{8,9},{9,8},{10,11... | collective-permute-start | bytes 172040 | tf_op jit(solution)/shard_map/ppermute | solution.py:114
  31.8 5.2 %collective-permute-start.20 = (bf16[32,896]{1,0:T(8,128)(2,1)S(1)}, bf16[32,896]{1,0:T(8,128)(2,1)S(1)}, u32[]{:S(2)}, u32[]{:S(2)}) collective-permute-start(bf16[32,896]{1,0:T(8,128)(2,1)S(1)} %collective-permute-done.18.refs_21_), channel_id=1, source_target_pairs={{0,2},{1,3},{2,0},{3,1},{4,6},{5,7},{6,4},{7,5},{8,10},{9,11},{10,... | collective-permute-start | bytes 172040 | tf_op jit(solution)/shard_map/ppermute | solution.py:114
  33.3 5.8 %collective-permute-start.13 = (bf16[32,1024]{1,0:T(8,128)(2,1)S(1)}, bf16[32,1024]{1,0:T(8,128)(2,1)S(1)}, u32[]{:S(2)}, u32[]{:S(2)}) collective-permute-start(bf16[32,1024]{1,0:T(8,128)(2,1)S(1)} %collective-permute-done.11.refs_13_), channel_id=1, source_target_pairs={{0,2},{1,3},{2,0},{3,1},{4,6},{5,7},{6,4},{7,5},{8,10},{9,11},{10,... | collective-permute-start | bytes 196616 | tf_op jit(solution)/shard_map/ppermute | solution.py:114
  33.8 5.5 %collective-permute-start.12 = (bf16[32,1024]{1,0:T(8,128)(2,1)S(1)}, bf16[32,1024]{1,0:T(8,128)(2,1)S(1)}, u32[]{:S(2)}, u32[]{:S(2)}) collective-permute-start(bf16[32,1024]{1,0:T(8,128)(2,1)S(1)} %collective-permute-done.11.refs_13_), channel_id=1, source_target_pairs={{0,1},{1,0},{2,3},{3,2},{4,5},{5,4},{6,7},{7,6},{8,9},{9,8},{10,11... | collective-permute-start | bytes 196616 | tf_op jit(solution)/shard_map/ppermute | solution.py:114
  35.8 2.3 %collective-permute-start.19 = (bf16[32,896]{1,0:T(8,128)(2,1)S(1)}, bf16[32,896]{1,0:T(8,128)(2,1)S(1)}, u32[]{:S(2)}, u32[]{:S(2)}) collective-permute-start(bf16[32,896]{1,0:T(8,128)(2,1)S(1)} %collective-permute-done.18.refs_21_), channel_id=1, source_target_pairs={{0,1},{1,0},{2,3},{3,2},{4,5},{5,4},{6,7},{7,6},{8,9},{9,8},{10,11... | collective-permute-start | bytes 172040 | tf_op jit(solution)/shard_map/ppermute | solution.py:114
  35.8 2.3 %collective-permute-start.17 = (bf16[32,896]{1,0:T(8,128)(2,1)S(1)}, bf16[32,896]{1,0:T(8,128)(2,1)S(1)}, u32[]{:S(2)}, u32[]{:S(2)}) collective-permute-start(bf16[32,896]{1,0:T(8,128)(2,1)S(1)} %collective-permute-done.16.refs_19_), channel_id=1, source_target_pairs={{0,1},{1,0},{2,3},{3,2},{4,5},{5,4},{6,7},{7,6},{8,9},{9,8},{10,11... | collective-permute-start | bytes 172040 | tf_op jit(solution)/shard_map/ppermute | solution.py:114
  37.0 4.4 %collective-permute-start.9 = (bf16[32,1024]{1,0:T(8,128)(2,1)S(1)}, bf16[32,1024]{1,0:T(8,128)(2,1)S(1)}, u32[]{:S(2)}, u32[]{:S(2)}) collective-permute-start(bf16[32,1024]{1,0:T(8,128)(2,1)S(1)} %collective-permute-done.7.refs_9_), channel_id=1, source_target_pairs={{0,2},{1,3},{2,0},{3,1},{4,6},{5,7},{6,4},{7,5},{8,10},{9,11},{10,... | collective-permute-start | bytes 196616 | tf_op jit(solution)/shard_map/ppermute | solution.py:114
  38.1 3.3 %collective-permute-start.8 = (bf16[32,1024]{1,0:T(8,128)(2,1)S(1)}, bf16[32,1024]{1,0:T(8,128)(2,1)S(1)}, u32[]{:S(2)}, u32[]{:S(2)}) collective-permute-start(bf16[32,1024]{1,0:T(8,128)(2,1)S(1)} %collective-permute-done.7.refs_9_), channel_id=1, source_target_pairs={{0,1},{1,0},{2,3},{3,2},{4,5},{5,4},{6,7},{7,6},{8,9},{9,8},{10,11... | collective-permute-start | bytes 196616 | tf_op jit(solution)/shard_map/ppermute | solution.py:114
  38.1 4.6 %collective-permute-start.5 = (bf16[32,1024]{1,0:T(8,128)(2,1)S(1)}, bf16[32,1024]{1,0:T(8,128)(2,1)S(1)}, u32[]{:S(2)}, u32[]{:S(2)}) collective-permute-start(bf16[32,1024]{1,0:T(8,128)(2,1)S(1)} %collective-permute-done.3.refs_5_), channel_id=1, source_target_pairs={{0,2},{1,3},{2,0},{3,1},{4,6},{5,7},{6,4},{7,5},{8,10},{9,11},{10,... | collective-permute-start | bytes 196616 | tf_op jit(solution)/shard_map/ppermute | solution.py:114
  39.1 3.6 %collective-permute-start.4 = (bf16[32,1024]{1,0:T(8,128)(2,1)S(1)}, bf16[32,1024]{1,0:T(8,128)(2,1)S(1)}, u32[]{:S(2)}, u32[]{:S(2)}) collective-permute-start(bf16[32,1024]{1,0:T(8,128)(2,1)S(1)} %collective-permute-done.3.refs_5_), channel_id=1, source_target_pairs={{0,1},{1,0},{2,3},{3,2},{4,5},{5,4},{6,7},{7,6},{8,9},{9,8},{10,11... | collective-permute-start | bytes 196616 | tf_op jit(solution)/shard_map/ppermute | solution.py:114
  39.3 3.9 %collective-permute-start.2 = (bf16[32,1024]{1,0:T(8,128)(2,1)S(1)}, bf16[32,1024]{1,0:T(8,128)(2,1)S(1)}, u32[]{:S(2)}, u32[]{:S(2)}) collective-permute-start(bf16[32,1024]{1,0:T(8,128)(2,1)S(1)} %collective-permute-done.1.refs_3_), channel_id=1, source_target_pairs={{0,1},{1,0},{2,3},{3,2},{4,5},{5,4},{6,7},{7,6},{8,9},{9,8},{10,11... | collective-permute-start | bytes 196616 | tf_op jit(solution)/shard_map/ppermute | solution.py:114
  41.4 1.9 %collective-permute-start.29 = (bf16[32,896]{1,0:T(8,128)(2,1)S(1)}, bf16[32,896]{1,0:T(8,128)(2,1)S(1)}, u32[]{:S(2)}, u32[]{:S(2)}) collective-permute-start(bf16[32,896]{1,0:T(8,128)(2,1)S(1)} %collective-permute-done.28.refs_31_), channel_id=1, source_target_pairs={{0,1},{1,0},{2,3},{3,2},{4,5},{5,4},{6,7},{7,6},{8,9},{9,8},{10,11... | collective-permute-start | bytes 172040 | tf_op jit(solution)/shard_map/ppermute | solution.py:114
  41.4 3.2 %collective-permute-start.14 = (bf16[32,1024]{1,0:T(8,128)(2,1)S(1)}, bf16[32,1024]{1,0:T(8,128)(2,1)S(1)}, u32[]{:S(2)}, u32[]{:S(2)}) collective-permute-start(bf16[32,1024]{1,0:T(8,128)(2,1)S(1)} %collective-permute-done.13.refs_15_), channel_id=1, source_target_pairs={{0,1},{1,0},{2,3},{3,2},{4,5},{5,4},{6,7},{7,6},{8,9},{9,8},{10,11... | collective-permute-start | bytes 196616 | tf_op jit(solution)/shard_map/ppermute | solution.py:114
  42.7 1.9 %collective-permute-start.10 = (bf16[32,1024]{1,0:T(8,128)(2,1)S(1)}, bf16[32,1024]{1,0:T(8,128)(2,1)S(1)}, u32[]{:S(2)}, u32[]{:S(2)}) collective-permute-start(bf16[32,1024]{1,0:T(8,128)(2,1)S(1)} %collective-permute-done.9.refs_11_), channel_id=1, source_target_pairs={{0,1},{1,0},{2,3},{3,2},{4,5},{5,4},{6,7},{7,6},{8,9},{9,8},{10,11... | collective-permute-start | bytes 196616 | tf_op jit(solution)/shard_map/ppermute | solution.py:114
  42.7 1.9 %collective-permute-start.6 = (bf16[32,1024]{1,0:T(8,128)(2,1)S(1)}, bf16[32,1024]{1,0:T(8,128)(2,1)S(1)}, u32[]{:S(2)}, u32[]{:S(2)}) collective-permute-start(bf16[32,1024]{1,0:T(8,128)(2,1)S(1)} %collective-permute-done.5.refs_7_), channel_id=1, source_target_pairs={{0,1},{1,0},{2,3},{3,2},{4,5},{5,4},{6,7},{7,6},{8,9},{9,8},{10,11... | collective-permute-start | bytes 196616 | tf_op jit(solution)/shard_map/ppermute | solution.py:114
  43.2 1.2 %collective-permute-start.25 = (bf16[32,896]{1,0:T(8,128)(2,1)S(1)}, bf16[32,896]{1,0:T(8,128)(2,1)S(1)}, u32[]{:S(2)}, u32[]{:S(2)}) collective-permute-start(bf16[32,896]{1,0:T(8,128)(2,1)S(1)} %collective-permute-done.24.refs_27_), channel_id=1, source_target_pairs={{0,1},{1,0},{2,3},{3,2},{4,5},{5,4},{6,7},{7,6},{8,9},{9,8},{10,11... | collective-permute-start | bytes 172040 | tf_op jit(solution)/shard_map/ppermute | solution.py:114
  43.3 1.3 %collective-permute-start.21 = (bf16[32,896]{1,0:T(8,128)(2,1)S(1)}, bf16[32,896]{1,0:T(8,128)(2,1)S(1)}, u32[]{:S(2)}, u32[]{:S(2)}) collective-permute-start(bf16[32,896]{1,0:T(8,128)(2,1)S(1)} %collective-permute-done.20.refs_23_), channel_id=1, source_target_pairs={{0,1},{1,0},{2,3},{3,2},{4,5},{5,4},{6,7},{7,6},{8,9},{9,8},{10,11... | collective-permute-start | bytes 172040 | tf_op jit(solution)/shard_map/ppermute | solution.py:114
  46.6 3.0 %collective-permute-start.32 = (f32[1024]{0:T(1024)S(1)}, f32[1024]{0:T(1024)S(1)}, u32[]{:S(2)}, u32[]{:S(2)}) collective-permute-start(f32[1024]{0:T(1024)S(1)} %bitcast.2), channel_id=1, source_target_pairs={{0,3},{1,2},{2,1},{3,0},{4,7},{5,6},{6,5},{7,4},{8,11},{9,10},{10,... | collective-permute-start | bytes 12296 | tf_op jit(solution)/shard_map/ppermute | solution.py:114
  47.6 3.6 %collective-permute-start.31 = (f32[1024]{0:T(1024)S(1)}, f32[1024]{0:T(1024)S(1)}, u32[]{:S(2)}, u32[]{:S(2)}) collective-permute-start(f32[1024]{0:T(1024)S(1)} %bitcast.3), channel_id=1, source_target_pairs={{0,2},{1,3},{2,0},{3,1},{4,6},{5,7},{6,4},{7,5},{8,10},{9,11},{10,... | collective-permute-start | bytes 12296 | tf_op jit(solution)/shard_map/ppermute | solution.py:114
  48.6 2.6 %collective-permute-start.30 = (f32[1024]{0:T(1024)S(1)}, f32[1024]{0:T(1024)S(1)}, u32[]{:S(2)}, u32[]{:S(2)}) collective-permute-start(f32[1024]{0:T(1024)S(1)} %bitcast.4), channel_id=1, source_target_pairs={{0,1},{1,0},{2,3},{3,2},{4,5},{5,4},{6,7},{7,6},{8,9},{9,8},{10,11... | collective-permute-start | bytes 12296 | tf_op jit(solution)/shard_map/ppermute | solution.py:114
  51.2 5.5 %collective-permute-start.35 = (f32[1024]{0:T(1024)S(1)}, f32[1024]{0:T(1024)S(1)}, u32[]{:S(2)}, u32[]{:S(2)}) collective-permute-start(f32[1024]{0:T(1024)S(1)} %maximum_maximum_fusion.1), channel_id=1, source_target_pairs={{0,12},{1,13},{2,14},{3,15},{4,8},{5,9},{6,10},{7,11},{8,4},{9,5},... | collective-permute-start | bytes 12296 | tf_op jit(solution)/shard_map/ppermute | solution.py:114
  53.8 4.5 %collective-permute-start.34 = (f32[1024]{0:T(1024)S(1)}, f32[1024]{0:T(1024)S(1)}, u32[]{:S(2)}, u32[]{:S(2)}) collective-permute-start(f32[1024]{0:T(1024)S(1)} %maximum_maximum_fusion.1), channel_id=1, source_target_pairs={{0,8},{1,9},{2,10},{3,11},{4,12},{5,13},{6,14},{7,15},{8,0},{9,1},... | collective-permute-start | bytes 12296 | tf_op jit(solution)/shard_map/ppermute | solution.py:114
  54.1 4.2 %collective-permute-start.33 = (f32[1024]{0:T(1024)S(1)}, f32[1024]{0:T(1024)S(1)}, u32[]{:S(2)}, u32[]{:S(2)}) collective-permute-start(f32[1024]{0:T(1024)S(1)} %maximum_maximum_fusion.1), channel_id=1, source_target_pairs={{0,4},{1,5},{2,6},{3,7},{4,0},{5,1},{6,2},{7,3},{8,12},{9,13},{10,... | collective-permute-start | bytes 12296 | tf_op jit(solution)/shard_map/ppermute | solution.py:114

commit v2 on v1

--- a/solution.py
+++ b/solution.py
@@ -49,28 +49,33 @@
     return parts[0] if len(parts) == 1 else jnp.concatenate(parts, axis=1)
 
 
-def correlate_kernel(sections, *refs):
-    count = len(sections)
-    streams, taps_ref, out_ref = refs[:count], refs[count], refs[count + 1]
-    held_ref, sems = refs[count + 2], refs[count + 3]
+def correlate_kernel(*refs):
+    strain_refs, taps_ref, out_ref = refs[:4], refs[4], refs[5]
+    held_strains, held_taps, strain_sems, taps_sems = refs[6:10], refs[10], refs[11], refs[12]
     rows, taps = taps_ref.shape[1], taps_ref.shape[2]
-    copies = [
-        pltpu.make_async_copy(taps_ref.at[section], held_ref.at[number], sems.at[number])
-        for number, section in enumerate(sections)
-    ]
-    for copy in copies:
+    strain_copies, taps_copies = [], []
+    for section, source in enumerate(strain_refs):
+        copy = pltpu.make_async_copy(source, held_strains[section], strain_sems.at[section])
         copy.start()
+        strain_copies.append(copy)
+    for section in range(len(strain_refs)):
+        copy = pltpu.make_async_copy(
+            taps_ref.at[section], held_taps.at[section], taps_sems.at[section]
+        )
+        copy.start()
+        taps_copies.append(copy)
     place = 0
-    for number in range(count):
-        blocks = (streams[number].shape[0] - taps) // LANE
+    for section, strain in enumerate(held_strains):
+        strain_copies[section].wait()
+        blocks = (strain.shape[0] - taps) // LANE
         tiles = taps // LANE + blocks - 1
+        held = held_taps.at[section]
         total = None
         for tile in range(0, tiles, CHUNK):
             size = min(CHUNK, tiles - tile)
-            frames = build_frames(streams[number], tile * LANE, size)
+            frames = build_frames(strain, tile * LANE, size)
             if tile == 0:
-                copies[number].wait()
-            held = held_ref.at[number]
+                taps_copies[section].wait()
             left = jnp.concatenate(
                 [shifted_taps(held, tile * LANE, size * LANE, u) for u in range(blocks)], axis=0
             )
@@ -81,31 +86,31 @@
             place += LANE
 
 
-def correlate(streams, basis_taps, sections):
-    _, rows, taps = basis_taps.shape
+def correlate(streams, basis_taps):
+    sections, rows, taps = basis_taps.shape
     padded = -(-rows // SUB) * SUB
     if padded != rows:
         basis_taps = jnp.pad(basis_taps, ((0, 0), (0, padded - rows), (0, 0)))
-    used = [streams[section] for section in sections]
-    samples = sum(x.shape[0] - taps for x in used)
+    samples = sum(x.shape[0] - taps for x in streams)
     out = pl.pallas_call(
-        functools.partial(correlate_kernel, sections),
+        correlate_kernel,
         out_shape=jax.ShapeDtypeStruct((padded, samples), jnp.bfloat16),
-        in_specs=[pl.BlockSpec(memory_space=pltpu.VMEM)] * len(used)
-        + [pl.BlockSpec(memory_space=pl.ANY)],
+        in_specs=[pl.BlockSpec(memory_space=pltpu.HBM)] * (sections + 1),
         out_specs=pl.BlockSpec(memory_space=pltpu.VMEM),
-        scratch_shapes=[
-            pltpu.VMEM((len(used), padded, taps), jnp.bfloat16),
-            pltpu.SemaphoreType.DMA((len(used),)),
+        scratch_shapes=[pltpu.VMEM(x.shape, x.dtype) for x in streams]
+        + [
+            pltpu.VMEM((sections, padded, taps), jnp.bfloat16),
+            pltpu.SemaphoreType.DMA((sections,)),
+            pltpu.SemaphoreType.DMA((sections,)),
         ],
-        compiler_params=pltpu.CompilerParams(vmem_limit_bytes=16 * 2**20),
+        compiler_params=pltpu.CompilerParams(vmem_limit_bytes=60 * 2**20),
         cost_estimate=pl.CostEstimate(
             flops=2 * padded * taps * samples,
-            bytes_accessed=2 * len(used) * padded * taps,
+            bytes_accessed=2 * sections * padded * taps,
             transcendentals=0,
         ),
         name="correlate",
-    )(*used, basis_taps)
+    )(*streams, basis_taps)
     return out[:rows]
 
 
@@ -116,7 +121,14 @@
 
 def gather_blocks(block):
     size = lax.axis_size("tmpl")
-    merge = block.shape[0] % SUB != 0
+    if block.shape[0] % SUB:
+        stride = 1
+        while stride < size:
+            radix = 4 if size // stride >= 4 else 2
+            others = [exchange(block, step * stride) for step in range(1, radix)]
+            block = jnp.concatenate([block] + others, axis=0)
+            stride *= radix
+        return [block]
     held = {0: block}
     top = size
     while top > 1:
@@ -126,18 +138,15 @@
             for step in range(1, radix):
                 held[place + step * stride] = exchange(own, step * stride)
         top = stride
-    blocks = [held[place] for place in range(size)]
-    return [jnp.concatenate(blocks, axis=0)] if merge else blocks
+    return [held[place] for place in range(size)]
 
 
 def maximum_over_group(values):
     size = lax.axis_size("tmpl")
     stride = 1
     while stride < size:
-        radix = 4 if size // stride >= 4 else 2
-        others = [exchange(values, step * stride) for step in range(1, radix)]
-        values = functools.reduce(jnp.maximum, others, values)
-        stride *= radix
+        values = jnp.maximum(values, exchange(values, stride))
+        stride *= 2
     return values
 
 
@@ -171,9 +180,8 @@
     )(offset, coeffs)
 
 
-def recon_kernel(fast_count, *refs):
-    coeffs_ref, snr_ref, peak_ref = refs[0], refs[-2], refs[-1]
-    fast_refs, slow_refs = refs[1 : 1 + fast_count], refs[1 + fast_count : -2]
+def recon_kernel(coeffs_ref, *refs):
+    pieces, snr_ref, peak_ref = refs[:-2], refs[-2], refs[-1]
     samples = snr_ref.shape[1]
     source = lax.broadcasted_iota(jnp.int32, (2 * LANE, 2 * LANE), 0) % LANE
     target = lax.broadcasted_iota(jnp.int32, (2 * LANE, 2 * LANE), 1) // 2
@@ -181,8 +189,7 @@
     running = None
     for section in (3, 2, 1, 0):
         width = samples >> section
-        offset = sum(samples >> s for s in range(1, section))
-        pieces = slow_refs if section else fast_refs
+        offset = sum(samples >> s for s in range(section))
         summed = []
         for place in range(0, width, 2 * LANE):
             size = min(2 * LANE, width)
@@ -211,28 +218,27 @@
                 )
 
 
-def reconstruct(coeffs, fast, slow, samples):
+def reconstruct(coeffs, blocks, samples):
     return pl.pallas_call(
-        functools.partial(recon_kernel, len(fast)),
+        recon_kernel,
         out_shape=(
             jax.ShapeDtypeStruct((coeffs.shape[1], samples), jnp.bfloat16),
             jax.ShapeDtypeStruct((1, samples), jnp.float32),
         ),
-        in_specs=[pl.BlockSpec(memory_space=pltpu.VMEM)] * (1 + len(fast) + len(slow)),
+        in_specs=[pl.BlockSpec(memory_space=pltpu.VMEM)] * (1 + len(blocks)),
         out_specs=(pl.BlockSpec(memory_space=pltpu.VMEM),) * 2,
         compiler_params=pltpu.CompilerParams(vmem_limit_bytes=16 * 2**20),
         name="reconstruct",
-    )(coeffs, *fast, *slow)
+    )(coeffs, *blocks)
 
 
 def per_device(strain_fast, strain_half, strain_quarter, strain_eighth, basis_taps, recon_coeffs):
     streams = (strain_fast, strain_half, strain_quarter, strain_eighth)
     samples = strain_fast.shape[0] - basis_taps.shape[2]
     offset = (lax.axis_index("tmpl") * basis_taps.shape[1]).astype(jnp.int32).reshape(1)
-    fast = gather_blocks(correlate(streams, basis_taps, (0,)))
-    slow = gather_blocks(correlate(streams, basis_taps, (1, 2, 3)))
+    blocks = gather_blocks(correlate(streams, basis_taps))
     coeffs = arrange(recon_coeffs, offset)
-    snr_series, local_peak = reconstruct(coeffs, fast, slow, samples)
+    snr_series, local_peak = reconstruct(coeffs, blocks, samples)
     peak_snr = maximum_over_group(local_peak.reshape(samples))
     return (snr_series, peak_snr)
 

time: 59.3 us -> 51.7 us (0.87)
  starting transfers between devices: 26.5 us -> 16.6 us
  waiting for transfers between devices: 14.9 us -> 20.9 us
  local copies, waits for them, and re-layouts: 4.48 us -> 0.01 us
  Pallas kernels: 11.7 us -> 12.7 us
    ppermute x36 -> x19, starting transfers between devices: 26.5 us -> 16.6 us  [exchange(): return lax.ppermute(block, 'tmpl', [(i, i ^ distance) for i in range(size)])]
    ppermute x36 -> x19, waiting for transfers between devices: 14.9 us -> 20.9 us  [exchange(): return lax.ppermute(block, 'tmpl', [(i, i ^ distance) for i in range(size)])]
    unnamed x14 -> x4, local copies, waits for them, and re-layouts: 4.48 us -> 0.01 us
    pallas_call x3 -> x2, Pallas kernels: 11 us -> 12 us  [the longest x1 10.1 us: correlate(): pl.pallas_call(correlate_kernel, out_shape=jax.ShapeDtypeStruct((padded,...]
  transfers between devices with their start and end apart: 36 -> 19, of which waited for: 11 -> 9; matrix products, arithmetic and copies ran while one was open for 0% -> 0% of each run, Pallas kernels for 6% -> 1%
where the time goes in v2:
time: 51.7 us; the launch traced here: 51.6 us
  waiting for transfers between devices  20.9 us (40%)
  starting transfers between devices  16.6 us (32%)
  Pallas kernels  12.7 us (25%)
  between operations  0.72 us (1%)
  other arithmetic  0.6 us (1%)
    ppermute x19, waiting for transfers between devices, exchange(): return lax.ppermute(block, 'tmpl', [(i, i ^ distance) for i in range(size)])  20.9 us
    ppermute x19, starting transfers between devices, exchange(): return lax.ppermute(block, 'tmpl', [(i, i ^ distance) for i in range(size)])  16.6 us
    pallas_call x1, Pallas kernels, correlate(): pl.pallas_call(correlate_kernel, out_shape=jax.ShapeDtypeStruct((padded,...  10.1 us
    pallas_call x1, Pallas kernels, reconstruct(): pl.pallas_call(recon_kernel, out_shape=(jax.ShapeDtypeStruct((coeffs.shap...  1.95 us
  transfers between devices with their start and end apart: 19, of which 9 were waited for; matrix products, arithmetic and copies ran while one was open for 0% of the time, Pallas kernels for 1%

profile of v2, /device:TPU:0, one launch (start us, length us, event | category | flops | bytes accessed | tf_op | source)
XLA Modules:
  0.0 51.6 jit_solution(9934544168312822478)
XLA Ops:
  0.6 0.0 copy-start
  0.6 10.1 %correlate.1.refs_0_ = bf16[32,1920]{1,0:T(8,128)(2,1)} custom-call(bf16[9216]{0:T(1024)(128)(2,1)} %refs_0_.1, bf16[8704]{0:T(1024)(128)(2,1)} %refs_1_.1, bf16[8448]{0:T(1024)(128)(2,1)} %refs_2_.1, bf16[8320]{0:T(1024)(128)(2,1)} %refs_3_.1, bf16[4,32,8192]{2,1,0:T(8,128)(2,1)} %refs_4_.1), custom_call_target="tpu_custom_call" | custom-call | flops 1006632960 | bytes 2097152 | tf_op jit(solution)/shard_map/correlate/pallas_call | solution.py:95
  10.7 0.0 copy-start.1
  10.7 5.1 %collective-permute-start.11 = (bf16[32,1920]{1,0:T(8,128)(2,1)}, bf16[32,1920]{1,0:T(8,128)(2,1)S(1)}, u32[]{:S(2)}, u32[]{:S(2)}) collective-permute-start(bf16[32,1920]{1,0:T(8,128)(2,1)} %correlate.1.refs_0_), channel_id=1, source_target_pairs={{0,12},{1,13},{2,14},{3,15},{4,8},{5,9},{6,10},{7,11},{8,4},{9,5},... | collective-permute-start | bytes 368648 | tf_op jit(solution)/shard_map/ppermute | solution.py:119
  15.8 0.0 collective-permute-start.7
  15.8 0.6 %collective-permute-start.3 = (bf16[32,1920]{1,0:T(8,128)(2,1)}, bf16[32,1920]{1,0:T(8,128)(2,1)S(1)}, u32[]{:S(2)}, u32[]{:S(2)}) collective-permute-start(bf16[32,1920]{1,0:T(8,128)(2,1)} %correlate.1.refs_0_), channel_id=1, source_target_pairs={{0,4},{1,5},{2,6},{3,7},{4,0},{5,1},{6,2},{7,3},{8,12},{9,13},{10,... | collective-permute-start | bytes 368648 | tf_op jit(solution)/shard_map/ppermute | solution.py:119
  16.5 1.7 %collective-permute-start.1 = (bf16[32,1920]{1,0:T(8,128)(2,1)}, bf16[32,1920]{1,0:T(8,128)(2,1)S(1)}, u32[]{:S(2)}, u32[]{:S(2)}) collective-permute-start(bf16[32,1920]{1,0:T(8,128)(2,1)} %correlate.1.refs_0_), channel_id=1, source_target_pairs={{0,2},{1,3},{2,0},{3,1},{4,6},{5,7},{6,4},{7,5},{8,10},{9,11},{10,... | collective-permute-start | bytes 368648 | tf_op jit(solution)/shard_map/ppermute | solution.py:119
  18.1 0.0 collective-permute-start
  18.1 2.2 %collective-permute-done.11.refs_12_ = bf16[32,1920]{1,0:T(8,128)(2,1)S(1)} collective-permute-done((bf16[32,1920]{1,0:T(8,128)(2,1)}, bf16[32,1920]{1,0:T(8,128)(2,1)S(1)}, u32[]{:S(2)}, u32[]{:S(2)}) %collective-permute-start.11) | collective-permute-done | bytes 122912 | tf_op jit(solution)/shard_map/ppermute | solution.py:119
  20.3 1.7 %collective-permute-start.13 = (bf16[32,1920]{1,0:T(8,128)(2,1)S(1)}, bf16[32,1920]{1,0:T(8,128)(2,1)S(1)}, u32[]{:S(2)}, u32[]{:S(2)}) collective-permute-start(bf16[32,1920]{1,0:T(8,128)(2,1)S(1)} %collective-permute-done.11.refs_12_), channel_id=1, source_target_pairs={{0,2},{1,3},{2,0},{3,1},{4,6},{5,7},{6,4},{7,5},{8,10},{9,11},{10,... | collective-permute-start | bytes 368648 | tf_op jit(solution)/shard_map/ppermute | solution.py:119
  22.0 4.4 %collective-permute-done.7.refs_8_ = bf16[32,1920]{1,0:T(8,128)(2,1)S(1)} collective-permute-done((bf16[32,1920]{1,0:T(8,128)(2,1)}, bf16[32,1920]{1,0:T(8,128)(2,1)S(1)}, u32[]{:S(2)}, u32[]{:S(2)}) %collective-permute-start.7) | collective-permute-done | bytes 122912 | tf_op jit(solution)/shard_map/ppermute | solution.py:119
  26.4 0.0 collective-permute-start.12
  26.4 0.0 collective-permute-done.3.refs_4_
  26.4 1.5 %collective-permute-start.9 = (bf16[32,1920]{1,0:T(8,128)(2,1)S(1)}, bf16[32,1920]{1,0:T(8,128)(2,1)S(1)}, u32[]{:S(2)}, u32[]{:S(2)}) collective-permute-start(bf16[32,1920]{1,0:T(8,128)(2,1)S(1)} %collective-permute-done.7.refs_8_), channel_id=1, source_target_pairs={{0,2},{1,3},{2,0},{3,1},{4,6},{5,7},{6,4},{7,5},{8,10},{9,11},{10,... | collective-permute-start | bytes 368648 | tf_op jit(solution)/shard_map/ppermute | solution.py:119
  27.9 0.0 collective-permute-done.1.refs_2_
  27.9 0.2 collective-permute-start.8
  28.2 0.0 collective-permute-done.refs_1_
  28.2 0.5 collective-permute-start.5
  28.7 0.0 collective-permute-done.13.refs_14_
  28.7 0.0 collective-permute-start.4
  28.7 0.0 collective-permute-done.12.refs_13_
  28.7 0.5 collective-permute-start.2
  29.2 3.3 %collective-permute-done.9.refs_10_ = bf16[32,1920]{1,0:T(8,128)(2,1)S(1)} collective-permute-done((bf16[32,1920]{1,0:T(8,128)(2,1)S(1)}, bf16[32,1920]{1,0:T(8,128)(2,1)S(1)}, u32[]{:S(2)}, u32[]{:S(2)}) %collective-permute-start.9) | collective-permute-done | bytes 122912 | tf_op jit(solution)/shard_map/ppermute | solution.py:119
  32.5 0.0 collective-permute-start.14
  32.5 0.0 collective-permute-done.8.refs_9_
  32.5 0.5 collective-permute-start.10
  33.1 1.7 %collective-permute-done.5.refs_6_ = bf16[32,1920]{1,0:T(8,128)(2,1)S(1)} collective-permute-done((bf16[32,1920]{1,0:T(8,128)(2,1)S(1)}, bf16[32,1920]{1,0:T(8,128)(2,1)S(1)}, u32[]{:S(2)}, u32[]{:S(2)}) %collective-permute-start.5) | collective-permute-done | bytes 122912 | tf_op jit(solution)/shard_map/ppermute | solution.py:119
  34.8 0.0 collective-permute-start.6
  34.8 0.0 copy-done
  34.8 0.7 %arrange.1.coeffs_ref = bf16[4,256,512]{2,1,0:T(8,128)(2,1)S(1)} custom-call(s32[1]{0:T(128)} %bitcast.offset_ref, bf16[4,256,512]{2,1,0:T(8,128)(2,1)S(1)} %copy-done), custom_call_target="tpu_custom_call" | custom-call | flops 536870912 | bytes 2097152 | tf_op jit(solution)/shard_map/arrange/pallas_call | solution.py:165
  35.5 0.0 collective-permute-done.4.refs_5_
  35.5 0.0 collective-permute-done.2.refs_3_
  35.5 0.0 collective-permute-done.14.refs_15_
  35.6 0.0 collective-permute-done.10.refs_11_
  35.6 0.6 %collective-permute-done.6.refs_7_ = bf16[32,1920]{1,0:T(8,128)(2,1)S(1)} collective-permute-done((bf16[32,1920]{1,0:T(8,128)(2,1)S(1)}, bf16[32,1920]{1,0:T(8,128)(2,1)S(1)}, u32[]{:S(2)}, u32[]{:S(2)}) %collective-permute-start.6) | collective-permute-done | bytes 122912 | tf_op jit(solution)/shard_map/ppermute | solution.py:119
  36.1 0.0 copy-done.1
  36.1 2.0 %reconstruct.1 = (bf16[256,1024]{1,0:T(8,128)(2,1)}, f32[1,1024]{1,0:T(1,128)S(1)}) custom-call(bf16[4,256,512]{2,1,0:T(8,128)(2,1)S(1)} %arrange.1.coeffs_ref, bf16[32,1920]{1,0:T(8,128)(2,1)S(1)} %copy-done.1, bf16[32,1920]{1,0:T(8,128)(2,1)S(1)} %collective-permute-done.refs_1_, bf16[32,1920]{1,0:T(8,128)(2,1)S(1)} %collective-permute-done.1.refs_2_, ...), custom_call_target="tpu_custom_call" | custom-call | tf_op jit(solution)/shard_map/reconstruct/pallas_call | solution.py:222
  38.1 0.1 collective-permute-start.15
  38.2 1.0 %collective-permute-done.15 = f32[1024]{0:T(1024)S(1)} collective-permute-done((f32[1024]{0:T(1024)S(1)}, f32[1024]{0:T(1024)S(1)}, u32[]{:S(2)}, u32[]{:S(2)}) %collective-permute-start.15) | collective-permute-done | bytes 4128 | tf_op jit(solution)/shard_map/ppermute | solution.py:119
  39.2 1.5 %collective-permute-start.16 = (f32[1024]{0:T(1024)S(1)}, f32[1024]{0:T(1024)S(1)}, u32[]{:S(2)}, u32[]{:S(2)}) collective-permute-start(f32[1024]{0:T(1024)S(1)} %max.12), channel_id=1, source_target_pairs={{0,2},{1,3},{2,0},{3,1},{4,6},{5,7},{6,4},{7,5},{8,10},{9,11},{10,... | collective-permute-start | bytes 12296 | tf_op jit(solution)/shard_map/ppermute | solution.py:119
  40.8 2.1 %collective-permute-done.16 = f32[1024]{0:T(1024)S(1)} collective-permute-done((f32[1024]{0:T(1024)S(1)}, f32[1024]{0:T(1024)S(1)}, u32[]{:S(2)}, u32[]{:S(2)}) %collective-permute-start.16) | collective-permute-done | bytes 4128 | tf_op jit(solution)/shard_map/ppermute | solution.py:119
  42.9 0.7 %collective-permute-start.17 = (f32[1024]{0:T(1024)S(1)}, f32[1024]{0:T(1024)S(1)}, u32[]{:S(2)}, u32[]{:S(2)}) collective-permute-start(f32[1024]{0:T(1024)S(1)} %max.13), channel_id=1, source_target_pairs={{0,4},{1,5},{2,6},{3,7},{4,0},{5,1},{6,2},{7,3},{8,12},{9,13},{10,... | collective-permute-start | bytes 12296 | tf_op jit(solution)/shard_map/ppermute | solution.py:119
  43.5 2.9 %collective-permute-done.17 = f32[1024]{0:T(1024)S(1)} collective-permute-done((f32[1024]{0:T(1024)S(1)}, f32[1024]{0:T(1024)S(1)}, u32[]{:S(2)}, u32[]{:S(2)}) %collective-permute-start.17) | collective-permute-done | bytes 4128 | tf_op jit(solution)/shard_map/ppermute | solution.py:119
  46.5 1.9 %collective-permute-start.18 = (f32[1024]{0:T(1024)S(1)}, f32[1024]{0:T(1024)S(1)}, u32[]{:S(2)}, u32[]{:S(2)}) collective-permute-start(f32[1024]{0:T(1024)S(1)} %max.14), channel_id=1, source_target_pairs={{0,8},{1,9},{2,10},{3,11},{4,12},{5,13},{6,14},{7,15},{8,0},{9,1},... | collective-permute-start | bytes 12296 | tf_op jit(solution)/shard_map/ppermute | solution.py:119
  48.3 2.6 %collective-permute-done.18 = f32[1024]{0:T(1024)S(1)} collective-permute-done((f32[1024]{0:T(1024)S(1)}, f32[1024]{0:T(1024)S(1)}, u32[]{:S(2)}, u32[]{:S(2)}) %collective-permute-start.18) | collective-permute-done | bytes 4128 | tf_op jit(solution)/shard_map/ppermute | solution.py:119
  51.0 0.6 %max.15 = f32[1024]{0:T(1024)} maximum(f32[1024]{0:T(1024)S(1)} %max.14, f32[1024]{0:T(1024)S(1)} %collective-permute-done.18) | non-fusion elementwise | flops 1024 | bytes 12288 | tf_op jit(solution)/shard_map/max | solution.py:148
  (3 shorter events, 0.0 us)
Async XLA Ops:
  0.6 34.2 %copy-start = (bf16[4,256,512]{2,1,0:T(8,128)(2,1)S(1)}, bf16[4,256,512]{2,1,0:T(8,128)(2,1)}, u32[]{:S(2)}) copy-start(bf16[4,256,512]{2,1,0:T(8,128)(2,1)} %coeffs_ref.1) | copy-start | bytes 3145732
  10.7 25.4 %copy-start.1 = (bf16[32,1920]{1,0:T(8,128)(2,1)S(1)}, bf16[32,1920]{1,0:T(8,128)(2,1)}, u32[]{:S(2)}) copy-start(bf16[32,1920]{1,0:T(8,128)(2,1)} %correlate.1.refs_0_) | copy-start | bytes 368644
  10.7 9.6 %collective-permute-start.11 = (bf16[32,1920]{1,0:T(8,128)(2,1)}, bf16[32,1920]{1,0:T(8,128)(2,1)S(1)}, u32[]{:S(2)}, u32[]{:S(2)}) collective-permute-start(bf16[32,1920]{1,0:T(8,128)(2,1)} %correlate.1.refs_0_), channel_id=1, source_target_pairs={{0,12},{1,13},{2,14},{3,15},{4,8},{5,9},{6,10},{7,11},{8,4},{9,5},... | collective-permute-start | bytes 368648 | tf_op jit(solution)/shard_map/ppermute | solution.py:119
  15.8 10.6 %collective-permute-start.7 = (bf16[32,1920]{1,0:T(8,128)(2,1)}, bf16[32,1920]{1,0:T(8,128)(2,1)S(1)}, u32[]{:S(2)}, u32[]{:S(2)}) collective-permute-start(bf16[32,1920]{1,0:T(8,128)(2,1)} %correlate.1.refs_0_), channel_id=1, source_target_pairs={{0,8},{1,9},{2,10},{3,11},{4,12},{5,13},{6,14},{7,15},{8,0},{9,1},... | collective-permute-start | bytes 368648 | tf_op jit(solution)/shard_map/ppermute | solution.py:119
  15.8 10.6 %collective-permute-start.3 = (bf16[32,1920]{1,0:T(8,128)(2,1)}, bf16[32,1920]{1,0:T(8,128)(2,1)S(1)}, u32[]{:S(2)}, u32[]{:S(2)}) collective-permute-start(bf16[32,1920]{1,0:T(8,128)(2,1)} %correlate.1.refs_0_), channel_id=1, source_target_pairs={{0,4},{1,5},{2,6},{3,7},{4,0},{5,1},{6,2},{7,3},{8,12},{9,13},{10,... | collective-permute-start | bytes 368648 | tf_op jit(solution)/shard_map/ppermute | solution.py:119
  16.5 11.5 %collective-permute-start.1 = (bf16[32,1920]{1,0:T(8,128)(2,1)}, bf16[32,1920]{1,0:T(8,128)(2,1)S(1)}, u32[]{:S(2)}, u32[]{:S(2)}) collective-permute-start(bf16[32,1920]{1,0:T(8,128)(2,1)} %correlate.1.refs_0_), channel_id=1, source_target_pairs={{0,2},{1,3},{2,0},{3,1},{4,6},{5,7},{6,4},{7,5},{8,10},{9,11},{10,... | collective-permute-start | bytes 368648 | tf_op jit(solution)/shard_map/ppermute | solution.py:119
  18.1 10.0 %collective-permute-start = (bf16[32,1920]{1,0:T(8,128)(2,1)}, bf16[32,1920]{1,0:T(8,128)(2,1)S(1)}, u32[]{:S(2)}, u32[]{:S(2)}) collective-permute-start(bf16[32,1920]{1,0:T(8,128)(2,1)} %correlate.1.refs_0_), channel_id=1, source_target_pairs={{0,1},{1,0},{2,3},{3,2},{4,5},{5,4},{6,7},{7,6},{8,9},{9,8},{10,11... | collective-permute-start | bytes 368648 | tf_op jit(solution)/shard_map/ppermute | solution.py:119
  20.3 8.4 %collective-permute-start.13 = (bf16[32,1920]{1,0:T(8,128)(2,1)S(1)}, bf16[32,1920]{1,0:T(8,128)(2,1)S(1)}, u32[]{:S(2)}, u32[]{:S(2)}) collective-permute-start(bf16[32,1920]{1,0:T(8,128)(2,1)S(1)} %collective-permute-done.11.refs_12_), channel_id=1, source_target_pairs={{0,2},{1,3},{2,0},{3,1},{4,6},{5,7},{6,4},{7,5},{8,10},{9,11},{10,... | collective-permute-start | bytes 368648 | tf_op jit(solution)/shard_map/ppermute | solution.py:119
  26.4 2.3 %collective-permute-start.12 = (bf16[32,1920]{1,0:T(8,128)(2,1)S(1)}, bf16[32,1920]{1,0:T(8,128)(2,1)S(1)}, u32[]{:S(2)}, u32[]{:S(2)}) collective-permute-start(bf16[32,1920]{1,0:T(8,128)(2,1)S(1)} %collective-permute-done.11.refs_12_), channel_id=1, source_target_pairs={{0,1},{1,0},{2,3},{3,2},{4,5},{5,4},{6,7},{7,6},{8,9},{9,8},{10,11... | collective-permute-start | bytes 368648 | tf_op jit(solution)/shard_map/ppermute | solution.py:119
  26.4 6.1 %collective-permute-start.9 = (bf16[32,1920]{1,0:T(8,128)(2,1)S(1)}, bf16[32,1920]{1,0:T(8,128)(2,1)S(1)}, u32[]{:S(2)}, u32[]{:S(2)}) collective-permute-start(bf16[32,1920]{1,0:T(8,128)(2,1)S(1)} %collective-permute-done.7.refs_8_), channel_id=1, source_target_pairs={{0,2},{1,3},{2,0},{3,1},{4,6},{5,7},{6,4},{7,5},{8,10},{9,11},{10,... | collective-permute-start | bytes 368648 | tf_op jit(solution)/shard_map/ppermute | solution.py:119
  27.9 4.6 %collective-permute-start.8 = (bf16[32,1920]{1,0:T(8,128)(2,1)S(1)}, bf16[32,1920]{1,0:T(8,128)(2,1)S(1)}, u32[]{:S(2)}, u32[]{:S(2)}) collective-permute-start(bf16[32,1920]{1,0:T(8,128)(2,1)S(1)} %collective-permute-done.7.refs_8_), channel_id=1, source_target_pairs={{0,1},{1,0},{2,3},{3,2},{4,5},{5,4},{6,7},{7,6},{8,9},{9,8},{10,11... | collective-permute-start | bytes 368648 | tf_op jit(solution)/shard_map/ppermute | solution.py:119
  28.2 6.6 %collective-permute-start.5 = (bf16[32,1920]{1,0:T(8,128)(2,1)S(1)}, bf16[32,1920]{1,0:T(8,128)(2,1)S(1)}, u32[]{:S(2)}, u32[]{:S(2)}) collective-permute-start(bf16[32,1920]{1,0:T(8,128)(2,1)S(1)} %collective-permute-done.3.refs_4_), channel_id=1, source_target_pairs={{0,2},{1,3},{2,0},{3,1},{4,6},{5,7},{6,4},{7,5},{8,10},{9,11},{10,... | collective-permute-start | bytes 368648 | tf_op jit(solution)/shard_map/ppermute | solution.py:119
  28.7 6.8 %collective-permute-start.4 = (bf16[32,1920]{1,0:T(8,128)(2,1)S(1)}, bf16[32,1920]{1,0:T(8,128)(2,1)S(1)}, u32[]{:S(2)}, u32[]{:S(2)}) collective-permute-start(bf16[32,1920]{1,0:T(8,128)(2,1)S(1)} %collective-permute-done.3.refs_4_), channel_id=1, source_target_pairs={{0,1},{1,0},{2,3},{3,2},{4,5},{5,4},{6,7},{7,6},{8,9},{9,8},{10,11... | collective-permute-start | bytes 368648 | tf_op jit(solution)/shard_map/ppermute | solution.py:119
  28.7 6.8 %collective-permute-start.2 = (bf16[32,1920]{1,0:T(8,128)(2,1)S(1)}, bf16[32,1920]{1,0:T(8,128)(2,1)S(1)}, u32[]{:S(2)}, u32[]{:S(2)}) collective-permute-start(bf16[32,1920]{1,0:T(8,128)(2,1)S(1)} %collective-permute-done.1.refs_2_), channel_id=1, source_target_pairs={{0,1},{1,0},{2,3},{3,2},{4,5},{5,4},{6,7},{7,6},{8,9},{9,8},{10,11... | collective-permute-start | bytes 368648 | tf_op jit(solution)/shard_map/ppermute | solution.py:119
  32.5 3.0 %collective-permute-start.14 = (bf16[32,1920]{1,0:T(8,128)(2,1)S(1)}, bf16[32,1920]{1,0:T(8,128)(2,1)S(1)}, u32[]{:S(2)}, u32[]{:S(2)}) collective-permute-start(bf16[32,1920]{1,0:T(8,128)(2,1)S(1)} %collective-permute-done.13.refs_14_), channel_id=1, source_target_pairs={{0,1},{1,0},{2,3},{3,2},{4,5},{5,4},{6,7},{7,6},{8,9},{9,8},{10,11... | collective-permute-start | bytes 368648 | tf_op jit(solution)/shard_map/ppermute | solution.py:119
  32.5 3.0 %collective-permute-start.10 = (bf16[32,1920]{1,0:T(8,128)(2,1)S(1)}, bf16[32,1920]{1,0:T(8,128)(2,1)S(1)}, u32[]{:S(2)}, u32[]{:S(2)}) collective-permute-start(bf16[32,1920]{1,0:T(8,128)(2,1)S(1)} %collective-permute-done.9.refs_10_), channel_id=1, source_target_pairs={{0,1},{1,0},{2,3},{3,2},{4,5},{5,4},{6,7},{7,6},{8,9},{9,8},{10,11... | collective-permute-start | bytes 368648 | tf_op jit(solution)/shard_map/ppermute | solution.py:119
  34.8 1.3 %collective-permute-start.6 = (bf16[32,1920]{1,0:T(8,128)(2,1)S(1)}, bf16[32,1920]{1,0:T(8,128)(2,1)S(1)}, u32[]{:S(2)}, u32[]{:S(2)}) collective-permute-start(bf16[32,1920]{1,0:T(8,128)(2,1)S(1)} %collective-permute-done.5.refs_6_), channel_id=1, source_target_pairs={{0,1},{1,0},{2,3},{3,2},{4,5},{5,4},{6,7},{7,6},{8,9},{9,8},{10,11... | collective-permute-start | bytes 368648 | tf_op jit(solution)/shard_map/ppermute | solution.py:119
  38.1 1.2 %collective-permute-start.15 = (f32[1024]{0:T(1024)S(1)}, f32[1024]{0:T(1024)S(1)}, u32[]{:S(2)}, u32[]{:S(2)}) collective-permute-start(f32[1024]{0:T(1024)S(1)} %bitcast.2), channel_id=1, source_target_pairs={{0,1},{1,0},{2,3},{3,2},{4,5},{5,4},{6,7},{7,6},{8,9},{9,8},{10,11... | collective-permute-start | bytes 12296 | tf_op jit(solution)/shard_map/ppermute | solution.py:119
  39.2 3.6 %collective-permute-start.16 = (f32[1024]{0:T(1024)S(1)}, f32[1024]{0:T(1024)S(1)}, u32[]{:S(2)}, u32[]{:S(2)}) collective-permute-start(f32[1024]{0:T(1024)S(1)} %max.12), channel_id=1, source_target_pairs={{0,2},{1,3},{2,0},{3,1},{4,6},{5,7},{6,4},{7,5},{8,10},{9,11},{10,... | collective-permute-start | bytes 12296 | tf_op jit(solution)/shard_map/ppermute | solution.py:119
  42.9 3.6 %collective-permute-start.17 = (f32[1024]{0:T(1024)S(1)}, f32[1024]{0:T(1024)S(1)}, u32[]{:S(2)}, u32[]{:S(2)}) collective-permute-start(f32[1024]{0:T(1024)S(1)} %max.13), channel_id=1, source_target_pairs={{0,4},{1,5},{2,6},{3,7},{4,0},{5,1},{6,2},{7,3},{8,12},{9,13},{10,... | collective-permute-start | bytes 12296 | tf_op jit(solution)/shard_map/ppermute | solution.py:119
  46.5 4.5 %collective-permute-start.18 = (f32[1024]{0:T(1024)S(1)}, f32[1024]{0:T(1024)S(1)}, u32[]{:S(2)}, u32[]{:S(2)}) collective-permute-start(f32[1024]{0:T(1024)S(1)} %max.14), channel_id=1, source_target_pairs={{0,8},{1,9},{2,10},{3,11},{4,12},{5,13},{6,14},{7,15},{8,0},{9,1},... | collective-permute-start | bytes 12296 | tf_op jit(solution)/shard_map/ppermute | solution.py:119

commit v3 on v2

--- a/solution.py
+++ b/solution.py
@@ -10,14 +10,16 @@
 LANE = 128
 CHUNK = 8
 SUB = 16
+ROWS = 8
 
 
 def shifted_rows(x_ref, start, tiles):
     width = (tiles + 1) * LANE
-    wide = jnp.broadcast_to(x_ref[pl.ds(start, width)].reshape(1, width), (SUB, width))
-    row = lax.broadcasted_iota(jnp.int32, (SUB, width), 0)
+    line = x_ref[pl.ds(start, width)].reshape(1, width).astype(jnp.float32)
+    wide = jnp.broadcast_to(line, (ROWS, width))
+    row = lax.broadcasted_iota(jnp.int32, (ROWS, width), 0)
     step = 1
-    while step < SUB:
+    while step < ROWS:
         moved = pltpu.roll(wide, width - step, axis=1)
         wide = jnp.where((row & step) != 0, moved, wide)
         step *= 2
@@ -28,11 +30,15 @@
     wide = shifted_rows(x_ref, start, tiles)
     width = wide.shape[1]
     moved = [wide]
-    for q in range(1, LANE // SUB):
-        moved.append(pltpu.roll(wide, width - SUB * q, axis=1))
+    for q in range(1, LANE // ROWS):
+        moved.append(pltpu.roll(wide, width - ROWS * q, axis=1))
+    pairs = [
+        jnp.concatenate(moved[q : q + 2], axis=0).astype(jnp.bfloat16)
+        for q in range(0, len(moved), 2)
+    ]
     pieces = []
     for tile in range(tiles):
-        pieces += [part[:, tile * LANE : (tile + 1) * LANE] for part in moved]
+        pieces += [part[:, tile * LANE : (tile + 1) * LANE] for part in pairs]
     return jnp.concatenate(pieces, axis=0)
 
 
@@ -134,20 +140,19 @@
     while top > 1:
         radix = 4 if top > 4 and top % 4 == 0 else 2
         stride = top // radix
-        for place, own in list(held.items()):
-            for step in range(1, radix):
-                held[place + step * stride] = exchange(own, step * stride)
+        for place in reversed(list(held)):
+            for step in reversed(range(1, radix)):
+                held[place + step * stride] = exchange(held[place], step * stride)
         top = stride
     return [held[place] for place in range(size)]
 
 
 def maximum_over_group(values):
     size = lax.axis_size("tmpl")
-    stride = 1
-    while stride < size:
-        values = jnp.maximum(values, exchange(values, stride))
-        stride *= 2
-    return values
+    tiles = values.reshape(1, -1, LANE)
+    copies = jnp.broadcast_to(tiles, (size,) + tiles.shape[1:])
+    others = lax.all_to_all(copies, "tmpl", split_axis=0, concat_axis=0, tiled=True)
+    return jnp.max(others, axis=0).reshape(values.shape)
 
 
 def arrange_kernel(offset_ref, coeffs_ref, out_ref):

time: 51.7 us -> 52.4 us (1.014)
  blocking collectives: 0 us -> 11.5 us
  waiting for transfers between devices: 20.9 us -> 12.2 us
  starting transfers between devices: 16.6 us -> 12.4 us
  Pallas kernels: 12.7 us -> 14.8 us
    all_to_all x0 -> x1, blocking collectives: none -> 11.5 us  [maximum_over_group(): lax.all_to_all(copies, 'tmpl', split_axis=0, concat_axis=0, tiled=True)]
    ppermute x19 -> x15, waiting for transfers between devices: 20.9 us -> 12.2 us  [exchange(): return lax.ppermute(block, 'tmpl', [(i, i ^ distance) for i in range(size)])]
    ppermute x19 -> x15, starting transfers between devices: 16.6 us -> 12.4 us  [exchange(): return lax.ppermute(block, 'tmpl', [(i, i ^ distance) for i in range(size)])]
    pallas_call x1, Pallas kernels: 10.1 us -> 12.1 us  [correlate(): pl.pallas_call(correlate_kernel, out_shape=jax.ShapeDtypeStruct((padded,...]
    reduce_max x0 -> x1, other arithmetic: none -> 0.61 us  [maximum_over_group(): return jnp.max(others, axis=0).reshape(values.shape)]
    max x4 -> x0, other arithmetic: 0.6 us -> none  [maximum_over_group(): values = jnp.maximum(values, exchange(values, stride))]
  transfers between devices with their start and end apart: 19 -> 15, of which waited for: 9 -> 5; matrix products, arithmetic and copies ran while one was open for 0% -> 0% of each run, Pallas kernels for 1% -> 1%
where the time goes in v3:
time: 52.4 us; the launch traced here: 52.3 us
  Pallas kernels  14.8 us (28%)
  starting transfers between devices  12.4 us (24%)
  waiting for transfers between devices  12.2 us (23%)
  blocking collectives  11.5 us (22%)
  between operations  0.71 us (1%)
  other arithmetic  0.61 us (1%)
    ppermute x15, starting transfers between devices, exchange(): return lax.ppermute(block, 'tmpl', [(i, i ^ distance) for i in range(size)])  12.4 us
    ppermute x15, waiting for transfers between devices, exchange(): return lax.ppermute(block, 'tmpl', [(i, i ^ distance) for i in range(size)])  12.2 us
    pallas_call x1, Pallas kernels, correlate(): pl.pallas_call(correlate_kernel, out_shape=jax.ShapeDtypeStruct((padded,...  12.1 us
    all_to_all x1, blocking collectives, maximum_over_group(): lax.all_to_all(copies, 'tmpl', split_axis=0, concat_axis=0, tiled=True)  11.5 us
    pallas_call x1, Pallas kernels, reconstruct(): pl.pallas_call(recon_kernel, out_shape=(jax.ShapeDtypeStruct((coeffs.shap...  1.95 us
  transfers between devices with their start and end apart: 15, of which 5 were waited for; matrix products, arithmetic and copies ran while one was open for 0% of the time, Pallas kernels for 1%

profile of v3, /device:TPU:0, one launch (start us, length us, event | category | flops | bytes accessed | tf_op | source)
XLA Modules:
  0.0 52.3 jit_solution(8455903538241974336)
XLA Ops:
  0.6 0.0 copy-start
  0.6 12.1 %correlate.1.refs_0_ = bf16[32,1920]{1,0:T(8,128)(2,1)} custom-call(bf16[9216]{0:T(1024)(128)(2,1)} %refs_0_.1, bf16[8704]{0:T(1024)(128)(2,1)} %refs_1_.1, bf16[8448]{0:T(1024)(128)(2,1)} %refs_2_.1, bf16[8320]{0:T(1024)(128)(2,1)} %refs_3_.1, bf16[4,32,8192]{2,1,0:T(8,128)(2,1)} %refs_4_.1), custom_call_target="tpu_custom_call" | custom-call | flops 1006632960 | bytes 2097152 | tf_op jit(solution)/shard_map/correlate/pallas_call | solution.py:101
  12.8 0.0 copy-start.1
  12.8 5.1 %collective-permute-start.11 = (bf16[32,1920]{1,0:T(8,128)(2,1)}, bf16[32,1920]{1,0:T(8,128)(2,1)S(1)}, u32[]{:S(2)}, u32[]{:S(2)}) collective-permute-start(bf16[32,1920]{1,0:T(8,128)(2,1)} %correlate.1.refs_0_), channel_id=1, source_target_pairs={{0,12},{1,13},{2,14},{3,15},{4,8},{5,9},{6,10},{7,11},{8,4},{9,5},... | collective-permute-start | bytes 368648 | tf_op jit(solution)/shard_map/ppermute | solution.py:125
  17.9 0.0 collective-permute-start.7
  17.9 0.6 %collective-permute-start.3 = (bf16[32,1920]{1,0:T(8,128)(2,1)}, bf16[32,1920]{1,0:T(8,128)(2,1)S(1)}, u32[]{:S(2)}, u32[]{:S(2)}) collective-permute-start(bf16[32,1920]{1,0:T(8,128)(2,1)} %correlate.1.refs_0_), channel_id=1, source_target_pairs={{0,4},{1,5},{2,6},{3,7},{4,0},{5,1},{6,2},{7,3},{8,12},{9,13},{10,... | collective-permute-start | bytes 368648 | tf_op jit(solution)/shard_map/ppermute | solution.py:125
  18.5 1.7 %collective-permute-start.1 = (bf16[32,1920]{1,0:T(8,128)(2,1)}, bf16[32,1920]{1,0:T(8,128)(2,1)S(1)}, u32[]{:S(2)}, u32[]{:S(2)}) collective-permute-start(bf16[32,1920]{1,0:T(8,128)(2,1)} %correlate.1.refs_0_), channel_id=1, source_target_pairs={{0,2},{1,3},{2,0},{3,1},{4,6},{5,7},{6,4},{7,5},{8,10},{9,11},{10,... | collective-permute-start | bytes 368648 | tf_op jit(solution)/shard_map/ppermute | solution.py:125
  20.2 0.0 collective-permute-start
  20.2 2.1 %collective-permute-done.11.refs_12_ = bf16[32,1920]{1,0:T(8,128)(2,1)S(1)} collective-permute-done((bf16[32,1920]{1,0:T(8,128)(2,1)}, bf16[32,1920]{1,0:T(8,128)(2,1)S(1)}, u32[]{:S(2)}, u32[]{:S(2)}) %collective-permute-start.11) | collective-permute-done | bytes 122912 | tf_op jit(solution)/shard_map/ppermute | solution.py:125
  22.4 1.7 %collective-permute-start.13 = (bf16[32,1920]{1,0:T(8,128)(2,1)S(1)}, bf16[32,1920]{1,0:T(8,128)(2,1)S(1)}, u32[]{:S(2)}, u32[]{:S(2)}) collective-permute-start(bf16[32,1920]{1,0:T(8,128)(2,1)S(1)} %collective-permute-done.11.refs_12_), channel_id=1, source_target_pairs={{0,2},{1,3},{2,0},{3,1},{4,6},{5,7},{6,4},{7,5},{8,10},{9,11},{10,... | collective-permute-start | bytes 368648 | tf_op jit(solution)/shard_map/ppermute | solution.py:125
  24.1 4.4 %collective-permute-done.7.refs_8_ = bf16[32,1920]{1,0:T(8,128)(2,1)S(1)} collective-permute-done((bf16[32,1920]{1,0:T(8,128)(2,1)}, bf16[32,1920]{1,0:T(8,128)(2,1)S(1)}, u32[]{:S(2)}, u32[]{:S(2)}) %collective-permute-start.7) | collective-permute-done | bytes 122912 | tf_op jit(solution)/shard_map/ppermute | solution.py:125
  28.5 0.0 collective-permute-start.12
  28.5 0.0 collective-permute-done.3.refs_4_
  28.5 1.5 %collective-permute-start.9 = (bf16[32,1920]{1,0:T(8,128)(2,1)S(1)}, bf16[32,1920]{1,0:T(8,128)(2,1)S(1)}, u32[]{:S(2)}, u32[]{:S(2)}) collective-permute-start(bf16[32,1920]{1,0:T(8,128)(2,1)S(1)} %collective-permute-done.7.refs_8_), channel_id=1, source_target_pairs={{0,2},{1,3},{2,0},{3,1},{4,6},{5,7},{6,4},{7,5},{8,10},{9,11},{10,... | collective-permute-start | bytes 368648 | tf_op jit(solution)/shard_map/ppermute | solution.py:125
  30.0 0.0 collective-permute-done.1.refs_2_
  30.0 0.2 collective-permute-start.8
  30.2 0.0 collective-permute-done.refs_1_
  30.2 0.5 collective-permute-start.5
  30.8 0.0 collective-permute-done.13.refs_14_
  30.8 0.0 collective-permute-start.4
  30.8 0.0 collective-permute-done.12.refs_13_
  30.8 0.5 collective-permute-start.2
  31.3 3.3 %collective-permute-done.9.refs_10_ = bf16[32,1920]{1,0:T(8,128)(2,1)S(1)} collective-permute-done((bf16[32,1920]{1,0:T(8,128)(2,1)S(1)}, bf16[32,1920]{1,0:T(8,128)(2,1)S(1)}, u32[]{:S(2)}, u32[]{:S(2)}) %collective-permute-start.9) | collective-permute-done | bytes 122912 | tf_op jit(solution)/shard_map/ppermute | solution.py:125
  34.6 0.0 collective-permute-start.14
  34.6 0.0 collective-permute-done.8.refs_9_
  34.6 0.5 collective-permute-start.10
  35.1 1.7 %collective-permute-done.5.refs_6_ = bf16[32,1920]{1,0:T(8,128)(2,1)S(1)} collective-permute-done((bf16[32,1920]{1,0:T(8,128)(2,1)S(1)}, bf16[32,1920]{1,0:T(8,128)(2,1)S(1)}, u32[]{:S(2)}, u32[]{:S(2)}) %collective-permute-start.5) | collective-permute-done | bytes 122912 | tf_op jit(solution)/shard_map/ppermute | solution.py:125
  36.9 0.0 collective-permute-start.6
  36.9 0.0 copy-done
  36.9 0.7 %arrange.1.coeffs_ref = bf16[4,256,512]{2,1,0:T(8,128)(2,1)S(1)} custom-call(s32[1]{0:T(128)} %bitcast.offset_ref, bf16[4,256,512]{2,1,0:T(8,128)(2,1)S(1)} %copy-done), custom_call_target="tpu_custom_call" | custom-call | flops 536870912 | bytes 2097152 | tf_op jit(solution)/shard_map/arrange/pallas_call | solution.py:170
  37.6 0.0 collective-permute-done.4.refs_5_
  37.6 0.0 collective-permute-done.2.refs_3_
  37.6 0.0 collective-permute-done.14.refs_15_
  37.6 0.0 collective-permute-done.10.refs_11_
  37.6 0.6 %collective-permute-done.6.refs_7_ = bf16[32,1920]{1,0:T(8,128)(2,1)S(1)} collective-permute-done((bf16[32,1920]{1,0:T(8,128)(2,1)S(1)}, bf16[32,1920]{1,0:T(8,128)(2,1)S(1)}, u32[]{:S(2)}, u32[]{:S(2)}) %collective-permute-start.6) | collective-permute-done | bytes 122912 | tf_op jit(solution)/shard_map/ppermute | solution.py:125
  38.2 0.0 copy-done.1
  38.2 2.0 %reconstruct.1 = (bf16[256,1024]{1,0:T(8,128)(2,1)}, f32[1,1024]{1,0:T(1,128)S(1)}) custom-call(bf16[4,256,512]{2,1,0:T(8,128)(2,1)S(1)} %arrange.1.coeffs_ref, bf16[32,1920]{1,0:T(8,128)(2,1)S(1)} %copy-done.1, bf16[32,1920]{1,0:T(8,128)(2,1)S(1)} %collective-permute-done.refs_1_, bf16[32,1920]{1,0:T(8,128)(2,1)S(1)} %collective-permute-done.1.refs_2_, ...), custom_call_target="tpu_custom_call" | custom-call | tf_op jit(solution)/shard_map/reconstruct/pallas_call | solution.py:227
  40.2 11.5 %all_to_all.5 = f32[16,8,128]{2,1,0:T(8,128)S(1)} all-to-all(f32[16,8,128]{2,1,0:T(8,128)S(1)} %broadcast_in_dim.8), channel_id=1, replica_groups=mesh['bank'=2,'tmpl'=16] {'tmpl'}, dimensions={0} | all-to-all | bytes 131072 | tf_op jit(solution)/shard_map/all_to_all | solution.py:154
  51.7 0.6 %reduce_max.9 = f32[8,128]{1,0:T(8,128)} reduce(f32[16,8,128]{2,1,0:T(8,128)S(1)} %all_to_all.5, f32[]{:T(128)} %constant.2.clone.1), dimensions={0}, to_apply=%region_0.0 | reduce | flops 15360 | bytes 69636 | tf_op jit(solution)/shard_map/reduce_max | solution.py:155
  (1 shorter events, 0.0 us)
Async XLA Ops:
  0.6 36.2 %copy-start = (bf16[4,256,512]{2,1,0:T(8,128)(2,1)S(1)}, bf16[4,256,512]{2,1,0:T(8,128)(2,1)}, u32[]{:S(2)}) copy-start(bf16[4,256,512]{2,1,0:T(8,128)(2,1)} %coeffs_ref.1) | copy-start | bytes 3145732
  12.8 25.4 %copy-start.1 = (bf16[32,1920]{1,0:T(8,128)(2,1)S(1)}, bf16[32,1920]{1,0:T(8,128)(2,1)}, u32[]{:S(2)}) copy-start(bf16[32,1920]{1,0:T(8,128)(2,1)} %correlate.1.refs_0_) | copy-start | bytes 368644
  12.8 9.6 %collective-permute-start.11 = (bf16[32,1920]{1,0:T(8,128)(2,1)}, bf16[32,1920]{1,0:T(8,128)(2,1)S(1)}, u32[]{:S(2)}, u32[]{:S(2)}) collective-permute-start(bf16[32,1920]{1,0:T(8,128)(2,1)} %correlate.1.refs_0_), channel_id=1, source_target_pairs={{0,12},{1,13},{2,14},{3,15},{4,8},{5,9},{6,10},{7,11},{8,4},{9,5},... | collective-permute-start | bytes 368648 | tf_op jit(solution)/shard_map/ppermute | solution.py:125
  17.9 10.6 %collective-permute-start.7 = (bf16[32,1920]{1,0:T(8,128)(2,1)}, bf16[32,1920]{1,0:T(8,128)(2,1)S(1)}, u32[]{:S(2)}, u32[]{:S(2)}) collective-permute-start(bf16[32,1920]{1,0:T(8,128)(2,1)} %correlate.1.refs_0_), channel_id=1, source_target_pairs={{0,8},{1,9},{2,10},{3,11},{4,12},{5,13},{6,14},{7,15},{8,0},{9,1},... | collective-permute-start | bytes 368648 | tf_op jit(solution)/shard_map/ppermute | solution.py:125
  17.9 10.6 %collective-permute-start.3 = (bf16[32,1920]{1,0:T(8,128)(2,1)}, bf16[32,1920]{1,0:T(8,128)(2,1)S(1)}, u32[]{:S(2)}, u32[]{:S(2)}) collective-permute-start(bf16[32,1920]{1,0:T(8,128)(2,1)} %correlate.1.refs_0_), channel_id=1, source_target_pairs={{0,4},{1,5},{2,6},{3,7},{4,0},{5,1},{6,2},{7,3},{8,12},{9,13},{10,... | collective-permute-start | bytes 368648 | tf_op jit(solution)/shard_map/ppermute | solution.py:125
  18.5 11.5 %collective-permute-start.1 = (bf16[32,1920]{1,0:T(8,128)(2,1)}, bf16[32,1920]{1,0:T(8,128)(2,1)S(1)}, u32[]{:S(2)}, u32[]{:S(2)}) collective-permute-start(bf16[32,1920]{1,0:T(8,128)(2,1)} %correlate.1.refs_0_), channel_id=1, source_target_pairs={{0,2},{1,3},{2,0},{3,1},{4,6},{5,7},{6,4},{7,5},{8,10},{9,11},{10,... | collective-permute-start | bytes 368648 | tf_op jit(solution)/shard_map/ppermute | solution.py:125
  20.2 10.0 %collective-permute-start = (bf16[32,1920]{1,0:T(8,128)(2,1)}, bf16[32,1920]{1,0:T(8,128)(2,1)S(1)}, u32[]{:S(2)}, u32[]{:S(2)}) collective-permute-start(bf16[32,1920]{1,0:T(8,128)(2,1)} %correlate.1.refs_0_), channel_id=1, source_target_pairs={{0,1},{1,0},{2,3},{3,2},{4,5},{5,4},{6,7},{7,6},{8,9},{9,8},{10,11... | collective-permute-start | bytes 368648 | tf_op jit(solution)/shard_map/ppermute | solution.py:125
  22.4 8.4 %collective-permute-start.13 = (bf16[32,1920]{1,0:T(8,128)(2,1)S(1)}, bf16[32,1920]{1,0:T(8,128)(2,1)S(1)}, u32[]{:S(2)}, u32[]{:S(2)}) collective-permute-start(bf16[32,1920]{1,0:T(8,128)(2,1)S(1)} %collective-permute-done.11.refs_12_), channel_id=1, source_target_pairs={{0,2},{1,3},{2,0},{3,1},{4,6},{5,7},{6,4},{7,5},{8,10},{9,11},{10,... | collective-permute-start | bytes 368648 | tf_op jit(solution)/shard_map/ppermute | solution.py:125
  28.5 2.3 %collective-permute-start.12 = (bf16[32,1920]{1,0:T(8,128)(2,1)S(1)}, bf16[32,1920]{1,0:T(8,128)(2,1)S(1)}, u32[]{:S(2)}, u32[]{:S(2)}) collective-permute-start(bf16[32,1920]{1,0:T(8,128)(2,1)S(1)} %collective-permute-done.11.refs_12_), channel_id=1, source_target_pairs={{0,1},{1,0},{2,3},{3,2},{4,5},{5,4},{6,7},{7,6},{8,9},{9,8},{10,11... | collective-permute-start | bytes 368648 | tf_op jit(solution)/shard_map/ppermute | solution.py:125
  28.5 6.1 %collective-permute-start.9 = (bf16[32,1920]{1,0:T(8,128)(2,1)S(1)}, bf16[32,1920]{1,0:T(8,128)(2,1)S(1)}, u32[]{:S(2)}, u32[]{:S(2)}) collective-permute-start(bf16[32,1920]{1,0:T(8,128)(2,1)S(1)} %collective-permute-done.7.refs_8_), channel_id=1, source_target_pairs={{0,2},{1,3},{2,0},{3,1},{4,6},{5,7},{6,4},{7,5},{8,10},{9,11},{10,... | collective-permute-start | bytes 368648 | tf_op jit(solution)/shard_map/ppermute | solution.py:125
  30.0 4.6 %collective-permute-start.8 = (bf16[32,1920]{1,0:T(8,128)(2,1)S(1)}, bf16[32,1920]{1,0:T(8,128)(2,1)S(1)}, u32[]{:S(2)}, u32[]{:S(2)}) collective-permute-start(bf16[32,1920]{1,0:T(8,128)(2,1)S(1)} %collective-permute-done.7.refs_8_), channel_id=1, source_target_pairs={{0,1},{1,0},{2,3},{3,2},{4,5},{5,4},{6,7},{7,6},{8,9},{9,8},{10,11... | collective-permute-start | bytes 368648 | tf_op jit(solution)/shard_map/ppermute | solution.py:125
  30.2 6.6 %collective-permute-start.5 = (bf16[32,1920]{1,0:T(8,128)(2,1)S(1)}, bf16[32,1920]{1,0:T(8,128)(2,1)S(1)}, u32[]{:S(2)}, u32[]{:S(2)}) collective-permute-start(bf16[32,1920]{1,0:T(8,128)(2,1)S(1)} %collective-permute-done.3.refs_4_), channel_id=1, source_target_pairs={{0,2},{1,3},{2,0},{3,1},{4,6},{5,7},{6,4},{7,5},{8,10},{9,11},{10,... | collective-permute-start | bytes 368648 | tf_op jit(solution)/shard_map/ppermute | solution.py:125
  30.8 6.8 %collective-permute-start.4 = (bf16[32,1920]{1,0:T(8,128)(2,1)S(1)}, bf16[32,1920]{1,0:T(8,128)(2,1)S(1)}, u32[]{:S(2)}, u32[]{:S(2)}) collective-permute-start(bf16[32,1920]{1,0:T(8,128)(2,1)S(1)} %collective-permute-done.3.refs_4_), channel_id=1, source_target_pairs={{0,1},{1,0},{2,3},{3,2},{4,5},{5,4},{6,7},{7,6},{8,9},{9,8},{10,11... | collective-permute-start | bytes 368648 | tf_op jit(solution)/shard_map/ppermute | solution.py:125
  30.8 6.8 %collective-permute-start.2 = (bf16[32,1920]{1,0:T(8,128)(2,1)S(1)}, bf16[32,1920]{1,0:T(8,128)(2,1)S(1)}, u32[]{:S(2)}, u32[]{:S(2)}) collective-permute-start(bf16[32,1920]{1,0:T(8,128)(2,1)S(1)} %collective-permute-done.1.refs_2_), channel_id=1, source_target_pairs={{0,1},{1,0},{2,3},{3,2},{4,5},{5,4},{6,7},{7,6},{8,9},{9,8},{10,11... | collective-permute-start | bytes 368648 | tf_op jit(solution)/shard_map/ppermute | solution.py:125
  34.6 3.0 %collective-permute-start.14 = (bf16[32,1920]{1,0:T(8,128)(2,1)S(1)}, bf16[32,1920]{1,0:T(8,128)(2,1)S(1)}, u32[]{:S(2)}, u32[]{:S(2)}) collective-permute-start(bf16[32,1920]{1,0:T(8,128)(2,1)S(1)} %collective-permute-done.13.refs_14_), channel_id=1, source_target_pairs={{0,1},{1,0},{2,3},{3,2},{4,5},{5,4},{6,7},{7,6},{8,9},{9,8},{10,11... | collective-permute-start | bytes 368648 | tf_op jit(solution)/shard_map/ppermute | solution.py:125
  34.6 3.0 %collective-permute-start.10 = (bf16[32,1920]{1,0:T(8,128)(2,1)S(1)}, bf16[32,1920]{1,0:T(8,128)(2,1)S(1)}, u32[]{:S(2)}, u32[]{:S(2)}) collective-permute-start(bf16[32,1920]{1,0:T(8,128)(2,1)S(1)} %collective-permute-done.9.refs_10_), channel_id=1, source_target_pairs={{0,1},{1,0},{2,3},{3,2},{4,5},{5,4},{6,7},{7,6},{8,9},{9,8},{10,11... | collective-permute-start | bytes 368648 | tf_op jit(solution)/shard_map/ppermute | solution.py:125
  36.9 1.3 %collective-permute-start.6 = (bf16[32,1920]{1,0:T(8,128)(2,1)S(1)}, bf16[32,1920]{1,0:T(8,128)(2,1)S(1)}, u32[]{:S(2)}, u32[]{:S(2)}) collective-permute-start(bf16[32,1920]{1,0:T(8,128)(2,1)S(1)} %collective-permute-done.5.refs_6_), channel_id=1, source_target_pairs={{0,1},{1,0},{2,3},{3,2},{4,5},{5,4},{6,7},{7,6},{8,9},{9,8},{10,11... | collective-permute-start | bytes 368648 | tf_op jit(solution)/shard_map/ppermute | solution.py:125

commit v4 on v2

--- a/solution.py
+++ b/solution.py
@@ -12,8 +12,8 @@
 SUB = 16
 
 
-def shifted_rows(x_ref, start, tiles):
-    width = (tiles + 1) * LANE
+def build_frames(x_ref, start, tiles, cols):
+    width = tiles * LANE + cols
     wide = jnp.broadcast_to(x_ref[pl.ds(start, width)].reshape(1, width), (SUB, width))
     row = lax.broadcasted_iota(jnp.int32, (SUB, width), 0)
     step = 1
@@ -21,69 +21,81 @@
         moved = pltpu.roll(wide, width - step, axis=1)
         wide = jnp.where((row & step) != 0, moved, wide)
         step *= 2
-    return wide
-
-
-def build_frames(x_ref, start, tiles):
-    wide = shifted_rows(x_ref, start, tiles)
-    width = wide.shape[1]
     moved = [wide]
     for q in range(1, LANE // SUB):
         moved.append(pltpu.roll(wide, width - SUB * q, axis=1))
     pieces = []
     for tile in range(tiles):
-        pieces += [part[:, tile * LANE : (tile + 1) * LANE] for part in moved]
+        pieces += [part[:, tile * LANE : tile * LANE + cols] for part in moved]
     return jnp.concatenate(pieces, axis=0)
-
-
-def shifted_taps(taps_ref, start, width, u):
-    rows, taps = taps_ref.shape
-    first, last = start - u * LANE, start - u * LANE + width
-    parts = []
-    if first < 0:
-        parts.append(jnp.zeros((rows, -first), taps_ref.dtype))
-    if last > 0 and first < taps:
-        parts.append(taps_ref[:, max(first, 0) : min(last, taps)])
-    if last > taps:
-        parts.append(jnp.zeros((rows, last - taps), taps_ref.dtype))
-    return parts[0] if len(parts) == 1 else jnp.concatenate(parts, axis=1)
 
 
 def correlate_kernel(*refs):
     strain_refs, taps_ref, out_ref = refs[:4], refs[4], refs[5]
     held_strains, held_taps, strain_sems, taps_sems = refs[6:10], refs[10], refs[11], refs[12]
+    sections = len(strain_refs)
     rows, taps = taps_ref.shape[1], taps_ref.shape[2]
-    strain_copies, taps_copies = [], []
+    pad = (held_taps.shape[2] - taps) // 2
+    copies = []
     for section, source in enumerate(strain_refs):
-        copy = pltpu.make_async_copy(source, held_strains[section], strain_sems.at[section])
+        copies.append(
+            pltpu.make_async_copy(source, held_strains[section], strain_sems.at[section])
+        )
+        copies.append(
+            pltpu.make_async_copy(
+                taps_ref.at[section],
+                held_taps.at[section, :, pl.ds(pad, taps)],
+                taps_sems.at[section],
+            )
+        )
+    for copy in copies:
         copy.start()
-        strain_copies.append(copy)
-    for section in range(len(strain_refs)):
-        copy = pltpu.make_async_copy(
-            taps_ref.at[section], held_taps.at[section], taps_sems.at[section]
+    samples = [ref.shape[0] - taps for ref in held_strains]
+    cols = [min(2 * LANE, count) for count in samples]
+    blocks = [count // size for count, size in zip(samples, cols)]
+    for section in range(sections):
+        if blocks[section] > 1:
+            zeros = jnp.zeros((rows, pad), held_taps.dtype)
+            held_taps[section, :, :pad] = zeros
+            held_taps[section, :, pad + taps :] = zeros
+    for copy in copies:
+        copy.wait()
+
+    def term(section, start, tiles):
+        frames = build_frames(held_strains[section], start, tiles, cols[section])
+        left = []
+        for u in range(blocks[section]):
+            first = pad + start - u * cols[section]
+            if not isinstance(first, int):
+                first = pl.multiple_of(first, LANE)
+            left.append(held_taps[section, :, pl.ds(first, tiles * LANE)])
+        left = left[0] if len(left) == 1 else jnp.concatenate(left, axis=0)
+        return jnp.dot(left, frames, preferred_element_type=jnp.float32)
+
+    def step(number, totals):
+        start = pl.multiple_of(number * (CHUNK * LANE), CHUNK * LANE)
+        return tuple(
+            total + term(section, start, CHUNK) for section, total in enumerate(totals)
         )
-        copy.start()
-        taps_copies.append(copy)
+
+    totals = lax.fori_loop(
+        0,
+        taps // (CHUNK * LANE),
+        step,
+        tuple(
+            jnp.zeros((blocks[section] * rows, cols[section]), jnp.float32)
+            for section in range(sections)
+        ),
+    )
     place = 0
-    for section, strain in enumerate(held_strains):
-        strain_copies[section].wait()
-        blocks = (strain.shape[0] - taps) // LANE
-        tiles = taps // LANE + blocks - 1
-        held = held_taps.at[section]
-        total = None
-        for tile in range(0, tiles, CHUNK):
-            size = min(CHUNK, tiles - tile)
-            frames = build_frames(strain, tile * LANE, size)
-            if tile == 0:
-                taps_copies[section].wait()
-            left = jnp.concatenate(
-                [shifted_taps(held, tile * LANE, size * LANE, u) for u in range(blocks)], axis=0
-            )
-            part = jnp.dot(left, frames, preferred_element_type=jnp.float32)
-            total = part if total is None else total + part
-        for u in range(blocks):
-            out_ref[:, place : place + LANE] = total[u * rows : (u + 1) * rows].astype(out_ref.dtype)
-            place += LANE
+    for section, total in enumerate(totals):
+        extra = (blocks[section] - 1) * cols[section] // LANE
+        for tile in range(0, extra, CHUNK):
+            total = total + term(section, taps + tile * LANE, min(CHUNK, extra - tile))
+        for u in range(blocks[section]):
+            part = total[u * rows : (u + 1) * rows].astype(out_ref.dtype)
+            out_ref[:, place : place + cols[section]] = part
+            place += cols[section]
 
 
 def correlate(streams, basis_taps):
@@ -92,6 +104,7 @@
     if padded != rows:
         basis_taps = jnp.pad(basis_taps, ((0, 0), (0, padded - rows), (0, 0)))
     samples = sum(x.shape[0] - taps for x in streams)
+    pad = max(x.shape[0] - taps for x in streams) - 2 * LANE
     out = pl.pallas_call(
         correlate_kernel,
         out_shape=jax.ShapeDtypeStruct((padded, samples), jnp.bfloat16),
@@ -99,7 +112,7 @@
         out_specs=pl.BlockSpec(memory_space=pltpu.VMEM),
         scratch_shapes=[pltpu.VMEM(x.shape, x.dtype) for x in streams]
         + [
-            pltpu.VMEM((sections, padded, taps), jnp.bfloat16),
+            pltpu.VMEM((sections, padded, taps + 2 * pad), jnp.bfloat16),
             pltpu.SemaphoreType.DMA((sections,)),
             pltpu.SemaphoreType.DMA((sections,)),
         ],
@@ -134,20 +147,23 @@
     while top > 1:
         radix = 4 if top > 4 and top % 4 == 0 else 2
         stride = top // radix
-        for place, own in list(held.items()):
-            for step in range(1, radix):
-                held[place + step * stride] = exchange(own, step * stride)
+        for place in reversed(list(held)):
+            for step in reversed(range(1, radix)):
+                held[place + step * stride] = exchange(held[place], step * stride)
         top = stride
     return [held[place] for place in range(size)]
 
 
 def maximum_over_group(values):
     size = lax.axis_size("tmpl")
-    stride = 1
-    while stride < size:
-        values = jnp.maximum(values, exchange(values, stride))
-        stride *= 2
-    return values
+    values = jnp.maximum(values, exchange(values, 1))
+    tiles = values.reshape(1, -1, LANE)
+    copies = jnp.broadcast_to(tiles, (size // 2,) + tiles.shape[1:])
+    groups = [list(range(core, size, 2)) for core in range(2)]
+    others = lax.all_to_all(
+        copies, "tmpl", split_axis=0, concat_axis=0, axis_index_groups=groups, tiled=True
+    )
+    return jnp.max(others, axis=0).reshape(values.shape)
 
 
 def arrange_kernel(offset_ref, coeffs_ref, out_ref):
@@ -181,7 +197,7 @@
 
 
 def recon_kernel(coeffs_ref, *refs):
-    pieces, snr_ref, peak_ref = refs[:-2], refs[-2], refs[-1]
+    pieces, snr_ref, peak_ref = refs[-3::-1], refs[-2], refs[-1]
     samples = snr_ref.shape[1]
     source = lax.broadcasted_iota(jnp.int32, (2 * LANE, 2 * LANE), 0) % LANE
     target = lax.broadcasted_iota(jnp.int32, (2 * LANE, 2 * LANE), 1) // 2
@@ -229,7 +245,7 @@
         out_specs=(pl.BlockSpec(memory_space=pltpu.VMEM),) * 2,
         compiler_params=pltpu.CompilerParams(vmem_limit_bytes=16 * 2**20),
         name="reconstruct",
-    )(coeffs, *blocks)
+    )(coeffs, *blocks[::-1])
 
 
 def per_device(strain_fast, strain_half, strain_quarter, strain_eighth, basis_taps, recon_coeffs):

time: 51.7 us -> 50.6 us (0.979)
  blocking collectives: 0 us -> 10.2 us
  starting transfers between devices: 16.6 us -> 10.9 us
  waiting for transfers between devices: 20.9 us -> 15.3 us
    all_to_all x0 -> x1, blocking collectives: none -> 10.2 us  [maximum_over_group(): lax.all_to_all(copies, 'tmpl', split_axis=0, concat_axis=0, axis_index_gr...]
    ppermute x19 -> x16, starting transfers between devices: 16.6 us -> 10.9 us  [exchange(): return lax.ppermute(block, 'tmpl', [(i, i ^ distance) for i in range(size)])]
    ppermute x19 -> x16, waiting for transfers between devices: 20.9 us -> 15.3 us  [exchange(): return lax.ppermute(block, 'tmpl', [(i, i ^ distance) for i in range(size)])]
    max x4 -> x0, other arithmetic: 0.6 us -> none  [maximum_over_group(): values = jnp.maximum(values, exchange(values, stride))]
    reduce_max x0 -> x1, other arithmetic: none -> 0.6 us  [maximum_over_group(): return jnp.max(others, axis=0).reshape(values.shape)]
  transfers between devices with their start and end apart: 19 -> 16, of which waited for: 9 -> 6; matrix products, arithmetic and copies ran while one was open for 0% -> 0% of each run, Pallas kernels for 1% -> 1%
where the time goes in v4:
time: 50.6 us; the launch traced here: 50.4 us
  waiting for transfers between devices  15.3 us (30%)
  Pallas kernels  12.8 us (25%)
  starting transfers between devices  10.9 us (22%)
  blocking collectives  10.2 us (20%)
  between operations  0.71 us (1%)
  other arithmetic  0.6 us (1%)
    ppermute x16, waiting for transfers between devices, exchange(): return lax.ppermute(block, 'tmpl', [(i, i ^ distance) for i in range(size)])  15.3 us
    ppermute x16, starting transfers between devices, exchange(): return lax.ppermute(block, 'tmpl', [(i, i ^ distance) for i in range(size)])  10.9 us
    all_to_all x1, blocking collectives, maximum_over_group(): lax.all_to_all(copies, 'tmpl', split_axis=0, concat_axis=0, axis_index_gr...  10.2 us
    pallas_call x1, Pallas kernels, correlate(): pl.pallas_call(correlate_kernel, out_shape=jax.ShapeDtypeStruct((padded,...  10.1 us
    pallas_call x1, Pallas kernels, reconstruct(): pl.pallas_call(recon_kernel, out_shape=(jax.ShapeDtypeStruct((coeffs.shap...  1.95 us
  transfers between devices with their start and end apart: 16, of which 6 were waited for; matrix products, arithmetic and copies ran while one was open for 0% of the time, Pallas kernels for 1%

profile of v4, /device:TPU:0, one launch (start us, length us, event | category | flops | bytes accessed | tf_op | source)
XLA Modules:
  0.0 50.4 jit_solution(16897900079724350282)
XLA Ops:
  0.6 0.0 copy-start
  0.6 10.1 %correlate.1.refs_15_ = bf16[32,1920]{1,0:T(8,128)(2,1)} custom-call(bf16[9216]{0:T(1024)(128)(2,1)} %refs_0_.1, bf16[8704]{0:T(1024)(128)(2,1)} %refs_1_.1, bf16[8448]{0:T(1024)(128)(2,1)} %refs_2_.1, bf16[8320]{0:T(1024)(128)(2,1)} %refs_3_.1, bf16[4,32,8192]{2,1,0:T(8,128)(2,1)} %refs_4_.1), custom_call_target="tpu_custom_call" | custom-call | flops 1006632960 | bytes 2097152 | tf_op jit(solution)/shard_map/correlate/pallas_call | solution.py:108
  10.8 0.0 copy-start.1
  10.8 3.0 %collective-permute-start.12 = (bf16[32,1920]{1,0:T(8,128)(2,1)}, bf16[32,1920]{1,0:T(8,128)(2,1)S(1)}, u32[]{:S(2)}, u32[]{:S(2)}) collective-permute-start(bf16[32,1920]{1,0:T(8,128)(2,1)} %correlate.1.refs_15_), channel_id=1, source_target_pairs={{0,2},{1,3},{2,0},{3,1},{4,6},{5,7},{6,4},{7,5},{8,10},{9,11},{10,... | collective-permute-start | bytes 368648 | tf_op jit(solution)/shard_map/ppermute | solution.py:132
  13.8 1.6 %collective-permute-start.8 = (bf16[32,1920]{1,0:T(8,128)(2,1)}, bf16[32,1920]{1,0:T(8,128)(2,1)S(1)}, u32[]{:S(2)}, u32[]{:S(2)}) collective-permute-start(bf16[32,1920]{1,0:T(8,128)(2,1)} %correlate.1.refs_15_), channel_id=1, source_target_pairs={{0,4},{1,5},{2,6},{3,7},{4,0},{5,1},{6,2},{7,3},{8,12},{9,13},{10,... | collective-permute-start | bytes 368648 | tf_op jit(solution)/shard_map/ppermute | solution.py:132
  15.4 0.0 collective-permute-start.14
  15.4 2.6 %collective-permute-start.4 = (bf16[32,1920]{1,0:T(8,128)(2,1)}, bf16[32,1920]{1,0:T(8,128)(2,1)S(1)}, u32[]{:S(2)}, u32[]{:S(2)}) collective-permute-start(bf16[32,1920]{1,0:T(8,128)(2,1)} %correlate.1.refs_15_), channel_id=1, source_target_pairs={{0,8},{1,9},{2,10},{3,11},{4,12},{5,13},{6,14},{7,15},{8,0},{9,1},... | collective-permute-start | bytes 368648 | tf_op jit(solution)/shard_map/ppermute | solution.py:132
  18.0 0.2 collective-permute-start
  18.2 0.0 collective-permute-done.12.refs_13_
  18.2 0.0 collective-permute-start.13
  18.2 0.7 %collective-permute-done.8.refs_11_ = bf16[32,1920]{1,0:T(8,128)(2,1)S(1)} collective-permute-done((bf16[32,1920]{1,0:T(8,128)(2,1)}, bf16[32,1920]{1,0:T(8,128)(2,1)S(1)}, u32[]{:S(2)}, u32[]{:S(2)}) %collective-permute-start.8) | collective-permute-done | bytes 122912 | tf_op jit(solution)/shard_map/ppermute | solution.py:132
  18.9 0.0 collective-permute-start.11
  18.9 0.0 collective-permute-done.14.refs_14_
  18.9 0.7 %collective-permute-start.9 = (bf16[32,1920]{1,0:T(8,128)(2,1)S(1)}, bf16[32,1920]{1,0:T(8,128)(2,1)S(1)}, u32[]{:S(2)}, u32[]{:S(2)}) collective-permute-start(bf16[32,1920]{1,0:T(8,128)(2,1)S(1)} %collective-permute-done.8.refs_11_), channel_id=1, source_target_pairs={{0,2},{1,3},{2,0},{3,1},{4,6},{5,7},{6,4},{7,5},{8,10},{9,11},{10,... | collective-permute-start | bytes 368648 | tf_op jit(solution)/shard_map/ppermute | solution.py:132
  19.6 8.0 %collective-permute-done.4.refs_7_ = bf16[32,1920]{1,0:T(8,128)(2,1)S(1)} collective-permute-done((bf16[32,1920]{1,0:T(8,128)(2,1)}, bf16[32,1920]{1,0:T(8,128)(2,1)S(1)}, u32[]{:S(2)}, u32[]{:S(2)}) %collective-permute-start.4) | collective-permute-done | bytes 122912 | tf_op jit(solution)/shard_map/ppermute | solution.py:132
  27.6 0.5 %collective-permute-start.5 = (bf16[32,1920]{1,0:T(8,128)(2,1)S(1)}, bf16[32,1920]{1,0:T(8,128)(2,1)S(1)}, u32[]{:S(2)}, u32[]{:S(2)}) collective-permute-start(bf16[32,1920]{1,0:T(8,128)(2,1)S(1)} %collective-permute-done.4.refs_7_), channel_id=1, source_target_pairs={{0,2},{1,3},{2,0},{3,1},{4,6},{5,7},{6,4},{7,5},{8,10},{9,11},{10,... | collective-permute-start | bytes 368648 | tf_op jit(solution)/shard_map/ppermute | solution.py:132
  28.1 0.0 collective-permute-done.refs_3_
  28.1 1.5 %collective-permute-start.1 = (bf16[32,1920]{1,0:T(8,128)(2,1)S(1)}, bf16[32,1920]{1,0:T(8,128)(2,1)S(1)}, u32[]{:S(2)}, u32[]{:S(2)}) collective-permute-start(bf16[32,1920]{1,0:T(8,128)(2,1)S(1)} %collective-permute-done.refs_3_), channel_id=1, source_target_pairs={{0,2},{1,3},{2,0},{3,1},{4,6},{5,7},{6,4},{7,5},{8,10},{9,11},{10,... | collective-permute-start | bytes 368648 | tf_op jit(solution)/shard_map/ppermute | solution.py:132
  29.6 0.0 collective-permute-done.13.refs_12_
  29.6 0.0 collective-permute-start.7
  29.7 0.0 collective-permute-done.11.refs_10_
  29.7 0.5 %collective-permute-start.3 = (bf16[32,1920]{1,0:T(8,128)(2,1)S(1)}, bf16[32,1920]{1,0:T(8,128)(2,1)S(1)}, u32[]{:S(2)}, u32[]{:S(2)}) collective-permute-start(bf16[32,1920]{1,0:T(8,128)(2,1)S(1)} %collective-permute-done.refs_3_), channel_id=1, source_target_pairs={{0,1},{1,0},{2,3},{3,2},{4,5},{5,4},{6,7},{7,6},{8,9},{9,8},{10,11... | collective-permute-start | bytes 368648 | tf_op jit(solution)/shard_map/ppermute | solution.py:132
  30.2 0.0 collective-permute-done.9.refs_9_
  30.2 0.1 collective-permute-start.10
  30.2 3.6 %collective-permute-done.5.refs_5_ = bf16[32,1920]{1,0:T(8,128)(2,1)S(1)} collective-permute-done((bf16[32,1920]{1,0:T(8,128)(2,1)S(1)}, bf16[32,1920]{1,0:T(8,128)(2,1)S(1)}, u32[]{:S(2)}, u32[]{:S(2)}) %collective-permute-start.5) | collective-permute-done | bytes 122912 | tf_op jit(solution)/shard_map/ppermute | solution.py:132
  33.8 0.0 collective-permute-start.6
  33.8 1.4 %collective-permute-done.1.refs_1_ = bf16[32,1920]{1,0:T(8,128)(2,1)S(1)} collective-permute-done((bf16[32,1920]{1,0:T(8,128)(2,1)S(1)}, bf16[32,1920]{1,0:T(8,128)(2,1)S(1)}, u32[]{:S(2)}, u32[]{:S(2)}) %collective-permute-start.1) | collective-permute-done | bytes 122912 | tf_op jit(solution)/shard_map/ppermute | solution.py:132
  35.2 0.0 collective-permute-start.2
  35.2 0.0 copy-done
  35.2 0.7 %arrange.1.coeffs_ref = bf16[4,256,512]{2,1,0:T(8,128)(2,1)S(1)} custom-call(s32[1]{0:T(128)} %bitcast.offset_ref, bf16[4,256,512]{2,1,0:T(8,128)(2,1)S(1)} %copy-done), custom_call_target="tpu_custom_call" | custom-call | flops 536870912 | bytes 2097152 | tf_op jit(solution)/shard_map/arrange/pallas_call | solution.py:181
  35.9 0.0 collective-permute-done.7.refs_6_
  35.9 0.0 collective-permute-done.3.refs_2_
  36.0 0.0 collective-permute-done.10.refs_8_
  36.0 0.0 collective-permute-done.6.refs_4_
  36.0 0.6 %collective-permute-done.2.refs_0_ = bf16[32,1920]{1,0:T(8,128)(2,1)S(1)} collective-permute-done((bf16[32,1920]{1,0:T(8,128)(2,1)S(1)}, bf16[32,1920]{1,0:T(8,128)(2,1)S(1)}, u32[]{:S(2)}, u32[]{:S(2)}) %collective-permute-start.2) | collective-permute-done | bytes 122912 | tf_op jit(solution)/shard_map/ppermute | solution.py:132
  36.5 0.0 copy-done.1
  36.5 1.9 %reconstruct.1 = (bf16[256,1024]{1,0:T(8,128)(2,1)}, f32[1,1024]{1,0:T(1,128)S(1)}) custom-call(bf16[4,256,512]{2,1,0:T(8,128)(2,1)S(1)} %arrange.1.coeffs_ref, bf16[32,1920]{1,0:T(8,128)(2,1)S(1)} %collective-permute-done.2.refs_0_, bf16[32,1920]{1,0:T(8,128)(2,1)S(1)} %collective-permute-done.1.refs_1_, ...), custom_call_target="tpu_custom_call" | custom-call | tf_op jit(solution)/shard_map/reconstruct/pallas_call | solution.py:238
  38.5 0.2 collective-permute-start.15
  38.6 1.0 %collective-permute-done.15 = f32[1024]{0:T(1024)S(1)} collective-permute-done((f32[1024]{0:T(1024)S(1)}, f32[1024]{0:T(1024)S(1)}, u32[]{:S(2)}, u32[]{:S(2)}) %collective-permute-start.15) | collective-permute-done | bytes 4128 | tf_op jit(solution)/shard_map/ppermute | solution.py:132
  39.7 10.2 %all_to_all.5 = f32[8,8,128]{2,1,0:T(8,128)S(1)} all-to-all(f32[8,8,128]{2,1,0:T(8,128)S(1)} %broadcast_in_dim.8), channel_id=1, replica_groups={{0,2,4,6,8,10,12,14},{1,3,5,7,9,11,13,15},{16,18,20,22,24,26,28,30},{17..., dimensions={0} | all-to-all | bytes 65536 | tf_op jit(solution)/shard_map/all_to_all | solution.py:163
  49.8 0.6 %reduce_max.9 = f32[8,128]{1,0:T(8,128)} reduce(f32[8,8,128]{2,1,0:T(8,128)S(1)} %all_to_all.5, f32[]{:T(128)} %constant.2.clone.1), dimensions={0}, to_apply=%region_0.0 | reduce | flops 7168 | bytes 36868 | tf_op jit(solution)/shard_map/reduce_max | solution.py:166
  (2 shorter events, 0.0 us)
Async XLA Ops:
  0.6 34.6 %copy-start = (bf16[4,256,512]{2,1,0:T(8,128)(2,1)S(1)}, bf16[4,256,512]{2,1,0:T(8,128)(2,1)}, u32[]{:S(2)}) copy-start(bf16[4,256,512]{2,1,0:T(8,128)(2,1)} %coeffs_ref.1) | copy-start | bytes 3145732
  10.8 25.8 %copy-start.1 = (bf16[32,1920]{1,0:T(8,128)(2,1)S(1)}, bf16[32,1920]{1,0:T(8,128)(2,1)}, u32[]{:S(2)}) copy-start(bf16[32,1920]{1,0:T(8,128)(2,1)} %correlate.1.refs_15_) | copy-start | bytes 368644
  10.8 7.4 %collective-permute-start.12 = (bf16[32,1920]{1,0:T(8,128)(2,1)}, bf16[32,1920]{1,0:T(8,128)(2,1)S(1)}, u32[]{:S(2)}, u32[]{:S(2)}) collective-permute-start(bf16[32,1920]{1,0:T(8,128)(2,1)} %correlate.1.refs_15_), channel_id=1, source_target_pairs={{0,2},{1,3},{2,0},{3,1},{4,6},{5,7},{6,4},{7,5},{8,10},{9,11},{10,... | collective-permute-start | bytes 368648 | tf_op jit(solution)/shard_map/ppermute | solution.py:132
  13.8 5.1 %collective-permute-start.8 = (bf16[32,1920]{1,0:T(8,128)(2,1)}, bf16[32,1920]{1,0:T(8,128)(2,1)S(1)}, u32[]{:S(2)}, u32[]{:S(2)}) collective-permute-start(bf16[32,1920]{1,0:T(8,128)(2,1)} %correlate.1.refs_15_), channel_id=1, source_target_pairs={{0,4},{1,5},{2,6},{3,7},{4,0},{5,1},{6,2},{7,3},{8,12},{9,13},{10,... | collective-permute-start | bytes 368648 | tf_op jit(solution)/shard_map/ppermute | solution.py:132
  15.4 3.5 %collective-permute-start.14 = (bf16[32,1920]{1,0:T(8,128)(2,1)}, bf16[32,1920]{1,0:T(8,128)(2,1)S(1)}, u32[]{:S(2)}, u32[]{:S(2)}) collective-permute-start(bf16[32,1920]{1,0:T(8,128)(2,1)} %correlate.1.refs_15_), channel_id=1, source_target_pairs={{0,1},{1,0},{2,3},{3,2},{4,5},{5,4},{6,7},{7,6},{8,9},{9,8},{10,11... | collective-permute-start | bytes 368648 | tf_op jit(solution)/shard_map/ppermute | solution.py:132
  15.4 12.2 %collective-permute-start.4 = (bf16[32,1920]{1,0:T(8,128)(2,1)}, bf16[32,1920]{1,0:T(8,128)(2,1)S(1)}, u32[]{:S(2)}, u32[]{:S(2)}) collective-permute-start(bf16[32,1920]{1,0:T(8,128)(2,1)} %correlate.1.refs_15_), channel_id=1, source_target_pairs={{0,8},{1,9},{2,10},{3,11},{4,12},{5,13},{6,14},{7,15},{8,0},{9,1},... | collective-permute-start | bytes 368648 | tf_op jit(solution)/shard_map/ppermute | solution.py:132
  18.0 10.1 %collective-permute-start = (bf16[32,1920]{1,0:T(8,128)(2,1)}, bf16[32,1920]{1,0:T(8,128)(2,1)S(1)}, u32[]{:S(2)}, u32[]{:S(2)}) collective-permute-start(bf16[32,1920]{1,0:T(8,128)(2,1)} %correlate.1.refs_15_), channel_id=1, source_target_pairs={{0,12},{1,13},{2,14},{3,15},{4,8},{5,9},{6,10},{7,11},{8,4},{9,5},... | collective-permute-start | bytes 368648 | tf_op jit(solution)/shard_map/ppermute | solution.py:132
  18.2 11.4 %collective-permute-start.13 = (bf16[32,1920]{1,0:T(8,128)(2,1)S(1)}, bf16[32,1920]{1,0:T(8,128)(2,1)S(1)}, u32[]{:S(2)}, u32[]{:S(2)}) collective-permute-start(bf16[32,1920]{1,0:T(8,128)(2,1)S(1)} %collective-permute-done.12.refs_13_), channel_id=1, source_target_pairs={{0,1},{1,0},{2,3},{3,2},{4,5},{5,4},{6,7},{7,6},{8,9},{9,8},{10,11... | collective-permute-start | bytes 368648 | tf_op jit(solution)/shard_map/ppermute | solution.py:132
  18.9 10.7 %collective-permute-start.11 = (bf16[32,1920]{1,0:T(8,128)(2,1)S(1)}, bf16[32,1920]{1,0:T(8,128)(2,1)S(1)}, u32[]{:S(2)}, u32[]{:S(2)}) collective-permute-start(bf16[32,1920]{1,0:T(8,128)(2,1)S(1)} %collective-permute-done.8.refs_11_), channel_id=1, source_target_pairs={{0,1},{1,0},{2,3},{3,2},{4,5},{5,4},{6,7},{7,6},{8,9},{9,8},{10,11... | collective-permute-start | bytes 368648 | tf_op jit(solution)/shard_map/ppermute | solution.py:132
  18.9 11.3 %collective-permute-start.9 = (bf16[32,1920]{1,0:T(8,128)(2,1)S(1)}, bf16[32,1920]{1,0:T(8,128)(2,1)S(1)}, u32[]{:S(2)}, u32[]{:S(2)}) collective-permute-start(bf16[32,1920]{1,0:T(8,128)(2,1)S(1)} %collective-permute-done.8.refs_11_), channel_id=1, source_target_pairs={{0,2},{1,3},{2,0},{3,1},{4,6},{5,7},{6,4},{7,5},{8,10},{9,11},{10,... | collective-permute-start | bytes 368648 | tf_op jit(solution)/shard_map/ppermute | solution.py:132
  27.6 6.2 %collective-permute-start.5 = (bf16[32,1920]{1,0:T(8,128)(2,1)S(1)}, bf16[32,1920]{1,0:T(8,128)(2,1)S(1)}, u32[]{:S(2)}, u32[]{:S(2)}) collective-permute-start(bf16[32,1920]{1,0:T(8,128)(2,1)S(1)} %collective-permute-done.4.refs_7_), channel_id=1, source_target_pairs={{0,2},{1,3},{2,0},{3,1},{4,6},{5,7},{6,4},{7,5},{8,10},{9,11},{10,... | collective-permute-start | bytes 368648 | tf_op jit(solution)/shard_map/ppermute | solution.py:132
  28.1 7.1 %collective-permute-start.1 = (bf16[32,1920]{1,0:T(8,128)(2,1)S(1)}, bf16[32,1920]{1,0:T(8,128)(2,1)S(1)}, u32[]{:S(2)}, u32[]{:S(2)}) collective-permute-start(bf16[32,1920]{1,0:T(8,128)(2,1)S(1)} %collective-permute-done.refs_3_), channel_id=1, source_target_pairs={{0,2},{1,3},{2,0},{3,1},{4,6},{5,7},{6,4},{7,5},{8,10},{9,11},{10,... | collective-permute-start | bytes 368648 | tf_op jit(solution)/shard_map/ppermute | solution.py:132
  29.6 6.3 %collective-permute-start.7 = (bf16[32,1920]{1,0:T(8,128)(2,1)S(1)}, bf16[32,1920]{1,0:T(8,128)(2,1)S(1)}, u32[]{:S(2)}, u32[]{:S(2)}) collective-permute-start(bf16[32,1920]{1,0:T(8,128)(2,1)S(1)} %collective-permute-done.4.refs_7_), channel_id=1, source_target_pairs={{0,1},{1,0},{2,3},{3,2},{4,5},{5,4},{6,7},{7,6},{8,9},{9,8},{10,11... | collective-permute-start | bytes 368648 | tf_op jit(solution)/shard_map/ppermute | solution.py:132
  29.7 6.3 %collective-permute-start.3 = (bf16[32,1920]{1,0:T(8,128)(2,1)S(1)}, bf16[32,1920]{1,0:T(8,128)(2,1)S(1)}, u32[]{:S(2)}, u32[]{:S(2)}) collective-permute-start(bf16[32,1920]{1,0:T(8,128)(2,1)S(1)} %collective-permute-done.refs_3_), channel_id=1, source_target_pairs={{0,1},{1,0},{2,3},{3,2},{4,5},{5,4},{6,7},{7,6},{8,9},{9,8},{10,11... | collective-permute-start | bytes 368648 | tf_op jit(solution)/shard_map/ppermute | solution.py:132
  30.2 5.8 %collective-permute-start.10 = (bf16[32,1920]{1,0:T(8,128)(2,1)S(1)}, bf16[32,1920]{1,0:T(8,128)(2,1)S(1)}, u32[]{:S(2)}, u32[]{:S(2)}) collective-permute-start(bf16[32,1920]{1,0:T(8,128)(2,1)S(1)} %collective-permute-done.9.refs_9_), channel_id=1, source_target_pairs={{0,1},{1,0},{2,3},{3,2},{4,5},{5,4},{6,7},{7,6},{8,9},{9,8},{10,11... | collective-permute-start | bytes 368648 | tf_op jit(solution)/shard_map/ppermute | solution.py:132
  33.8 2.1 %collective-permute-start.6 = (bf16[32,1920]{1,0:T(8,128)(2,1)S(1)}, bf16[32,1920]{1,0:T(8,128)(2,1)S(1)}, u32[]{:S(2)}, u32[]{:S(2)}) collective-permute-start(bf16[32,1920]{1,0:T(8,128)(2,1)S(1)} %collective-permute-done.5.refs_5_), channel_id=1, source_target_pairs={{0,1},{1,0},{2,3},{3,2},{4,5},{5,4},{6,7},{7,6},{8,9},{9,8},{10,11... | collective-permute-start | bytes 368648 | tf_op jit(solution)/shard_map/ppermute | solution.py:132
  35.2 1.3 %collective-permute-start.2 = (bf16[32,1920]{1,0:T(8,128)(2,1)S(1)}, bf16[32,1920]{1,0:T(8,128)(2,1)S(1)}, u32[]{:S(2)}, u32[]{:S(2)}) collective-permute-start(bf16[32,1920]{1,0:T(8,128)(2,1)S(1)} %collective-permute-done.1.refs_1_), channel_id=1, source_target_pairs={{0,1},{1,0},{2,3},{3,2},{4,5},{5,4},{6,7},{7,6},{8,9},{9,8},{10,11... | collective-permute-start | bytes 368648 | tf_op jit(solution)/shard_map/ppermute | solution.py:132
  38.5 1.2 %collective-permute-start.15 = (f32[1024]{0:T(1024)S(1)}, f32[1024]{0:T(1024)S(1)}, u32[]{:S(2)}, u32[]{:S(2)}) collective-permute-start(f32[1024]{0:T(1024)S(1)} %bitcast.5), channel_id=1, source_target_pairs={{0,1},{1,0},{2,3},{3,2},{4,5},{5,4},{6,7},{7,6},{8,9},{9,8},{10,11... | collective-permute-start | bytes 12296 | tf_op jit(solution)/shard_map/ppermute | solution.py:132

commit v5 on v4

--- a/solution.py
+++ b/solution.py
@@ -12,90 +12,141 @@
 SUB = 16
 
 
-def build_frames(x_ref, start, tiles, cols):
-    width = tiles * LANE + cols
-    wide = jnp.broadcast_to(x_ref[pl.ds(start, width)].reshape(1, width), (SUB, width))
-    row = lax.broadcasted_iota(jnp.int32, (SUB, width), 0)
-    step = 1
-    while step < SUB:
-        moved = pltpu.roll(wide, width - step, axis=1)
-        wide = jnp.where((row & step) != 0, moved, wide)
-        step *= 2
-    moved = [wide]
-    for q in range(1, LANE // SUB):
-        moved.append(pltpu.roll(wide, width - SUB * q, axis=1))
-    pieces = []
-    for tile in range(tiles):
-        pieces += [part[:, tile * LANE : tile * LANE + cols] for part in moved]
-    return jnp.concatenate(pieces, axis=0)
-
-
 def correlate_kernel(*refs):
     strain_refs, taps_ref, out_ref = refs[:4], refs[4], refs[5]
-    held_strains, held_taps, strain_sems, taps_sems = refs[6:10], refs[10], refs[11], refs[12]
+    held_strains = refs[6:10]
+    held_taps, line_ref, row_ref, wide_ref, strain_sems, taps_sems = refs[10:]
     sections = len(strain_refs)
     rows, taps = taps_ref.shape[1], taps_ref.shape[2]
-    pad = (held_taps.shape[2] - taps) // 2
-    copies = []
+    lines = [ref.shape[0] for ref in held_strains]
+    blocks = [count - taps // LANE for count in lines]
+    slot = line_ref.shape[0] // sections
+    every = sections * slot
+    pad = (max(blocks) - 1) * LANE
+    strain_copies, taps_copies = [], []
     for section, source in enumerate(strain_refs):
-        copies.append(
+        strain_copies.append(
             pltpu.make_async_copy(source, held_strains[section], strain_sems.at[section])
         )
-        copies.append(
+        taps_copies.append(
             pltpu.make_async_copy(
                 taps_ref.at[section],
                 held_taps.at[section, :, pl.ds(pad, taps)],
                 taps_sems.at[section],
             )
         )
-    for copy in copies:
+    for copy in strain_copies + taps_copies:
         copy.start()
-    samples = [ref.shape[0] - taps for ref in held_strains]
-    cols = [min(2 * LANE, count) for count in samples]
-    blocks = [count // size for count, size in zip(samples, cols)]
     for section in range(sections):
-        if blocks[section] > 1:
-            zeros = jnp.zeros((rows, pad), held_taps.dtype)
-            held_taps[section, :, :pad] = zeros
-            held_taps[section, :, pad + taps :] = zeros
-    for copy in copies:
+        held_taps[section, :, :pad] = jnp.zeros((rows, pad), held_taps.dtype)
+        after = held_taps.shape[2] - pad - taps
+        held_taps[section, :, pad + taps :] = jnp.zeros((rows, after), held_taps.dtype)
+
+    for section, copy in enumerate(strain_copies):
         copy.wait()
-
-    def term(section, start, tiles):
-        frames = build_frames(held_strains[section], start, tiles, cols[section])
-        left = []
+        first = section * slot
+        line_ref[first : first + lines[section], :] = held_strains[section][...].astype(jnp.float32)
+        if slot > lines[section]:
+            line_ref[first + lines[section] : first + slot, :] = jnp.zeros(
+                (slot - lines[section], LANE), jnp.float32
+            )
+    pairs = jnp.concatenate(
+        [
+            line_ref[...].astype(jnp.bfloat16),
+            jnp.concatenate([line_ref[1:, :], jnp.zeros((1, LANE), jnp.float32)], axis=0).astype(
+                jnp.bfloat16
+            ),
+        ],
+        axis=1,
+    )
+    source = lax.broadcasted_iota(jnp.int32, (2 * LANE, 2 * LANE), 0)
+    target = lax.broadcasted_iota(jnp.int32, (2 * LANE, 2 * LANE), 1)
+    target = target % LANE + target // LANE
+    for r in range(0, SUB, 2):
+        select = jnp.where(source == target + r, 1.0, 0.0).astype(jnp.bfloat16)
+        moved = jnp.dot(pairs, select, preferred_element_type=jnp.float32)
+        row_ref[r * every : (r + 1) * every, :] = moved[:, :LANE]
+        row_ref[(r + 1) * every : (r + 2) * every, :] = moved[:, LANE:]
+
+    def place_rows(number, carry):
+        for line in range(SUB):
+            line = number * SUB + line
+            piece = row_ref[pl.ds(line, SUB, stride=every), :].astype(jnp.bfloat16)
+            wide_ref[:, pl.ds(pl.multiple_of(line * LANE, LANE), LANE)] = piece
+        return carry
+
+    lax.fori_loop(0, every // SUB, place_rows, 0)
+    wide_ref[:, every * LANE :] = jnp.zeros((SUB, LANE), wide_ref.dtype)
+    for copy in taps_copies:
+        copy.wait()
+
+    def frames(section, tile, tiles):
+        width = (tiles + 1) * LANE
+        first = (section * slot + tile) * LANE
+        if not isinstance(first, int):
+            first = pl.multiple_of(first, LANE)
+        wide = wide_ref[:, pl.ds(first, width)]
+        moved = [wide]
+        for q in range(1, LANE // SUB):
+            moved.append(pltpu.roll(wide, width - SUB * q, axis=1))
+        pieces = []
+        for number in range(tiles):
+            pieces += [part[:, number * LANE : (number + 1) * LANE] for part in moved]
+        return jnp.concatenate(pieces, axis=0)
+
+    def shifted(section, tile, tiles):
+        pieces = []
         for u in range(blocks[section]):
-            first = pad + start - u * cols[section]
+            first = pad + (tile - u) * LANE
             if not isinstance(first, int):
                 first = pl.multiple_of(first, LANE)
-            left.append(held_taps[section, :, pl.ds(first, tiles * LANE)])
-        left = left[0] if len(left) == 1 else jnp.concatenate(left, axis=0)
-        return jnp.dot(left, frames, preferred_element_type=jnp.float32)
+            pieces.append(held_taps[section, :, pl.ds(first, tiles * LANE)])
+        return pieces
+
+    def term(group, tile, tiles):
+        left, right = [], []
+        for section in group:
+            left += shifted(section, tile, tiles)
+            right.append(frames(section, tile, tiles))
+        left = jnp.concatenate(left, axis=0) if len(left) > 1 else left[0]
+        right = jnp.concatenate(right, axis=1) if len(right) > 1 else right[0]
+        both = jnp.dot(left, right, preferred_element_type=jnp.float32)
+        parts, row = [], 0
+        for number, section in enumerate(group):
+            height = blocks[section] * rows
+            parts.append(both[row : row + height, number * LANE : (number + 1) * LANE])
+            row += height
+        return parts
+
+    groups = [list(range(first, min(first + 2, sections))) for first in range(0, sections, 2)]
 
     def step(number, totals):
-        start = pl.multiple_of(number * (CHUNK * LANE), CHUNK * LANE)
-        return tuple(
-            total + term(section, start, CHUNK) for section, total in enumerate(totals)
-        )
+        parts = []
+        for group in groups:
+            parts += term(group, number * CHUNK, CHUNK)
+        return tuple(total + part for total, part in zip(totals, parts))
 
     totals = lax.fori_loop(
         0,
         taps // (CHUNK * LANE),
         step,
-        tuple(
-            jnp.zeros((blocks[section] * rows, cols[section]), jnp.float32)
-            for section in range(sections)
-        ),
+        tuple(jnp.zeros((count * rows, LANE), jnp.float32) for count in blocks),
     )
+    totals = list(totals)
+    for group in groups:
+        end = max(blocks[section] for section in group) - 1
+        for tile in range(0, end, CHUNK):
+            active = [section for section in group if blocks[section] - 1 > tile]
+            for section, part in zip(
+                active, term(active, taps // LANE + tile, min(CHUNK, end - tile))
+            ):
+                totals[section] = totals[section] + part
     place = 0
     for section, total in enumerate(totals):
-        extra = (blocks[section] - 1) * cols[section] // LANE
-        for tile in range(0, extra, CHUNK):
-            total = total + term(section, taps + tile * LANE, min(CHUNK, extra - tile))
         for u in range(blocks[section]):
             part = total[u * rows : (u + 1) * rows].astype(out_ref.dtype)
-            out_ref[:, place : place + cols[section]] = part
-            place += cols[section]
+            out_ref[:, place : place + LANE] = part
+            place += LANE
 
 
 def correlate(streams, basis_taps):
@@ -104,15 +155,20 @@
     if padded != rows:
         basis_taps = jnp.pad(basis_taps, ((0, 0), (0, padded - rows), (0, 0)))
     samples = sum(x.shape[0] - taps for x in streams)
-    pad = max(x.shape[0] - taps for x in streams) - 2 * LANE
+    longest = max(x.shape[0] for x in streams)
+    slot = -(-longest // (8 * LANE)) * 8
+    lines = [x.reshape(-1, LANE) for x in streams]
     out = pl.pallas_call(
         correlate_kernel,
         out_shape=jax.ShapeDtypeStruct((padded, samples), jnp.bfloat16),
         in_specs=[pl.BlockSpec(memory_space=pltpu.HBM)] * (sections + 1),
         out_specs=pl.BlockSpec(memory_space=pltpu.VMEM),
-        scratch_shapes=[pltpu.VMEM(x.shape, x.dtype) for x in streams]
+        scratch_shapes=[pltpu.VMEM(x.shape, x.dtype) for x in lines]
         + [
-            pltpu.VMEM((sections, padded, taps + 2 * pad), jnp.bfloat16),
+            pltpu.VMEM((sections, padded, 2 * longest - taps), jnp.bfloat16),
+            pltpu.VMEM((sections * slot, LANE), jnp.float32),
+            pltpu.VMEM((SUB * sections * slot, LANE), jnp.float32),
+            pltpu.VMEM((SUB, (sections * slot + 1) * LANE), jnp.bfloat16),
             pltpu.SemaphoreType.DMA((sections,)),
             pltpu.SemaphoreType.DMA((sections,)),
         ],
@@ -123,7 +179,7 @@
             transcendentals=0,
         ),
         name="correlate",
-    )(*streams, basis_taps)
+    )(*lines, basis_taps)
     return out[:rows]
 
 
@@ -143,27 +199,23 @@
             stride *= radix
         return [block]
     held = {0: block}
-    top = size
-    while top > 1:
-        radix = 4 if top > 4 and top % 4 == 0 else 2
-        stride = top // radix
-        for place in reversed(list(held)):
-            for step in reversed(range(1, radix)):
-                held[place + step * stride] = exchange(held[place], step * stride)
-        top = stride
+    for place in range(1, size):
+        if place & 1:
+            continue
+        high = 1 << (place.bit_length() - 1)
+        held[place] = exchange(held[0 if place == high else high], place if place == high else place ^ high)
+    for place in range(1, size, 2):
+        held[place] = exchange(held[place ^ 1], 1)
     return [held[place] for place in range(size)]
 
 
 def maximum_over_group(values):
     size = lax.axis_size("tmpl")
-    values = jnp.maximum(values, exchange(values, 1))
-    tiles = values.reshape(1, -1, LANE)
-    copies = jnp.broadcast_to(tiles, (size // 2,) + tiles.shape[1:])
-    groups = [list(range(core, size, 2)) for core in range(2)]
-    others = lax.all_to_all(
-        copies, "tmpl", split_axis=0, concat_axis=0, axis_index_groups=groups, tiled=True
-    )
-    return jnp.max(others, axis=0).reshape(values.shape)
+    radix = 4 if size > 4 and size % 4 == 0 else 2
+    near = [list(range(first, first + radix)) for first in range(0, size, radix)]
+    far = [list(range(first, size, radix)) for first in range(radix)]
+    values = lax.pmax(values, "tmpl", axis_index_groups=near)
+    return lax.pmax(values, "tmpl", axis_index_groups=far)
 
 
 def arrange_kernel(offset_ref, coeffs_ref, out_ref):

time: 50.6 us -> 52.8 us (1.043)
  blocking collectives: 10.2 us -> 18.8 us
  waiting for transfers between devices: 15.3 us -> 9.37 us
  starting transfers between devices: 10.9 us -> 11.8 us
  Pallas kernels: 12.8 us -> 12 us
  other arithmetic: 0.6 us -> 0 us
    pmax x0 -> x2, blocking collectives: none -> 18.8 us  [the longest x1 12.9 us: maximum_over_group(): return lax.pmax(values, 'tmpl', axis_index_groups=far)]
    all_to_all x1 -> x0, blocking collectives: 10.2 us -> none  [maximum_over_group(): lax.all_to_all(copies, 'tmpl', split_axis=0, concat_axis=0, axis_index_gr...]
    ppermute x16 -> x15, waiting for transfers between devices: 15.3 us -> 9.37 us  [exchange(): return lax.ppermute(block, 'tmpl', [(i, i ^ distance) for i in range(size)])]
    ppermute x16 -> x15, starting transfers between devices: 10.9 us -> 11.8 us  [exchange(): return lax.ppermute(block, 'tmpl', [(i, i ^ distance) for i in range(size)])]
    pallas_call x1, Pallas kernels: 10.1 us -> 9.29 us  [correlate(): pl.pallas_call(correlate_kernel, out_shape=jax.ShapeDtypeStruct((padded,...]
    reduce_max x1 -> x0, other arithmetic: 0.6 us -> none  [maximum_over_group(): return jnp.max(others, axis=0).reshape(values.shape)]
  transfers between devices with their start and end apart: 16 -> 15, of which waited for: 6 -> 6; matrix products, arithmetic and copies ran while one was open for 0% -> 0% of each run, Pallas kernels for 1% -> 1%
where the time goes in v5:
time: 52.8 us; the launch traced here: 52.6 us
  blocking collectives  18.8 us (36%)
  Pallas kernels  12 us (23%)
  starting transfers between devices  11.8 us (22%)
  waiting for transfers between devices  9.37 us (18%)
  between operations  0.71 us (1%)
    pmax x1, blocking collectives, maximum_over_group(): return lax.pmax(values, 'tmpl', axis_index_groups=far)  12.9 us
    ppermute x15, starting transfers between devices, exchange(): return lax.ppermute(block, 'tmpl', [(i, i ^ distance) for i in range(size)])  11.8 us
    ppermute x15, waiting for transfers between devices, exchange(): return lax.ppermute(block, 'tmpl', [(i, i ^ distance) for i in range(size)])  9.37 us
    pallas_call x1, Pallas kernels, correlate(): pl.pallas_call(correlate_kernel, out_shape=jax.ShapeDtypeStruct((padded,...  9.29 us
    pmax x1, blocking collectives, maximum_over_group(): values = lax.pmax(values, 'tmpl', axis_index_groups=near)  5.88 us
    pallas_call x1, Pallas kernels, reconstruct(): pl.pallas_call(recon_kernel, out_shape=(jax.ShapeDtypeStruct((coeffs.shap...  1.95 us
  transfers between devices with their start and end apart: 15, of which 6 were waited for; matrix products, arithmetic and copies ran while one was open for 0% of the time, Pallas kernels for 1%

profile of v5, /device:TPU:0, one launch (start us, length us, event | category | flops | bytes accessed | tf_op | source)
XLA Modules:
  0.0 52.6 jit_solution(6594581162333421439)
XLA Ops:
  0.6 0.0 copy-start
  0.6 9.3 %correlate.1.refs_15_ = bf16[32,1920]{1,0:T(8,128)(2,1)} custom-call(bf16[72,128]{1,0:T(8,128)(2,1)} %bitcast.7, bf16[68,128]{1,0:T(8,128)(2,1)} %bitcast.8, bf16[66,128]{1,0:T(8,128)(2,1)} %bitcast.9, bf16[65,128]{1,0:T(8,128)(2,1)} %bitcast.10, bf16[4,32,8192]{2,1,0:T(8,128)(2,1)} %refs_4_.1), custom_call_target="tpu_custom_call" | custom-call | flops 1006632960 | bytes 2097152 | tf_op jit(solution)/shard_map/correlate/pallas_call | solution.py:161
  9.9 0.0 copy-start.1
  9.9 3.0 %collective-permute-start.12 = (bf16[32,1920]{1,0:T(8,128)(2,1)}, bf16[32,1920]{1,0:T(8,128)(2,1)S(1)}, u32[]{:S(2)}, u32[]{:S(2)}) collective-permute-start(bf16[32,1920]{1,0:T(8,128)(2,1)} %correlate.1.refs_15_), channel_id=1, source_target_pairs={{0,2},{1,3},{2,0},{3,1},{4,6},{5,7},{6,4},{7,5},{8,10},{9,11},{10,... | collective-permute-start | bytes 368648 | tf_op jit(solution)/shard_map/ppermute | solution.py:188
  13.0 1.6 %collective-permute-start.8 = (bf16[32,1920]{1,0:T(8,128)(2,1)}, bf16[32,1920]{1,0:T(8,128)(2,1)S(1)}, u32[]{:S(2)}, u32[]{:S(2)}) collective-permute-start(bf16[32,1920]{1,0:T(8,128)(2,1)} %correlate.1.refs_15_), channel_id=1, source_target_pairs={{0,4},{1,5},{2,6},{3,7},{4,0},{5,1},{6,2},{7,3},{8,12},{9,13},{10,... | collective-permute-start | bytes 368648 | tf_op jit(solution)/shard_map/ppermute | solution.py:188
  14.6 2.6 %collective-permute-start = (bf16[32,1920]{1,0:T(8,128)(2,1)}, bf16[32,1920]{1,0:T(8,128)(2,1)S(1)}, u32[]{:S(2)}, u32[]{:S(2)}) collective-permute-start(bf16[32,1920]{1,0:T(8,128)(2,1)} %correlate.1.refs_15_), channel_id=1, source_target_pairs={{0,8},{1,9},{2,10},{3,11},{4,12},{5,13},{6,14},{7,15},{8,0},{9,1},... | collective-permute-start | bytes 368648 | tf_op jit(solution)/shard_map/ppermute | solution.py:188
  17.1 0.0 collective-permute-start.14
  17.1 0.0 collective-permute-done.12.refs_13_
  17.2 0.5 collective-permute-start.13
  17.7 1.8 %collective-permute-done.8.refs_11_ = bf16[32,1920]{1,0:T(8,128)(2,1)S(1)} collective-permute-done((bf16[32,1920]{1,0:T(8,128)(2,1)}, bf16[32,1920]{1,0:T(8,128)(2,1)S(1)}, u32[]{:S(2)}, u32[]{:S(2)}) %collective-permute-start.8) | collective-permute-done | bytes 122912 | tf_op jit(solution)/shard_map/ppermute | solution.py:188
  19.5 0.0 collective-permute-start.11
  19.5 0.1 collective-permute-start.9
  19.5 3.3 %collective-permute-done.refs_7_ = bf16[32,1920]{1,0:T(8,128)(2,1)S(1)} collective-permute-done((bf16[32,1920]{1,0:T(8,128)(2,1)}, bf16[32,1920]{1,0:T(8,128)(2,1)S(1)}, u32[]{:S(2)}, u32[]{:S(2)}) %collective-permute-start) | collective-permute-done | bytes 122912 | tf_op jit(solution)/shard_map/ppermute | solution.py:188
  22.9 0.5 collective-permute-start.5
  23.4 0.0 collective-permute-done.14.refs_14_
  23.4 0.3 collective-permute-start.3
  23.7 0.0 collective-permute-done.13.refs_12_
  23.7 2.7 %collective-permute-start.1 = (bf16[32,1920]{1,0:T(8,128)(2,1)S(1)}, bf16[32,1920]{1,0:T(8,128)(2,1)S(1)}, u32[]{:S(2)}, u32[]{:S(2)}) collective-permute-start(bf16[32,1920]{1,0:T(8,128)(2,1)S(1)} %collective-permute-done.refs_7_), channel_id=1, source_target_pairs={{0,6},{1,7},{2,4},{3,5},{4,2},{5,3},{6,0},{7,1},{8,14},{9,15},{10,... | collective-permute-start | bytes 368648 | tf_op jit(solution)/shard_map/ppermute | solution.py:188
  26.4 0.0 collective-permute-done.11.refs_10_
  26.4 0.0 collective-permute-start.7
  26.4 0.5 %collective-permute-done.9.refs_9_ = bf16[32,1920]{1,0:T(8,128)(2,1)S(1)} collective-permute-done((bf16[32,1920]{1,0:T(8,128)(2,1)S(1)}, bf16[32,1920]{1,0:T(8,128)(2,1)S(1)}, u32[]{:S(2)}, u32[]{:S(2)}) %collective-permute-start.9) | collective-permute-done | bytes 122912 | tf_op jit(solution)/shard_map/ppermute | solution.py:188
  26.9 0.0 collective-permute-start.10
  26.9 2.2 %collective-permute-done.5.refs_5_ = bf16[32,1920]{1,0:T(8,128)(2,1)S(1)} collective-permute-done((bf16[32,1920]{1,0:T(8,128)(2,1)S(1)}, bf16[32,1920]{1,0:T(8,128)(2,1)S(1)}, u32[]{:S(2)}, u32[]{:S(2)}) %collective-permute-start.5) | collective-permute-done | bytes 122912 | tf_op jit(solution)/shard_map/ppermute | solution.py:188
  29.2 0.0 collective-permute-start.6
  29.2 0.0 collective-permute-done.3.refs_3_
  29.2 0.5 collective-permute-start.4
  29.7 0.8 %collective-permute-done.1.refs_1_ = bf16[32,1920]{1,0:T(8,128)(2,1)S(1)} collective-permute-done((bf16[32,1920]{1,0:T(8,128)(2,1)S(1)}, bf16[32,1920]{1,0:T(8,128)(2,1)S(1)}, u32[]{:S(2)}, u32[]{:S(2)}) %collective-permute-start.1) | collective-permute-done | bytes 122912 | tf_op jit(solution)/shard_map/ppermute | solution.py:188
  30.5 0.0 collective-permute-start.2
  30.5 0.0 copy-done
  30.5 0.7 %arrange.1.coeffs_ref = bf16[4,256,512]{2,1,0:T(8,128)(2,1)S(1)} custom-call(s32[1]{0:T(128)} %bitcast.offset_ref, bf16[4,256,512]{2,1,0:T(8,128)(2,1)S(1)} %copy-done), custom_call_target="tpu_custom_call" | custom-call | flops 536870912 | bytes 2097152 | tf_op jit(solution)/shard_map/arrange/pallas_call | solution.py:233
  31.3 0.0 collective-permute-done.7.refs_6_
  31.3 0.0 collective-permute-done.10.refs_8_
  31.3 0.0 collective-permute-done.6.refs_4_
  31.3 0.0 collective-permute-done.4.refs_2_
  31.3 0.6 %collective-permute-done.2.refs_0_ = bf16[32,1920]{1,0:T(8,128)(2,1)S(1)} collective-permute-done((bf16[32,1920]{1,0:T(8,128)(2,1)S(1)}, bf16[32,1920]{1,0:T(8,128)(2,1)S(1)}, u32[]{:S(2)}, u32[]{:S(2)}) %collective-permute-start.2) | collective-permute-done | bytes 122912 | tf_op jit(solution)/shard_map/ppermute | solution.py:188
  31.9 0.0 copy-done.1
  31.9 1.9 %reconstruct.1 = (bf16[256,1024]{1,0:T(8,128)(2,1)}, f32[1,1024]{1,0:T(1,128)S(1)}) custom-call(bf16[4,256,512]{2,1,0:T(8,128)(2,1)S(1)} %arrange.1.coeffs_ref, bf16[32,1920]{1,0:T(8,128)(2,1)S(1)} %collective-permute-done.2.refs_0_, bf16[32,1920]{1,0:T(8,128)(2,1)S(1)} %collective-permute-done.1.refs_1_, ...), custom_call_target="tpu_custom_call" | custom-call | tf_op jit(solution)/shard_map/reconstruct/pallas_call | solution.py:290
  33.8 5.9 %pmax.14 = f32[1024]{0:T(1024)S(1)} all-reduce(f32[1024]{0:T(1024)S(1)} %bitcast.6), channel_id=1, replica_groups={{0,1,2,3},{4,5,6,7},{8,9,10,11},{12,13,14,15},{16,17,18,19},{20,21,22,2..., use_global_device_ids=true, to_apply=%region_0.0 | all-reduce | flops 1024 | bytes 8192 | tf_op jit(solution)/shard_map/pmax | solution.py:217
  39.7 12.9 %pmax.15 = f32[1024]{0:T(1024)} all-reduce(f32[1024]{0:T(1024)S(1)} %pmax.14), channel_id=1, replica_groups={{0,4,8,12},{1,5,9,13},{2,6,10,14},{3,7,11,15},{16,20,24,28},{17,21,25,2..., use_global_device_ids=true, to_apply=%region_1.0 | all-reduce | flops 1024 | bytes 8192 | tf_op jit(solution)/shard_map/pmax | solution.py:218
Async XLA Ops:
  0.6 29.9 %copy-start = (bf16[4,256,512]{2,1,0:T(8,128)(2,1)S(1)}, bf16[4,256,512]{2,1,0:T(8,128)(2,1)}, u32[]{:S(2)}) copy-start(bf16[4,256,512]{2,1,0:T(8,128)(2,1)} %coeffs_ref.1) | copy-start | bytes 3145732
  9.9 21.9 %copy-start.1 = (bf16[32,1920]{1,0:T(8,128)(2,1)S(1)}, bf16[32,1920]{1,0:T(8,128)(2,1)}, u32[]{:S(2)}) copy-start(bf16[32,1920]{1,0:T(8,128)(2,1)} %correlate.1.refs_15_) | copy-start | bytes 368644
  9.9 7.2 %collective-permute-start.12 = (bf16[32,1920]{1,0:T(8,128)(2,1)}, bf16[32,1920]{1,0:T(8,128)(2,1)S(1)}, u32[]{:S(2)}, u32[]{:S(2)}) collective-permute-start(bf16[32,1920]{1,0:T(8,128)(2,1)} %correlate.1.refs_15_), channel_id=1, source_target_pairs={{0,2},{1,3},{2,0},{3,1},{4,6},{5,7},{6,4},{7,5},{8,10},{9,11},{10,... | collective-permute-start | bytes 368648 | tf_op jit(solution)/shard_map/ppermute | solution.py:188
  13.0 6.5 %collective-permute-start.8 = (bf16[32,1920]{1,0:T(8,128)(2,1)}, bf16[32,1920]{1,0:T(8,128)(2,1)S(1)}, u32[]{:S(2)}, u32[]{:S(2)}) collective-permute-start(bf16[32,1920]{1,0:T(8,128)(2,1)} %correlate.1.refs_15_), channel_id=1, source_target_pairs={{0,4},{1,5},{2,6},{3,7},{4,0},{5,1},{6,2},{7,3},{8,12},{9,13},{10,... | collective-permute-start | bytes 368648 | tf_op jit(solution)/shard_map/ppermute | solution.py:188
  14.6 8.3 %collective-permute-start = (bf16[32,1920]{1,0:T(8,128)(2,1)}, bf16[32,1920]{1,0:T(8,128)(2,1)S(1)}, u32[]{:S(2)}, u32[]{:S(2)}) collective-permute-start(bf16[32,1920]{1,0:T(8,128)(2,1)} %correlate.1.refs_15_), channel_id=1, source_target_pairs={{0,8},{1,9},{2,10},{3,11},{4,12},{5,13},{6,14},{7,15},{8,0},{9,1},... | collective-permute-start | bytes 368648 | tf_op jit(solution)/shard_map/ppermute | solution.py:188
  17.1 6.2 %collective-permute-start.14 = (bf16[32,1920]{1,0:T(8,128)(2,1)}, bf16[32,1920]{1,0:T(8,128)(2,1)S(1)}, u32[]{:S(2)}, u32[]{:S(2)}) collective-permute-start(bf16[32,1920]{1,0:T(8,128)(2,1)} %correlate.1.refs_15_), channel_id=1, source_target_pairs={{0,1},{1,0},{2,3},{3,2},{4,5},{5,4},{6,7},{7,6},{8,9},{9,8},{10,11... | collective-permute-start | bytes 368648 | tf_op jit(solution)/shard_map/ppermute | solution.py:188
  17.2 6.6 %collective-permute-start.13 = (bf16[32,1920]{1,0:T(8,128)(2,1)S(1)}, bf16[32,1920]{1,0:T(8,128)(2,1)S(1)}, u32[]{:S(2)}, u32[]{:S(2)}) collective-permute-start(bf16[32,1920]{1,0:T(8,128)(2,1)S(1)} %collective-permute-done.12.refs_13_), channel_id=1, source_target_pairs={{0,1},{1,0},{2,3},{3,2},{4,5},{5,4},{6,7},{7,6},{8,9},{9,8},{10,11... | collective-permute-start | bytes 368648 | tf_op jit(solution)/shard_map/ppermute | solution.py:188
  19.5 6.9 %collective-permute-start.11 = (bf16[32,1920]{1,0:T(8,128)(2,1)S(1)}, bf16[32,1920]{1,0:T(8,128)(2,1)S(1)}, u32[]{:S(2)}, u32[]{:S(2)}) collective-permute-start(bf16[32,1920]{1,0:T(8,128)(2,1)S(1)} %collective-permute-done.8.refs_11_), channel_id=1, source_target_pairs={{0,1},{1,0},{2,3},{3,2},{4,5},{5,4},{6,7},{7,6},{8,9},{9,8},{10,11... | collective-permute-start | bytes 368648 | tf_op jit(solution)/shard_map/ppermute | solution.py:188
  19.5 7.4 %collective-permute-start.9 = (bf16[32,1920]{1,0:T(8,128)(2,1)S(1)}, bf16[32,1920]{1,0:T(8,128)(2,1)S(1)}, u32[]{:S(2)}, u32[]{:S(2)}) collective-permute-start(bf16[32,1920]{1,0:T(8,128)(2,1)S(1)} %collective-permute-done.8.refs_11_), channel_id=1, source_target_pairs={{0,2},{1,3},{2,0},{3,1},{4,6},{5,7},{6,4},{7,5},{8,10},{9,11},{10,... | collective-permute-start | bytes 368648 | tf_op jit(solution)/shard_map/ppermute | solution.py:188
  22.9 6.3 %collective-permute-start.5 = (bf16[32,1920]{1,0:T(8,128)(2,1)S(1)}, bf16[32,1920]{1,0:T(8,128)(2,1)S(1)}, u32[]{:S(2)}, u32[]{:S(2)}) collective-permute-start(bf16[32,1920]{1,0:T(8,128)(2,1)S(1)} %collective-permute-done.refs_7_), channel_id=1, source_target_pairs={{0,2},{1,3},{2,0},{3,1},{4,6},{5,7},{6,4},{7,5},{8,10},{9,11},{10,... | collective-permute-start | bytes 368648 | tf_op jit(solution)/shard_map/ppermute | solution.py:188
  23.4 5.8 %collective-permute-start.3 = (bf16[32,1920]{1,0:T(8,128)(2,1)S(1)}, bf16[32,1920]{1,0:T(8,128)(2,1)S(1)}, u32[]{:S(2)}, u32[]{:S(2)}) collective-permute-start(bf16[32,1920]{1,0:T(8,128)(2,1)S(1)} %collective-permute-done.refs_7_), channel_id=1, source_target_pairs={{0,4},{1,5},{2,6},{3,7},{4,0},{5,1},{6,2},{7,3},{8,12},{9,13},{10,... | collective-permute-start | bytes 368648 | tf_op jit(solution)/shard_map/ppermute | solution.py:188
  23.7 6.8 %collective-permute-start.1 = (bf16[32,1920]{1,0:T(8,128)(2,1)S(1)}, bf16[32,1920]{1,0:T(8,128)(2,1)S(1)}, u32[]{:S(2)}, u32[]{:S(2)}) collective-permute-start(bf16[32,1920]{1,0:T(8,128)(2,1)S(1)} %collective-permute-done.refs_7_), channel_id=1, source_target_pairs={{0,6},{1,7},{2,4},{3,5},{4,2},{5,3},{6,0},{7,1},{8,14},{9,15},{10,... | collective-permute-start | bytes 368648 | tf_op jit(solution)/shard_map/ppermute | solution.py:188
  26.4 4.9 %collective-permute-start.7 = (bf16[32,1920]{1,0:T(8,128)(2,1)S(1)}, bf16[32,1920]{1,0:T(8,128)(2,1)S(1)}, u32[]{:S(2)}, u32[]{:S(2)}) collective-permute-start(bf16[32,1920]{1,0:T(8,128)(2,1)S(1)} %collective-permute-done.refs_7_), channel_id=1, source_target_pairs={{0,1},{1,0},{2,3},{3,2},{4,5},{5,4},{6,7},{7,6},{8,9},{9,8},{10,11... | collective-permute-start | bytes 368648 | tf_op jit(solution)/shard_map/ppermute | solution.py:188
  26.9 4.4 %collective-permute-start.10 = (bf16[32,1920]{1,0:T(8,128)(2,1)S(1)}, bf16[32,1920]{1,0:T(8,128)(2,1)S(1)}, u32[]{:S(2)}, u32[]{:S(2)}) collective-permute-start(bf16[32,1920]{1,0:T(8,128)(2,1)S(1)} %collective-permute-done.9.refs_9_), channel_id=1, source_target_pairs={{0,1},{1,0},{2,3},{3,2},{4,5},{5,4},{6,7},{7,6},{8,9},{9,8},{10,11... | collective-permute-start | bytes 368648 | tf_op jit(solution)/shard_map/ppermute | solution.py:188
  29.2 2.1 %collective-permute-start.6 = (bf16[32,1920]{1,0:T(8,128)(2,1)S(1)}, bf16[32,1920]{1,0:T(8,128)(2,1)S(1)}, u32[]{:S(2)}, u32[]{:S(2)}) collective-permute-start(bf16[32,1920]{1,0:T(8,128)(2,1)S(1)} %collective-permute-done.5.refs_5_), channel_id=1, source_target_pairs={{0,1},{1,0},{2,3},{3,2},{4,5},{5,4},{6,7},{7,6},{8,9},{9,8},{10,11... | collective-permute-start | bytes 368648 | tf_op jit(solution)/shard_map/ppermute | solution.py:188
  29.2 2.1 %collective-permute-start.4 = (bf16[32,1920]{1,0:T(8,128)(2,1)S(1)}, bf16[32,1920]{1,0:T(8,128)(2,1)S(1)}, u32[]{:S(2)}, u32[]{:S(2)}) collective-permute-start(bf16[32,1920]{1,0:T(8,128)(2,1)S(1)} %collective-permute-done.3.refs_3_), channel_id=1, source_target_pairs={{0,1},{1,0},{2,3},{3,2},{4,5},{5,4},{6,7},{7,6},{8,9},{9,8},{10,11... | collective-permute-start | bytes 368648 | tf_op jit(solution)/shard_map/ppermute | solution.py:188
  30.5 1.3 %collective-permute-start.2 = (bf16[32,1920]{1,0:T(8,128)(2,1)S(1)}, bf16[32,1920]{1,0:T(8,128)(2,1)S(1)}, u32[]{:S(2)}, u32[]{:S(2)}) collective-permute-start(bf16[32,1920]{1,0:T(8,128)(2,1)S(1)} %collective-permute-done.1.refs_1_), channel_id=1, source_target_pairs={{0,1},{1,0},{2,3},{3,2},{4,5},{5,4},{6,7},{7,6},{8,9},{9,8},{10,11... | collective-permute-start | bytes 368648 | tf_op jit(solution)/shard_map/ppermute | solution.py:188

commit v6 on v5

--- a/solution.py
+++ b/solution.py
@@ -8,7 +8,9 @@
 from jax.sharding import PartitionSpec as P
 
 LANE = 128
-CHUNK = 8
+CHUNK = 16
+ROLLS = 4
+HANDED = (0, 1, 2, 3, 8, 9, 4, 5, 6, 7, 14, 15, 12, 13, 10, 11)
 SUB = 16
 
 
@@ -80,6 +82,12 @@
     for copy in taps_copies:
         copy.wait()
 
+    extra = LANE // SUB - ROLLS
+    source = lax.broadcasted_iota(jnp.int32, (2 * LANE, extra * LANE), 0)
+    target = lax.broadcasted_iota(jnp.int32, (2 * LANE, extra * LANE), 1)
+    target = target % LANE + (target // LANE + ROLLS) * SUB
+    shifts = jnp.where(source == target, 1.0, 0.0).astype(jnp.bfloat16)
+
     def frames(section, tile, tiles):
         width = (tiles + 1) * LANE
         first = (section * slot + tile) * LANE
@@ -87,11 +95,19 @@
             first = pl.multiple_of(first, LANE)
         wide = wide_ref[:, pl.ds(first, width)]
         moved = [wide]
-        for q in range(1, LANE // SUB):
+        for q in range(1, ROLLS):
             moved.append(pltpu.roll(wide, width - SUB * q, axis=1))
+        stacked = jnp.concatenate(
+            [wide[:, number * LANE : (number + 2) * LANE] for number in range(tiles)], axis=0
+        )
+        rest = jnp.dot(stacked, shifts, preferred_element_type=jnp.float32).astype(wide.dtype)
         pieces = []
         for number in range(tiles):
             pieces += [part[:, number * LANE : (number + 1) * LANE] for part in moved]
+            pieces += [
+                rest[number * SUB : (number + 1) * SUB, q * LANE : (q + 1) * LANE]
+                for q in range(LANE // SUB - ROLLS)
+            ]
         return jnp.concatenate(pieces, axis=0)
 
     def shifted(section, tile, tiles):
@@ -211,11 +227,10 @@
 
 def maximum_over_group(values):
     size = lax.axis_size("tmpl")
-    radix = 4 if size > 4 and size % 4 == 0 else 2
-    near = [list(range(first, first + radix)) for first in range(0, size, radix)]
-    far = [list(range(first, size, radix)) for first in range(radix)]
-    values = lax.pmax(values, "tmpl", axis_index_groups=near)
-    return lax.pmax(values, "tmpl", axis_index_groups=far)
+    tiles = values.reshape(1, -1, LANE)
+    copies = jnp.broadcast_to(tiles, (size,) + tiles.shape[1:])
+    others = lax.all_to_all(copies, "tmpl", split_axis=0, concat_axis=0, tiled=True)
+    return jnp.max(others, axis=0).reshape(values.shape)
 
 
 def arrange_kernel(offset_ref, coeffs_ref, out_ref):
@@ -248,8 +263,9 @@
     )(offset, coeffs)
 
 
-def recon_kernel(coeffs_ref, *refs):
-    pieces, snr_ref, peak_ref = refs[-3::-1], refs[-2], refs[-1]
+def recon_kernel(order, coeffs_ref, *refs):
+    pieces = [refs[order.index(place)] for place in range(len(order))]
+    snr_ref, peak_ref = refs[-2], refs[-1]
     samples = snr_ref.shape[1]
     source = lax.broadcasted_iota(jnp.int32, (2 * LANE, 2 * LANE), 0) % LANE
     target = lax.broadcasted_iota(jnp.int32, (2 * LANE, 2 * LANE), 1) // 2
@@ -287,8 +303,9 @@
 
 
 def reconstruct(coeffs, blocks, samples):
+    order = HANDED if len(HANDED) == len(blocks) else tuple(range(len(blocks)))
     return pl.pallas_call(
-        recon_kernel,
+        functools.partial(recon_kernel, order),
         out_shape=(
             jax.ShapeDtypeStruct((coeffs.shape[1], samples), jnp.bfloat16),
             jax.ShapeDtypeStruct((1, samples), jnp.float32),
@@ -297,7 +314,7 @@
         out_specs=(pl.BlockSpec(memory_space=pltpu.VMEM),) * 2,
         compiler_params=pltpu.CompilerParams(vmem_limit_bytes=16 * 2**20),
         name="reconstruct",
-    )(coeffs, *blocks[::-1])
+    )(coeffs, *[blocks[place] for place in order])
 
 
 def per_device(strain_fast, strain_half, strain_quarter, strain_eighth, basis_taps, recon_coeffs):

time: 52.8 us -> 45.9 us (0.87)
  blocking collectives: 18.8 us -> 11.4 us
  waiting for transfers between devices: 9.37 us -> 6.36 us
  starting transfers between devices: 11.8 us -> 13.9 us
  Pallas kernels: 12 us -> 12.7 us
  other arithmetic: 0 us -> 0.61 us
    pmax x2 -> x0, blocking collectives: 18.8 us -> none  [the longest x1 12.9 us: maximum_over_group(): return lax.pmax(values, 'tmpl', axis_index_groups=far)]
    all_to_all x0 -> x1, blocking collectives: none -> 11.4 us  [maximum_over_group(): lax.all_to_all(copies, 'tmpl', split_axis=0, concat_axis=0, tiled=True)]
    ppermute x15, waiting for transfers between devices: 9.37 us -> 6.36 us  [exchange(): return lax.ppermute(block, 'tmpl', [(i, i ^ distance) for i in range(size)])]
    ppermute x15, starting transfers between devices: 11.8 us -> 13.9 us  [exchange(): return lax.ppermute(block, 'tmpl', [(i, i ^ distance) for i in range(size)])]
    pallas_call x1, Pallas kernels: 9.29 us -> 10 us  [correlate(): pl.pallas_call(correlate_kernel, out_shape=jax.ShapeDtypeStruct((padded,...]
    reduce_max x0 -> x1, other arithmetic: none -> 0.61 us  [maximum_over_group(): return jnp.max(others, axis=0).reshape(values.shape)]
  transfers between devices with their start and end apart: 15 -> 15, of which waited for: 6 -> 7; matrix products, arithmetic and copies ran while one was open for 0% -> 0% of each run, Pallas kernels for 1% -> 2%
where the time goes in v6:
time: 45.9 us; the launch traced here: 45.7 us
  starting transfers between devices  13.9 us (30%)
  Pallas kernels  12.7 us (28%)
  blocking collectives  11.4 us (25%)
  waiting for transfers between devices  6.36 us (14%)
  between operations  0.71 us (2%)
  other arithmetic  0.61 us (1%)
    ppermute x15, starting transfers between devices, exchange(): return lax.ppermute(block, 'tmpl', [(i, i ^ distance) for i in range(size)])  13.9 us
    all_to_all x1, blocking collectives, maximum_over_group(): lax.all_to_all(copies, 'tmpl', split_axis=0, concat_axis=0, tiled=True)  11.4 us
    pallas_call x1, Pallas kernels, correlate(): pl.pallas_call(correlate_kernel, out_shape=jax.ShapeDtypeStruct((padded,...  10 us
    ppermute x15, waiting for transfers between devices, exchange(): return lax.ppermute(block, 'tmpl', [(i, i ^ distance) for i in range(size)])  6.36 us
    pallas_call x1, Pallas kernels, reconstruct(): pl.pallas_call(functools.partial(recon_kernel, order), out_shape=(jax.Sha...  1.95 us
  transfers between devices with their start and end apart: 15, of which 7 were waited for; matrix products, arithmetic and copies ran while one was open for 0% of the time, Pallas kernels for 2%

profile of v6, /device:TPU:0, one launch (start us, length us, event | category | flops | bytes accessed | tf_op | source)
XLA Modules:
  0.0 45.7 jit_solution(13714662412561353935)
XLA Ops:
  0.6 0.0 copy-start
  0.6 10.0 %correlate.1.refs_0_ = bf16[32,1920]{1,0:T(8,128)(2,1)} custom-call(bf16[72,128]{1,0:T(8,128)(2,1)} %bitcast.9, bf16[68,128]{1,0:T(8,128)(2,1)} %bitcast.10, bf16[66,128]{1,0:T(8,128)(2,1)} %bitcast.11, bf16[65,128]{1,0:T(8,128)(2,1)} %bitcast.12, bf16[4,32,8192]{2,1,0:T(8,128)(2,1)} %refs_4_.1), custom_call_target="tpu_custom_call" | custom-call | flops 1006632960 | bytes 2097152 | tf_op jit(solution)/shard_map/correlate/pallas_call | solution.py:177
  10.6 0.0 copy-start.1
  10.7 3.1 %collective-permute-start.5 = (bf16[32,1920]{1,0:T(8,128)(2,1)}, bf16[32,1920]{1,0:T(8,128)(2,1)S(1)}, u32[]{:S(2)}, u32[]{:S(2)}) collective-permute-start(bf16[32,1920]{1,0:T(8,128)(2,1)} %correlate.1.refs_0_), channel_id=1, source_target_pairs={{0,4},{1,5},{2,6},{3,7},{4,0},{5,1},{6,2},{7,3},{8,12},{9,13},{10,... | collective-permute-start | bytes 368648 | tf_op jit(solution)/shard_map/ppermute | solution.py:204
  13.7 2.6 %collective-permute-start.3 = (bf16[32,1920]{1,0:T(8,128)(2,1)}, bf16[32,1920]{1,0:T(8,128)(2,1)S(1)}, u32[]{:S(2)}, u32[]{:S(2)}) collective-permute-start(bf16[32,1920]{1,0:T(8,128)(2,1)} %correlate.1.refs_0_), channel_id=1, source_target_pairs={{0,8},{1,9},{2,10},{3,11},{4,12},{5,13},{6,14},{7,15},{8,0},{9,1},... | collective-permute-start | bytes 368648 | tf_op jit(solution)/shard_map/ppermute | solution.py:204
  16.3 1.5 %collective-permute-start.1 = (bf16[32,1920]{1,0:T(8,128)(2,1)}, bf16[32,1920]{1,0:T(8,128)(2,1)S(1)}, u32[]{:S(2)}, u32[]{:S(2)}) collective-permute-start(bf16[32,1920]{1,0:T(8,128)(2,1)} %correlate.1.refs_0_), channel_id=1, source_target_pairs={{0,2},{1,3},{2,0},{3,1},{4,6},{5,7},{6,4},{7,5},{8,10},{9,11},{10,... | collective-permute-start | bytes 368648 | tf_op jit(solution)/shard_map/ppermute | solution.py:204
  17.9 0.0 collective-permute-start
  17.9 0.8 %collective-permute-done.5.refs_6_ = bf16[32,1920]{1,0:T(8,128)(2,1)S(1)} collective-permute-done((bf16[32,1920]{1,0:T(8,128)(2,1)}, bf16[32,1920]{1,0:T(8,128)(2,1)S(1)}, u32[]{:S(2)}, u32[]{:S(2)}) %collective-permute-start.5) | collective-permute-done | bytes 122912 | tf_op jit(solution)/shard_map/ppermute | solution.py:204
  18.7 1.9 %collective-permute-start.7 = (bf16[32,1920]{1,0:T(8,128)(2,1)S(1)}, bf16[32,1920]{1,0:T(8,128)(2,1)S(1)}, u32[]{:S(2)}, u32[]{:S(2)}) collective-permute-start(bf16[32,1920]{1,0:T(8,128)(2,1)S(1)} %collective-permute-done.5.refs_6_), channel_id=1, source_target_pairs={{0,2},{1,3},{2,0},{3,1},{4,6},{5,7},{6,4},{7,5},{8,10},{9,11},{10,... | collective-permute-start | bytes 368648 | tf_op jit(solution)/shard_map/ppermute | solution.py:204
  20.6 0.0 collective-permute-start.6
  20.6 1.7 %collective-permute-done.3.refs_4_ = bf16[32,1920]{1,0:T(8,128)(2,1)S(1)} collective-permute-done((bf16[32,1920]{1,0:T(8,128)(2,1)}, bf16[32,1920]{1,0:T(8,128)(2,1)S(1)}, u32[]{:S(2)}, u32[]{:S(2)}) %collective-permute-start.3) | collective-permute-done | bytes 122912 | tf_op jit(solution)/shard_map/ppermute | solution.py:204
  22.3 1.5 %collective-permute-start.13 = (bf16[32,1920]{1,0:T(8,128)(2,1)S(1)}, bf16[32,1920]{1,0:T(8,128)(2,1)S(1)}, u32[]{:S(2)}, u32[]{:S(2)}) collective-permute-start(bf16[32,1920]{1,0:T(8,128)(2,1)S(1)} %collective-permute-done.3.refs_4_), channel_id=1, source_target_pairs={{0,2},{1,3},{2,0},{3,1},{4,6},{5,7},{6,4},{7,5},{8,10},{9,11},{10,... | collective-permute-start | bytes 368648 | tf_op jit(solution)/shard_map/ppermute | solution.py:204
  23.9 0.0 collective-permute-done.1.refs_2_
  23.9 0.4 collective-permute-start.11
  24.3 0.0 collective-permute-done.refs_1_
  24.3 1.5 %collective-permute-start.9 = (bf16[32,1920]{1,0:T(8,128)(2,1)S(1)}, bf16[32,1920]{1,0:T(8,128)(2,1)S(1)}, u32[]{:S(2)}, u32[]{:S(2)}) collective-permute-start(bf16[32,1920]{1,0:T(8,128)(2,1)S(1)} %collective-permute-done.3.refs_4_), channel_id=1, source_target_pairs={{0,6},{1,7},{2,4},{3,5},{4,2},{5,3},{6,0},{7,1},{8,14},{9,15},{10,... | collective-permute-start | bytes 368648 | tf_op jit(solution)/shard_map/ppermute | solution.py:204
  25.8 0.0 collective-permute-done.7.refs_8_
  25.8 0.0 collective-permute-start.4
  25.8 0.0 collective-permute-done.6.refs_7_
  25.9 0.5 %collective-permute-start.2 = (bf16[32,1920]{1,0:T(8,128)(2,1)S(1)}, bf16[32,1920]{1,0:T(8,128)(2,1)S(1)}, u32[]{:S(2)}, u32[]{:S(2)}) collective-permute-start(bf16[32,1920]{1,0:T(8,128)(2,1)S(1)} %collective-permute-done.1.refs_2_), channel_id=1, source_target_pairs={{0,1},{1,0},{2,3},{3,2},{4,5},{5,4},{6,7},{7,6},{8,9},{9,8},{10,11... | collective-permute-start | bytes 368648 | tf_op jit(solution)/shard_map/ppermute | solution.py:204
  26.4 2.2 %collective-permute-done.13.refs_14_ = bf16[32,1920]{1,0:T(8,128)(2,1)S(1)} collective-permute-done((bf16[32,1920]{1,0:T(8,128)(2,1)S(1)}, bf16[32,1920]{1,0:T(8,128)(2,1)S(1)}, u32[]{:S(2)}, u32[]{:S(2)}) %collective-permute-start.13) | collective-permute-done | bytes 122912 | tf_op jit(solution)/shard_map/ppermute | solution.py:204
  28.5 0.0 collective-permute-start.8
  28.5 0.2 collective-permute-done.11.refs_12_
  28.7 0.3 collective-permute-start.14
  29.1 1.1 %collective-permute-done.9.refs_10_ = bf16[32,1920]{1,0:T(8,128)(2,1)S(1)} collective-permute-done((bf16[32,1920]{1,0:T(8,128)(2,1)S(1)}, bf16[32,1920]{1,0:T(8,128)(2,1)S(1)}, u32[]{:S(2)}, u32[]{:S(2)}) %collective-permute-start.9) | collective-permute-done | bytes 122912 | tf_op jit(solution)/shard_map/ppermute | solution.py:204
  30.2 0.0 collective-permute-start.12
  30.2 0.0 collective-permute-done.4.refs_5_
  30.2 0.5 %collective-permute-start.10 = (bf16[32,1920]{1,0:T(8,128)(2,1)S(1)}, bf16[32,1920]{1,0:T(8,128)(2,1)S(1)}, u32[]{:S(2)}, u32[]{:S(2)}) collective-permute-start(bf16[32,1920]{1,0:T(8,128)(2,1)S(1)} %collective-permute-done.9.refs_10_), channel_id=1, source_target_pairs={{0,1},{1,0},{2,3},{3,2},{4,5},{5,4},{6,7},{7,6},{8,9},{9,8},{10,11... | collective-permute-start | bytes 368648 | tf_op jit(solution)/shard_map/ppermute | solution.py:204
  30.7 0.0 copy-done
  30.7 0.7 %arrange.1.coeffs_ref = bf16[4,256,512]{2,1,0:T(8,128)(2,1)S(1)} custom-call(s32[1]{0:T(128)} %bitcast.offset_ref, bf16[4,256,512]{2,1,0:T(8,128)(2,1)S(1)} %copy-done), custom_call_target="tpu_custom_call" | custom-call | flops 536870912 | bytes 2097152 | tf_op jit(solution)/shard_map/arrange/pallas_call | solution.py:248
  31.4 0.0 collective-permute-done.2.refs_3_
  31.5 0.0 collective-permute-done.8.refs_9_
  31.5 0.0 collective-permute-done.14.refs_15_
  31.5 0.1 collective-permute-done.12.refs_13_
  31.5 0.2 collective-permute-done.10.refs_11_
  31.7 0.0 copy-done.1
  31.7 2.0 %reconstruct.1 = (bf16[256,1024]{1,0:T(8,128)(2,1)}, f32[1,1024]{1,0:T(1,128)S(1)}) custom-call(bf16[4,256,512]{2,1,0:T(8,128)(2,1)S(1)} %arrange.1.coeffs_ref, bf16[32,1920]{1,0:T(8,128)(2,1)S(1)} %copy-done.1, bf16[32,1920]{1,0:T(8,128)(2,1)S(1)} %collective-permute-done.refs_1_, bf16[32,1920]{1,0:T(8,128)(2,1)S(1)} %collective-permute-done.1.refs_2_, ...), custom_call_target="tpu_custom_call" | custom-call | tf_op jit(solution)/shard_map/reconstruct/pallas_call | solution.py:307
  33.7 11.4 %all_to_all.5 = f32[16,8,128]{2,1,0:T(8,128)S(1)} all-to-all(f32[16,8,128]{2,1,0:T(8,128)S(1)} %broadcast_in_dim.8), channel_id=1, replica_groups=mesh['bank'=2,'tmpl'=16] {'tmpl'}, dimensions={0} | all-to-all | bytes 131072 | tf_op jit(solution)/shard_map/all_to_all | solution.py:232
  45.1 0.6 %reduce_max.9 = f32[8,128]{1,0:T(8,128)} reduce(f32[16,8,128]{2,1,0:T(8,128)S(1)} %all_to_all.5, f32[]{:T(128)} %constant.2.clone.1), dimensions={0}, to_apply=%region_0.0 | reduce | flops 15360 | bytes 69636 | tf_op jit(solution)/shard_map/reduce_max | solution.py:233
  (1 shorter events, 0.0 us)
Async XLA Ops:
  0.6 30.1 %copy-start = (bf16[4,256,512]{2,1,0:T(8,128)(2,1)S(1)}, bf16[4,256,512]{2,1,0:T(8,128)(2,1)}, u32[]{:S(2)}) copy-start(bf16[4,256,512]{2,1,0:T(8,128)(2,1)} %coeffs_ref.1) | copy-start | bytes 3145732
  10.6 21.1 %copy-start.1 = (bf16[32,1920]{1,0:T(8,128)(2,1)S(1)}, bf16[32,1920]{1,0:T(8,128)(2,1)}, u32[]{:S(2)}) copy-start(bf16[32,1920]{1,0:T(8,128)(2,1)} %correlate.1.refs_0_) | copy-start | bytes 368644
  10.7 8.0 %collective-permute-start.5 = (bf16[32,1920]{1,0:T(8,128)(2,1)}, bf16[32,1920]{1,0:T(8,128)(2,1)S(1)}, u32[]{:S(2)}, u32[]{:S(2)}) collective-permute-start(bf16[32,1920]{1,0:T(8,128)(2,1)} %correlate.1.refs_0_), channel_id=1, source_target_pairs={{0,4},{1,5},{2,6},{3,7},{4,0},{5,1},{6,2},{7,3},{8,12},{9,13},{10,... | collective-permute-start | bytes 368648 | tf_op jit(solution)/shard_map/ppermute | solution.py:204
  13.7 8.6 %collective-permute-start.3 = (bf16[32,1920]{1,0:T(8,128)(2,1)}, bf16[32,1920]{1,0:T(8,128)(2,1)S(1)}, u32[]{:S(2)}, u32[]{:S(2)}) collective-permute-start(bf16[32,1920]{1,0:T(8,128)(2,1)} %correlate.1.refs_0_), channel_id=1, source_target_pairs={{0,8},{1,9},{2,10},{3,11},{4,12},{5,13},{6,14},{7,15},{8,0},{9,1},... | collective-permute-start | bytes 368648 | tf_op jit(solution)/shard_map/ppermute | solution.py:204
  16.3 7.5 %collective-permute-start.1 = (bf16[32,1920]{1,0:T(8,128)(2,1)}, bf16[32,1920]{1,0:T(8,128)(2,1)S(1)}, u32[]{:S(2)}, u32[]{:S(2)}) collective-permute-start(bf16[32,1920]{1,0:T(8,128)(2,1)} %correlate.1.refs_0_), channel_id=1, source_target_pairs={{0,2},{1,3},{2,0},{3,1},{4,6},{5,7},{6,4},{7,5},{8,10},{9,11},{10,... | collective-permute-start | bytes 368648 | tf_op jit(solution)/shard_map/ppermute | solution.py:204
  17.9 6.4 %collective-permute-start = (bf16[32,1920]{1,0:T(8,128)(2,1)}, bf16[32,1920]{1,0:T(8,128)(2,1)S(1)}, u32[]{:S(2)}, u32[]{:S(2)}) collective-permute-start(bf16[32,1920]{1,0:T(8,128)(2,1)} %correlate.1.refs_0_), channel_id=1, source_target_pairs={{0,1},{1,0},{2,3},{3,2},{4,5},{5,4},{6,7},{7,6},{8,9},{9,8},{10,11... | collective-permute-start | bytes 368648 | tf_op jit(solution)/shard_map/ppermute | solution.py:204
  18.7 7.1 %collective-permute-start.7 = (bf16[32,1920]{1,0:T(8,128)(2,1)S(1)}, bf16[32,1920]{1,0:T(8,128)(2,1)S(1)}, u32[]{:S(2)}, u32[]{:S(2)}) collective-permute-start(bf16[32,1920]{1,0:T(8,128)(2,1)S(1)} %collective-permute-done.5.refs_6_), channel_id=1, source_target_pairs={{0,2},{1,3},{2,0},{3,1},{4,6},{5,7},{6,4},{7,5},{8,10},{9,11},{10,... | collective-permute-start | bytes 368648 | tf_op jit(solution)/shard_map/ppermute | solution.py:204
  20.6 5.3 %collective-permute-start.6 = (bf16[32,1920]{1,0:T(8,128)(2,1)S(1)}, bf16[32,1920]{1,0:T(8,128)(2,1)S(1)}, u32[]{:S(2)}, u32[]{:S(2)}) collective-permute-start(bf16[32,1920]{1,0:T(8,128)(2,1)S(1)} %collective-permute-done.5.refs_6_), channel_id=1, source_target_pairs={{0,1},{1,0},{2,3},{3,2},{4,5},{5,4},{6,7},{7,6},{8,9},{9,8},{10,11... | collective-permute-start | bytes 368648 | tf_op jit(solution)/shard_map/ppermute | solution.py:204
  22.3 6.2 %collective-permute-start.13 = (bf16[32,1920]{1,0:T(8,128)(2,1)S(1)}, bf16[32,1920]{1,0:T(8,128)(2,1)S(1)}, u32[]{:S(2)}, u32[]{:S(2)}) collective-permute-start(bf16[32,1920]{1,0:T(8,128)(2,1)S(1)} %collective-permute-done.3.refs_4_), channel_id=1, source_target_pairs={{0,2},{1,3},{2,0},{3,1},{4,6},{5,7},{6,4},{7,5},{8,10},{9,11},{10,... | collective-permute-start | bytes 368648 | tf_op jit(solution)/shard_map/ppermute | solution.py:204
  23.9 4.9 %collective-permute-start.11 = (bf16[32,1920]{1,0:T(8,128)(2,1)S(1)}, bf16[32,1920]{1,0:T(8,128)(2,1)S(1)}, u32[]{:S(2)}, u32[]{:S(2)}) collective-permute-start(bf16[32,1920]{1,0:T(8,128)(2,1)S(1)} %collective-permute-done.3.refs_4_), channel_id=1, source_target_pairs={{0,4},{1,5},{2,6},{3,7},{4,0},{5,1},{6,2},{7,3},{8,12},{9,13},{10,... | collective-permute-start | bytes 368648 | tf_op jit(solution)/shard_map/ppermute | solution.py:204
  24.3 5.9 %collective-permute-start.9 = (bf16[32,1920]{1,0:T(8,128)(2,1)S(1)}, bf16[32,1920]{1,0:T(8,128)(2,1)S(1)}, u32[]{:S(2)}, u32[]{:S(2)}) collective-permute-start(bf16[32,1920]{1,0:T(8,128)(2,1)S(1)} %collective-permute-done.3.refs_4_), channel_id=1, source_target_pairs={{0,6},{1,7},{2,4},{3,5},{4,2},{5,3},{6,0},{7,1},{8,14},{9,15},{10,... | collective-permute-start | bytes 368648 | tf_op jit(solution)/shard_map/ppermute | solution.py:204
  25.8 4.4 %collective-permute-start.4 = (bf16[32,1920]{1,0:T(8,128)(2,1)S(1)}, bf16[32,1920]{1,0:T(8,128)(2,1)S(1)}, u32[]{:S(2)}, u32[]{:S(2)}) collective-permute-start(bf16[32,1920]{1,0:T(8,128)(2,1)S(1)} %collective-permute-done.3.refs_4_), channel_id=1, source_target_pairs={{0,1},{1,0},{2,3},{3,2},{4,5},{5,4},{6,7},{7,6},{8,9},{9,8},{10,11... | collective-permute-start | bytes 368648 | tf_op jit(solution)/shard_map/ppermute | solution.py:204
  25.9 5.6 %collective-permute-start.2 = (bf16[32,1920]{1,0:T(8,128)(2,1)S(1)}, bf16[32,1920]{1,0:T(8,128)(2,1)S(1)}, u32[]{:S(2)}, u32[]{:S(2)}) collective-permute-start(bf16[32,1920]{1,0:T(8,128)(2,1)S(1)} %collective-permute-done.1.refs_2_), channel_id=1, source_target_pairs={{0,1},{1,0},{2,3},{3,2},{4,5},{5,4},{6,7},{7,6},{8,9},{9,8},{10,11... | collective-permute-start | bytes 368648 | tf_op jit(solution)/shard_map/ppermute | solution.py:204
  28.5 2.9 %collective-permute-start.8 = (bf16[32,1920]{1,0:T(8,128)(2,1)S(1)}, bf16[32,1920]{1,0:T(8,128)(2,1)S(1)}, u32[]{:S(2)}, u32[]{:S(2)}) collective-permute-start(bf16[32,1920]{1,0:T(8,128)(2,1)S(1)} %collective-permute-done.7.refs_8_), channel_id=1, source_target_pairs={{0,1},{1,0},{2,3},{3,2},{4,5},{5,4},{6,7},{7,6},{8,9},{9,8},{10,11... | collective-permute-start | bytes 368648 | tf_op jit(solution)/shard_map/ppermute | solution.py:204
  28.7 2.7 %collective-permute-start.14 = (bf16[32,1920]{1,0:T(8,128)(2,1)S(1)}, bf16[32,1920]{1,0:T(8,128)(2,1)S(1)}, u32[]{:S(2)}, u32[]{:S(2)}) collective-permute-start(bf16[32,1920]{1,0:T(8,128)(2,1)S(1)} %collective-permute-done.13.refs_14_), channel_id=1, source_target_pairs={{0,1},{1,0},{2,3},{3,2},{4,5},{5,4},{6,7},{7,6},{8,9},{9,8},{10,11... | collective-permute-start | bytes 368648 | tf_op jit(solution)/shard_map/ppermute | solution.py:204
  30.2 1.3 %collective-permute-start.12 = (bf16[32,1920]{1,0:T(8,128)(2,1)S(1)}, bf16[32,1920]{1,0:T(8,128)(2,1)S(1)}, u32[]{:S(2)}, u32[]{:S(2)}) collective-permute-start(bf16[32,1920]{1,0:T(8,128)(2,1)S(1)} %collective-permute-done.11.refs_12_), channel_id=1, source_target_pairs={{0,1},{1,0},{2,3},{3,2},{4,5},{5,4},{6,7},{7,6},{8,9},{9,8},{10,11... | collective-permute-start | bytes 368648 | tf_op jit(solution)/shard_map/ppermute | solution.py:204
  30.2 1.5 %collective-permute-start.10 = (bf16[32,1920]{1,0:T(8,128)(2,1)S(1)}, bf16[32,1920]{1,0:T(8,128)(2,1)S(1)}, u32[]{:S(2)}, u32[]{:S(2)}) collective-permute-start(bf16[32,1920]{1,0:T(8,128)(2,1)S(1)} %collective-permute-done.9.refs_10_), channel_id=1, source_target_pairs={{0,1},{1,0},{2,3},{3,2},{4,5},{5,4},{6,7},{7,6},{8,9},{9,8},{10,11... | collective-permute-start | bytes 368648 | tf_op jit(solution)/shard_map/ppermute | solution.py:204

commit v7 on v6

--- a/solution.py
+++ b/solution.py
@@ -8,23 +8,26 @@
 from jax.sharding import PartitionSpec as P
 
 LANE = 128
-CHUNK = 16
+CHUNK = 8
+SUB = 16
+ROWS = 8
 ROLLS = 4
-HANDED = (0, 1, 2, 3, 8, 9, 4, 5, 6, 7, 14, 15, 12, 13, 10, 11)
+TIED = 1
+HANDED = (0, 1, 2, 3, 8, 9, 4, 5, 6, 7, 12, 13, 14, 15, 10, 11)
 SUB = 16
 
 
 def correlate_kernel(*refs):
     strain_refs, taps_ref, out_ref = refs[:4], refs[4], refs[5]
-    held_strains = refs[6:10]
-    held_taps, line_ref, row_ref, wide_ref, strain_sems, taps_sems = refs[10:]
+    held_strains, held_taps, line_ref, total_ref = refs[6:10], refs[10], refs[11], refs[12]
+    even_refs, odd_refs, strain_sems, taps_sems = refs[13:15], refs[15:17], refs[17], refs[18]
     sections = len(strain_refs)
     rows, taps = taps_ref.shape[1], taps_ref.shape[2]
     lines = [ref.shape[0] for ref in held_strains]
     blocks = [count - taps // LANE for count in lines]
     slot = line_ref.shape[0] // sections
-    every = sections * slot
     pad = (max(blocks) - 1) * LANE
+    groups = ((0, 1), (2, 3))
     strain_copies, taps_copies = [], []
     for section, source in enumerate(strain_refs):
         strain_copies.append(
@@ -39,48 +42,11 @@
         )
     for copy in strain_copies + taps_copies:
         copy.start()
+    after = held_taps.shape[2] - pad - taps
     for section in range(sections):
         held_taps[section, :, :pad] = jnp.zeros((rows, pad), held_taps.dtype)
-        after = held_taps.shape[2] - pad - taps
         held_taps[section, :, pad + taps :] = jnp.zeros((rows, after), held_taps.dtype)
-
-    for section, copy in enumerate(strain_copies):
-        copy.wait()
-        first = section * slot
-        line_ref[first : first + lines[section], :] = held_strains[section][...].astype(jnp.float32)
-        if slot > lines[section]:
-            line_ref[first + lines[section] : first + slot, :] = jnp.zeros(
-                (slot - lines[section], LANE), jnp.float32
-            )
-    pairs = jnp.concatenate(
-        [
-            line_ref[...].astype(jnp.bfloat16),
-            jnp.concatenate([line_ref[1:, :], jnp.zeros((1, LANE), jnp.float32)], axis=0).astype(
-                jnp.bfloat16
-            ),
-        ],
-        axis=1,
-    )
-    source = lax.broadcasted_iota(jnp.int32, (2 * LANE, 2 * LANE), 0)
-    target = lax.broadcasted_iota(jnp.int32, (2 * LANE, 2 * LANE), 1)
-    target = target % LANE + target // LANE
-    for r in range(0, SUB, 2):
-        select = jnp.where(source == target + r, 1.0, 0.0).astype(jnp.bfloat16)
-        moved = jnp.dot(pairs, select, preferred_element_type=jnp.float32)
-        row_ref[r * every : (r + 1) * every, :] = moved[:, :LANE]
-        row_ref[(r + 1) * every : (r + 2) * every, :] = moved[:, LANE:]
-
-    def place_rows(number, carry):
-        for line in range(SUB):
-            line = number * SUB + line
-            piece = row_ref[pl.ds(line, SUB, stride=every), :].astype(jnp.bfloat16)
-            wide_ref[:, pl.ds(pl.multiple_of(line * LANE, LANE), LANE)] = piece
-        return carry
-
-    lax.fori_loop(0, every // SUB, place_rows, 0)
-    wide_ref[:, every * LANE :] = jnp.zeros((SUB, LANE), wide_ref.dtype)
-    for copy in taps_copies:
-        copy.wait()
+    total_ref[...] = jnp.zeros(total_ref.shape, total_ref.dtype)
 
     extra = LANE // SUB - ROLLS
     source = lax.broadcasted_iota(jnp.int32, (2 * LANE, extra * LANE), 0)
@@ -88,80 +54,104 @@
     target = target % LANE + (target // LANE + ROLLS) * SUB
     shifts = jnp.where(source == target, 1.0, 0.0).astype(jnp.bfloat16)
 
-    def frames(section, tile, tiles):
-        width = (tiles + 1) * LANE
-        first = (section * slot + tile) * LANE
-        if not isinstance(first, int):
-            first = pl.multiple_of(first, LANE)
-        wide = wide_ref[:, pl.ds(first, width)]
+    for section, copy in enumerate(strain_copies):
+        copy.wait()
+        first = section * slot
+        line_ref[first : first + lines[section], :] = held_strains[section][...].astype(jnp.float32)
+        line_ref[first + lines[section] : first + slot, :] = jnp.zeros(
+            (slot - lines[section], LANE), jnp.float32
+        )
+
+    width = (CHUNK + 1) * LANE
+    row = lax.broadcasted_iota(jnp.int32, (ROWS, width), 0)
+
+    def build(frames, section, chunk):
+        first = section * slot + chunk * CHUNK
+        wide = jnp.concatenate(
+            [
+                jnp.broadcast_to(line_ref[pl.ds(first + number, 1), :], (ROWS, LANE))
+                for number in range(CHUNK + 1)
+            ],
+            axis=1,
+        )
+        for step in (1, 2, 4):
+            moved = pltpu.roll(wide, width - step, axis=1)
+            wide = jnp.where((row & step) != 0, moved, wide)
+        wide = jnp.concatenate([wide, pltpu.roll(wide, width - ROWS, axis=1)], axis=0)
+        wide = wide.astype(jnp.bfloat16)
         moved = [wide]
         for q in range(1, ROLLS):
             moved.append(pltpu.roll(wide, width - SUB * q, axis=1))
         stacked = jnp.concatenate(
-            [wide[:, number * LANE : (number + 2) * LANE] for number in range(tiles)], axis=0
+            [wide[:, number * LANE : (number + 2) * LANE] for number in range(CHUNK)], axis=0
         )
         rest = jnp.dot(stacked, shifts, preferred_element_type=jnp.float32).astype(wide.dtype)
-        pieces = []
-        for number in range(tiles):
-            pieces += [part[:, number * LANE : (number + 1) * LANE] for part in moved]
+        for number in range(CHUNK):
+            pieces = [part[:, number * LANE : (number + 1) * LANE] for part in moved]
             pieces += [
                 rest[number * SUB : (number + 1) * SUB, q * LANE : (q + 1) * LANE]
-                for q in range(LANE // SUB - ROLLS)
+                for q in range(extra)
             ]
-        return jnp.concatenate(pieces, axis=0)
-
-    def shifted(section, tile, tiles):
+            half = section % 2
+            frames[number * LANE : (number + 1) * LANE, half * LANE : (half + 1) * LANE] = (
+                jnp.concatenate(pieces, axis=0)
+            )
+
+    def shifted(section, chunk, tiles):
         pieces = []
         for u in range(blocks[section]):
-            first = pad + (tile - u) * LANE
+            first = pad + (chunk * CHUNK - u) * LANE
             if not isinstance(first, int):
                 first = pl.multiple_of(first, LANE)
             pieces.append(held_taps[section, :, pl.ds(first, tiles * LANE)])
         return pieces
 
-    def term(group, tile, tiles):
-        left, right = [], []
+    def accumulate(frames, group, chunk, tiles=CHUNK):
+        left = []
         for section in group:
-            left += shifted(section, tile, tiles)
-            right.append(frames(section, tile, tiles))
+            left += shifted(section, chunk, tiles)
         left = jnp.concatenate(left, axis=0) if len(left) > 1 else left[0]
-        right = jnp.concatenate(right, axis=1) if len(right) > 1 else right[0]
-        both = jnp.dot(left, right, preferred_element_type=jnp.float32)
-        parts, row = [], 0
-        for number, section in enumerate(group):
-            height = blocks[section] * rows
-            parts.append(both[row : row + height, number * LANE : (number + 1) * LANE])
-            row += height
-        return parts
-
-    groups = [list(range(first, min(first + 2, sections))) for first in range(0, sections, 2)]
-
-    def step(number, totals):
-        parts = []
-        for group in groups:
-            parts += term(group, number * CHUNK, CHUNK)
-        return tuple(total + part for total, part in zip(totals, parts))
-
-    totals = lax.fori_loop(
-        0,
-        taps // (CHUNK * LANE),
-        step,
-        tuple(jnp.zeros((count * rows, LANE), jnp.float32) for count in blocks),
-    )
-    totals = list(totals)
-    for group in groups:
-        end = max(blocks[section] for section in group) - 1
-        for tile in range(0, end, CHUNK):
-            active = [section for section in group if blocks[section] - 1 > tile]
-            for section, part in zip(
-                active, term(active, taps // LANE + tile, min(CHUNK, end - tile))
-            ):
-                totals[section] = totals[section] + part
+        both = jnp.dot(
+            left, frames[: tiles * LANE, :], preferred_element_type=jnp.float32
+        )
+        height = 0
+        for section in group:
+            size = blocks[section] * rows
+            half = section % 2
+            at = sum(blocks[:section]) * rows
+            total_ref[at : at + size, :] += both[
+                height : height + size, half * LANE : (half + 1) * LANE
+            ]
+            height += size
+
+    def build_all(frames, chunk):
+        for section in range(sections):
+            build(frames[section // 2], section, chunk)
+
+    build_all(even_refs, 0)
+    for copy in taps_copies:
+        copy.wait()
+
+    def step(number, carry):
+        for group, frames in zip(groups, even_refs):
+            accumulate(frames, group, 2 * number)
+        build_all(odd_refs, 2 * number + 1)
+        for group, frames in zip(groups, odd_refs):
+            accumulate(frames, group, 2 * number + 1)
+        build_all(even_refs, 2 * number + 2)
+        return carry
+
+    chunks = taps // (CHUNK * LANE)
+    lax.fori_loop(0, chunks // 2, step, 0)
+    for group, frames in zip(groups, even_refs):
+        active = [section for section in group if blocks[section] > 1]
+        if active:
+            accumulate(frames, active, chunks, max(blocks[section] for section in active) - 1)
     place = 0
-    for section, total in enumerate(totals):
+    for section in range(sections):
         for u in range(blocks[section]):
-            part = total[u * rows : (u + 1) * rows].astype(out_ref.dtype)
-            out_ref[:, place : place + LANE] = part
+            at = (sum(blocks[:section]) + u) * rows
+            out_ref[:, place : place + LANE] = total_ref[at : at + rows, :].astype(out_ref.dtype)
             place += LANE
 
 
@@ -172,7 +162,7 @@
         basis_taps = jnp.pad(basis_taps, ((0, 0), (0, padded - rows), (0, 0)))
     samples = sum(x.shape[0] - taps for x in streams)
     longest = max(x.shape[0] for x in streams)
-    slot = -(-longest // (8 * LANE)) * 8
+    slot = -(-(longest + LANE) // (8 * LANE)) * 8
     lines = [x.reshape(-1, LANE) for x in streams]
     out = pl.pallas_call(
         correlate_kernel,
@@ -183,8 +173,10 @@
         + [
             pltpu.VMEM((sections, padded, 2 * longest - taps), jnp.bfloat16),
             pltpu.VMEM((sections * slot, LANE), jnp.float32),
-            pltpu.VMEM((SUB * sections * slot, LANE), jnp.float32),
-            pltpu.VMEM((SUB, (sections * slot + 1) * LANE), jnp.bfloat16),
+            pltpu.VMEM((samples // LANE * padded, LANE), jnp.float32),
+        ]
+        + [pltpu.VMEM((CHUNK * LANE, 2 * LANE), jnp.bfloat16)] * 4
+        + [
             pltpu.SemaphoreType.DMA((sections,)),
             pltpu.SemaphoreType.DMA((sections,)),
         ],
@@ -204,7 +196,7 @@
     return lax.ppermute(block, "tmpl", [(i, i ^ distance) for i in range(size)])
 
 
-def gather_blocks(block):
+def gather_blocks(block, ready):
     size = lax.axis_size("tmpl")
     if block.shape[0] % SUB:
         stride = 1
@@ -213,16 +205,17 @@
             others = [exchange(block, step * stride) for step in range(1, radix)]
             block = jnp.concatenate([block] + others, axis=0)
             stride *= radix
-        return [block]
+        return [block], ready
     held = {0: block}
-    for place in range(1, size):
-        if place & 1:
-            continue
+    for place in range(2, size, 2):
         high = 1 << (place.bit_length() - 1)
-        held[place] = exchange(held[0 if place == high else high], place if place == high else place ^ high)
+        held[place] = exchange(held[place ^ high and high], place ^ high or place)
     for place in range(1, size, 2):
-        held[place] = exchange(held[place ^ 1], 1)
-    return [held[place] for place in range(size)]
+        source = held[place ^ 1]
+        if place == TIED:
+            source, ready = lax.optimization_barrier((source, ready))
+        held[place] = exchange(source, 1)
+    return [held[place] for place in range(size)], ready
 
 
 def maximum_over_group(values):
@@ -321,8 +314,8 @@
     streams = (strain_fast, strain_half, strain_quarter, strain_eighth)
     samples = strain_fast.shape[0] - basis_taps.shape[2]
     offset = (lax.axis_index("tmpl") * basis_taps.shape[1]).astype(jnp.int32).reshape(1)
-    blocks = gather_blocks(correlate(streams, basis_taps))
     coeffs = arrange(recon_coeffs, offset)
+    blocks, coeffs = gather_blocks(correlate(streams, basis_taps), coeffs)
     snr_series, local_peak = reconstruct(coeffs, blocks, samples)
     peak_snr = maximum_over_group(local_peak.reshape(samples))
     return (snr_series, peak_snr)

time: 45.9 us -> 46.3 us (level)
  blocking collectives: 11.4 us -> 11.9 us
    all_to_all x1, blocking collectives: 11.4 us -> 11.9 us  [maximum_over_group(): lax.all_to_all(copies, 'tmpl', split_axis=0, concat_axis=0, tiled=True)]
  transfers between devices with their start and end apart: 15 -> 15, of which waited for: 7 -> 9; matrix products, arithmetic and copies ran while one was open for 0% -> 0% of each run, Pallas kernels for 2% -> 2%
where the time goes in v7:
time: 46.3 us; the launch traced here: 46.1 us
  starting transfers between devices  13.6 us (29%)
  Pallas kernels  12.6 us (27%)
  blocking collectives  11.9 us (26%)
  waiting for transfers between devices  6.7 us (14%)
  between operations  0.7 us (2%)
  other arithmetic  0.61 us (1%)
    ppermute x15, starting transfers between devices, exchange(): return lax.ppermute(block, 'tmpl', [(i, i ^ distance) for i in range(size)])  13.6 us
    all_to_all x1, blocking collectives, maximum_over_group(): lax.all_to_all(copies, 'tmpl', split_axis=0, concat_axis=0, tiled=True)  11.9 us
    pallas_call x1, Pallas kernels, correlate(): pl.pallas_call(correlate_kernel, out_shape=jax.ShapeDtypeStruct((padded,...  9.9 us
    ppermute x15, waiting for transfers between devices, exchange(): return lax.ppermute(block, 'tmpl', [(i, i ^ distance) for i in range(size)])  6.7 us
    pallas_call x1, Pallas kernels, reconstruct(): pl.pallas_call(functools.partial(recon_kernel, order), out_shape=(jax.Sha...  1.95 us
  transfers between devices with their start and end apart: 15, of which 9 were waited for; matrix products, arithmetic and copies ran while one was open for 0% of the time, Pallas kernels for 2%

profile of v7, /device:TPU:0, one launch (start us, length us, event | category | flops | bytes accessed | tf_op | source)
XLA Modules:
  0.0 46.1 jit_solution(10252026124223023312)
XLA Ops:
  0.6 0.0 copy-start
  0.6 9.9 %correlate.1.refs_0_ = bf16[32,1920]{1,0:T(8,128)(2,1)} custom-call(bf16[72,128]{1,0:T(8,128)(2,1)} %bitcast.9, bf16[68,128]{1,0:T(8,128)(2,1)} %bitcast.10, bf16[66,128]{1,0:T(8,128)(2,1)} %bitcast.11, bf16[65,128]{1,0:T(8,128)(2,1)} %bitcast.12, bf16[4,32,8192]{2,1,0:T(8,128)(2,1)} %refs_4_.1), custom_call_target="tpu_custom_call" | custom-call | flops 1006632960 | bytes 2097152 | tf_op jit(solution)/shard_map/correlate/pallas_call | solution.py:167
  10.5 0.0 copy-start.1
  10.6 3.1 %collective-permute-start.5 = (bf16[32,1920]{1,0:T(8,128)(2,1)}, bf16[32,1920]{1,0:T(8,128)(2,1)S(1)}, u32[]{:S(2)}, u32[]{:S(2)}) collective-permute-start(bf16[32,1920]{1,0:T(8,128)(2,1)} %correlate.1.refs_0_), channel_id=1, source_target_pairs={{0,4},{1,5},{2,6},{3,7},{4,0},{5,1},{6,2},{7,3},{8,12},{9,13},{10,... | collective-permute-start | bytes 368648 | tf_op jit(solution)/shard_map/ppermute | solution.py:196
  13.6 2.6 %collective-permute-start.3 = (bf16[32,1920]{1,0:T(8,128)(2,1)}, bf16[32,1920]{1,0:T(8,128)(2,1)S(1)}, u32[]{:S(2)}, u32[]{:S(2)}) collective-permute-start(bf16[32,1920]{1,0:T(8,128)(2,1)} %correlate.1.refs_0_), channel_id=1, source_target_pairs={{0,8},{1,9},{2,10},{3,11},{4,12},{5,13},{6,14},{7,15},{8,0},{9,1},... | collective-permute-start | bytes 368648 | tf_op jit(solution)/shard_map/ppermute | solution.py:196
  16.2 1.5 %collective-permute-start.1 = (bf16[32,1920]{1,0:T(8,128)(2,1)}, bf16[32,1920]{1,0:T(8,128)(2,1)S(1)}, u32[]{:S(2)}, u32[]{:S(2)}) collective-permute-start(bf16[32,1920]{1,0:T(8,128)(2,1)} %correlate.1.refs_0_), channel_id=1, source_target_pairs={{0,2},{1,3},{2,0},{3,1},{4,6},{5,7},{6,4},{7,5},{8,10},{9,11},{10,... | collective-permute-start | bytes 368648 | tf_op jit(solution)/shard_map/ppermute | solution.py:196
  17.8 0.0 copy-done
  17.8 0.7 %arrange.1.coeffs_ref = bf16[4,256,512]{2,1,0:T(8,128)(2,1)S(1)} custom-call(s32[1]{0:T(128)} %bitcast.4.offset_ref, bf16[4,256,512]{2,1,0:T(8,128)(2,1)S(1)} %copy-done), custom_call_target="tpu_custom_call" | custom-call | flops 536870912 | bytes 2097152 | tf_op jit(solution)/shard_map/arrange/pallas_call | solution.py:241
  18.5 0.0 copy-done.1
  18.5 0.1 collective-permute-start
  18.6 0.1 collective-permute-done.5.refs_6_
  18.6 1.8 %collective-permute-start.7 = (bf16[32,1920]{1,0:T(8,128)(2,1)S(1)}, bf16[32,1920]{1,0:T(8,128)(2,1)S(1)}, u32[]{:S(2)}, u32[]{:S(2)}) collective-permute-start(bf16[32,1920]{1,0:T(8,128)(2,1)S(1)} %collective-permute-done.5.refs_6_), channel_id=1, source_target_pairs={{0,2},{1,3},{2,0},{3,1},{4,6},{5,7},{6,4},{7,5},{8,10},{9,11},{10,... | collective-permute-start | bytes 368648 | tf_op jit(solution)/shard_map/ppermute | solution.py:196
  20.5 0.0 collective-permute-start.6
  20.5 1.8 %collective-permute-done.3.refs_4_ = bf16[32,1920]{1,0:T(8,128)(2,1)S(1)} collective-permute-done((bf16[32,1920]{1,0:T(8,128)(2,1)}, bf16[32,1920]{1,0:T(8,128)(2,1)S(1)}, u32[]{:S(2)}, u32[]{:S(2)}) %collective-permute-start.3) | collective-permute-done | bytes 122912 | tf_op jit(solution)/shard_map/ppermute | solution.py:196
  22.2 1.5 %collective-permute-start.13 = (bf16[32,1920]{1,0:T(8,128)(2,1)S(1)}, bf16[32,1920]{1,0:T(8,128)(2,1)S(1)}, u32[]{:S(2)}, u32[]{:S(2)}) collective-permute-start(bf16[32,1920]{1,0:T(8,128)(2,1)S(1)} %collective-permute-done.3.refs_4_), channel_id=1, source_target_pairs={{0,2},{1,3},{2,0},{3,1},{4,6},{5,7},{6,4},{7,5},{8,10},{9,11},{10,... | collective-permute-start | bytes 368648 | tf_op jit(solution)/shard_map/ppermute | solution.py:196
  23.8 0.0 collective-permute-done.1.refs_2_
  23.8 0.4 collective-permute-start.11
  24.1 0.0 collective-permute-done.refs_1_
  24.1 1.6 %collective-permute-start.9 = (bf16[32,1920]{1,0:T(8,128)(2,1)S(1)}, bf16[32,1920]{1,0:T(8,128)(2,1)S(1)}, u32[]{:S(2)}, u32[]{:S(2)}) collective-permute-start(bf16[32,1920]{1,0:T(8,128)(2,1)S(1)} %collective-permute-done.3.refs_4_), channel_id=1, source_target_pairs={{0,4},{1,5},{2,6},{3,7},{4,0},{5,1},{6,2},{7,3},{8,12},{9,13},{10,... | collective-permute-start | bytes 368648 | tf_op jit(solution)/shard_map/ppermute | solution.py:196
  25.7 0.4 collective-permute-done.7.refs_8_
  26.1 0.0 collective-permute-start.4
  26.1 0.0 collective-permute-done.6.refs_7_
  26.1 0.5 %collective-permute-start.2 = (bf16[32,1920]{1,0:T(8,128)(2,1)S(1)}, bf16[32,1920]{1,0:T(8,128)(2,1)S(1)}, u32[]{:S(2)}, u32[]{:S(2)}) collective-permute-start(bf16[32,1920]{1,0:T(8,128)(2,1)S(1)} %collective-permute-done.1.refs_2_), channel_id=1, source_target_pairs={{0,1},{1,0},{2,3},{3,2},{4,5},{5,4},{6,7},{7,6},{8,9},{9,8},{10,11... | collective-permute-start | bytes 368648 | tf_op jit(solution)/shard_map/ppermute | solution.py:196
  26.6 1.7 %collective-permute-done.13.refs_14_ = bf16[32,1920]{1,0:T(8,128)(2,1)S(1)} collective-permute-done((bf16[32,1920]{1,0:T(8,128)(2,1)S(1)}, bf16[32,1920]{1,0:T(8,128)(2,1)S(1)}, u32[]{:S(2)}, u32[]{:S(2)}) %collective-permute-start.13) | collective-permute-done | bytes 122912 | tf_op jit(solution)/shard_map/ppermute | solution.py:196
  28.3 0.0 collective-permute-start.8
  28.3 1.3 %collective-permute-done.11.refs_12_ = bf16[32,1920]{1,0:T(8,128)(2,1)S(1)} collective-permute-done((bf16[32,1920]{1,0:T(8,128)(2,1)S(1)}, bf16[32,1920]{1,0:T(8,128)(2,1)S(1)}, u32[]{:S(2)}, u32[]{:S(2)}) %collective-permute-start.11) | collective-permute-done | bytes 122912 | tf_op jit(solution)/shard_map/ppermute | solution.py:196
  29.6 0.0 collective-permute-start.14
  29.6 0.5 %collective-permute-done.9.refs_10_ = bf16[32,1920]{1,0:T(8,128)(2,1)S(1)} collective-permute-done((bf16[32,1920]{1,0:T(8,128)(2,1)S(1)}, bf16[32,1920]{1,0:T(8,128)(2,1)S(1)}, u32[]{:S(2)}, u32[]{:S(2)}) %collective-permute-start.9) | collective-permute-done | bytes 122912 | tf_op jit(solution)/shard_map/ppermute | solution.py:196
  30.1 0.0 collective-permute-start.12
  30.1 0.0 collective-permute-done.4.refs_5_
  30.1 0.5 %collective-permute-start.10 = (bf16[32,1920]{1,0:T(8,128)(2,1)S(1)}, bf16[32,1920]{1,0:T(8,128)(2,1)S(1)}, u32[]{:S(2)}, u32[]{:S(2)}) collective-permute-start(bf16[32,1920]{1,0:T(8,128)(2,1)S(1)} %collective-permute-done.9.refs_10_), channel_id=1, source_target_pairs={{0,1},{1,0},{2,3},{3,2},{4,5},{5,4},{6,7},{7,6},{8,9},{9,8},{10,11... | collective-permute-start | bytes 368648 | tf_op jit(solution)/shard_map/ppermute | solution.py:196
  30.6 0.0 collective-permute-done.2.refs_3_
  30.6 0.0 collective-permute-done.8.refs_9_
  30.6 0.3 collective-permute-done.14.refs_15_
  30.9 0.5 %collective-permute-done.12.refs_13_ = bf16[32,1920]{1,0:T(8,128)(2,1)S(1)} collective-permute-done((bf16[32,1920]{1,0:T(8,128)(2,1)S(1)}, bf16[32,1920]{1,0:T(8,128)(2,1)S(1)}, u32[]{:S(2)}, u32[]{:S(2)}) %collective-permute-start.12) | collective-permute-done | bytes 122912 | tf_op jit(solution)/shard_map/ppermute | solution.py:196
  31.5 0.2 collective-permute-done.10.refs_11_
  31.6 2.0 %reconstruct.1 = (bf16[256,1024]{1,0:T(8,128)(2,1)}, f32[1,1024]{1,0:T(1,128)S(1)}) custom-call(bf16[4,256,512]{2,1,0:T(8,128)(2,1)S(1)} %arrange.1.coeffs_ref, bf16[32,1920]{1,0:T(8,128)(2,1)S(1)} %copy-done.1, bf16[32,1920]{1,0:T(8,128)(2,1)S(1)} %collective-permute-done.refs_1_, bf16[32,1920]{1,0:T(8,128)(2,1)S(1)} %collective-permute-done.1.refs_2_, ...), custom_call_target="tpu_custom_call" | custom-call | tf_op jit(solution)/shard_map/reconstruct/pallas_call | solution.py:300
  33.6 11.9 %all_to_all.5 = f32[16,8,128]{2,1,0:T(8,128)S(1)} all-to-all(f32[16,8,128]{2,1,0:T(8,128)S(1)} %broadcast_in_dim.8), channel_id=1, replica_groups=mesh['bank'=2,'tmpl'=16] {'tmpl'}, dimensions={0} | all-to-all | bytes 131072 | tf_op jit(solution)/shard_map/all_to_all | solution.py:225
  45.5 0.6 %reduce_max.9 = f32[8,128]{1,0:T(8,128)} reduce(f32[16,8,128]{2,1,0:T(8,128)S(1)} %all_to_all.5, f32[]{:T(128)} %constant.2.clone.1), dimensions={0}, to_apply=%region_0.0 | reduce | flops 15360 | bytes 69636 | tf_op jit(solution)/shard_map/reduce_max | solution.py:226
  (1 shorter events, 0.0 us)
Async XLA Ops:
  0.6 17.1 %copy-start = (bf16[4,256,512]{2,1,0:T(8,128)(2,1)S(1)}, bf16[4,256,512]{2,1,0:T(8,128)(2,1)}, u32[]{:S(2)}) copy-start(bf16[4,256,512]{2,1,0:T(8,128)(2,1)} %coeffs_ref.1) | copy-start | bytes 3145732
  10.5 7.9 %copy-start.1 = (bf16[32,1920]{1,0:T(8,128)(2,1)S(1)}, bf16[32,1920]{1,0:T(8,128)(2,1)}, u32[]{:S(2)}) copy-start(bf16[32,1920]{1,0:T(8,128)(2,1)} %correlate.1.refs_0_) | copy-start | bytes 368644
  10.6 8.1 %collective-permute-start.5 = (bf16[32,1920]{1,0:T(8,128)(2,1)}, bf16[32,1920]{1,0:T(8,128)(2,1)S(1)}, u32[]{:S(2)}, u32[]{:S(2)}) collective-permute-start(bf16[32,1920]{1,0:T(8,128)(2,1)} %correlate.1.refs_0_), channel_id=1, source_target_pairs={{0,4},{1,5},{2,6},{3,7},{4,0},{5,1},{6,2},{7,3},{8,12},{9,13},{10,... | collective-permute-start | bytes 368648 | tf_op jit(solution)/shard_map/ppermute | solution.py:196
  13.6 8.6 %collective-permute-start.3 = (bf16[32,1920]{1,0:T(8,128)(2,1)}, bf16[32,1920]{1,0:T(8,128)(2,1)S(1)}, u32[]{:S(2)}, u32[]{:S(2)}) collective-permute-start(bf16[32,1920]{1,0:T(8,128)(2,1)} %correlate.1.refs_0_), channel_id=1, source_target_pairs={{0,8},{1,9},{2,10},{3,11},{4,12},{5,13},{6,14},{7,15},{8,0},{9,1},... | collective-permute-start | bytes 368648 | tf_op jit(solution)/shard_map/ppermute | solution.py:196
  16.2 7.5 %collective-permute-start.1 = (bf16[32,1920]{1,0:T(8,128)(2,1)}, bf16[32,1920]{1,0:T(8,128)(2,1)S(1)}, u32[]{:S(2)}, u32[]{:S(2)}) collective-permute-start(bf16[32,1920]{1,0:T(8,128)(2,1)} %correlate.1.refs_0_), channel_id=1, source_target_pairs={{0,2},{1,3},{2,0},{3,1},{4,6},{5,7},{6,4},{7,5},{8,10},{9,11},{10,... | collective-permute-start | bytes 368648 | tf_op jit(solution)/shard_map/ppermute | solution.py:196
  18.5 5.6 %collective-permute-start = (bf16[32,1920]{1,0:T(8,128)(2,1)S(1)}, bf16[32,1920]{1,0:T(8,128)(2,1)S(1)}, u32[]{:S(2)}, u32[]{:S(2)}) collective-permute-start(bf16[32,1920]{1,0:T(8,128)(2,1)S(1)} %copy-done.1), channel_id=1, source_target_pairs={{0,1},{1,0},{2,3},{3,2},{4,5},{5,4},{6,7},{7,6},{8,9},{9,8},{10,11... | collective-permute-start | bytes 368648 | tf_op jit(solution)/shard_map/ppermute | solution.py:196
  18.6 7.5 %collective-permute-start.7 = (bf16[32,1920]{1,0:T(8,128)(2,1)S(1)}, bf16[32,1920]{1,0:T(8,128)(2,1)S(1)}, u32[]{:S(2)}, u32[]{:S(2)}) collective-permute-start(bf16[32,1920]{1,0:T(8,128)(2,1)S(1)} %collective-permute-done.5.refs_6_), channel_id=1, source_target_pairs={{0,2},{1,3},{2,0},{3,1},{4,6},{5,7},{6,4},{7,5},{8,10},{9,11},{10,... | collective-permute-start | bytes 368648 | tf_op jit(solution)/shard_map/ppermute | solution.py:196
  20.5 5.6 %collective-permute-start.6 = (bf16[32,1920]{1,0:T(8,128)(2,1)S(1)}, bf16[32,1920]{1,0:T(8,128)(2,1)S(1)}, u32[]{:S(2)}, u32[]{:S(2)}) collective-permute-start(bf16[32,1920]{1,0:T(8,128)(2,1)S(1)} %collective-permute-done.5.refs_6_), channel_id=1, source_target_pairs={{0,1},{1,0},{2,3},{3,2},{4,5},{5,4},{6,7},{7,6},{8,9},{9,8},{10,11... | collective-permute-start | bytes 368648 | tf_op jit(solution)/shard_map/ppermute | solution.py:196
  22.2 6.1 %collective-permute-start.13 = (bf16[32,1920]{1,0:T(8,128)(2,1)S(1)}, bf16[32,1920]{1,0:T(8,128)(2,1)S(1)}, u32[]{:S(2)}, u32[]{:S(2)}) collective-permute-start(bf16[32,1920]{1,0:T(8,128)(2,1)S(1)} %collective-permute-done.3.refs_4_), channel_id=1, source_target_pairs={{0,2},{1,3},{2,0},{3,1},{4,6},{5,7},{6,4},{7,5},{8,10},{9,11},{10,... | collective-permute-start | bytes 368648 | tf_op jit(solution)/shard_map/ppermute | solution.py:196
  23.8 5.8 %collective-permute-start.11 = (bf16[32,1920]{1,0:T(8,128)(2,1)S(1)}, bf16[32,1920]{1,0:T(8,128)(2,1)S(1)}, u32[]{:S(2)}, u32[]{:S(2)}) collective-permute-start(bf16[32,1920]{1,0:T(8,128)(2,1)S(1)} %collective-permute-done.3.refs_4_), channel_id=1, source_target_pairs={{0,6},{1,7},{2,4},{3,5},{4,2},{5,3},{6,0},{7,1},{8,14},{9,15},{10,... | collective-permute-start | bytes 368648 | tf_op jit(solution)/shard_map/ppermute | solution.py:196
  24.1 6.0 %collective-permute-start.9 = (bf16[32,1920]{1,0:T(8,128)(2,1)S(1)}, bf16[32,1920]{1,0:T(8,128)(2,1)S(1)}, u32[]{:S(2)}, u32[]{:S(2)}) collective-permute-start(bf16[32,1920]{1,0:T(8,128)(2,1)S(1)} %collective-permute-done.3.refs_4_), channel_id=1, source_target_pairs={{0,4},{1,5},{2,6},{3,7},{4,0},{5,1},{6,2},{7,3},{8,12},{9,13},{10,... | collective-permute-start | bytes 368648 | tf_op jit(solution)/shard_map/ppermute | solution.py:196
  26.1 4.0 %collective-permute-start.4 = (bf16[32,1920]{1,0:T(8,128)(2,1)S(1)}, bf16[32,1920]{1,0:T(8,128)(2,1)S(1)}, u32[]{:S(2)}, u32[]{:S(2)}) collective-permute-start(bf16[32,1920]{1,0:T(8,128)(2,1)S(1)} %collective-permute-done.3.refs_4_), channel_id=1, source_target_pairs={{0,1},{1,0},{2,3},{3,2},{4,5},{5,4},{6,7},{7,6},{8,9},{9,8},{10,11... | collective-permute-start | bytes 368648 | tf_op jit(solution)/shard_map/ppermute | solution.py:196
  26.1 4.5 %collective-permute-start.2 = (bf16[32,1920]{1,0:T(8,128)(2,1)S(1)}, bf16[32,1920]{1,0:T(8,128)(2,1)S(1)}, u32[]{:S(2)}, u32[]{:S(2)}) collective-permute-start(bf16[32,1920]{1,0:T(8,128)(2,1)S(1)} %collective-permute-done.1.refs_2_), channel_id=1, source_target_pairs={{0,1},{1,0},{2,3},{3,2},{4,5},{5,4},{6,7},{7,6},{8,9},{9,8},{10,11... | collective-permute-start | bytes 368648 | tf_op jit(solution)/shard_map/ppermute | solution.py:196
  28.3 2.3 %collective-permute-start.8 = (bf16[32,1920]{1,0:T(8,128)(2,1)S(1)}, bf16[32,1920]{1,0:T(8,128)(2,1)S(1)}, u32[]{:S(2)}, u32[]{:S(2)}) collective-permute-start(bf16[32,1920]{1,0:T(8,128)(2,1)S(1)} %collective-permute-done.7.refs_8_), channel_id=1, source_target_pairs={{0,1},{1,0},{2,3},{3,2},{4,5},{5,4},{6,7},{7,6},{8,9},{9,8},{10,11... | collective-permute-start | bytes 368648 | tf_op jit(solution)/shard_map/ppermute | solution.py:196
  29.6 1.3 %collective-permute-start.14 = (bf16[32,1920]{1,0:T(8,128)(2,1)S(1)}, bf16[32,1920]{1,0:T(8,128)(2,1)S(1)}, u32[]{:S(2)}, u32[]{:S(2)}) collective-permute-start(bf16[32,1920]{1,0:T(8,128)(2,1)S(1)} %collective-permute-done.13.refs_14_), channel_id=1, source_target_pairs={{0,1},{1,0},{2,3},{3,2},{4,5},{5,4},{6,7},{7,6},{8,9},{9,8},{10,11... | collective-permute-start | bytes 368648 | tf_op jit(solution)/shard_map/ppermute | solution.py:196
  30.1 1.3 %collective-permute-start.12 = (bf16[32,1920]{1,0:T(8,128)(2,1)S(1)}, bf16[32,1920]{1,0:T(8,128)(2,1)S(1)}, u32[]{:S(2)}, u32[]{:S(2)}) collective-permute-start(bf16[32,1920]{1,0:T(8,128)(2,1)S(1)} %collective-permute-done.11.refs_12_), channel_id=1, source_target_pairs={{0,1},{1,0},{2,3},{3,2},{4,5},{5,4},{6,7},{7,6},{8,9},{9,8},{10,11... | collective-permute-start | bytes 368648 | tf_op jit(solution)/shard_map/ppermute | solution.py:196
  30.1 1.5 %collective-permute-start.10 = (bf16[32,1920]{1,0:T(8,128)(2,1)S(1)}, bf16[32,1920]{1,0:T(8,128)(2,1)S(1)}, u32[]{:S(2)}, u32[]{:S(2)}) collective-permute-start(bf16[32,1920]{1,0:T(8,128)(2,1)S(1)} %collective-permute-done.9.refs_10_), channel_id=1, source_target_pairs={{0,1},{1,0},{2,3},{3,2},{4,5},{5,4},{6,7},{7,6},{8,9},{9,8},{10,11... | collective-permute-start | bytes 368648 | tf_op jit(solution)/shard_map/ppermute | solution.py:196

commit v8 on v7

--- a/solution.py
+++ b/solution.py
@@ -28,20 +28,29 @@
     slot = line_ref.shape[0] // sections
     pad = (max(blocks) - 1) * LANE
     groups = ((0, 1), (2, 3))
-    strain_copies, taps_copies = [], []
+    strain_copies = []
     for section, source in enumerate(strain_refs):
         strain_copies.append(
             pltpu.make_async_copy(source, held_strains[section], strain_sems.at[section])
         )
-        taps_copies.append(
-            pltpu.make_async_copy(
-                taps_ref.at[section],
-                held_taps.at[section, :, pl.ds(pad, taps)],
-                taps_sems.at[section],
-            )
-        )
-    for copy in strain_copies + taps_copies:
+    for copy in strain_copies:
         copy.start()
+    span = CHUNK * LANE
+    chunks = taps // span
+
+    def taps_copy(section, chunk):
+        first = chunk * span
+        if not isinstance(first, int):
+            first = pl.multiple_of(first, span)
+        return pltpu.make_async_copy(
+            taps_ref.at[section, :, pl.ds(first, span)],
+            held_taps.at[section, :, pl.ds(pad + first, span)],
+            taps_sems.at[section, chunk],
+        )
+
+    for chunk in range(chunks):
+        for section in range(sections):
+            taps_copy(section, chunk).start()
     after = held_taps.shape[2] - pad - taps
     for section in range(sections):
         held_taps[section, :, :pad] = jnp.zeros((rows, pad), held_taps.dtype)
@@ -128,20 +137,23 @@
         for section in range(sections):
             build(frames[section // 2], section, chunk)
 
+    def arrive(chunk):
+        for section in range(sections):
+            taps_copy(section, chunk).wait()
+
     build_all(even_refs, 0)
-    for copy in taps_copies:
-        copy.wait()
 
     def step(number, carry):
+        arrive(2 * number)
         for group, frames in zip(groups, even_refs):
             accumulate(frames, group, 2 * number)
         build_all(odd_refs, 2 * number + 1)
+        arrive(2 * number + 1)
         for group, frames in zip(groups, odd_refs):
             accumulate(frames, group, 2 * number + 1)
         build_all(even_refs, 2 * number + 2)
         return carry
 
-    chunks = taps // (CHUNK * LANE)
     lax.fori_loop(0, chunks // 2, step, 0)
     for group, frames in zip(groups, even_refs):
         active = [section for section in group if blocks[section] > 1]
@@ -166,7 +178,7 @@
     lines = [x.reshape(-1, LANE) for x in streams]
     out = pl.pallas_call(
         correlate_kernel,
-        out_shape=jax.ShapeDtypeStruct((padded, samples), jnp.bfloat16),
+        out_shape=pltpu.VMEM((padded, samples), jnp.bfloat16),
         in_specs=[pl.BlockSpec(memory_space=pltpu.HBM)] * (sections + 1),
         out_specs=pl.BlockSpec(memory_space=pltpu.VMEM),
         scratch_shapes=[pltpu.VMEM(x.shape, x.dtype) for x in lines]
@@ -178,7 +190,7 @@
         + [pltpu.VMEM((CHUNK * LANE, 2 * LANE), jnp.bfloat16)] * 4
         + [
             pltpu.SemaphoreType.DMA((sections,)),
-            pltpu.SemaphoreType.DMA((sections,)),
+            pltpu.SemaphoreType.DMA((sections, taps // (CHUNK * LANE))),
         ],
         compiler_params=pltpu.CompilerParams(vmem_limit_bytes=60 * 2**20),
         cost_estimate=pl.CostEstimate(

time: 46.3 us -> 46 us (level)
  transfers between devices with their start and end apart: 15 -> 15, of which waited for: 9 -> 7; matrix products, arithmetic and copies ran while one was open for 0% -> 0% of each run, Pallas kernels for 2% -> 2%
where the time goes in v8:
time: 46 us; the launch traced here: 45.9 us
  starting transfers between devices  14 us (30%)
  Pallas kernels  12.5 us (27%)
  blocking collectives  11.7 us (25%)
  waiting for transfers between devices  6.27 us (14%)
  between operations  0.69 us (2%)
  other arithmetic  0.61 us (1%)
    ppermute x15, starting transfers between devices, exchange(): return lax.ppermute(block, 'tmpl', [(i, i ^ distance) for i in range(size)])  14 us
    all_to_all x1, blocking collectives, maximum_over_group(): lax.all_to_all(copies, 'tmpl', split_axis=0, concat_axis=0, tiled=True)  11.7 us
    pallas_call x1, Pallas kernels, correlate(): pl.pallas_call(correlate_kernel, out_shape=pltpu.VMEM((padded, samples),...  9.86 us
    ppermute x15, waiting for transfers between devices, exchange(): return lax.ppermute(block, 'tmpl', [(i, i ^ distance) for i in range(size)])  6.27 us
    pallas_call x1, Pallas kernels, reconstruct(): pl.pallas_call(functools.partial(recon_kernel, order), out_shape=(jax.Sha...  1.97 us
  transfers between devices with their start and end apart: 15, of which 7 were waited for; matrix products, arithmetic and copies ran while one was open for 0% of the time, Pallas kernels for 2%

profile of v8, /device:TPU:0, one launch (start us, length us, event | category | flops | bytes accessed | tf_op | source)
XLA Modules:
  0.0 45.9 jit_solution(5900998070451928444)
XLA Ops:
  0.6 0.0 copy-start
  0.6 9.9 %correlate.1.refs_0_ = bf16[32,1920]{1,0:T(8,128)(2,1)S(1)} custom-call(bf16[72,128]{1,0:T(8,128)(2,1)} %bitcast.9, bf16[68,128]{1,0:T(8,128)(2,1)} %bitcast.10, bf16[66,128]{1,0:T(8,128)(2,1)} %bitcast.11, bf16[65,128]{1,0:T(8,128)(2,1)} %bitcast.12, bf16[4,32,8192]{2,1,0:T(8,128)(2,1)} %refs_4_.1), custom_call_target="tpu_custom_call" | custom-call | flops 1006632960 | bytes 2097152 | tf_op jit(solution)/shard_map/correlate/pallas_call | solution.py:179
  10.5 3.1 %collective-permute-start.5 = (bf16[32,1920]{1,0:T(8,128)(2,1)S(1)}, bf16[32,1920]{1,0:T(8,128)(2,1)S(1)}, u32[]{:S(2)}, u32[]{:S(2)}) collective-permute-start(bf16[32,1920]{1,0:T(8,128)(2,1)S(1)} %correlate.1.refs_0_), channel_id=1, source_target_pairs={{0,4},{1,5},{2,6},{3,7},{4,0},{5,1},{6,2},{7,3},{8,12},{9,13},{10,... | collective-permute-start | bytes 368648 | tf_op jit(solution)/shard_map/ppermute | solution.py:208
  13.6 2.6 %collective-permute-start.3 = (bf16[32,1920]{1,0:T(8,128)(2,1)S(1)}, bf16[32,1920]{1,0:T(8,128)(2,1)S(1)}, u32[]{:S(2)}, u32[]{:S(2)}) collective-permute-start(bf16[32,1920]{1,0:T(8,128)(2,1)S(1)} %correlate.1.refs_0_), channel_id=1, source_target_pairs={{0,8},{1,9},{2,10},{3,11},{4,12},{5,13},{6,14},{7,15},{8,0},{9,1},... | collective-permute-start | bytes 368648 | tf_op jit(solution)/shard_map/ppermute | solution.py:208
  16.2 1.5 %collective-permute-start.1 = (bf16[32,1920]{1,0:T(8,128)(2,1)S(1)}, bf16[32,1920]{1,0:T(8,128)(2,1)S(1)}, u32[]{:S(2)}, u32[]{:S(2)}) collective-permute-start(bf16[32,1920]{1,0:T(8,128)(2,1)S(1)} %correlate.1.refs_0_), channel_id=1, source_target_pairs={{0,2},{1,3},{2,0},{3,1},{4,6},{5,7},{6,4},{7,5},{8,10},{9,11},{10,... | collective-permute-start | bytes 368648 | tf_op jit(solution)/shard_map/ppermute | solution.py:208
  17.7 0.0 copy-done
  17.7 0.7 %arrange.1.coeffs_ref = bf16[4,256,512]{2,1,0:T(8,128)(2,1)S(1)} custom-call(s32[1]{0:T(128)} %bitcast.4.offset_ref, bf16[4,256,512]{2,1,0:T(8,128)(2,1)S(1)} %copy-done), custom_call_target="tpu_custom_call" | custom-call | flops 536870912 | bytes 2097152 | tf_op jit(solution)/shard_map/arrange/pallas_call | solution.py:253
  18.4 0.1 collective-permute-start
  18.5 0.0 collective-permute-done.5.refs_6_
  18.5 1.7 %collective-permute-start.7 = (bf16[32,1920]{1,0:T(8,128)(2,1)S(1)}, bf16[32,1920]{1,0:T(8,128)(2,1)S(1)}, u32[]{:S(2)}, u32[]{:S(2)}) collective-permute-start(bf16[32,1920]{1,0:T(8,128)(2,1)S(1)} %collective-permute-done.5.refs_6_), channel_id=1, source_target_pairs={{0,2},{1,3},{2,0},{3,1},{4,6},{5,7},{6,4},{7,5},{8,10},{9,11},{10,... | collective-permute-start | bytes 368648 | tf_op jit(solution)/shard_map/ppermute | solution.py:208
  20.2 0.0 collective-permute-start.6
  20.2 1.7 %collective-permute-done.3.refs_4_ = bf16[32,1920]{1,0:T(8,128)(2,1)S(1)} collective-permute-done((bf16[32,1920]{1,0:T(8,128)(2,1)S(1)}, bf16[32,1920]{1,0:T(8,128)(2,1)S(1)}, u32[]{:S(2)}, u32[]{:S(2)}) %collective-permute-start.3) | collective-permute-done | bytes 122912 | tf_op jit(solution)/shard_map/ppermute | solution.py:208
  22.0 1.5 %collective-permute-start.13 = (bf16[32,1920]{1,0:T(8,128)(2,1)S(1)}, bf16[32,1920]{1,0:T(8,128)(2,1)S(1)}, u32[]{:S(2)}, u32[]{:S(2)}) collective-permute-start(bf16[32,1920]{1,0:T(8,128)(2,1)S(1)} %collective-permute-done.3.refs_4_), channel_id=1, source_target_pairs={{0,2},{1,3},{2,0},{3,1},{4,6},{5,7},{6,4},{7,5},{8,10},{9,11},{10,... | collective-permute-start | bytes 368648 | tf_op jit(solution)/shard_map/ppermute | solution.py:208
  23.5 0.0 collective-permute-done.1.refs_2_
  23.5 0.4 collective-permute-start.11
  23.9 0.0 collective-permute-done.refs_1_
  23.9 1.6 %collective-permute-start.9 = (bf16[32,1920]{1,0:T(8,128)(2,1)S(1)}, bf16[32,1920]{1,0:T(8,128)(2,1)S(1)}, u32[]{:S(2)}, u32[]{:S(2)}) collective-permute-start(bf16[32,1920]{1,0:T(8,128)(2,1)S(1)} %collective-permute-done.3.refs_4_), channel_id=1, source_target_pairs={{0,4},{1,5},{2,6},{3,7},{4,0},{5,1},{6,2},{7,3},{8,12},{9,13},{10,... | collective-permute-start | bytes 368648 | tf_op jit(solution)/shard_map/ppermute | solution.py:208
  25.5 0.6 %collective-permute-done.7.refs_8_ = bf16[32,1920]{1,0:T(8,128)(2,1)S(1)} collective-permute-done((bf16[32,1920]{1,0:T(8,128)(2,1)S(1)}, bf16[32,1920]{1,0:T(8,128)(2,1)S(1)}, u32[]{:S(2)}, u32[]{:S(2)}) %collective-permute-start.7) | collective-permute-done | bytes 122912 | tf_op jit(solution)/shard_map/ppermute | solution.py:208
  26.0 0.0 collective-permute-start.4
  26.0 0.0 collective-permute-done.6.refs_7_
  26.0 0.5 %collective-permute-start.2 = (bf16[32,1920]{1,0:T(8,128)(2,1)S(1)}, bf16[32,1920]{1,0:T(8,128)(2,1)S(1)}, u32[]{:S(2)}, u32[]{:S(2)}) collective-permute-start(bf16[32,1920]{1,0:T(8,128)(2,1)S(1)} %collective-permute-done.1.refs_2_), channel_id=1, source_target_pairs={{0,1},{1,0},{2,3},{3,2},{4,5},{5,4},{6,7},{7,6},{8,9},{9,8},{10,11... | collective-permute-start | bytes 368648 | tf_op jit(solution)/shard_map/ppermute | solution.py:208
  26.5 3.0 %collective-permute-done.13.refs_14_ = bf16[32,1920]{1,0:T(8,128)(2,1)S(1)} collective-permute-done((bf16[32,1920]{1,0:T(8,128)(2,1)S(1)}, bf16[32,1920]{1,0:T(8,128)(2,1)S(1)}, u32[]{:S(2)}, u32[]{:S(2)}) %collective-permute-start.13) | collective-permute-done | bytes 122912 | tf_op jit(solution)/shard_map/ppermute | solution.py:208
  29.5 0.0 collective-permute-start.8
  29.5 0.0 collective-permute-done.11.refs_12_
  29.5 0.5 %collective-permute-start.14 = (bf16[32,1920]{1,0:T(8,128)(2,1)S(1)}, bf16[32,1920]{1,0:T(8,128)(2,1)S(1)}, u32[]{:S(2)}, u32[]{:S(2)}) collective-permute-start(bf16[32,1920]{1,0:T(8,128)(2,1)S(1)} %collective-permute-done.13.refs_14_), channel_id=1, source_target_pairs={{0,1},{1,0},{2,3},{3,2},{4,5},{5,4},{6,7},{7,6},{8,9},{9,8},{10,11... | collective-permute-start | bytes 368648 | tf_op jit(solution)/shard_map/ppermute | solution.py:208
  30.0 0.0 collective-permute-done.9.refs_10_
  30.0 0.1 collective-permute-start.12
  30.1 0.0 collective-permute-done.4.refs_5_
  30.1 0.4 collective-permute-start.10
  30.6 0.0 collective-permute-done.2.refs_3_
  30.6 0.3 collective-permute-done.8.refs_9_
  30.9 0.2 collective-permute-done.14.refs_15_
  31.0 0.3 collective-permute-done.12.refs_13_
  31.4 0.2 collective-permute-done.10.refs_11_
  31.5 2.0 %reconstruct.1 = (bf16[256,1024]{1,0:T(8,128)(2,1)}, f32[1,1024]{1,0:T(1,128)S(1)}) custom-call(bf16[4,256,512]{2,1,0:T(8,128)(2,1)S(1)} %arrange.1.coeffs_ref, bf16[32,1920]{1,0:T(8,128)(2,1)S(1)} %correlate.1.refs_0_, bf16[32,1920]{1,0:T(8,128)(2,1)S(1)} %collective-permute-done.refs_1_, bf16[32,1920]{1,0:T(8,128)(2,1)S(1)} %collective-permute-done.1.refs_2_, ...), custom_call_target="tpu_custom_call" | custom-call | tf_op jit(solution)/shard_map/reconstruct/pallas_call | solution.py:312
  33.5 11.7 %all_to_all.5 = f32[16,8,128]{2,1,0:T(8,128)S(1)} all-to-all(f32[16,8,128]{2,1,0:T(8,128)S(1)} %broadcast_in_dim.8), channel_id=1, replica_groups=mesh['bank'=2,'tmpl'=16] {'tmpl'}, dimensions={0} | all-to-all | bytes 131072 | tf_op jit(solution)/shard_map/all_to_all | solution.py:237
  45.3 0.6 %reduce_max.9 = f32[8,128]{1,0:T(8,128)} reduce(f32[16,8,128]{2,1,0:T(8,128)S(1)} %all_to_all.5, f32[]{:T(128)} %constant.2.clone.1), dimensions={0}, to_apply=%region_0.0 | reduce | flops 15360 | bytes 69636 | tf_op jit(solution)/shard_map/reduce_max | solution.py:238
  (1 shorter events, 0.0 us)
Async XLA Ops:
  0.6 17.1 %copy-start = (bf16[4,256,512]{2,1,0:T(8,128)(2,1)S(1)}, bf16[4,256,512]{2,1,0:T(8,128)(2,1)}, u32[]{:S(2)}) copy-start(bf16[4,256,512]{2,1,0:T(8,128)(2,1)} %coeffs_ref.1) | copy-start | bytes 3145732
  10.5 8.0 %collective-permute-start.5 = (bf16[32,1920]{1,0:T(8,128)(2,1)S(1)}, bf16[32,1920]{1,0:T(8,128)(2,1)S(1)}, u32[]{:S(2)}, u32[]{:S(2)}) collective-permute-start(bf16[32,1920]{1,0:T(8,128)(2,1)S(1)} %correlate.1.refs_0_), channel_id=1, source_target_pairs={{0,4},{1,5},{2,6},{3,7},{4,0},{5,1},{6,2},{7,3},{8,12},{9,13},{10,... | collective-permute-start | bytes 368648 | tf_op jit(solution)/shard_map/ppermute | solution.py:208
  13.6 8.4 %collective-permute-start.3 = (bf16[32,1920]{1,0:T(8,128)(2,1)S(1)}, bf16[32,1920]{1,0:T(8,128)(2,1)S(1)}, u32[]{:S(2)}, u32[]{:S(2)}) collective-permute-start(bf16[32,1920]{1,0:T(8,128)(2,1)S(1)} %correlate.1.refs_0_), channel_id=1, source_target_pairs={{0,8},{1,9},{2,10},{3,11},{4,12},{5,13},{6,14},{7,15},{8,0},{9,1},... | collective-permute-start | bytes 368648 | tf_op jit(solution)/shard_map/ppermute | solution.py:208
  16.2 7.3 %collective-permute-start.1 = (bf16[32,1920]{1,0:T(8,128)(2,1)S(1)}, bf16[32,1920]{1,0:T(8,128)(2,1)S(1)}, u32[]{:S(2)}, u32[]{:S(2)}) collective-permute-start(bf16[32,1920]{1,0:T(8,128)(2,1)S(1)} %correlate.1.refs_0_), channel_id=1, source_target_pairs={{0,2},{1,3},{2,0},{3,1},{4,6},{5,7},{6,4},{7,5},{8,10},{9,11},{10,... | collective-permute-start | bytes 368648 | tf_op jit(solution)/shard_map/ppermute | solution.py:208
  18.4 5.4 %collective-permute-start = (bf16[32,1920]{1,0:T(8,128)(2,1)S(1)}, bf16[32,1920]{1,0:T(8,128)(2,1)S(1)}, u32[]{:S(2)}, u32[]{:S(2)}) collective-permute-start(bf16[32,1920]{1,0:T(8,128)(2,1)S(1)} %correlate.1.refs_0_), channel_id=1, source_target_pairs={{0,1},{1,0},{2,3},{3,2},{4,5},{5,4},{6,7},{7,6},{8,9},{9,8},{10,11... | collective-permute-start | bytes 368648 | tf_op jit(solution)/shard_map/ppermute | solution.py:208
  18.5 7.5 %collective-permute-start.7 = (bf16[32,1920]{1,0:T(8,128)(2,1)S(1)}, bf16[32,1920]{1,0:T(8,128)(2,1)S(1)}, u32[]{:S(2)}, u32[]{:S(2)}) collective-permute-start(bf16[32,1920]{1,0:T(8,128)(2,1)S(1)} %collective-permute-done.5.refs_6_), channel_id=1, source_target_pairs={{0,2},{1,3},{2,0},{3,1},{4,6},{5,7},{6,4},{7,5},{8,10},{9,11},{10,... | collective-permute-start | bytes 368648 | tf_op jit(solution)/shard_map/ppermute | solution.py:208
  20.2 5.8 %collective-permute-start.6 = (bf16[32,1920]{1,0:T(8,128)(2,1)S(1)}, bf16[32,1920]{1,0:T(8,128)(2,1)S(1)}, u32[]{:S(2)}, u32[]{:S(2)}) collective-permute-start(bf16[32,1920]{1,0:T(8,128)(2,1)S(1)} %collective-permute-done.5.refs_6_), channel_id=1, source_target_pairs={{0,1},{1,0},{2,3},{3,2},{4,5},{5,4},{6,7},{7,6},{8,9},{9,8},{10,11... | collective-permute-start | bytes 368648 | tf_op jit(solution)/shard_map/ppermute | solution.py:208
  22.0 7.6 %collective-permute-start.13 = (bf16[32,1920]{1,0:T(8,128)(2,1)S(1)}, bf16[32,1920]{1,0:T(8,128)(2,1)S(1)}, u32[]{:S(2)}, u32[]{:S(2)}) collective-permute-start(bf16[32,1920]{1,0:T(8,128)(2,1)S(1)} %collective-permute-done.3.refs_4_), channel_id=1, source_target_pairs={{0,2},{1,3},{2,0},{3,1},{4,6},{5,7},{6,4},{7,5},{8,10},{9,11},{10,... | collective-permute-start | bytes 368648 | tf_op jit(solution)/shard_map/ppermute | solution.py:208
  23.5 6.0 %collective-permute-start.11 = (bf16[32,1920]{1,0:T(8,128)(2,1)S(1)}, bf16[32,1920]{1,0:T(8,128)(2,1)S(1)}, u32[]{:S(2)}, u32[]{:S(2)}) collective-permute-start(bf16[32,1920]{1,0:T(8,128)(2,1)S(1)} %collective-permute-done.3.refs_4_), channel_id=1, source_target_pairs={{0,6},{1,7},{2,4},{3,5},{4,2},{5,3},{6,0},{7,1},{8,14},{9,15},{10,... | collective-permute-start | bytes 368648 | tf_op jit(solution)/shard_map/ppermute | solution.py:208
  23.9 6.2 %collective-permute-start.9 = (bf16[32,1920]{1,0:T(8,128)(2,1)S(1)}, bf16[32,1920]{1,0:T(8,128)(2,1)S(1)}, u32[]{:S(2)}, u32[]{:S(2)}) collective-permute-start(bf16[32,1920]{1,0:T(8,128)(2,1)S(1)} %collective-permute-done.3.refs_4_), channel_id=1, source_target_pairs={{0,4},{1,5},{2,6},{3,7},{4,0},{5,1},{6,2},{7,3},{8,12},{9,13},{10,... | collective-permute-start | bytes 368648 | tf_op jit(solution)/shard_map/ppermute | solution.py:208
  26.0 4.1 %collective-permute-start.4 = (bf16[32,1920]{1,0:T(8,128)(2,1)S(1)}, bf16[32,1920]{1,0:T(8,128)(2,1)S(1)}, u32[]{:S(2)}, u32[]{:S(2)}) collective-permute-start(bf16[32,1920]{1,0:T(8,128)(2,1)S(1)} %collective-permute-done.3.refs_4_), channel_id=1, source_target_pairs={{0,1},{1,0},{2,3},{3,2},{4,5},{5,4},{6,7},{7,6},{8,9},{9,8},{10,11... | collective-permute-start | bytes 368648 | tf_op jit(solution)/shard_map/ppermute | solution.py:208
  26.0 4.5 %collective-permute-start.2 = (bf16[32,1920]{1,0:T(8,128)(2,1)S(1)}, bf16[32,1920]{1,0:T(8,128)(2,1)S(1)}, u32[]{:S(2)}, u32[]{:S(2)}) collective-permute-start(bf16[32,1920]{1,0:T(8,128)(2,1)S(1)} %collective-permute-done.1.refs_2_), channel_id=1, source_target_pairs={{0,1},{1,0},{2,3},{3,2},{4,5},{5,4},{6,7},{7,6},{8,9},{9,8},{10,11... | collective-permute-start | bytes 368648 | tf_op jit(solution)/shard_map/ppermute | solution.py:208
  29.5 1.3 %collective-permute-start.8 = (bf16[32,1920]{1,0:T(8,128)(2,1)S(1)}, bf16[32,1920]{1,0:T(8,128)(2,1)S(1)}, u32[]{:S(2)}, u32[]{:S(2)}) collective-permute-start(bf16[32,1920]{1,0:T(8,128)(2,1)S(1)} %collective-permute-done.7.refs_8_), channel_id=1, source_target_pairs={{0,1},{1,0},{2,3},{3,2},{4,5},{5,4},{6,7},{7,6},{8,9},{9,8},{10,11... | collective-permute-start | bytes 368648 | tf_op jit(solution)/shard_map/ppermute | solution.py:208
  29.5 1.5 %collective-permute-start.14 = (bf16[32,1920]{1,0:T(8,128)(2,1)S(1)}, bf16[32,1920]{1,0:T(8,128)(2,1)S(1)}, u32[]{:S(2)}, u32[]{:S(2)}) collective-permute-start(bf16[32,1920]{1,0:T(8,128)(2,1)S(1)} %collective-permute-done.13.refs_14_), channel_id=1, source_target_pairs={{0,1},{1,0},{2,3},{3,2},{4,5},{5,4},{6,7},{7,6},{8,9},{9,8},{10,11... | collective-permute-start | bytes 368648 | tf_op jit(solution)/shard_map/ppermute | solution.py:208
  30.0 1.3 %collective-permute-start.12 = (bf16[32,1920]{1,0:T(8,128)(2,1)S(1)}, bf16[32,1920]{1,0:T(8,128)(2,1)S(1)}, u32[]{:S(2)}, u32[]{:S(2)}) collective-permute-start(bf16[32,1920]{1,0:T(8,128)(2,1)S(1)} %collective-permute-done.11.refs_12_), channel_id=1, source_target_pairs={{0,1},{1,0},{2,3},{3,2},{4,5},{5,4},{6,7},{7,6},{8,9},{9,8},{10,11... | collective-permute-start | bytes 368648 | tf_op jit(solution)/shard_map/ppermute | solution.py:208
  30.1 1.4 %collective-permute-start.10 = (bf16[32,1920]{1,0:T(8,128)(2,1)S(1)}, bf16[32,1920]{1,0:T(8,128)(2,1)S(1)}, u32[]{:S(2)}, u32[]{:S(2)}) collective-permute-start(bf16[32,1920]{1,0:T(8,128)(2,1)S(1)} %collective-permute-done.9.refs_10_), channel_id=1, source_target_pairs={{0,1},{1,0},{2,3},{3,2},{4,5},{5,4},{6,7},{7,6},{8,9},{9,8},{10,11... | collective-permute-start | bytes 368648 | tf_op jit(solution)/shard_map/ppermute | solution.py:208

commit v9 on v7

--- a/solution.py
+++ b/solution.py
@@ -18,34 +18,16 @@
 
 
 def correlate_kernel(*refs):
-    strain_refs, taps_ref, out_ref = refs[:4], refs[4], refs[5]
-    held_strains, held_taps, line_ref, total_ref = refs[6:10], refs[10], refs[11], refs[12]
-    even_refs, odd_refs, strain_sems, taps_sems = refs[13:15], refs[15:17], refs[17], refs[18]
-    sections = len(strain_refs)
+    strains, taps_ref, out_ref = refs[:4], refs[4], refs[5]
+    line_ref, total_ref, even_refs, odd_refs = refs[6], refs[7], refs[8:10], refs[10:12]
+    sections = len(strains)
     rows, taps = taps_ref.shape[1], taps_ref.shape[2]
-    lines = [ref.shape[0] for ref in held_strains]
+    lines = [ref.shape[0] for ref in strains]
     blocks = [count - taps // LANE for count in lines]
     slot = line_ref.shape[0] // sections
-    pad = (max(blocks) - 1) * LANE
+    span = CHUNK * LANE
+    chunks = taps // span
     groups = ((0, 1), (2, 3))
-    strain_copies, taps_copies = [], []
-    for section, source in enumerate(strain_refs):
-        strain_copies.append(
-            pltpu.make_async_copy(source, held_strains[section], strain_sems.at[section])
-        )
-        taps_copies.append(
-            pltpu.make_async_copy(
-                taps_ref.at[section],
-                held_taps.at[section, :, pl.ds(pad, taps)],
-                taps_sems.at[section],
-            )
-        )
-    for copy in strain_copies + taps_copies:
-        copy.start()
-    after = held_taps.shape[2] - pad - taps
-    for section in range(sections):
-        held_taps[section, :, :pad] = jnp.zeros((rows, pad), held_taps.dtype)
-        held_taps[section, :, pad + taps :] = jnp.zeros((rows, after), held_taps.dtype)
     total_ref[...] = jnp.zeros(total_ref.shape, total_ref.dtype)
 
     extra = LANE // SUB - ROLLS
@@ -54,10 +36,9 @@
     target = target % LANE + (target // LANE + ROLLS) * SUB
     shifts = jnp.where(source == target, 1.0, 0.0).astype(jnp.bfloat16)
 
-    for section, copy in enumerate(strain_copies):
-        copy.wait()
+    for section, strain in enumerate(strains):
         first = section * slot
-        line_ref[first : first + lines[section], :] = held_strains[section][...].astype(jnp.float32)
+        line_ref[first : first + lines[section], :] = strain[...].astype(jnp.float32)
         line_ref[first + lines[section] : first + slot, :] = jnp.zeros(
             (slot - lines[section], LANE), jnp.float32
         )
@@ -100,10 +81,18 @@
     def shifted(section, chunk, tiles):
         pieces = []
         for u in range(blocks[section]):
-            first = pad + (chunk * CHUNK - u) * LANE
+            first, size = (chunk * CHUNK - u) * LANE, tiles * LANE
             if not isinstance(first, int):
-                first = pl.multiple_of(first, LANE)
-            pieces.append(held_taps[section, :, pl.ds(first, tiles * LANE)])
+                pieces.append(taps_ref[section, :, pl.ds(pl.multiple_of(first, LANE), size)])
+                continue
+            parts = []
+            if first < 0:
+                parts.append(jnp.zeros((rows, -first), taps_ref.dtype))
+            if first < taps:
+                parts.append(taps_ref[section, :, max(first, 0) : min(first + size, taps)])
+            if first + size > taps:
+                parts.append(jnp.zeros((rows, first + size - max(first, taps)), taps_ref.dtype))
+            pieces.append(jnp.concatenate(parts, axis=1) if len(parts) > 1 else parts[0])
         return pieces
 
     def accumulate(frames, group, chunk, tiles=CHUNK):
@@ -128,21 +117,27 @@
         for section in range(sections):
             build(frames[section // 2], section, chunk)
 
+    def accumulate_all(frames, chunk):
+        for group, part in zip(groups, frames):
+            accumulate(part, group, chunk)
+
     build_all(even_refs, 0)
-    for copy in taps_copies:
-        copy.wait()
+    accumulate_all(even_refs, 0)
+    build_all(odd_refs, 1)
 
     def step(number, carry):
-        for group, frames in zip(groups, even_refs):
-            accumulate(frames, group, 2 * number)
+        accumulate_all(odd_refs, 2 * number - 1)
+        build_all(even_refs, 2 * number)
+        accumulate_all(even_refs, 2 * number)
         build_all(odd_refs, 2 * number + 1)
-        for group, frames in zip(groups, odd_refs):
-            accumulate(frames, group, 2 * number + 1)
-        build_all(even_refs, 2 * number + 2)
         return carry
 
-    chunks = taps // (CHUNK * LANE)
-    lax.fori_loop(0, chunks // 2, step, 0)
+    lax.fori_loop(1, chunks // 2, step, 0)
+    accumulate_all(odd_refs, chunks - 1)
+    for group, frames in zip(groups, even_refs):
+        active = [section for section in group if blocks[section] > 1]
+        for section in active:
+            build(frames, section, chunks)
     for group, frames in zip(groups, even_refs):
         active = [section for section in group if blocks[section] > 1]
         if active:
@@ -166,20 +161,14 @@
     lines = [x.reshape(-1, LANE) for x in streams]
     out = pl.pallas_call(
         correlate_kernel,
-        out_shape=jax.ShapeDtypeStruct((padded, samples), jnp.bfloat16),
-        in_specs=[pl.BlockSpec(memory_space=pltpu.HBM)] * (sections + 1),
+        out_shape=pltpu.VMEM((padded, samples), jnp.bfloat16),
+        in_specs=[pl.BlockSpec(memory_space=pltpu.VMEM)] * (sections + 1),
         out_specs=pl.BlockSpec(memory_space=pltpu.VMEM),
-        scratch_shapes=[pltpu.VMEM(x.shape, x.dtype) for x in lines]
-        + [
-            pltpu.VMEM((sections, padded, 2 * longest - taps), jnp.bfloat16),
+        scratch_shapes=[
             pltpu.VMEM((sections * slot, LANE), jnp.float32),
             pltpu.VMEM((samples // LANE * padded, LANE), jnp.float32),
         ]
-        + [pltpu.VMEM((CHUNK * LANE, 2 * LANE), jnp.bfloat16)] * 4
-        + [
-            pltpu.SemaphoreType.DMA((sections,)),
-            pltpu.SemaphoreType.DMA((sections,)),
-        ],
+        + [pltpu.VMEM((CHUNK * LANE, 2 * LANE), jnp.bfloat16)] * 4,
         compiler_params=pltpu.CompilerParams(vmem_limit_bytes=60 * 2**20),
         cost_estimate=pl.CostEstimate(
             flops=2 * padded * taps * samples,

time: 46.3 us -> 45.4 us (0.981)
  Pallas kernels: 12.6 us -> 11.9 us
    pallas_call x1, Pallas kernels: 9.9 us -> 9.22 us  [correlate(): pl.pallas_call(correlate_kernel, out_shape=pltpu.VMEM((padded, samples),...]
  transfers between devices with their start and end apart: 15 -> 15, of which waited for: 9 -> 7; matrix products, arithmetic and copies ran while one was open for 0% -> 0% of each run, Pallas kernels for 2% -> 2%
where the time goes in v9:
time: 45.4 us; the launch traced here: 45.2 us
  starting transfers between devices  14 us (31%)
  Pallas kernels  11.9 us (26%)
  blocking collectives  11.7 us (26%)
  waiting for transfers between devices  6.28 us (14%)
  between operations  0.68 us (1%)
  other arithmetic  0.61 us (1%)
    ppermute x15, starting transfers between devices, exchange(): return lax.ppermute(block, 'tmpl', [(i, i ^ distance) for i in range(size)])  14 us
    all_to_all x1, blocking collectives, maximum_over_group(): lax.all_to_all(copies, 'tmpl', split_axis=0, concat_axis=0, tiled=True)  11.7 us
    pallas_call x1, Pallas kernels, correlate(): pl.pallas_call(correlate_kernel, out_shape=pltpu.VMEM((padded, samples),...  9.22 us
    ppermute x15, waiting for transfers between devices, exchange(): return lax.ppermute(block, 'tmpl', [(i, i ^ distance) for i in range(size)])  6.28 us
    pallas_call x1, Pallas kernels, reconstruct(): pl.pallas_call(functools.partial(recon_kernel, order), out_shape=(jax.Sha...  1.97 us
  transfers between devices with their start and end apart: 15, of which 7 were waited for; matrix products, arithmetic and copies ran while one was open for 0% of the time, Pallas kernels for 2%

profile of v9, /device:TPU:0, one launch (start us, length us, event | category | flops | bytes accessed | tf_op | source)
XLA Modules:
  0.0 45.2 jit_solution(16048700878169019710)
XLA Ops:
  0.6 0.0 copy-start
  0.6 9.2 %correlate.1.refs_0_ = bf16[32,1920]{1,0:T(8,128)(2,1)S(1)} custom-call(bf16[72,128]{1,0:T(8,128)(2,1)} %bitcast.9, bf16[68,128]{1,0:T(8,128)(2,1)} %bitcast.10, bf16[66,128]{1,0:T(8,128)(2,1)} %bitcast.11, bf16[65,128]{1,0:T(8,128)(2,1)} %bitcast.12, bf16[4,32,8192]{2,1,0:T(8,128)(2,1)} %refs_4_.1), custom_call_target="tpu_custom_call" | custom-call | flops 1006632960 | bytes 2097152 | tf_op jit(solution)/shard_map/correlate/pallas_call | solution.py:162
  9.9 3.1 %collective-permute-start.5 = (bf16[32,1920]{1,0:T(8,128)(2,1)S(1)}, bf16[32,1920]{1,0:T(8,128)(2,1)S(1)}, u32[]{:S(2)}, u32[]{:S(2)}) collective-permute-start(bf16[32,1920]{1,0:T(8,128)(2,1)S(1)} %correlate.1.refs_0_), channel_id=1, source_target_pairs={{0,4},{1,5},{2,6},{3,7},{4,0},{5,1},{6,2},{7,3},{8,12},{9,13},{10,... | collective-permute-start | bytes 368648 | tf_op jit(solution)/shard_map/ppermute | solution.py:185
  13.0 2.6 %collective-permute-start.3 = (bf16[32,1920]{1,0:T(8,128)(2,1)S(1)}, bf16[32,1920]{1,0:T(8,128)(2,1)S(1)}, u32[]{:S(2)}, u32[]{:S(2)}) collective-permute-start(bf16[32,1920]{1,0:T(8,128)(2,1)S(1)} %correlate.1.refs_0_), channel_id=1, source_target_pairs={{0,8},{1,9},{2,10},{3,11},{4,12},{5,13},{6,14},{7,15},{8,0},{9,1},... | collective-permute-start | bytes 368648 | tf_op jit(solution)/shard_map/ppermute | solution.py:185
  15.5 1.5 %collective-permute-start.1 = (bf16[32,1920]{1,0:T(8,128)(2,1)S(1)}, bf16[32,1920]{1,0:T(8,128)(2,1)S(1)}, u32[]{:S(2)}, u32[]{:S(2)}) collective-permute-start(bf16[32,1920]{1,0:T(8,128)(2,1)S(1)} %correlate.1.refs_0_), channel_id=1, source_target_pairs={{0,2},{1,3},{2,0},{3,1},{4,6},{5,7},{6,4},{7,5},{8,10},{9,11},{10,... | collective-permute-start | bytes 368648 | tf_op jit(solution)/shard_map/ppermute | solution.py:185
  17.1 0.0 copy-done
  17.1 0.7 %arrange.1.coeffs_ref = bf16[4,256,512]{2,1,0:T(8,128)(2,1)S(1)} custom-call(s32[1]{0:T(128)} %bitcast.4.offset_ref, bf16[4,256,512]{2,1,0:T(8,128)(2,1)S(1)} %copy-done), custom_call_target="tpu_custom_call" | custom-call | flops 536870912 | bytes 2097152 | tf_op jit(solution)/shard_map/arrange/pallas_call | solution.py:230
  17.8 0.1 collective-permute-start
  17.9 0.0 collective-permute-done.5.refs_6_
  17.9 1.7 %collective-permute-start.7 = (bf16[32,1920]{1,0:T(8,128)(2,1)S(1)}, bf16[32,1920]{1,0:T(8,128)(2,1)S(1)}, u32[]{:S(2)}, u32[]{:S(2)}) collective-permute-start(bf16[32,1920]{1,0:T(8,128)(2,1)S(1)} %collective-permute-done.5.refs_6_), channel_id=1, source_target_pairs={{0,2},{1,3},{2,0},{3,1},{4,6},{5,7},{6,4},{7,5},{8,10},{9,11},{10,... | collective-permute-start | bytes 368648 | tf_op jit(solution)/shard_map/ppermute | solution.py:185
  19.6 0.0 collective-permute-start.6
  19.6 1.7 %collective-permute-done.3.refs_4_ = bf16[32,1920]{1,0:T(8,128)(2,1)S(1)} collective-permute-done((bf16[32,1920]{1,0:T(8,128)(2,1)S(1)}, bf16[32,1920]{1,0:T(8,128)(2,1)S(1)}, u32[]{:S(2)}, u32[]{:S(2)}) %collective-permute-start.3) | collective-permute-done | bytes 122912 | tf_op jit(solution)/shard_map/ppermute | solution.py:185
  21.3 1.5 %collective-permute-start.13 = (bf16[32,1920]{1,0:T(8,128)(2,1)S(1)}, bf16[32,1920]{1,0:T(8,128)(2,1)S(1)}, u32[]{:S(2)}, u32[]{:S(2)}) collective-permute-start(bf16[32,1920]{1,0:T(8,128)(2,1)S(1)} %collective-permute-done.3.refs_4_), channel_id=1, source_target_pairs={{0,2},{1,3},{2,0},{3,1},{4,6},{5,7},{6,4},{7,5},{8,10},{9,11},{10,... | collective-permute-start | bytes 368648 | tf_op jit(solution)/shard_map/ppermute | solution.py:185
  22.8 0.0 collective-permute-done.1.refs_2_
  22.8 0.4 collective-permute-start.11
  23.2 0.0 collective-permute-done.refs_1_
  23.2 1.6 %collective-permute-start.9 = (bf16[32,1920]{1,0:T(8,128)(2,1)S(1)}, bf16[32,1920]{1,0:T(8,128)(2,1)S(1)}, u32[]{:S(2)}, u32[]{:S(2)}) collective-permute-start(bf16[32,1920]{1,0:T(8,128)(2,1)S(1)} %collective-permute-done.3.refs_4_), channel_id=1, source_target_pairs={{0,4},{1,5},{2,6},{3,7},{4,0},{5,1},{6,2},{7,3},{8,12},{9,13},{10,... | collective-permute-start | bytes 368648 | tf_op jit(solution)/shard_map/ppermute | solution.py:185
  24.8 0.6 %collective-permute-done.7.refs_8_ = bf16[32,1920]{1,0:T(8,128)(2,1)S(1)} collective-permute-done((bf16[32,1920]{1,0:T(8,128)(2,1)S(1)}, bf16[32,1920]{1,0:T(8,128)(2,1)S(1)}, u32[]{:S(2)}, u32[]{:S(2)}) %collective-permute-start.7) | collective-permute-done | bytes 122912 | tf_op jit(solution)/shard_map/ppermute | solution.py:185
  25.4 0.0 collective-permute-start.4
  25.4 0.0 collective-permute-done.6.refs_7_
  25.4 0.5 %collective-permute-start.2 = (bf16[32,1920]{1,0:T(8,128)(2,1)S(1)}, bf16[32,1920]{1,0:T(8,128)(2,1)S(1)}, u32[]{:S(2)}, u32[]{:S(2)}) collective-permute-start(bf16[32,1920]{1,0:T(8,128)(2,1)S(1)} %collective-permute-done.1.refs_2_), channel_id=1, source_target_pairs={{0,1},{1,0},{2,3},{3,2},{4,5},{5,4},{6,7},{7,6},{8,9},{9,8},{10,11... | collective-permute-start | bytes 368648 | tf_op jit(solution)/shard_map/ppermute | solution.py:185
  25.9 3.0 %collective-permute-done.13.refs_14_ = bf16[32,1920]{1,0:T(8,128)(2,1)S(1)} collective-permute-done((bf16[32,1920]{1,0:T(8,128)(2,1)S(1)}, bf16[32,1920]{1,0:T(8,128)(2,1)S(1)}, u32[]{:S(2)}, u32[]{:S(2)}) %collective-permute-start.13) | collective-permute-done | bytes 122912 | tf_op jit(solution)/shard_map/ppermute | solution.py:185
  28.9 0.0 collective-permute-start.8
  28.9 0.0 collective-permute-done.11.refs_12_
  28.9 0.5 %collective-permute-start.14 = (bf16[32,1920]{1,0:T(8,128)(2,1)S(1)}, bf16[32,1920]{1,0:T(8,128)(2,1)S(1)}, u32[]{:S(2)}, u32[]{:S(2)}) collective-permute-start(bf16[32,1920]{1,0:T(8,128)(2,1)S(1)} %collective-permute-done.13.refs_14_), channel_id=1, source_target_pairs={{0,1},{1,0},{2,3},{3,2},{4,5},{5,4},{6,7},{7,6},{8,9},{9,8},{10,11... | collective-permute-start | bytes 368648 | tf_op jit(solution)/shard_map/ppermute | solution.py:185
  29.4 0.0 collective-permute-done.9.refs_10_
  29.4 0.1 collective-permute-start.12
  29.5 0.0 collective-permute-done.4.refs_5_
  29.5 0.4 collective-permute-start.10
  29.9 0.0 collective-permute-done.2.refs_3_
  29.9 0.3 collective-permute-done.8.refs_9_
  30.2 0.2 collective-permute-done.14.refs_15_
  30.4 0.3 collective-permute-done.12.refs_13_
  30.7 0.2 collective-permute-done.10.refs_11_
  30.9 2.0 %reconstruct.1 = (bf16[256,1024]{1,0:T(8,128)(2,1)}, f32[1,1024]{1,0:T(1,128)S(1)}) custom-call(bf16[4,256,512]{2,1,0:T(8,128)(2,1)S(1)} %arrange.1.coeffs_ref, bf16[32,1920]{1,0:T(8,128)(2,1)S(1)} %correlate.1.refs_0_, bf16[32,1920]{1,0:T(8,128)(2,1)S(1)} %collective-permute-done.refs_1_, bf16[32,1920]{1,0:T(8,128)(2,1)S(1)} %collective-permute-done.1.refs_2_, ...), custom_call_target="tpu_custom_call" | custom-call | tf_op jit(solution)/shard_map/reconstruct/pallas_call | solution.py:289
  32.9 11.7 %all_to_all.5 = f32[16,8,128]{2,1,0:T(8,128)S(1)} all-to-all(f32[16,8,128]{2,1,0:T(8,128)S(1)} %broadcast_in_dim.8), channel_id=1, replica_groups=mesh['bank'=2,'tmpl'=16] {'tmpl'}, dimensions={0} | all-to-all | bytes 131072 | tf_op jit(solution)/shard_map/all_to_all | solution.py:214
  44.6 0.6 %reduce_max.9 = f32[8,128]{1,0:T(8,128)} reduce(f32[16,8,128]{2,1,0:T(8,128)S(1)} %all_to_all.5, f32[]{:T(128)} %constant.2.clone.1), dimensions={0}, to_apply=%region_0.0 | reduce | flops 15360 | bytes 69636 | tf_op jit(solution)/shard_map/reduce_max | solution.py:215
  (1 shorter events, 0.0 us)
Async XLA Ops:
  0.6 16.4 %copy-start = (bf16[4,256,512]{2,1,0:T(8,128)(2,1)S(1)}, bf16[4,256,512]{2,1,0:T(8,128)(2,1)}, u32[]{:S(2)}) copy-start(bf16[4,256,512]{2,1,0:T(8,128)(2,1)} %coeffs_ref.1) | copy-start | bytes 3145732
  9.9 8.0 %collective-permute-start.5 = (bf16[32,1920]{1,0:T(8,128)(2,1)S(1)}, bf16[32,1920]{1,0:T(8,128)(2,1)S(1)}, u32[]{:S(2)}, u32[]{:S(2)}) collective-permute-start(bf16[32,1920]{1,0:T(8,128)(2,1)S(1)} %correlate.1.refs_0_), channel_id=1, source_target_pairs={{0,4},{1,5},{2,6},{3,7},{4,0},{5,1},{6,2},{7,3},{8,12},{9,13},{10,... | collective-permute-start | bytes 368648 | tf_op jit(solution)/shard_map/ppermute | solution.py:185
  13.0 8.4 %collective-permute-start.3 = (bf16[32,1920]{1,0:T(8,128)(2,1)S(1)}, bf16[32,1920]{1,0:T(8,128)(2,1)S(1)}, u32[]{:S(2)}, u32[]{:S(2)}) collective-permute-start(bf16[32,1920]{1,0:T(8,128)(2,1)S(1)} %correlate.1.refs_0_), channel_id=1, source_target_pairs={{0,8},{1,9},{2,10},{3,11},{4,12},{5,13},{6,14},{7,15},{8,0},{9,1},... | collective-permute-start | bytes 368648 | tf_op jit(solution)/shard_map/ppermute | solution.py:185
  15.5 7.3 %collective-permute-start.1 = (bf16[32,1920]{1,0:T(8,128)(2,1)S(1)}, bf16[32,1920]{1,0:T(8,128)(2,1)S(1)}, u32[]{:S(2)}, u32[]{:S(2)}) collective-permute-start(bf16[32,1920]{1,0:T(8,128)(2,1)S(1)} %correlate.1.refs_0_), channel_id=1, source_target_pairs={{0,2},{1,3},{2,0},{3,1},{4,6},{5,7},{6,4},{7,5},{8,10},{9,11},{10,... | collective-permute-start | bytes 368648 | tf_op jit(solution)/shard_map/ppermute | solution.py:185
  17.8 5.4 %collective-permute-start = (bf16[32,1920]{1,0:T(8,128)(2,1)S(1)}, bf16[32,1920]{1,0:T(8,128)(2,1)S(1)}, u32[]{:S(2)}, u32[]{:S(2)}) collective-permute-start(bf16[32,1920]{1,0:T(8,128)(2,1)S(1)} %correlate.1.refs_0_), channel_id=1, source_target_pairs={{0,1},{1,0},{2,3},{3,2},{4,5},{5,4},{6,7},{7,6},{8,9},{9,8},{10,11... | collective-permute-start | bytes 368648 | tf_op jit(solution)/shard_map/ppermute | solution.py:185
  17.9 7.5 %collective-permute-start.7 = (bf16[32,1920]{1,0:T(8,128)(2,1)S(1)}, bf16[32,1920]{1,0:T(8,128)(2,1)S(1)}, u32[]{:S(2)}, u32[]{:S(2)}) collective-permute-start(bf16[32,1920]{1,0:T(8,128)(2,1)S(1)} %collective-permute-done.5.refs_6_), channel_id=1, source_target_pairs={{0,2},{1,3},{2,0},{3,1},{4,6},{5,7},{6,4},{7,5},{8,10},{9,11},{10,... | collective-permute-start | bytes 368648 | tf_op jit(solution)/shard_map/ppermute | solution.py:185
  19.6 5.8 %collective-permute-start.6 = (bf16[32,1920]{1,0:T(8,128)(2,1)S(1)}, bf16[32,1920]{1,0:T(8,128)(2,1)S(1)}, u32[]{:S(2)}, u32[]{:S(2)}) collective-permute-start(bf16[32,1920]{1,0:T(8,128)(2,1)S(1)} %collective-permute-done.5.refs_6_), channel_id=1, source_target_pairs={{0,1},{1,0},{2,3},{3,2},{4,5},{5,4},{6,7},{7,6},{8,9},{9,8},{10,11... | collective-permute-start | bytes 368648 | tf_op jit(solution)/shard_map/ppermute | solution.py:185
  21.3 7.6 %collective-permute-start.13 = (bf16[32,1920]{1,0:T(8,128)(2,1)S(1)}, bf16[32,1920]{1,0:T(8,128)(2,1)S(1)}, u32[]{:S(2)}, u32[]{:S(2)}) collective-permute-start(bf16[32,1920]{1,0:T(8,128)(2,1)S(1)} %collective-permute-done.3.refs_4_), channel_id=1, source_target_pairs={{0,2},{1,3},{2,0},{3,1},{4,6},{5,7},{6,4},{7,5},{8,10},{9,11},{10,... | collective-permute-start | bytes 368648 | tf_op jit(solution)/shard_map/ppermute | solution.py:185
  22.8 6.1 %collective-permute-start.11 = (bf16[32,1920]{1,0:T(8,128)(2,1)S(1)}, bf16[32,1920]{1,0:T(8,128)(2,1)S(1)}, u32[]{:S(2)}, u32[]{:S(2)}) collective-permute-start(bf16[32,1920]{1,0:T(8,128)(2,1)S(1)} %collective-permute-done.3.refs_4_), channel_id=1, source_target_pairs={{0,6},{1,7},{2,4},{3,5},{4,2},{5,3},{6,0},{7,1},{8,14},{9,15},{10,... | collective-permute-start | bytes 368648 | tf_op jit(solution)/shard_map/ppermute | solution.py:185
  23.2 6.2 %collective-permute-start.9 = (bf16[32,1920]{1,0:T(8,128)(2,1)S(1)}, bf16[32,1920]{1,0:T(8,128)(2,1)S(1)}, u32[]{:S(2)}, u32[]{:S(2)}) collective-permute-start(bf16[32,1920]{1,0:T(8,128)(2,1)S(1)} %collective-permute-done.3.refs_4_), channel_id=1, source_target_pairs={{0,4},{1,5},{2,6},{3,7},{4,0},{5,1},{6,2},{7,3},{8,12},{9,13},{10,... | collective-permute-start | bytes 368648 | tf_op jit(solution)/shard_map/ppermute | solution.py:185
  25.4 4.1 %collective-permute-start.4 = (bf16[32,1920]{1,0:T(8,128)(2,1)S(1)}, bf16[32,1920]{1,0:T(8,128)(2,1)S(1)}, u32[]{:S(2)}, u32[]{:S(2)}) collective-permute-start(bf16[32,1920]{1,0:T(8,128)(2,1)S(1)} %collective-permute-done.3.refs_4_), channel_id=1, source_target_pairs={{0,1},{1,0},{2,3},{3,2},{4,5},{5,4},{6,7},{7,6},{8,9},{9,8},{10,11... | collective-permute-start | bytes 368648 | tf_op jit(solution)/shard_map/ppermute | solution.py:185
  25.4 4.5 %collective-permute-start.2 = (bf16[32,1920]{1,0:T(8,128)(2,1)S(1)}, bf16[32,1920]{1,0:T(8,128)(2,1)S(1)}, u32[]{:S(2)}, u32[]{:S(2)}) collective-permute-start(bf16[32,1920]{1,0:T(8,128)(2,1)S(1)} %collective-permute-done.1.refs_2_), channel_id=1, source_target_pairs={{0,1},{1,0},{2,3},{3,2},{4,5},{5,4},{6,7},{7,6},{8,9},{9,8},{10,11... | collective-permute-start | bytes 368648 | tf_op jit(solution)/shard_map/ppermute | solution.py:185
  28.9 1.3 %collective-permute-start.8 = (bf16[32,1920]{1,0:T(8,128)(2,1)S(1)}, bf16[32,1920]{1,0:T(8,128)(2,1)S(1)}, u32[]{:S(2)}, u32[]{:S(2)}) collective-permute-start(bf16[32,1920]{1,0:T(8,128)(2,1)S(1)} %collective-permute-done.7.refs_8_), channel_id=1, source_target_pairs={{0,1},{1,0},{2,3},{3,2},{4,5},{5,4},{6,7},{7,6},{8,9},{9,8},{10,11... | collective-permute-start | bytes 368648 | tf_op jit(solution)/shard_map/ppermute | solution.py:185
  28.9 1.5 %collective-permute-start.14 = (bf16[32,1920]{1,0:T(8,128)(2,1)S(1)}, bf16[32,1920]{1,0:T(8,128)(2,1)S(1)}, u32[]{:S(2)}, u32[]{:S(2)}) collective-permute-start(bf16[32,1920]{1,0:T(8,128)(2,1)S(1)} %collective-permute-done.13.refs_14_), channel_id=1, source_target_pairs={{0,1},{1,0},{2,3},{3,2},{4,5},{5,4},{6,7},{7,6},{8,9},{9,8},{10,11... | collective-permute-start | bytes 368648 | tf_op jit(solution)/shard_map/ppermute | solution.py:185
  29.4 1.3 %collective-permute-start.12 = (bf16[32,1920]{1,0:T(8,128)(2,1)S(1)}, bf16[32,1920]{1,0:T(8,128)(2,1)S(1)}, u32[]{:S(2)}, u32[]{:S(2)}) collective-permute-start(bf16[32,1920]{1,0:T(8,128)(2,1)S(1)} %collective-permute-done.11.refs_12_), channel_id=1, source_target_pairs={{0,1},{1,0},{2,3},{3,2},{4,5},{5,4},{6,7},{7,6},{8,9},{9,8},{10,11... | collective-permute-start | bytes 368648 | tf_op jit(solution)/shard_map/ppermute | solution.py:185
  29.5 1.4 %collective-permute-start.10 = (bf16[32,1920]{1,0:T(8,128)(2,1)S(1)}, bf16[32,1920]{1,0:T(8,128)(2,1)S(1)}, u32[]{:S(2)}, u32[]{:S(2)}) collective-permute-start(bf16[32,1920]{1,0:T(8,128)(2,1)S(1)} %collective-permute-done.9.refs_10_), channel_id=1, source_target_pairs={{0,1},{1,0},{2,3},{3,2},{4,5},{5,4},{6,7},{7,6},{8,9},{9,8},{10,11... | collective-permute-start | bytes 368648 | tf_op jit(solution)/shard_map/ppermute | solution.py:185

commit v10 on v9

--- a/solution.py
+++ b/solution.py
@@ -8,7 +8,7 @@
 from jax.sharding import PartitionSpec as P
 
 LANE = 128
-CHUNK = 8
+CHUNK = 16
 SUB = 16
 ROWS = 8
 ROLLS = 4
@@ -18,9 +18,15 @@
 
 
 def correlate_kernel(*refs):
-    strains, taps_ref, out_ref = refs[:4], refs[4], refs[5]
-    line_ref, total_ref, even_refs, odd_refs = refs[6], refs[7], refs[8:10], refs[10:12]
+    strains, source_ref, out_ref, taps_ref, sems = refs[:4], refs[4], refs[5], refs[6], refs[7]
+    line_ref, total_ref, even_refs, odd_refs = refs[8], refs[9], refs[10:12], refs[12:14]
     sections = len(strains)
+    copies = [
+        pltpu.make_async_copy(source_ref.at[section], taps_ref.at[section], sems.at[section])
+        for section in range(sections)
+    ]
+    for copy in copies:
+        copy.start()
     rows, taps = taps_ref.shape[1], taps_ref.shape[2]
     lines = [ref.shape[0] for ref in strains]
     blocks = [count - taps // LANE for count in lines]
@@ -43,15 +49,14 @@
             (slot - lines[section], LANE), jnp.float32
         )
 
-    width = (CHUNK + 1) * LANE
-    row = lax.broadcasted_iota(jnp.int32, (ROWS, width), 0)
-
-    def build(frames, section, chunk):
+    def build(frames, section, chunk, tiles=CHUNK):
+        width = (tiles + 1) * LANE
+        row = lax.broadcasted_iota(jnp.int32, (ROWS, width), 0)
         first = section * slot + chunk * CHUNK
         wide = jnp.concatenate(
             [
                 jnp.broadcast_to(line_ref[pl.ds(first + number, 1), :], (ROWS, LANE))
-                for number in range(CHUNK + 1)
+                for number in range(tiles + 1)
             ],
             axis=1,
         )
@@ -64,10 +69,10 @@
         for q in range(1, ROLLS):
             moved.append(pltpu.roll(wide, width - SUB * q, axis=1))
         stacked = jnp.concatenate(
-            [wide[:, number * LANE : (number + 2) * LANE] for number in range(CHUNK)], axis=0
+            [wide[:, number * LANE : (number + 2) * LANE] for number in range(tiles)], axis=0
         )
         rest = jnp.dot(stacked, shifts, preferred_element_type=jnp.float32).astype(wide.dtype)
-        for number in range(CHUNK):
+        for number in range(tiles):
             pieces = [part[:, number * LANE : (number + 1) * LANE] for part in moved]
             pieces += [
                 rest[number * SUB : (number + 1) * SUB, q * LANE : (q + 1) * LANE]
@@ -122,6 +127,8 @@
             accumulate(part, group, chunk)
 
     build_all(even_refs, 0)
+    for copy in copies:
+        copy.wait()
     accumulate_all(even_refs, 0)
     build_all(odd_refs, 1)
 
@@ -136,12 +143,11 @@
     accumulate_all(odd_refs, chunks - 1)
     for group, frames in zip(groups, even_refs):
         active = [section for section in group if blocks[section] > 1]
-        for section in active:
-            build(frames, section, chunks)
-    for group, frames in zip(groups, even_refs):
-        active = [section for section in group if blocks[section] > 1]
         if active:
-            accumulate(frames, active, chunks, max(blocks[section] for section in active) - 1)
+            tiles = max(blocks[section] for section in active) - 1
+            for section in active:
+                build(frames, section, chunks, tiles)
+            accumulate(frames, active, chunks, tiles)
     place = 0
     for section in range(sections):
         for u in range(blocks[section]):
@@ -162,9 +168,12 @@
     out = pl.pallas_call(
         correlate_kernel,
         out_shape=pltpu.VMEM((padded, samples), jnp.bfloat16),
-        in_specs=[pl.BlockSpec(memory_space=pltpu.VMEM)] * (sections + 1),
+        in_specs=[pl.BlockSpec(memory_space=pltpu.VMEM)] * sections
+        + [pl.BlockSpec(memory_space=pltpu.HBM)],
         out_specs=pl.BlockSpec(memory_space=pltpu.VMEM),
         scratch_shapes=[
+            pltpu.VMEM((sections, padded, taps), jnp.bfloat16),
+            pltpu.SemaphoreType.DMA((sections,)),
             pltpu.VMEM((sections * slot, LANE), jnp.float32),
             pltpu.VMEM((samples // LANE * padded, LANE), jnp.float32),
         ]

time: 45.4 us -> 43.5 us (0.958)
  Pallas kernels: 11.9 us -> 9.93 us
    pallas_call x1, Pallas kernels: 9.22 us -> 7.25 us  [correlate(): pl.pallas_call(correlate_kernel, out_shape=pltpu.VMEM((padded, samples),...]
where the time goes in v10:
time: 43.5 us; the launch traced here: 43.3 us
  starting transfers between devices  14 us (32%)
  blocking collectives  11.7 us (27%)
  Pallas kernels  9.93 us (23%)
  waiting for transfers between devices  6.27 us (14%)
  between operations  0.69 us (2%)
  other arithmetic  0.61 us (1%)
    ppermute x15, starting transfers between devices, exchange(): return lax.ppermute(block, 'tmpl', [(i, i ^ distance) for i in range(size)])  14 us
    all_to_all x1, blocking collectives, maximum_over_group(): lax.all_to_all(copies, 'tmpl', split_axis=0, concat_axis=0, tiled=True)  11.7 us
    pallas_call x1, Pallas kernels, correlate(): pl.pallas_call(correlate_kernel, out_shape=pltpu.VMEM((padded, samples),...  7.25 us
    ppermute x15, waiting for transfers between devices, exchange(): return lax.ppermute(block, 'tmpl', [(i, i ^ distance) for i in range(size)])  6.27 us
    pallas_call x1, Pallas kernels, reconstruct(): pl.pallas_call(functools.partial(recon_kernel, order), out_shape=(jax.Sha...  1.97 us
  transfers between devices with their start and end apart: 15, of which 7 were waited for; matrix products, arithmetic and copies ran while one was open for 0% of the time, Pallas kernels for 2%

profile of v10, /device:TPU:0, one launch (start us, length us, event | category | flops | bytes accessed | tf_op | source)
XLA Modules:
  0.0 43.3 jit_solution(16707723328096069635)
XLA Ops:
  0.6 0.0 copy-start
  0.6 7.2 %correlate.1.refs_0_ = bf16[32,1920]{1,0:T(8,128)(2,1)S(1)} custom-call(bf16[72,128]{1,0:T(8,128)(2,1)} %bitcast.9, bf16[68,128]{1,0:T(8,128)(2,1)} %bitcast.10, bf16[66,128]{1,0:T(8,128)(2,1)} %bitcast.11, bf16[65,128]{1,0:T(8,128)(2,1)} %bitcast.12, bf16[4,32,8192]{2,1,0:T(8,128)(2,1)} %refs_4_.1), custom_call_target="tpu_custom_call" | custom-call | flops 1006632960 | bytes 2097152 | tf_op jit(solution)/shard_map/correlate/pallas_call | solution.py:168
  7.9 3.1 %collective-permute-start.5 = (bf16[32,1920]{1,0:T(8,128)(2,1)S(1)}, bf16[32,1920]{1,0:T(8,128)(2,1)S(1)}, u32[]{:S(2)}, u32[]{:S(2)}) collective-permute-start(bf16[32,1920]{1,0:T(8,128)(2,1)S(1)} %correlate.1.refs_0_), channel_id=1, source_target_pairs={{0,4},{1,5},{2,6},{3,7},{4,0},{5,1},{6,2},{7,3},{8,12},{9,13},{10,... | collective-permute-start | bytes 368648 | tf_op jit(solution)/shard_map/ppermute | solution.py:194
  11.0 2.6 %collective-permute-start.3 = (bf16[32,1920]{1,0:T(8,128)(2,1)S(1)}, bf16[32,1920]{1,0:T(8,128)(2,1)S(1)}, u32[]{:S(2)}, u32[]{:S(2)}) collective-permute-start(bf16[32,1920]{1,0:T(8,128)(2,1)S(1)} %correlate.1.refs_0_), channel_id=1, source_target_pairs={{0,8},{1,9},{2,10},{3,11},{4,12},{5,13},{6,14},{7,15},{8,0},{9,1},... | collective-permute-start | bytes 368648 | tf_op jit(solution)/shard_map/ppermute | solution.py:194
  13.6 1.5 %collective-permute-start.1 = (bf16[32,1920]{1,0:T(8,128)(2,1)S(1)}, bf16[32,1920]{1,0:T(8,128)(2,1)S(1)}, u32[]{:S(2)}, u32[]{:S(2)}) collective-permute-start(bf16[32,1920]{1,0:T(8,128)(2,1)S(1)} %correlate.1.refs_0_), channel_id=1, source_target_pairs={{0,2},{1,3},{2,0},{3,1},{4,6},{5,7},{6,4},{7,5},{8,10},{9,11},{10,... | collective-permute-start | bytes 368648 | tf_op jit(solution)/shard_map/ppermute | solution.py:194
  15.1 0.0 copy-done
  15.1 0.7 %arrange.1.coeffs_ref = bf16[4,256,512]{2,1,0:T(8,128)(2,1)S(1)} custom-call(s32[1]{0:T(128)} %bitcast.4.offset_ref, bf16[4,256,512]{2,1,0:T(8,128)(2,1)S(1)} %copy-done), custom_call_target="tpu_custom_call" | custom-call | flops 536870912 | bytes 2097152 | tf_op jit(solution)/shard_map/arrange/pallas_call | solution.py:239
  15.8 0.1 collective-permute-start
  15.9 0.0 collective-permute-done.5.refs_6_
  15.9 1.7 %collective-permute-start.7 = (bf16[32,1920]{1,0:T(8,128)(2,1)S(1)}, bf16[32,1920]{1,0:T(8,128)(2,1)S(1)}, u32[]{:S(2)}, u32[]{:S(2)}) collective-permute-start(bf16[32,1920]{1,0:T(8,128)(2,1)S(1)} %collective-permute-done.5.refs_6_), channel_id=1, source_target_pairs={{0,2},{1,3},{2,0},{3,1},{4,6},{5,7},{6,4},{7,5},{8,10},{9,11},{10,... | collective-permute-start | bytes 368648 | tf_op jit(solution)/shard_map/ppermute | solution.py:194
  17.6 0.0 collective-permute-start.6
  17.6 1.7 %collective-permute-done.3.refs_4_ = bf16[32,1920]{1,0:T(8,128)(2,1)S(1)} collective-permute-done((bf16[32,1920]{1,0:T(8,128)(2,1)S(1)}, bf16[32,1920]{1,0:T(8,128)(2,1)S(1)}, u32[]{:S(2)}, u32[]{:S(2)}) %collective-permute-start.3) | collective-permute-done | bytes 122912 | tf_op jit(solution)/shard_map/ppermute | solution.py:194
  19.4 1.5 %collective-permute-start.13 = (bf16[32,1920]{1,0:T(8,128)(2,1)S(1)}, bf16[32,1920]{1,0:T(8,128)(2,1)S(1)}, u32[]{:S(2)}, u32[]{:S(2)}) collective-permute-start(bf16[32,1920]{1,0:T(8,128)(2,1)S(1)} %collective-permute-done.3.refs_4_), channel_id=1, source_target_pairs={{0,2},{1,3},{2,0},{3,1},{4,6},{5,7},{6,4},{7,5},{8,10},{9,11},{10,... | collective-permute-start | bytes 368648 | tf_op jit(solution)/shard_map/ppermute | solution.py:194
  20.9 0.0 collective-permute-done.1.refs_2_
  20.9 0.4 collective-permute-start.11
  21.3 0.0 collective-permute-done.refs_1_
  21.3 1.6 %collective-permute-start.9 = (bf16[32,1920]{1,0:T(8,128)(2,1)S(1)}, bf16[32,1920]{1,0:T(8,128)(2,1)S(1)}, u32[]{:S(2)}, u32[]{:S(2)}) collective-permute-start(bf16[32,1920]{1,0:T(8,128)(2,1)S(1)} %collective-permute-done.3.refs_4_), channel_id=1, source_target_pairs={{0,4},{1,5},{2,6},{3,7},{4,0},{5,1},{6,2},{7,3},{8,12},{9,13},{10,... | collective-permute-start | bytes 368648 | tf_op jit(solution)/shard_map/ppermute | solution.py:194
  22.9 0.6 %collective-permute-done.7.refs_8_ = bf16[32,1920]{1,0:T(8,128)(2,1)S(1)} collective-permute-done((bf16[32,1920]{1,0:T(8,128)(2,1)S(1)}, bf16[32,1920]{1,0:T(8,128)(2,1)S(1)}, u32[]{:S(2)}, u32[]{:S(2)}) %collective-permute-start.7) | collective-permute-done | bytes 122912 | tf_op jit(solution)/shard_map/ppermute | solution.py:194
  23.4 0.0 collective-permute-start.4
  23.4 0.0 collective-permute-done.6.refs_7_
  23.4 0.5 %collective-permute-start.2 = (bf16[32,1920]{1,0:T(8,128)(2,1)S(1)}, bf16[32,1920]{1,0:T(8,128)(2,1)S(1)}, u32[]{:S(2)}, u32[]{:S(2)}) collective-permute-start(bf16[32,1920]{1,0:T(8,128)(2,1)S(1)} %collective-permute-done.1.refs_2_), channel_id=1, source_target_pairs={{0,1},{1,0},{2,3},{3,2},{4,5},{5,4},{6,7},{7,6},{8,9},{9,8},{10,11... | collective-permute-start | bytes 368648 | tf_op jit(solution)/shard_map/ppermute | solution.py:194
  23.9 3.0 %collective-permute-done.13.refs_14_ = bf16[32,1920]{1,0:T(8,128)(2,1)S(1)} collective-permute-done((bf16[32,1920]{1,0:T(8,128)(2,1)S(1)}, bf16[32,1920]{1,0:T(8,128)(2,1)S(1)}, u32[]{:S(2)}, u32[]{:S(2)}) %collective-permute-start.13) | collective-permute-done | bytes 122912 | tf_op jit(solution)/shard_map/ppermute | solution.py:194
  26.9 0.0 collective-permute-start.8
  26.9 0.0 collective-permute-done.11.refs_12_
  26.9 0.5 %collective-permute-start.14 = (bf16[32,1920]{1,0:T(8,128)(2,1)S(1)}, bf16[32,1920]{1,0:T(8,128)(2,1)S(1)}, u32[]{:S(2)}, u32[]{:S(2)}) collective-permute-start(bf16[32,1920]{1,0:T(8,128)(2,1)S(1)} %collective-permute-done.13.refs_14_), channel_id=1, source_target_pairs={{0,1},{1,0},{2,3},{3,2},{4,5},{5,4},{6,7},{7,6},{8,9},{9,8},{10,11... | collective-permute-start | bytes 368648 | tf_op jit(solution)/shard_map/ppermute | solution.py:194
  27.4 0.0 collective-permute-done.9.refs_10_
  27.4 0.1 collective-permute-start.12
  27.5 0.0 collective-permute-done.4.refs_5_
  27.5 0.4 %collective-permute-start.10 = (bf16[32,1920]{1,0:T(8,128)(2,1)S(1)}, bf16[32,1920]{1,0:T(8,128)(2,1)S(1)}, u32[]{:S(2)}, u32[]{:S(2)}) collective-permute-start(bf16[32,1920]{1,0:T(8,128)(2,1)S(1)} %collective-permute-done.9.refs_10_), channel_id=1, source_target_pairs={{0,1},{1,0},{2,3},{3,2},{4,5},{5,4},{6,7},{7,6},{8,9},{9,8},{10,11... | collective-permute-start | bytes 368648 | tf_op jit(solution)/shard_map/ppermute | solution.py:194
  27.9 0.0 collective-permute-done.2.refs_3_
  28.0 0.3 collective-permute-done.8.refs_9_
  28.3 0.2 collective-permute-done.14.refs_15_
  28.4 0.3 collective-permute-done.12.refs_13_
  28.8 0.2 collective-permute-done.10.refs_11_
  28.9 2.0 %reconstruct.1 = (bf16[256,1024]{1,0:T(8,128)(2,1)}, f32[1,1024]{1,0:T(1,128)S(1)}) custom-call(bf16[4,256,512]{2,1,0:T(8,128)(2,1)S(1)} %arrange.1.coeffs_ref, bf16[32,1920]{1,0:T(8,128)(2,1)S(1)} %correlate.1.refs_0_, bf16[32,1920]{1,0:T(8,128)(2,1)S(1)} %collective-permute-done.refs_1_, bf16[32,1920]{1,0:T(8,128)(2,1)S(1)} %collective-permute-done.1.refs_2_, ...), custom_call_target="tpu_custom_call" | custom-call | tf_op jit(solution)/shard_map/reconstruct/pallas_call | solution.py:298
  30.9 11.7 %all_to_all.5 = f32[16,8,128]{2,1,0:T(8,128)S(1)} all-to-all(f32[16,8,128]{2,1,0:T(8,128)S(1)} %broadcast_in_dim.8), channel_id=1, replica_groups=mesh['bank'=2,'tmpl'=16] {'tmpl'}, dimensions={0} | all-to-all | bytes 131072 | tf_op jit(solution)/shard_map/all_to_all | solution.py:223
  42.7 0.6 %reduce_max.9 = f32[8,128]{1,0:T(8,128)} reduce(f32[16,8,128]{2,1,0:T(8,128)S(1)} %all_to_all.5, f32[]{:T(128)} %constant.2.clone.1), dimensions={0}, to_apply=%region_0.0 | reduce | flops 15360 | bytes 69636 | tf_op jit(solution)/shard_map/reduce_max | solution.py:224
  (1 shorter events, 0.0 us)
Async XLA Ops:
  0.6 14.5 %copy-start = (bf16[4,256,512]{2,1,0:T(8,128)(2,1)S(1)}, bf16[4,256,512]{2,1,0:T(8,128)(2,1)}, u32[]{:S(2)}) copy-start(bf16[4,256,512]{2,1,0:T(8,128)(2,1)} %coeffs_ref.1) | copy-start | bytes 3145732
  7.9 8.0 %collective-permute-start.5 = (bf16[32,1920]{1,0:T(8,128)(2,1)S(1)}, bf16[32,1920]{1,0:T(8,128)(2,1)S(1)}, u32[]{:S(2)}, u32[]{:S(2)}) collective-permute-start(bf16[32,1920]{1,0:T(8,128)(2,1)S(1)} %correlate.1.refs_0_), channel_id=1, source_target_pairs={{0,4},{1,5},{2,6},{3,7},{4,0},{5,1},{6,2},{7,3},{8,12},{9,13},{10,... | collective-permute-start | bytes 368648 | tf_op jit(solution)/shard_map/ppermute | solution.py:194
  11.0 8.4 %collective-permute-start.3 = (bf16[32,1920]{1,0:T(8,128)(2,1)S(1)}, bf16[32,1920]{1,0:T(8,128)(2,1)S(1)}, u32[]{:S(2)}, u32[]{:S(2)}) collective-permute-start(bf16[32,1920]{1,0:T(8,128)(2,1)S(1)} %correlate.1.refs_0_), channel_id=1, source_target_pairs={{0,8},{1,9},{2,10},{3,11},{4,12},{5,13},{6,14},{7,15},{8,0},{9,1},... | collective-permute-start | bytes 368648 | tf_op jit(solution)/shard_map/ppermute | solution.py:194
  13.6 7.3 %collective-permute-start.1 = (bf16[32,1920]{1,0:T(8,128)(2,1)S(1)}, bf16[32,1920]{1,0:T(8,128)(2,1)S(1)}, u32[]{:S(2)}, u32[]{:S(2)}) collective-permute-start(bf16[32,1920]{1,0:T(8,128)(2,1)S(1)} %correlate.1.refs_0_), channel_id=1, source_target_pairs={{0,2},{1,3},{2,0},{3,1},{4,6},{5,7},{6,4},{7,5},{8,10},{9,11},{10,... | collective-permute-start | bytes 368648 | tf_op jit(solution)/shard_map/ppermute | solution.py:194
  15.8 5.4 %collective-permute-start = (bf16[32,1920]{1,0:T(8,128)(2,1)S(1)}, bf16[32,1920]{1,0:T(8,128)(2,1)S(1)}, u32[]{:S(2)}, u32[]{:S(2)}) collective-permute-start(bf16[32,1920]{1,0:T(8,128)(2,1)S(1)} %correlate.1.refs_0_), channel_id=1, source_target_pairs={{0,1},{1,0},{2,3},{3,2},{4,5},{5,4},{6,7},{7,6},{8,9},{9,8},{10,11... | collective-permute-start | bytes 368648 | tf_op jit(solution)/shard_map/ppermute | solution.py:194
  15.9 7.5 %collective-permute-start.7 = (bf16[32,1920]{1,0:T(8,128)(2,1)S(1)}, bf16[32,1920]{1,0:T(8,128)(2,1)S(1)}, u32[]{:S(2)}, u32[]{:S(2)}) collective-permute-start(bf16[32,1920]{1,0:T(8,128)(2,1)S(1)} %collective-permute-done.5.refs_6_), channel_id=1, source_target_pairs={{0,2},{1,3},{2,0},{3,1},{4,6},{5,7},{6,4},{7,5},{8,10},{9,11},{10,... | collective-permute-start | bytes 368648 | tf_op jit(solution)/shard_map/ppermute | solution.py:194
  17.6 5.8 %collective-permute-start.6 = (bf16[32,1920]{1,0:T(8,128)(2,1)S(1)}, bf16[32,1920]{1,0:T(8,128)(2,1)S(1)}, u32[]{:S(2)}, u32[]{:S(2)}) collective-permute-start(bf16[32,1920]{1,0:T(8,128)(2,1)S(1)} %collective-permute-done.5.refs_6_), channel_id=1, source_target_pairs={{0,1},{1,0},{2,3},{3,2},{4,5},{5,4},{6,7},{7,6},{8,9},{9,8},{10,11... | collective-permute-start | bytes 368648 | tf_op jit(solution)/shard_map/ppermute | solution.py:194
  19.4 7.6 %collective-permute-start.13 = (bf16[32,1920]{1,0:T(8,128)(2,1)S(1)}, bf16[32,1920]{1,0:T(8,128)(2,1)S(1)}, u32[]{:S(2)}, u32[]{:S(2)}) collective-permute-start(bf16[32,1920]{1,0:T(8,128)(2,1)S(1)} %collective-permute-done.3.refs_4_), channel_id=1, source_target_pairs={{0,2},{1,3},{2,0},{3,1},{4,6},{5,7},{6,4},{7,5},{8,10},{9,11},{10,... | collective-permute-start | bytes 368648 | tf_op jit(solution)/shard_map/ppermute | solution.py:194
  20.9 6.0 %collective-permute-start.11 = (bf16[32,1920]{1,0:T(8,128)(2,1)S(1)}, bf16[32,1920]{1,0:T(8,128)(2,1)S(1)}, u32[]{:S(2)}, u32[]{:S(2)}) collective-permute-start(bf16[32,1920]{1,0:T(8,128)(2,1)S(1)} %collective-permute-done.3.refs_4_), channel_id=1, source_target_pairs={{0,6},{1,7},{2,4},{3,5},{4,2},{5,3},{6,0},{7,1},{8,14},{9,15},{10,... | collective-permute-start | bytes 368648 | tf_op jit(solution)/shard_map/ppermute | solution.py:194
  21.3 6.2 %collective-permute-start.9 = (bf16[32,1920]{1,0:T(8,128)(2,1)S(1)}, bf16[32,1920]{1,0:T(8,128)(2,1)S(1)}, u32[]{:S(2)}, u32[]{:S(2)}) collective-permute-start(bf16[32,1920]{1,0:T(8,128)(2,1)S(1)} %collective-permute-done.3.refs_4_), channel_id=1, source_target_pairs={{0,4},{1,5},{2,6},{3,7},{4,0},{5,1},{6,2},{7,3},{8,12},{9,13},{10,... | collective-permute-start | bytes 368648 | tf_op jit(solution)/shard_map/ppermute | solution.py:194
  23.4 4.1 %collective-permute-start.4 = (bf16[32,1920]{1,0:T(8,128)(2,1)S(1)}, bf16[32,1920]{1,0:T(8,128)(2,1)S(1)}, u32[]{:S(2)}, u32[]{:S(2)}) collective-permute-start(bf16[32,1920]{1,0:T(8,128)(2,1)S(1)} %collective-permute-done.3.refs_4_), channel_id=1, source_target_pairs={{0,1},{1,0},{2,3},{3,2},{4,5},{5,4},{6,7},{7,6},{8,9},{9,8},{10,11... | collective-permute-start | bytes 368648 | tf_op jit(solution)/shard_map/ppermute | solution.py:194
  23.4 4.5 %collective-permute-start.2 = (bf16[32,1920]{1,0:T(8,128)(2,1)S(1)}, bf16[32,1920]{1,0:T(8,128)(2,1)S(1)}, u32[]{:S(2)}, u32[]{:S(2)}) collective-permute-start(bf16[32,1920]{1,0:T(8,128)(2,1)S(1)} %collective-permute-done.1.refs_2_), channel_id=1, source_target_pairs={{0,1},{1,0},{2,3},{3,2},{4,5},{5,4},{6,7},{7,6},{8,9},{9,8},{10,11... | collective-permute-start | bytes 368648 | tf_op jit(solution)/shard_map/ppermute | solution.py:194
  26.9 1.3 %collective-permute-start.8 = (bf16[32,1920]{1,0:T(8,128)(2,1)S(1)}, bf16[32,1920]{1,0:T(8,128)(2,1)S(1)}, u32[]{:S(2)}, u32[]{:S(2)}) collective-permute-start(bf16[32,1920]{1,0:T(8,128)(2,1)S(1)} %collective-permute-done.7.refs_8_), channel_id=1, source_target_pairs={{0,1},{1,0},{2,3},{3,2},{4,5},{5,4},{6,7},{7,6},{8,9},{9,8},{10,11... | collective-permute-start | bytes 368648 | tf_op jit(solution)/shard_map/ppermute | solution.py:194
  26.9 1.5 %collective-permute-start.14 = (bf16[32,1920]{1,0:T(8,128)(2,1)S(1)}, bf16[32,1920]{1,0:T(8,128)(2,1)S(1)}, u32[]{:S(2)}, u32[]{:S(2)}) collective-permute-start(bf16[32,1920]{1,0:T(8,128)(2,1)S(1)} %collective-permute-done.13.refs_14_), channel_id=1, source_target_pairs={{0,1},{1,0},{2,3},{3,2},{4,5},{5,4},{6,7},{7,6},{8,9},{9,8},{10,11... | collective-permute-start | bytes 368648 | tf_op jit(solution)/shard_map/ppermute | solution.py:194
  27.4 1.3 %collective-permute-start.12 = (bf16[32,1920]{1,0:T(8,128)(2,1)S(1)}, bf16[32,1920]{1,0:T(8,128)(2,1)S(1)}, u32[]{:S(2)}, u32[]{:S(2)}) collective-permute-start(bf16[32,1920]{1,0:T(8,128)(2,1)S(1)} %collective-permute-done.11.refs_12_), channel_id=1, source_target_pairs={{0,1},{1,0},{2,3},{3,2},{4,5},{5,4},{6,7},{7,6},{8,9},{9,8},{10,11... | collective-permute-start | bytes 368648 | tf_op jit(solution)/shard_map/ppermute | solution.py:194
  27.5 1.4 %collective-permute-start.10 = (bf16[32,1920]{1,0:T(8,128)(2,1)S(1)}, bf16[32,1920]{1,0:T(8,128)(2,1)S(1)}, u32[]{:S(2)}, u32[]{:S(2)}) collective-permute-start(bf16[32,1920]{1,0:T(8,128)(2,1)S(1)} %collective-permute-done.9.refs_10_), channel_id=1, source_target_pairs={{0,1},{1,0},{2,3},{3,2},{4,5},{5,4},{6,7},{7,6},{8,9},{9,8},{10,11... | collective-permute-start | bytes 368648 | tf_op jit(solution)/shard_map/ppermute | solution.py:194

commit v11 on v10

--- a/solution.py
+++ b/solution.py
@@ -8,7 +8,7 @@
 from jax.sharding import PartitionSpec as P
 
 LANE = 128
-CHUNK = 16
+CHUNK = 32
 SUB = 16
 ROWS = 8
 ROLLS = 4
@@ -256,41 +256,51 @@
 
 def recon_kernel(order, coeffs_ref, *refs):
     pieces = [refs[order.index(place)] for place in range(len(order))]
-    snr_ref, peak_ref = refs[-2], refs[-1]
+    out_ref, peak_ref, snr_ref, sems = refs[-4:]
     samples = snr_ref.shape[1]
-    source = lax.broadcasted_iota(jnp.int32, (2 * LANE, 2 * LANE), 0) % LANE
-    target = lax.broadcasted_iota(jnp.int32, (2 * LANE, 2 * LANE), 1) // 2
+    wide = 2 * LANE
+    source = lax.broadcasted_iota(jnp.int32, (wide, wide), 0) % LANE
+    target = lax.broadcasted_iota(jnp.int32, (wide, wide), 1) // 2
     repeat = jnp.where(source == target, 1.0, 0.0).astype(jnp.bfloat16)
-    running = None
-    for section in (3, 2, 1, 0):
-        width = samples >> section
-        offset = sum(samples >> s for s in range(section))
-        summed = []
-        for place in range(0, width, 2 * LANE):
-            size = min(2 * LANE, width)
-            first = offset + place
-            basis = jnp.concatenate([ref[:, first : first + size] for ref in pieces], axis=0)
-            part = jnp.dot(coeffs_ref[section], basis, preferred_element_type=jnp.float32)
-            if running is not None:
-                coarse = running[place // (2 * LANE)]
-                high = coarse.astype(jnp.bfloat16)
-                low = (coarse - high.astype(jnp.float32)).astype(jnp.bfloat16)
-                part = part + jnp.dot(
-                    jnp.concatenate([high, low], axis=1),
-                    repeat,
-                    preferred_element_type=jnp.float32,
-                )
-            summed.append(part)
-        running = []
-        for part in summed:
-            running += [part[:, at : at + LANE] for at in range(0, part.shape[1], LANE)]
+    copies = []
+
+    def total(section, place, size):
+        first = sum(samples >> s for s in range(section)) + place
+        basis = jnp.concatenate([ref[:, first : first + size] for ref in pieces], axis=0)
+        part = jnp.dot(coeffs_ref[section], basis, preferred_element_type=jnp.float32)
+        if section == 3:
+            return part
+        coarse = held[section + 1][place // wide]
+        high = coarse.astype(jnp.bfloat16)
+        low = (coarse - high.astype(jnp.float32)).astype(jnp.bfloat16)
+        return part + jnp.dot(
+            jnp.concatenate([high, low], axis=1), repeat, preferred_element_type=jnp.float32
+        )
+
+    held = {section: [] for section in range(4)}
+
+    def extend(section):
+        place = len(held[section]) * LANE
+        size = min(wide, samples >> section)
+        if section < 3 and len(held[section + 1]) <= place // wide:
+            extend(section + 1)
+        part = total(section, place, size)
+        held[section] += [part[:, at : at + LANE] for at in range(0, size, LANE)]
         if section == 0:
-            for number, part in enumerate(summed):
-                place = number * 2 * LANE
-                snr_ref[:, place : place + 2 * LANE] = part.astype(snr_ref.dtype)
-                peak_ref[:, place : place + 2 * LANE] = jnp.max(
-                    jnp.abs(part), axis=0, keepdims=True
-                )
+            snr_ref[:, place : place + size] = part.astype(snr_ref.dtype)
+            copy = pltpu.make_async_copy(
+                snr_ref.at[:, pl.ds(place, size)],
+                out_ref.at[:, pl.ds(place, size)],
+                sems.at[place // wide],
+            )
+            copy.start()
+            copies.append(copy)
+            peak_ref[:, place : place + size] = jnp.max(jnp.abs(part), axis=0, keepdims=True)
+
+    while len(held[0]) * LANE < samples:
+        extend(0)
+    for copy in copies:
+        copy.wait()
 
 
 def reconstruct(coeffs, blocks, samples):
@@ -302,7 +312,14 @@
             jax.ShapeDtypeStruct((1, samples), jnp.float32),
         ),
         in_specs=[pl.BlockSpec(memory_space=pltpu.VMEM)] * (1 + len(blocks)),
-        out_specs=(pl.BlockSpec(memory_space=pltpu.VMEM),) * 2,
+        out_specs=(
+            pl.BlockSpec(memory_space=pltpu.HBM),
+            pl.BlockSpec(memory_space=pltpu.VMEM),
+        ),
+        scratch_shapes=[
+            pltpu.VMEM((coeffs.shape[1], samples), jnp.bfloat16),
+            pltpu.SemaphoreType.DMA((samples // (2 * LANE),)),
+        ],
         compiler_params=pltpu.CompilerParams(vmem_limit_bytes=16 * 2**20),
         name="reconstruct",
     )(coeffs, *[blocks[place] for place in order])

time: 43.5 us -> 43.3 us (level)
  no operation moved by 1% of the time
where the time goes in v11:
time: 43.3 us; the launch traced here: 43.1 us
  starting transfers between devices  14 us (32%)
  blocking collectives  11.7 us (27%)
  Pallas kernels  9.81 us (23%)
  waiting for transfers between devices  6.27 us (14%)
  between operations  0.7 us (2%)
  other arithmetic  0.61 us (1%)
    ppermute x15, starting transfers between devices, exchange(): return lax.ppermute(block, 'tmpl', [(i, i ^ distance) for i in range(size)])  14 us
    all_to_all x1, blocking collectives, maximum_over_group(): lax.all_to_all(copies, 'tmpl', split_axis=0, concat_axis=0, tiled=True)  11.7 us
    pallas_call x1, Pallas kernels, correlate(): pl.pallas_call(correlate_kernel, out_shape=pltpu.VMEM((padded, samples),...  6.91 us
    ppermute x15, waiting for transfers between devices, exchange(): return lax.ppermute(block, 'tmpl', [(i, i ^ distance) for i in range(size)])  6.27 us
    pallas_call x1, Pallas kernels, reconstruct(): pl.pallas_call(functools.partial(recon_kernel, order), out_shape=(jax.Sha...  2.18 us
  transfers between devices with their start and end apart: 15, of which 7 were waited for; matrix products, arithmetic and copies ran while one was open for 0% of the time, Pallas kernels for 2%

profile of v11, /device:TPU:0, one launch (start us, length us, event | category | flops | bytes accessed | tf_op | source)
XLA Modules:
  0.0 43.1 jit_solution(1127015534558642747)
XLA Ops:
  0.6 0.0 copy-start
  0.6 6.9 %correlate.1.refs_0_ = bf16[32,1920]{1,0:T(8,128)(2,1)S(1)} custom-call(bf16[72,128]{1,0:T(8,128)(2,1)} %bitcast.9, bf16[68,128]{1,0:T(8,128)(2,1)} %bitcast.10, bf16[66,128]{1,0:T(8,128)(2,1)} %bitcast.11, bf16[65,128]{1,0:T(8,128)(2,1)} %bitcast.12, bf16[4,32,8192]{2,1,0:T(8,128)(2,1)} %refs_4_.1), custom_call_target="tpu_custom_call" | custom-call | flops 1006632960 | bytes 2097152 | tf_op jit(solution)/shard_map/correlate/pallas_call | solution.py:168
  7.6 3.1 %collective-permute-start.5 = (bf16[32,1920]{1,0:T(8,128)(2,1)S(1)}, bf16[32,1920]{1,0:T(8,128)(2,1)S(1)}, u32[]{:S(2)}, u32[]{:S(2)}) collective-permute-start(bf16[32,1920]{1,0:T(8,128)(2,1)S(1)} %correlate.1.refs_0_), channel_id=1, source_target_pairs={{0,4},{1,5},{2,6},{3,7},{4,0},{5,1},{6,2},{7,3},{8,12},{9,13},{10,... | collective-permute-start | bytes 368648 | tf_op jit(solution)/shard_map/ppermute | solution.py:194
  10.6 2.6 %collective-permute-start.3 = (bf16[32,1920]{1,0:T(8,128)(2,1)S(1)}, bf16[32,1920]{1,0:T(8,128)(2,1)S(1)}, u32[]{:S(2)}, u32[]{:S(2)}) collective-permute-start(bf16[32,1920]{1,0:T(8,128)(2,1)S(1)} %correlate.1.refs_0_), channel_id=1, source_target_pairs={{0,8},{1,9},{2,10},{3,11},{4,12},{5,13},{6,14},{7,15},{8,0},{9,1},... | collective-permute-start | bytes 368648 | tf_op jit(solution)/shard_map/ppermute | solution.py:194
  13.2 1.5 %collective-permute-start.1 = (bf16[32,1920]{1,0:T(8,128)(2,1)S(1)}, bf16[32,1920]{1,0:T(8,128)(2,1)S(1)}, u32[]{:S(2)}, u32[]{:S(2)}) collective-permute-start(bf16[32,1920]{1,0:T(8,128)(2,1)S(1)} %correlate.1.refs_0_), channel_id=1, source_target_pairs={{0,2},{1,3},{2,0},{3,1},{4,6},{5,7},{6,4},{7,5},{8,10},{9,11},{10,... | collective-permute-start | bytes 368648 | tf_op jit(solution)/shard_map/ppermute | solution.py:194
  14.8 0.0 copy-done
  14.8 0.7 %arrange.1.coeffs_ref = bf16[4,256,512]{2,1,0:T(8,128)(2,1)S(1)} custom-call(s32[1]{0:T(128)} %bitcast.4.offset_ref, bf16[4,256,512]{2,1,0:T(8,128)(2,1)S(1)} %copy-done), custom_call_target="tpu_custom_call" | custom-call | flops 536870912 | bytes 2097152 | tf_op jit(solution)/shard_map/arrange/pallas_call | solution.py:239
  15.5 0.1 collective-permute-start
  15.6 0.0 collective-permute-done.5.refs_6_
  15.6 1.7 %collective-permute-start.7 = (bf16[32,1920]{1,0:T(8,128)(2,1)S(1)}, bf16[32,1920]{1,0:T(8,128)(2,1)S(1)}, u32[]{:S(2)}, u32[]{:S(2)}) collective-permute-start(bf16[32,1920]{1,0:T(8,128)(2,1)S(1)} %collective-permute-done.5.refs_6_), channel_id=1, source_target_pairs={{0,2},{1,3},{2,0},{3,1},{4,6},{5,7},{6,4},{7,5},{8,10},{9,11},{10,... | collective-permute-start | bytes 368648 | tf_op jit(solution)/shard_map/ppermute | solution.py:194
  17.3 0.0 collective-permute-start.6
  17.3 1.7 %collective-permute-done.3.refs_4_ = bf16[32,1920]{1,0:T(8,128)(2,1)S(1)} collective-permute-done((bf16[32,1920]{1,0:T(8,128)(2,1)S(1)}, bf16[32,1920]{1,0:T(8,128)(2,1)S(1)}, u32[]{:S(2)}, u32[]{:S(2)}) %collective-permute-start.3) | collective-permute-done | bytes 122912 | tf_op jit(solution)/shard_map/ppermute | solution.py:194
  19.0 1.5 %collective-permute-start.13 = (bf16[32,1920]{1,0:T(8,128)(2,1)S(1)}, bf16[32,1920]{1,0:T(8,128)(2,1)S(1)}, u32[]{:S(2)}, u32[]{:S(2)}) collective-permute-start(bf16[32,1920]{1,0:T(8,128)(2,1)S(1)} %collective-permute-done.3.refs_4_), channel_id=1, source_target_pairs={{0,2},{1,3},{2,0},{3,1},{4,6},{5,7},{6,4},{7,5},{8,10},{9,11},{10,... | collective-permute-start | bytes 368648 | tf_op jit(solution)/shard_map/ppermute | solution.py:194
  20.5 0.0 collective-permute-done.1.refs_2_
  20.5 0.4 collective-permute-start.11
  20.9 0.0 collective-permute-done.refs_1_
  20.9 1.6 %collective-permute-start.9 = (bf16[32,1920]{1,0:T(8,128)(2,1)S(1)}, bf16[32,1920]{1,0:T(8,128)(2,1)S(1)}, u32[]{:S(2)}, u32[]{:S(2)}) collective-permute-start(bf16[32,1920]{1,0:T(8,128)(2,1)S(1)} %collective-permute-done.3.refs_4_), channel_id=1, source_target_pairs={{0,4},{1,5},{2,6},{3,7},{4,0},{5,1},{6,2},{7,3},{8,12},{9,13},{10,... | collective-permute-start | bytes 368648 | tf_op jit(solution)/shard_map/ppermute | solution.py:194
  22.5 0.6 %collective-permute-done.7.refs_8_ = bf16[32,1920]{1,0:T(8,128)(2,1)S(1)} collective-permute-done((bf16[32,1920]{1,0:T(8,128)(2,1)S(1)}, bf16[32,1920]{1,0:T(8,128)(2,1)S(1)}, u32[]{:S(2)}, u32[]{:S(2)}) %collective-permute-start.7) | collective-permute-done | bytes 122912 | tf_op jit(solution)/shard_map/ppermute | solution.py:194
  23.1 0.0 collective-permute-start.4
  23.1 0.0 collective-permute-done.6.refs_7_
  23.1 0.5 %collective-permute-start.2 = (bf16[32,1920]{1,0:T(8,128)(2,1)S(1)}, bf16[32,1920]{1,0:T(8,128)(2,1)S(1)}, u32[]{:S(2)}, u32[]{:S(2)}) collective-permute-start(bf16[32,1920]{1,0:T(8,128)(2,1)S(1)} %collective-permute-done.1.refs_2_), channel_id=1, source_target_pairs={{0,1},{1,0},{2,3},{3,2},{4,5},{5,4},{6,7},{7,6},{8,9},{9,8},{10,11... | collective-permute-start | bytes 368648 | tf_op jit(solution)/shard_map/ppermute | solution.py:194
  23.6 3.0 %collective-permute-done.13.refs_14_ = bf16[32,1920]{1,0:T(8,128)(2,1)S(1)} collective-permute-done((bf16[32,1920]{1,0:T(8,128)(2,1)S(1)}, bf16[32,1920]{1,0:T(8,128)(2,1)S(1)}, u32[]{:S(2)}, u32[]{:S(2)}) %collective-permute-start.13) | collective-permute-done | bytes 122912 | tf_op jit(solution)/shard_map/ppermute | solution.py:194
  26.6 0.0 collective-permute-start.8
  26.6 0.0 collective-permute-done.11.refs_12_
  26.6 0.5 %collective-permute-start.14 = (bf16[32,1920]{1,0:T(8,128)(2,1)S(1)}, bf16[32,1920]{1,0:T(8,128)(2,1)S(1)}, u32[]{:S(2)}, u32[]{:S(2)}) collective-permute-start(bf16[32,1920]{1,0:T(8,128)(2,1)S(1)} %collective-permute-done.13.refs_14_), channel_id=1, source_target_pairs={{0,1},{1,0},{2,3},{3,2},{4,5},{5,4},{6,7},{7,6},{8,9},{9,8},{10,11... | collective-permute-start | bytes 368648 | tf_op jit(solution)/shard_map/ppermute | solution.py:194
  27.1 0.0 collective-permute-done.9.refs_10_
  27.1 0.1 collective-permute-start.12
  27.2 0.0 collective-permute-done.4.refs_5_
  27.2 0.4 %collective-permute-start.10 = (bf16[32,1920]{1,0:T(8,128)(2,1)S(1)}, bf16[32,1920]{1,0:T(8,128)(2,1)S(1)}, u32[]{:S(2)}, u32[]{:S(2)}) collective-permute-start(bf16[32,1920]{1,0:T(8,128)(2,1)S(1)} %collective-permute-done.9.refs_10_), channel_id=1, source_target_pairs={{0,1},{1,0},{2,3},{3,2},{4,5},{5,4},{6,7},{7,6},{8,9},{9,8},{10,11... | collective-permute-start | bytes 368648 | tf_op jit(solution)/shard_map/ppermute | solution.py:194
  27.6 0.0 collective-permute-done.2.refs_3_
  27.6 0.3 collective-permute-done.8.refs_9_
  27.9 0.2 collective-permute-done.14.refs_15_
  28.1 0.3 collective-permute-done.12.refs_13_
  28.4 0.2 collective-permute-done.10.refs_11_
  28.6 2.2 %reconstruct.1 = (bf16[256,1024]{1,0:T(8,128)(2,1)}, f32[1,1024]{1,0:T(1,128)S(1)}) custom-call(bf16[4,256,512]{2,1,0:T(8,128)(2,1)S(1)} %arrange.1.coeffs_ref, bf16[32,1920]{1,0:T(8,128)(2,1)S(1)} %correlate.1.refs_0_, bf16[32,1920]{1,0:T(8,128)(2,1)S(1)} %collective-permute-done.refs_1_, bf16[32,1920]{1,0:T(8,128)(2,1)S(1)} %collective-permute-done.1.refs_2_, ...), custom_call_target="tpu_custom_call" | custom-call | tf_op jit(solution)/shard_map/reconstruct/pallas_call | solution.py:308
  30.8 11.7 %all_to_all.5 = f32[16,8,128]{2,1,0:T(8,128)S(1)} all-to-all(f32[16,8,128]{2,1,0:T(8,128)S(1)} %broadcast_in_dim.8), channel_id=1, replica_groups=mesh['bank'=2,'tmpl'=16] {'tmpl'}, dimensions={0} | all-to-all | bytes 131072 | tf_op jit(solution)/shard_map/all_to_all | solution.py:223
  42.5 0.6 %reduce_max.9 = f32[8,128]{1,0:T(8,128)} reduce(f32[16,8,128]{2,1,0:T(8,128)S(1)} %all_to_all.5, f32[]{:T(128)} %constant.2.clone.1), dimensions={0}, to_apply=%region_0.0 | reduce | flops 15360 | bytes 69636 | tf_op jit(solution)/shard_map/reduce_max | solution.py:224
  (1 shorter events, 0.0 us)
Async XLA Ops:
  0.6 14.1 %copy-start = (bf16[4,256,512]{2,1,0:T(8,128)(2,1)S(1)}, bf16[4,256,512]{2,1,0:T(8,128)(2,1)}, u32[]{:S(2)}) copy-start(bf16[4,256,512]{2,1,0:T(8,128)(2,1)} %coeffs_ref.1) | copy-start | bytes 3145732
  7.6 8.0 %collective-permute-start.5 = (bf16[32,1920]{1,0:T(8,128)(2,1)S(1)}, bf16[32,1920]{1,0:T(8,128)(2,1)S(1)}, u32[]{:S(2)}, u32[]{:S(2)}) collective-permute-start(bf16[32,1920]{1,0:T(8,128)(2,1)S(1)} %correlate.1.refs_0_), channel_id=1, source_target_pairs={{0,4},{1,5},{2,6},{3,7},{4,0},{5,1},{6,2},{7,3},{8,12},{9,13},{10,... | collective-permute-start | bytes 368648 | tf_op jit(solution)/shard_map/ppermute | solution.py:194
  10.6 8.4 %collective-permute-start.3 = (bf16[32,1920]{1,0:T(8,128)(2,1)S(1)}, bf16[32,1920]{1,0:T(8,128)(2,1)S(1)}, u32[]{:S(2)}, u32[]{:S(2)}) collective-permute-start(bf16[32,1920]{1,0:T(8,128)(2,1)S(1)} %correlate.1.refs_0_), channel_id=1, source_target_pairs={{0,8},{1,9},{2,10},{3,11},{4,12},{5,13},{6,14},{7,15},{8,0},{9,1},... | collective-permute-start | bytes 368648 | tf_op jit(solution)/shard_map/ppermute | solution.py:194
  13.2 7.3 %collective-permute-start.1 = (bf16[32,1920]{1,0:T(8,128)(2,1)S(1)}, bf16[32,1920]{1,0:T(8,128)(2,1)S(1)}, u32[]{:S(2)}, u32[]{:S(2)}) collective-permute-start(bf16[32,1920]{1,0:T(8,128)(2,1)S(1)} %correlate.1.refs_0_), channel_id=1, source_target_pairs={{0,2},{1,3},{2,0},{3,1},{4,6},{5,7},{6,4},{7,5},{8,10},{9,11},{10,... | collective-permute-start | bytes 368648 | tf_op jit(solution)/shard_map/ppermute | solution.py:194
  15.5 5.4 %collective-permute-start = (bf16[32,1920]{1,0:T(8,128)(2,1)S(1)}, bf16[32,1920]{1,0:T(8,128)(2,1)S(1)}, u32[]{:S(2)}, u32[]{:S(2)}) collective-permute-start(bf16[32,1920]{1,0:T(8,128)(2,1)S(1)} %correlate.1.refs_0_), channel_id=1, source_target_pairs={{0,1},{1,0},{2,3},{3,2},{4,5},{5,4},{6,7},{7,6},{8,9},{9,8},{10,11... | collective-permute-start | bytes 368648 | tf_op jit(solution)/shard_map/ppermute | solution.py:194
  15.6 7.5 %collective-permute-start.7 = (bf16[32,1920]{1,0:T(8,128)(2,1)S(1)}, bf16[32,1920]{1,0:T(8,128)(2,1)S(1)}, u32[]{:S(2)}, u32[]{:S(2)}) collective-permute-start(bf16[32,1920]{1,0:T(8,128)(2,1)S(1)} %collective-permute-done.5.refs_6_), channel_id=1, source_target_pairs={{0,2},{1,3},{2,0},{3,1},{4,6},{5,7},{6,4},{7,5},{8,10},{9,11},{10,... | collective-permute-start | bytes 368648 | tf_op jit(solution)/shard_map/ppermute | solution.py:194
  17.3 5.8 %collective-permute-start.6 = (bf16[32,1920]{1,0:T(8,128)(2,1)S(1)}, bf16[32,1920]{1,0:T(8,128)(2,1)S(1)}, u32[]{:S(2)}, u32[]{:S(2)}) collective-permute-start(bf16[32,1920]{1,0:T(8,128)(2,1)S(1)} %collective-permute-done.5.refs_6_), channel_id=1, source_target_pairs={{0,1},{1,0},{2,3},{3,2},{4,5},{5,4},{6,7},{7,6},{8,9},{9,8},{10,11... | collective-permute-start | bytes 368648 | tf_op jit(solution)/shard_map/ppermute | solution.py:194
  19.0 7.6 %collective-permute-start.13 = (bf16[32,1920]{1,0:T(8,128)(2,1)S(1)}, bf16[32,1920]{1,0:T(8,128)(2,1)S(1)}, u32[]{:S(2)}, u32[]{:S(2)}) collective-permute-start(bf16[32,1920]{1,0:T(8,128)(2,1)S(1)} %collective-permute-done.3.refs_4_), channel_id=1, source_target_pairs={{0,2},{1,3},{2,0},{3,1},{4,6},{5,7},{6,4},{7,5},{8,10},{9,11},{10,... | collective-permute-start | bytes 368648 | tf_op jit(solution)/shard_map/ppermute | solution.py:194
  20.5 6.0 %collective-permute-start.11 = (bf16[32,1920]{1,0:T(8,128)(2,1)S(1)}, bf16[32,1920]{1,0:T(8,128)(2,1)S(1)}, u32[]{:S(2)}, u32[]{:S(2)}) collective-permute-start(bf16[32,1920]{1,0:T(8,128)(2,1)S(1)} %collective-permute-done.3.refs_4_), channel_id=1, source_target_pairs={{0,6},{1,7},{2,4},{3,5},{4,2},{5,3},{6,0},{7,1},{8,14},{9,15},{10,... | collective-permute-start | bytes 368648 | tf_op jit(solution)/shard_map/ppermute | solution.py:194
  20.9 6.2 %collective-permute-start.9 = (bf16[32,1920]{1,0:T(8,128)(2,1)S(1)}, bf16[32,1920]{1,0:T(8,128)(2,1)S(1)}, u32[]{:S(2)}, u32[]{:S(2)}) collective-permute-start(bf16[32,1920]{1,0:T(8,128)(2,1)S(1)} %collective-permute-done.3.refs_4_), channel_id=1, source_target_pairs={{0,4},{1,5},{2,6},{3,7},{4,0},{5,1},{6,2},{7,3},{8,12},{9,13},{10,... | collective-permute-start | bytes 368648 | tf_op jit(solution)/shard_map/ppermute | solution.py:194
  23.1 4.1 %collective-permute-start.4 = (bf16[32,1920]{1,0:T(8,128)(2,1)S(1)}, bf16[32,1920]{1,0:T(8,128)(2,1)S(1)}, u32[]{:S(2)}, u32[]{:S(2)}) collective-permute-start(bf16[32,1920]{1,0:T(8,128)(2,1)S(1)} %collective-permute-done.3.refs_4_), channel_id=1, source_target_pairs={{0,1},{1,0},{2,3},{3,2},{4,5},{5,4},{6,7},{7,6},{8,9},{9,8},{10,11... | collective-permute-start | bytes 368648 | tf_op jit(solution)/shard_map/ppermute | solution.py:194
  23.1 4.5 %collective-permute-start.2 = (bf16[32,1920]{1,0:T(8,128)(2,1)S(1)}, bf16[32,1920]{1,0:T(8,128)(2,1)S(1)}, u32[]{:S(2)}, u32[]{:S(2)}) collective-permute-start(bf16[32,1920]{1,0:T(8,128)(2,1)S(1)} %collective-permute-done.1.refs_2_), channel_id=1, source_target_pairs={{0,1},{1,0},{2,3},{3,2},{4,5},{5,4},{6,7},{7,6},{8,9},{9,8},{10,11... | collective-permute-start | bytes 368648 | tf_op jit(solution)/shard_map/ppermute | solution.py:194
  26.6 1.3 %collective-permute-start.8 = (bf16[32,1920]{1,0:T(8,128)(2,1)S(1)}, bf16[32,1920]{1,0:T(8,128)(2,1)S(1)}, u32[]{:S(2)}, u32[]{:S(2)}) collective-permute-start(bf16[32,1920]{1,0:T(8,128)(2,1)S(1)} %collective-permute-done.7.refs_8_), channel_id=1, source_target_pairs={{0,1},{1,0},{2,3},{3,2},{4,5},{5,4},{6,7},{7,6},{8,9},{9,8},{10,11... | collective-permute-start | bytes 368648 | tf_op jit(solution)/shard_map/ppermute | solution.py:194
  26.6 1.5 %collective-permute-start.14 = (bf16[32,1920]{1,0:T(8,128)(2,1)S(1)}, bf16[32,1920]{1,0:T(8,128)(2,1)S(1)}, u32[]{:S(2)}, u32[]{:S(2)}) collective-permute-start(bf16[32,1920]{1,0:T(8,128)(2,1)S(1)} %collective-permute-done.13.refs_14_), channel_id=1, source_target_pairs={{0,1},{1,0},{2,3},{3,2},{4,5},{5,4},{6,7},{7,6},{8,9},{9,8},{10,11... | collective-permute-start | bytes 368648 | tf_op jit(solution)/shard_map/ppermute | solution.py:194
  27.1 1.3 %collective-permute-start.12 = (bf16[32,1920]{1,0:T(8,128)(2,1)S(1)}, bf16[32,1920]{1,0:T(8,128)(2,1)S(1)}, u32[]{:S(2)}, u32[]{:S(2)}) collective-permute-start(bf16[32,1920]{1,0:T(8,128)(2,1)S(1)} %collective-permute-done.11.refs_12_), channel_id=1, source_target_pairs={{0,1},{1,0},{2,3},{3,2},{4,5},{5,4},{6,7},{7,6},{8,9},{9,8},{10,11... | collective-permute-start | bytes 368648 | tf_op jit(solution)/shard_map/ppermute | solution.py:194
  27.2 1.4 %collective-permute-start.10 = (bf16[32,1920]{1,0:T(8,128)(2,1)S(1)}, bf16[32,1920]{1,0:T(8,128)(2,1)S(1)}, u32[]{:S(2)}, u32[]{:S(2)}) collective-permute-start(bf16[32,1920]{1,0:T(8,128)(2,1)S(1)} %collective-permute-done.9.refs_10_), channel_id=1, source_target_pairs={{0,1},{1,0},{2,3},{3,2},{4,5},{5,4},{6,7},{7,6},{8,9},{9,8},{10,11... | collective-permute-start | bytes 368648 | tf_op jit(solution)/shard_map/ppermute | solution.py:194

commit v12 on v10

--- a/solution.py
+++ b/solution.py
@@ -8,10 +8,9 @@
 from jax.sharding import PartitionSpec as P
 
 LANE = 128
-CHUNK = 16
+CHUNK = 32
 SUB = 16
 ROWS = 8
-ROLLS = 4
 TIED = 1
 HANDED = (0, 1, 2, 3, 8, 9, 4, 5, 6, 7, 12, 13, 14, 15, 10, 11)
 SUB = 16
@@ -36,12 +35,6 @@
     groups = ((0, 1), (2, 3))
     total_ref[...] = jnp.zeros(total_ref.shape, total_ref.dtype)
 
-    extra = LANE // SUB - ROLLS
-    source = lax.broadcasted_iota(jnp.int32, (2 * LANE, extra * LANE), 0)
-    target = lax.broadcasted_iota(jnp.int32, (2 * LANE, extra * LANE), 1)
-    target = target % LANE + (target // LANE + ROLLS) * SUB
-    shifts = jnp.where(source == target, 1.0, 0.0).astype(jnp.bfloat16)
-
     for section, strain in enumerate(strains):
         first = section * slot
         line_ref[first : first + lines[section], :] = strain[...].astype(jnp.float32)
@@ -66,18 +59,10 @@
         wide = jnp.concatenate([wide, pltpu.roll(wide, width - ROWS, axis=1)], axis=0)
         wide = wide.astype(jnp.bfloat16)
         moved = [wide]
-        for q in range(1, ROLLS):
+        for q in range(1, LANE // SUB):
             moved.append(pltpu.roll(wide, width - SUB * q, axis=1))
-        stacked = jnp.concatenate(
-            [wide[:, number * LANE : (number + 2) * LANE] for number in range(tiles)], axis=0
-        )
-        rest = jnp.dot(stacked, shifts, preferred_element_type=jnp.float32).astype(wide.dtype)
         for number in range(tiles):
             pieces = [part[:, number * LANE : (number + 1) * LANE] for part in moved]
-            pieces += [
-                rest[number * SUB : (number + 1) * SUB, q * LANE : (q + 1) * LANE]
-                for q in range(extra)
-            ]
             half = section % 2
             frames[number * LANE : (number + 1) * LANE, half * LANE : (half + 1) * LANE] = (
                 jnp.concatenate(pieces, axis=0)

time: 43.5 us -> 44.6 us (1.025)
  Pallas kernels: 9.93 us -> 11.1 us
    pallas_call x1, Pallas kernels: 7.25 us -> 8.45 us  [correlate(): pl.pallas_call(correlate_kernel, out_shape=pltpu.VMEM((padded, samples),...]
where the time goes in v12:
time: 44.6 us; the launch traced here: 44.5 us
  starting transfers between devices  14 us (31%)
  blocking collectives  11.7 us (26%)
  Pallas kernels  11.1 us (25%)
  waiting for transfers between devices  6.27 us (14%)
  between operations  0.69 us (2%)
  other arithmetic  0.61 us (1%)
    ppermute x15, starting transfers between devices, exchange(): return lax.ppermute(block, 'tmpl', [(i, i ^ distance) for i in range(size)])  14 us
    all_to_all x1, blocking collectives, maximum_over_group(): lax.all_to_all(copies, 'tmpl', split_axis=0, concat_axis=0, tiled=True)  11.7 us
    pallas_call x1, Pallas kernels, correlate(): pl.pallas_call(correlate_kernel, out_shape=pltpu.VMEM((padded, samples),...  8.45 us
    ppermute x15, waiting for transfers between devices, exchange(): return lax.ppermute(block, 'tmpl', [(i, i ^ distance) for i in range(size)])  6.27 us
    pallas_call x1, Pallas kernels, reconstruct(): pl.pallas_call(functools.partial(recon_kernel, order), out_shape=(jax.Sha...  1.97 us
  transfers between devices with their start and end apart: 15, of which 7 were waited for; matrix products, arithmetic and copies ran while one was open for 0% of the time, Pallas kernels for 2%

profile of v12, /device:TPU:0, one launch (start us, length us, event | category | flops | bytes accessed | tf_op | source)
XLA Modules:
  0.0 44.5 jit_solution(13123214446000901823)
XLA Ops:
  0.6 0.0 copy-start
  0.6 8.4 %correlate.1.refs_0_ = bf16[32,1920]{1,0:T(8,128)(2,1)S(1)} custom-call(bf16[72,128]{1,0:T(8,128)(2,1)} %bitcast.9, bf16[68,128]{1,0:T(8,128)(2,1)} %bitcast.10, bf16[66,128]{1,0:T(8,128)(2,1)} %bitcast.11, bf16[65,128]{1,0:T(8,128)(2,1)} %bitcast.12, bf16[4,32,8192]{2,1,0:T(8,128)(2,1)} %refs_4_.1), custom_call_target="tpu_custom_call" | custom-call | flops 1006632960 | bytes 2097152 | tf_op jit(solution)/shard_map/correlate/pallas_call | solution.py:153
  9.1 3.1 %collective-permute-start.5 = (bf16[32,1920]{1,0:T(8,128)(2,1)S(1)}, bf16[32,1920]{1,0:T(8,128)(2,1)S(1)}, u32[]{:S(2)}, u32[]{:S(2)}) collective-permute-start(bf16[32,1920]{1,0:T(8,128)(2,1)S(1)} %correlate.1.refs_0_), channel_id=1, source_target_pairs={{0,4},{1,5},{2,6},{3,7},{4,0},{5,1},{6,2},{7,3},{8,12},{9,13},{10,... | collective-permute-start | bytes 368648 | tf_op jit(solution)/shard_map/ppermute | solution.py:179
  12.2 2.6 %collective-permute-start.3 = (bf16[32,1920]{1,0:T(8,128)(2,1)S(1)}, bf16[32,1920]{1,0:T(8,128)(2,1)S(1)}, u32[]{:S(2)}, u32[]{:S(2)}) collective-permute-start(bf16[32,1920]{1,0:T(8,128)(2,1)S(1)} %correlate.1.refs_0_), channel_id=1, source_target_pairs={{0,8},{1,9},{2,10},{3,11},{4,12},{5,13},{6,14},{7,15},{8,0},{9,1},... | collective-permute-start | bytes 368648 | tf_op jit(solution)/shard_map/ppermute | solution.py:179
  14.8 1.5 %collective-permute-start.1 = (bf16[32,1920]{1,0:T(8,128)(2,1)S(1)}, bf16[32,1920]{1,0:T(8,128)(2,1)S(1)}, u32[]{:S(2)}, u32[]{:S(2)}) collective-permute-start(bf16[32,1920]{1,0:T(8,128)(2,1)S(1)} %correlate.1.refs_0_), channel_id=1, source_target_pairs={{0,2},{1,3},{2,0},{3,1},{4,6},{5,7},{6,4},{7,5},{8,10},{9,11},{10,... | collective-permute-start | bytes 368648 | tf_op jit(solution)/shard_map/ppermute | solution.py:179
  16.3 0.0 copy-done
  16.3 0.7 %arrange.1.coeffs_ref = bf16[4,256,512]{2,1,0:T(8,128)(2,1)S(1)} custom-call(s32[1]{0:T(128)} %bitcast.4.offset_ref, bf16[4,256,512]{2,1,0:T(8,128)(2,1)S(1)} %copy-done), custom_call_target="tpu_custom_call" | custom-call | flops 536870912 | bytes 2097152 | tf_op jit(solution)/shard_map/arrange/pallas_call | solution.py:224
  17.0 0.1 collective-permute-start
  17.1 0.0 collective-permute-done.5.refs_6_
  17.1 1.7 %collective-permute-start.7 = (bf16[32,1920]{1,0:T(8,128)(2,1)S(1)}, bf16[32,1920]{1,0:T(8,128)(2,1)S(1)}, u32[]{:S(2)}, u32[]{:S(2)}) collective-permute-start(bf16[32,1920]{1,0:T(8,128)(2,1)S(1)} %collective-permute-done.5.refs_6_), channel_id=1, source_target_pairs={{0,2},{1,3},{2,0},{3,1},{4,6},{5,7},{6,4},{7,5},{8,10},{9,11},{10,... | collective-permute-start | bytes 368648 | tf_op jit(solution)/shard_map/ppermute | solution.py:179
  18.8 0.0 collective-permute-start.6
  18.8 1.7 %collective-permute-done.3.refs_4_ = bf16[32,1920]{1,0:T(8,128)(2,1)S(1)} collective-permute-done((bf16[32,1920]{1,0:T(8,128)(2,1)S(1)}, bf16[32,1920]{1,0:T(8,128)(2,1)S(1)}, u32[]{:S(2)}, u32[]{:S(2)}) %collective-permute-start.3) | collective-permute-done | bytes 122912 | tf_op jit(solution)/shard_map/ppermute | solution.py:179
  20.6 1.5 %collective-permute-start.13 = (bf16[32,1920]{1,0:T(8,128)(2,1)S(1)}, bf16[32,1920]{1,0:T(8,128)(2,1)S(1)}, u32[]{:S(2)}, u32[]{:S(2)}) collective-permute-start(bf16[32,1920]{1,0:T(8,128)(2,1)S(1)} %collective-permute-done.3.refs_4_), channel_id=1, source_target_pairs={{0,2},{1,3},{2,0},{3,1},{4,6},{5,7},{6,4},{7,5},{8,10},{9,11},{10,... | collective-permute-start | bytes 368648 | tf_op jit(solution)/shard_map/ppermute | solution.py:179
  22.1 0.0 collective-permute-done.1.refs_2_
  22.1 0.4 collective-permute-start.11
  22.5 0.0 collective-permute-done.refs_1_
  22.5 1.6 %collective-permute-start.9 = (bf16[32,1920]{1,0:T(8,128)(2,1)S(1)}, bf16[32,1920]{1,0:T(8,128)(2,1)S(1)}, u32[]{:S(2)}, u32[]{:S(2)}) collective-permute-start(bf16[32,1920]{1,0:T(8,128)(2,1)S(1)} %collective-permute-done.3.refs_4_), channel_id=1, source_target_pairs={{0,4},{1,5},{2,6},{3,7},{4,0},{5,1},{6,2},{7,3},{8,12},{9,13},{10,... | collective-permute-start | bytes 368648 | tf_op jit(solution)/shard_map/ppermute | solution.py:179
  24.0 0.6 %collective-permute-done.7.refs_8_ = bf16[32,1920]{1,0:T(8,128)(2,1)S(1)} collective-permute-done((bf16[32,1920]{1,0:T(8,128)(2,1)S(1)}, bf16[32,1920]{1,0:T(8,128)(2,1)S(1)}, u32[]{:S(2)}, u32[]{:S(2)}) %collective-permute-start.7) | collective-permute-done | bytes 122912 | tf_op jit(solution)/shard_map/ppermute | solution.py:179
  24.6 0.0 collective-permute-start.4
  24.6 0.0 collective-permute-done.6.refs_7_
  24.6 0.5 %collective-permute-start.2 = (bf16[32,1920]{1,0:T(8,128)(2,1)S(1)}, bf16[32,1920]{1,0:T(8,128)(2,1)S(1)}, u32[]{:S(2)}, u32[]{:S(2)}) collective-permute-start(bf16[32,1920]{1,0:T(8,128)(2,1)S(1)} %collective-permute-done.1.refs_2_), channel_id=1, source_target_pairs={{0,1},{1,0},{2,3},{3,2},{4,5},{5,4},{6,7},{7,6},{8,9},{9,8},{10,11... | collective-permute-start | bytes 368648 | tf_op jit(solution)/shard_map/ppermute | solution.py:179
  25.1 3.0 %collective-permute-done.13.refs_14_ = bf16[32,1920]{1,0:T(8,128)(2,1)S(1)} collective-permute-done((bf16[32,1920]{1,0:T(8,128)(2,1)S(1)}, bf16[32,1920]{1,0:T(8,128)(2,1)S(1)}, u32[]{:S(2)}, u32[]{:S(2)}) %collective-permute-start.13) | collective-permute-done | bytes 122912 | tf_op jit(solution)/shard_map/ppermute | solution.py:179
  28.1 0.0 collective-permute-start.8
  28.1 0.0 collective-permute-done.11.refs_12_
  28.1 0.5 %collective-permute-start.14 = (bf16[32,1920]{1,0:T(8,128)(2,1)S(1)}, bf16[32,1920]{1,0:T(8,128)(2,1)S(1)}, u32[]{:S(2)}, u32[]{:S(2)}) collective-permute-start(bf16[32,1920]{1,0:T(8,128)(2,1)S(1)} %collective-permute-done.13.refs_14_), channel_id=1, source_target_pairs={{0,1},{1,0},{2,3},{3,2},{4,5},{5,4},{6,7},{7,6},{8,9},{9,8},{10,11... | collective-permute-start | bytes 368648 | tf_op jit(solution)/shard_map/ppermute | solution.py:179
  28.6 0.0 collective-permute-done.9.refs_10_
  28.6 0.1 collective-permute-start.12
  28.7 0.0 collective-permute-done.4.refs_5_
  28.7 0.4 collective-permute-start.10
  29.1 0.0 collective-permute-done.2.refs_3_
  29.2 0.3 collective-permute-done.8.refs_9_
  29.5 0.2 collective-permute-done.14.refs_15_
  29.6 0.3 collective-permute-done.12.refs_13_
  30.0 0.2 collective-permute-done.10.refs_11_
  30.1 2.0 %reconstruct.1 = (bf16[256,1024]{1,0:T(8,128)(2,1)}, f32[1,1024]{1,0:T(1,128)S(1)}) custom-call(bf16[4,256,512]{2,1,0:T(8,128)(2,1)S(1)} %arrange.1.coeffs_ref, bf16[32,1920]{1,0:T(8,128)(2,1)S(1)} %correlate.1.refs_0_, bf16[32,1920]{1,0:T(8,128)(2,1)S(1)} %collective-permute-done.refs_1_, bf16[32,1920]{1,0:T(8,128)(2,1)S(1)} %collective-permute-done.1.refs_2_, ...), custom_call_target="tpu_custom_call" | custom-call | tf_op jit(solution)/shard_map/reconstruct/pallas_call | solution.py:283
  32.1 11.7 %all_to_all.5 = f32[16,8,128]{2,1,0:T(8,128)S(1)} all-to-all(f32[16,8,128]{2,1,0:T(8,128)S(1)} %broadcast_in_dim.8), channel_id=1, replica_groups=mesh['bank'=2,'tmpl'=16] {'tmpl'}, dimensions={0} | all-to-all | bytes 131072 | tf_op jit(solution)/shard_map/all_to_all | solution.py:208
  43.8 0.6 %reduce_max.9 = f32[8,128]{1,0:T(8,128)} reduce(f32[16,8,128]{2,1,0:T(8,128)S(1)} %all_to_all.5, f32[]{:T(128)} %constant.2.clone.1), dimensions={0}, to_apply=%region_0.0 | reduce | flops 15360 | bytes 69636 | tf_op jit(solution)/shard_map/reduce_max | solution.py:209
  (1 shorter events, 0.0 us)
Async XLA Ops:
  0.6 15.7 %copy-start = (bf16[4,256,512]{2,1,0:T(8,128)(2,1)S(1)}, bf16[4,256,512]{2,1,0:T(8,128)(2,1)}, u32[]{:S(2)}) copy-start(bf16[4,256,512]{2,1,0:T(8,128)(2,1)} %coeffs_ref.1) | copy-start | bytes 3145732
  9.1 8.0 %collective-permute-start.5 = (bf16[32,1920]{1,0:T(8,128)(2,1)S(1)}, bf16[32,1920]{1,0:T(8,128)(2,1)S(1)}, u32[]{:S(2)}, u32[]{:S(2)}) collective-permute-start(bf16[32,1920]{1,0:T(8,128)(2,1)S(1)} %correlate.1.refs_0_), channel_id=1, source_target_pairs={{0,4},{1,5},{2,6},{3,7},{4,0},{5,1},{6,2},{7,3},{8,12},{9,13},{10,... | collective-permute-start | bytes 368648 | tf_op jit(solution)/shard_map/ppermute | solution.py:179
  12.2 8.4 %collective-permute-start.3 = (bf16[32,1920]{1,0:T(8,128)(2,1)S(1)}, bf16[32,1920]{1,0:T(8,128)(2,1)S(1)}, u32[]{:S(2)}, u32[]{:S(2)}) collective-permute-start(bf16[32,1920]{1,0:T(8,128)(2,1)S(1)} %correlate.1.refs_0_), channel_id=1, source_target_pairs={{0,8},{1,9},{2,10},{3,11},{4,12},{5,13},{6,14},{7,15},{8,0},{9,1},... | collective-permute-start | bytes 368648 | tf_op jit(solution)/shard_map/ppermute | solution.py:179
  14.8 7.3 %collective-permute-start.1 = (bf16[32,1920]{1,0:T(8,128)(2,1)S(1)}, bf16[32,1920]{1,0:T(8,128)(2,1)S(1)}, u32[]{:S(2)}, u32[]{:S(2)}) collective-permute-start(bf16[32,1920]{1,0:T(8,128)(2,1)S(1)} %correlate.1.refs_0_), channel_id=1, source_target_pairs={{0,2},{1,3},{2,0},{3,1},{4,6},{5,7},{6,4},{7,5},{8,10},{9,11},{10,... | collective-permute-start | bytes 368648 | tf_op jit(solution)/shard_map/ppermute | solution.py:179
  17.0 5.4 %collective-permute-start = (bf16[32,1920]{1,0:T(8,128)(2,1)S(1)}, bf16[32,1920]{1,0:T(8,128)(2,1)S(1)}, u32[]{:S(2)}, u32[]{:S(2)}) collective-permute-start(bf16[32,1920]{1,0:T(8,128)(2,1)S(1)} %correlate.1.refs_0_), channel_id=1, source_target_pairs={{0,1},{1,0},{2,3},{3,2},{4,5},{5,4},{6,7},{7,6},{8,9},{9,8},{10,11... | collective-permute-start | bytes 368648 | tf_op jit(solution)/shard_map/ppermute | solution.py:179
  17.1 7.5 %collective-permute-start.7 = (bf16[32,1920]{1,0:T(8,128)(2,1)S(1)}, bf16[32,1920]{1,0:T(8,128)(2,1)S(1)}, u32[]{:S(2)}, u32[]{:S(2)}) collective-permute-start(bf16[32,1920]{1,0:T(8,128)(2,1)S(1)} %collective-permute-done.5.refs_6_), channel_id=1, source_target_pairs={{0,2},{1,3},{2,0},{3,1},{4,6},{5,7},{6,4},{7,5},{8,10},{9,11},{10,... | collective-permute-start | bytes 368648 | tf_op jit(solution)/shard_map/ppermute | solution.py:179
  18.8 5.8 %collective-permute-start.6 = (bf16[32,1920]{1,0:T(8,128)(2,1)S(1)}, bf16[32,1920]{1,0:T(8,128)(2,1)S(1)}, u32[]{:S(2)}, u32[]{:S(2)}) collective-permute-start(bf16[32,1920]{1,0:T(8,128)(2,1)S(1)} %collective-permute-done.5.refs_6_), channel_id=1, source_target_pairs={{0,1},{1,0},{2,3},{3,2},{4,5},{5,4},{6,7},{7,6},{8,9},{9,8},{10,11... | collective-permute-start | bytes 368648 | tf_op jit(solution)/shard_map/ppermute | solution.py:179
  20.6 7.6 %collective-permute-start.13 = (bf16[32,1920]{1,0:T(8,128)(2,1)S(1)}, bf16[32,1920]{1,0:T(8,128)(2,1)S(1)}, u32[]{:S(2)}, u32[]{:S(2)}) collective-permute-start(bf16[32,1920]{1,0:T(8,128)(2,1)S(1)} %collective-permute-done.3.refs_4_), channel_id=1, source_target_pairs={{0,2},{1,3},{2,0},{3,1},{4,6},{5,7},{6,4},{7,5},{8,10},{9,11},{10,... | collective-permute-start | bytes 368648 | tf_op jit(solution)/shard_map/ppermute | solution.py:179
  22.1 6.0 %collective-permute-start.11 = (bf16[32,1920]{1,0:T(8,128)(2,1)S(1)}, bf16[32,1920]{1,0:T(8,128)(2,1)S(1)}, u32[]{:S(2)}, u32[]{:S(2)}) collective-permute-start(bf16[32,1920]{1,0:T(8,128)(2,1)S(1)} %collective-permute-done.3.refs_4_), channel_id=1, source_target_pairs={{0,6},{1,7},{2,4},{3,5},{4,2},{5,3},{6,0},{7,1},{8,14},{9,15},{10,... | collective-permute-start | bytes 368648 | tf_op jit(solution)/shard_map/ppermute | solution.py:179
  22.5 6.2 %collective-permute-start.9 = (bf16[32,1920]{1,0:T(8,128)(2,1)S(1)}, bf16[32,1920]{1,0:T(8,128)(2,1)S(1)}, u32[]{:S(2)}, u32[]{:S(2)}) collective-permute-start(bf16[32,1920]{1,0:T(8,128)(2,1)S(1)} %collective-permute-done.3.refs_4_), channel_id=1, source_target_pairs={{0,4},{1,5},{2,6},{3,7},{4,0},{5,1},{6,2},{7,3},{8,12},{9,13},{10,... | collective-permute-start | bytes 368648 | tf_op jit(solution)/shard_map/ppermute | solution.py:179
  24.6 4.1 %collective-permute-start.4 = (bf16[32,1920]{1,0:T(8,128)(2,1)S(1)}, bf16[32,1920]{1,0:T(8,128)(2,1)S(1)}, u32[]{:S(2)}, u32[]{:S(2)}) collective-permute-start(bf16[32,1920]{1,0:T(8,128)(2,1)S(1)} %collective-permute-done.3.refs_4_), channel_id=1, source_target_pairs={{0,1},{1,0},{2,3},{3,2},{4,5},{5,4},{6,7},{7,6},{8,9},{9,8},{10,11... | collective-permute-start | bytes 368648 | tf_op jit(solution)/shard_map/ppermute | solution.py:179
  24.6 4.5 %collective-permute-start.2 = (bf16[32,1920]{1,0:T(8,128)(2,1)S(1)}, bf16[32,1920]{1,0:T(8,128)(2,1)S(1)}, u32[]{:S(2)}, u32[]{:S(2)}) collective-permute-start(bf16[32,1920]{1,0:T(8,128)(2,1)S(1)} %collective-permute-done.1.refs_2_), channel_id=1, source_target_pairs={{0,1},{1,0},{2,3},{3,2},{4,5},{5,4},{6,7},{7,6},{8,9},{9,8},{10,11... | collective-permute-start | bytes 368648 | tf_op jit(solution)/shard_map/ppermute | solution.py:179
  28.1 1.3 %collective-permute-start.8 = (bf16[32,1920]{1,0:T(8,128)(2,1)S(1)}, bf16[32,1920]{1,0:T(8,128)(2,1)S(1)}, u32[]{:S(2)}, u32[]{:S(2)}) collective-permute-start(bf16[32,1920]{1,0:T(8,128)(2,1)S(1)} %collective-permute-done.7.refs_8_), channel_id=1, source_target_pairs={{0,1},{1,0},{2,3},{3,2},{4,5},{5,4},{6,7},{7,6},{8,9},{9,8},{10,11... | collective-permute-start | bytes 368648 | tf_op jit(solution)/shard_map/ppermute | solution.py:179
  28.1 1.5 %collective-permute-start.14 = (bf16[32,1920]{1,0:T(8,128)(2,1)S(1)}, bf16[32,1920]{1,0:T(8,128)(2,1)S(1)}, u32[]{:S(2)}, u32[]{:S(2)}) collective-permute-start(bf16[32,1920]{1,0:T(8,128)(2,1)S(1)} %collective-permute-done.13.refs_14_), channel_id=1, source_target_pairs={{0,1},{1,0},{2,3},{3,2},{4,5},{5,4},{6,7},{7,6},{8,9},{9,8},{10,11... | collective-permute-start | bytes 368648 | tf_op jit(solution)/shard_map/ppermute | solution.py:179
  28.6 1.3 %collective-permute-start.12 = (bf16[32,1920]{1,0:T(8,128)(2,1)S(1)}, bf16[32,1920]{1,0:T(8,128)(2,1)S(1)}, u32[]{:S(2)}, u32[]{:S(2)}) collective-permute-start(bf16[32,1920]{1,0:T(8,128)(2,1)S(1)} %collective-permute-done.11.refs_12_), channel_id=1, source_target_pairs={{0,1},{1,0},{2,3},{3,2},{4,5},{5,4},{6,7},{7,6},{8,9},{9,8},{10,11... | collective-permute-start | bytes 368648 | tf_op jit(solution)/shard_map/ppermute | solution.py:179
  28.7 1.4 %collective-permute-start.10 = (bf16[32,1920]{1,0:T(8,128)(2,1)S(1)}, bf16[32,1920]{1,0:T(8,128)(2,1)S(1)}, u32[]{:S(2)}, u32[]{:S(2)}) collective-permute-start(bf16[32,1920]{1,0:T(8,128)(2,1)S(1)} %collective-permute-done.9.refs_10_), channel_id=1, source_target_pairs={{0,1},{1,0},{2,3},{3,2},{4,5},{5,4},{6,7},{7,6},{8,9},{9,8},{10,11... | collective-permute-start | bytes 368648 | tf_op jit(solution)/shard_map/ppermute | solution.py:179

commit v13 on v10

--- a/solution.py
+++ b/solution.py
@@ -8,10 +8,10 @@
 from jax.sharding import PartitionSpec as P
 
 LANE = 128
-CHUNK = 16
+CHUNK = 32
 SUB = 16
 ROWS = 8
-ROLLS = 4
+ROLLS = 2
 TIED = 1
 HANDED = (0, 1, 2, 3, 8, 9, 4, 5, 6, 7, 12, 13, 14, 15, 10, 11)
 SUB = 16

time: 43.5 us -> 43.4 us (level)
  no operation moved by 1% of the time
where the time goes in v13:
time: 43.4 us; the launch traced here: 43.2 us
  starting transfers between devices  14 us (32%)
  blocking collectives  11.7 us (27%)
  Pallas kernels  9.92 us (23%)
  waiting for transfers between devices  6.27 us (14%)
  between operations  0.69 us (2%)
  other arithmetic  0.61 us (1%)
    ppermute x15, starting transfers between devices, exchange(): return lax.ppermute(block, 'tmpl', [(i, i ^ distance) for i in range(size)])  14 us
    all_to_all x1, blocking collectives, maximum_over_group(): lax.all_to_all(copies, 'tmpl', split_axis=0, concat_axis=0, tiled=True)  11.7 us
    pallas_call x1, Pallas kernels, correlate(): pl.pallas_call(correlate_kernel, out_shape=pltpu.VMEM((padded, samples),...  7.22 us
    ppermute x15, waiting for transfers between devices, exchange(): return lax.ppermute(block, 'tmpl', [(i, i ^ distance) for i in range(size)])  6.27 us
    pallas_call x1, Pallas kernels, reconstruct(): pl.pallas_call(functools.partial(recon_kernel, order), out_shape=(jax.Sha...  1.97 us
  transfers between devices with their start and end apart: 15, of which 7 were waited for; matrix products, arithmetic and copies ran while one was open for 0% of the time, Pallas kernels for 2%

profile of v13, /device:TPU:0, one launch (start us, length us, event | category | flops | bytes accessed | tf_op | source)
XLA Modules:
  0.0 43.2 jit_solution(12808771170946073622)
XLA Ops:
  0.6 0.0 copy-start
  0.6 7.2 %correlate.1.refs_0_ = bf16[32,1920]{1,0:T(8,128)(2,1)S(1)} custom-call(bf16[72,128]{1,0:T(8,128)(2,1)} %bitcast.9, bf16[68,128]{1,0:T(8,128)(2,1)} %bitcast.10, bf16[66,128]{1,0:T(8,128)(2,1)} %bitcast.11, bf16[65,128]{1,0:T(8,128)(2,1)} %bitcast.12, bf16[4,32,8192]{2,1,0:T(8,128)(2,1)} %refs_4_.1), custom_call_target="tpu_custom_call" | custom-call | flops 1006632960 | bytes 2097152 | tf_op jit(solution)/shard_map/correlate/pallas_call | solution.py:168
  7.9 3.1 %collective-permute-start.5 = (bf16[32,1920]{1,0:T(8,128)(2,1)S(1)}, bf16[32,1920]{1,0:T(8,128)(2,1)S(1)}, u32[]{:S(2)}, u32[]{:S(2)}) collective-permute-start(bf16[32,1920]{1,0:T(8,128)(2,1)S(1)} %correlate.1.refs_0_), channel_id=1, source_target_pairs={{0,4},{1,5},{2,6},{3,7},{4,0},{5,1},{6,2},{7,3},{8,12},{9,13},{10,... | collective-permute-start | bytes 368648 | tf_op jit(solution)/shard_map/ppermute | solution.py:194
  11.0 2.6 %collective-permute-start.3 = (bf16[32,1920]{1,0:T(8,128)(2,1)S(1)}, bf16[32,1920]{1,0:T(8,128)(2,1)S(1)}, u32[]{:S(2)}, u32[]{:S(2)}) collective-permute-start(bf16[32,1920]{1,0:T(8,128)(2,1)S(1)} %correlate.1.refs_0_), channel_id=1, source_target_pairs={{0,8},{1,9},{2,10},{3,11},{4,12},{5,13},{6,14},{7,15},{8,0},{9,1},... | collective-permute-start | bytes 368648 | tf_op jit(solution)/shard_map/ppermute | solution.py:194
  13.6 1.5 %collective-permute-start.1 = (bf16[32,1920]{1,0:T(8,128)(2,1)S(1)}, bf16[32,1920]{1,0:T(8,128)(2,1)S(1)}, u32[]{:S(2)}, u32[]{:S(2)}) collective-permute-start(bf16[32,1920]{1,0:T(8,128)(2,1)S(1)} %correlate.1.refs_0_), channel_id=1, source_target_pairs={{0,2},{1,3},{2,0},{3,1},{4,6},{5,7},{6,4},{7,5},{8,10},{9,11},{10,... | collective-permute-start | bytes 368648 | tf_op jit(solution)/shard_map/ppermute | solution.py:194
  15.1 0.0 copy-done
  15.1 0.7 %arrange.1.coeffs_ref = bf16[4,256,512]{2,1,0:T(8,128)(2,1)S(1)} custom-call(s32[1]{0:T(128)} %bitcast.4.offset_ref, bf16[4,256,512]{2,1,0:T(8,128)(2,1)S(1)} %copy-done), custom_call_target="tpu_custom_call" | custom-call | flops 536870912 | bytes 2097152 | tf_op jit(solution)/shard_map/arrange/pallas_call | solution.py:239
  15.8 0.1 collective-permute-start
  15.9 0.0 collective-permute-done.5.refs_6_
  15.9 1.7 %collective-permute-start.7 = (bf16[32,1920]{1,0:T(8,128)(2,1)S(1)}, bf16[32,1920]{1,0:T(8,128)(2,1)S(1)}, u32[]{:S(2)}, u32[]{:S(2)}) collective-permute-start(bf16[32,1920]{1,0:T(8,128)(2,1)S(1)} %collective-permute-done.5.refs_6_), channel_id=1, source_target_pairs={{0,2},{1,3},{2,0},{3,1},{4,6},{5,7},{6,4},{7,5},{8,10},{9,11},{10,... | collective-permute-start | bytes 368648 | tf_op jit(solution)/shard_map/ppermute | solution.py:194
  17.6 0.0 collective-permute-start.6
  17.6 1.7 %collective-permute-done.3.refs_4_ = bf16[32,1920]{1,0:T(8,128)(2,1)S(1)} collective-permute-done((bf16[32,1920]{1,0:T(8,128)(2,1)S(1)}, bf16[32,1920]{1,0:T(8,128)(2,1)S(1)}, u32[]{:S(2)}, u32[]{:S(2)}) %collective-permute-start.3) | collective-permute-done | bytes 122912 | tf_op jit(solution)/shard_map/ppermute | solution.py:194
  19.3 1.5 %collective-permute-start.13 = (bf16[32,1920]{1,0:T(8,128)(2,1)S(1)}, bf16[32,1920]{1,0:T(8,128)(2,1)S(1)}, u32[]{:S(2)}, u32[]{:S(2)}) collective-permute-start(bf16[32,1920]{1,0:T(8,128)(2,1)S(1)} %collective-permute-done.3.refs_4_), channel_id=1, source_target_pairs={{0,2},{1,3},{2,0},{3,1},{4,6},{5,7},{6,4},{7,5},{8,10},{9,11},{10,... | collective-permute-start | bytes 368648 | tf_op jit(solution)/shard_map/ppermute | solution.py:194
  20.8 0.0 collective-permute-done.1.refs_2_
  20.8 0.4 collective-permute-start.11
  21.2 0.0 collective-permute-done.refs_1_
  21.2 1.6 %collective-permute-start.9 = (bf16[32,1920]{1,0:T(8,128)(2,1)S(1)}, bf16[32,1920]{1,0:T(8,128)(2,1)S(1)}, u32[]{:S(2)}, u32[]{:S(2)}) collective-permute-start(bf16[32,1920]{1,0:T(8,128)(2,1)S(1)} %collective-permute-done.3.refs_4_), channel_id=1, source_target_pairs={{0,4},{1,5},{2,6},{3,7},{4,0},{5,1},{6,2},{7,3},{8,12},{9,13},{10,... | collective-permute-start | bytes 368648 | tf_op jit(solution)/shard_map/ppermute | solution.py:194
  22.8 0.6 %collective-permute-done.7.refs_8_ = bf16[32,1920]{1,0:T(8,128)(2,1)S(1)} collective-permute-done((bf16[32,1920]{1,0:T(8,128)(2,1)S(1)}, bf16[32,1920]{1,0:T(8,128)(2,1)S(1)}, u32[]{:S(2)}, u32[]{:S(2)}) %collective-permute-start.7) | collective-permute-done | bytes 122912 | tf_op jit(solution)/shard_map/ppermute | solution.py:194
  23.4 0.0 collective-permute-start.4
  23.4 0.0 collective-permute-done.6.refs_7_
  23.4 0.5 %collective-permute-start.2 = (bf16[32,1920]{1,0:T(8,128)(2,1)S(1)}, bf16[32,1920]{1,0:T(8,128)(2,1)S(1)}, u32[]{:S(2)}, u32[]{:S(2)}) collective-permute-start(bf16[32,1920]{1,0:T(8,128)(2,1)S(1)} %collective-permute-done.1.refs_2_), channel_id=1, source_target_pairs={{0,1},{1,0},{2,3},{3,2},{4,5},{5,4},{6,7},{7,6},{8,9},{9,8},{10,11... | collective-permute-start | bytes 368648 | tf_op jit(solution)/shard_map/ppermute | solution.py:194
  23.9 3.0 %collective-permute-done.13.refs_14_ = bf16[32,1920]{1,0:T(8,128)(2,1)S(1)} collective-permute-done((bf16[32,1920]{1,0:T(8,128)(2,1)S(1)}, bf16[32,1920]{1,0:T(8,128)(2,1)S(1)}, u32[]{:S(2)}, u32[]{:S(2)}) %collective-permute-start.13) | collective-permute-done | bytes 122912 | tf_op jit(solution)/shard_map/ppermute | solution.py:194
  26.9 0.0 collective-permute-start.8
  26.9 0.0 collective-permute-done.11.refs_12_
  26.9 0.5 %collective-permute-start.14 = (bf16[32,1920]{1,0:T(8,128)(2,1)S(1)}, bf16[32,1920]{1,0:T(8,128)(2,1)S(1)}, u32[]{:S(2)}, u32[]{:S(2)}) collective-permute-start(bf16[32,1920]{1,0:T(8,128)(2,1)S(1)} %collective-permute-done.13.refs_14_), channel_id=1, source_target_pairs={{0,1},{1,0},{2,3},{3,2},{4,5},{5,4},{6,7},{7,6},{8,9},{9,8},{10,11... | collective-permute-start | bytes 368648 | tf_op jit(solution)/shard_map/ppermute | solution.py:194
  27.4 0.0 collective-permute-done.9.refs_10_
  27.4 0.1 collective-permute-start.12
  27.5 0.0 collective-permute-done.4.refs_5_
  27.5 0.4 %collective-permute-start.10 = (bf16[32,1920]{1,0:T(8,128)(2,1)S(1)}, bf16[32,1920]{1,0:T(8,128)(2,1)S(1)}, u32[]{:S(2)}, u32[]{:S(2)}) collective-permute-start(bf16[32,1920]{1,0:T(8,128)(2,1)S(1)} %collective-permute-done.9.refs_10_), channel_id=1, source_target_pairs={{0,1},{1,0},{2,3},{3,2},{4,5},{5,4},{6,7},{7,6},{8,9},{9,8},{10,11... | collective-permute-start | bytes 368648 | tf_op jit(solution)/shard_map/ppermute | solution.py:194
  27.9 0.0 collective-permute-done.2.refs_3_
  27.9 0.3 collective-permute-done.8.refs_9_
  28.2 0.2 collective-permute-done.14.refs_15_
  28.4 0.3 collective-permute-done.12.refs_13_
  28.7 0.2 collective-permute-done.10.refs_11_
  28.9 2.0 %reconstruct.1 = (bf16[256,1024]{1,0:T(8,128)(2,1)}, f32[1,1024]{1,0:T(1,128)S(1)}) custom-call(bf16[4,256,512]{2,1,0:T(8,128)(2,1)S(1)} %arrange.1.coeffs_ref, bf16[32,1920]{1,0:T(8,128)(2,1)S(1)} %correlate.1.refs_0_, bf16[32,1920]{1,0:T(8,128)(2,1)S(1)} %collective-permute-done.refs_1_, bf16[32,1920]{1,0:T(8,128)(2,1)S(1)} %collective-permute-done.1.refs_2_, ...), custom_call_target="tpu_custom_call" | custom-call | tf_op jit(solution)/shard_map/reconstruct/pallas_call | solution.py:298
  30.9 11.7 %all_to_all.5 = f32[16,8,128]{2,1,0:T(8,128)S(1)} all-to-all(f32[16,8,128]{2,1,0:T(8,128)S(1)} %broadcast_in_dim.8), channel_id=1, replica_groups=mesh['bank'=2,'tmpl'=16] {'tmpl'}, dimensions={0} | all-to-all | bytes 131072 | tf_op jit(solution)/shard_map/all_to_all | solution.py:223
  42.6 0.6 %reduce_max.9 = f32[8,128]{1,0:T(8,128)} reduce(f32[16,8,128]{2,1,0:T(8,128)S(1)} %all_to_all.5, f32[]{:T(128)} %constant.2.clone.1), dimensions={0}, to_apply=%region_0.0 | reduce | flops 15360 | bytes 69636 | tf_op jit(solution)/shard_map/reduce_max | solution.py:224
  (1 shorter events, 0.0 us)
Async XLA Ops:
  0.6 14.4 %copy-start = (bf16[4,256,512]{2,1,0:T(8,128)(2,1)S(1)}, bf16[4,256,512]{2,1,0:T(8,128)(2,1)}, u32[]{:S(2)}) copy-start(bf16[4,256,512]{2,1,0:T(8,128)(2,1)} %coeffs_ref.1) | copy-start | bytes 3145732
  7.9 8.0 %collective-permute-start.5 = (bf16[32,1920]{1,0:T(8,128)(2,1)S(1)}, bf16[32,1920]{1,0:T(8,128)(2,1)S(1)}, u32[]{:S(2)}, u32[]{:S(2)}) collective-permute-start(bf16[32,1920]{1,0:T(8,128)(2,1)S(1)} %correlate.1.refs_0_), channel_id=1, source_target_pairs={{0,4},{1,5},{2,6},{3,7},{4,0},{5,1},{6,2},{7,3},{8,12},{9,13},{10,... | collective-permute-start | bytes 368648 | tf_op jit(solution)/shard_map/ppermute | solution.py:194
  11.0 8.4 %collective-permute-start.3 = (bf16[32,1920]{1,0:T(8,128)(2,1)S(1)}, bf16[32,1920]{1,0:T(8,128)(2,1)S(1)}, u32[]{:S(2)}, u32[]{:S(2)}) collective-permute-start(bf16[32,1920]{1,0:T(8,128)(2,1)S(1)} %correlate.1.refs_0_), channel_id=1, source_target_pairs={{0,8},{1,9},{2,10},{3,11},{4,12},{5,13},{6,14},{7,15},{8,0},{9,1},... | collective-permute-start | bytes 368648 | tf_op jit(solution)/shard_map/ppermute | solution.py:194
  13.6 7.3 %collective-permute-start.1 = (bf16[32,1920]{1,0:T(8,128)(2,1)S(1)}, bf16[32,1920]{1,0:T(8,128)(2,1)S(1)}, u32[]{:S(2)}, u32[]{:S(2)}) collective-permute-start(bf16[32,1920]{1,0:T(8,128)(2,1)S(1)} %correlate.1.refs_0_), channel_id=1, source_target_pairs={{0,2},{1,3},{2,0},{3,1},{4,6},{5,7},{6,4},{7,5},{8,10},{9,11},{10,... | collective-permute-start | bytes 368648 | tf_op jit(solution)/shard_map/ppermute | solution.py:194
  15.8 5.4 %collective-permute-start = (bf16[32,1920]{1,0:T(8,128)(2,1)S(1)}, bf16[32,1920]{1,0:T(8,128)(2,1)S(1)}, u32[]{:S(2)}, u32[]{:S(2)}) collective-permute-start(bf16[32,1920]{1,0:T(8,128)(2,1)S(1)} %correlate.1.refs_0_), channel_id=1, source_target_pairs={{0,1},{1,0},{2,3},{3,2},{4,5},{5,4},{6,7},{7,6},{8,9},{9,8},{10,11... | collective-permute-start | bytes 368648 | tf_op jit(solution)/shard_map/ppermute | solution.py:194
  15.9 7.5 %collective-permute-start.7 = (bf16[32,1920]{1,0:T(8,128)(2,1)S(1)}, bf16[32,1920]{1,0:T(8,128)(2,1)S(1)}, u32[]{:S(2)}, u32[]{:S(2)}) collective-permute-start(bf16[32,1920]{1,0:T(8,128)(2,1)S(1)} %collective-permute-done.5.refs_6_), channel_id=1, source_target_pairs={{0,2},{1,3},{2,0},{3,1},{4,6},{5,7},{6,4},{7,5},{8,10},{9,11},{10,... | collective-permute-start | bytes 368648 | tf_op jit(solution)/shard_map/ppermute | solution.py:194
  17.6 5.8 %collective-permute-start.6 = (bf16[32,1920]{1,0:T(8,128)(2,1)S(1)}, bf16[32,1920]{1,0:T(8,128)(2,1)S(1)}, u32[]{:S(2)}, u32[]{:S(2)}) collective-permute-start(bf16[32,1920]{1,0:T(8,128)(2,1)S(1)} %collective-permute-done.5.refs_6_), channel_id=1, source_target_pairs={{0,1},{1,0},{2,3},{3,2},{4,5},{5,4},{6,7},{7,6},{8,9},{9,8},{10,11... | collective-permute-start | bytes 368648 | tf_op jit(solution)/shard_map/ppermute | solution.py:194
  19.3 7.6 %collective-permute-start.13 = (bf16[32,1920]{1,0:T(8,128)(2,1)S(1)}, bf16[32,1920]{1,0:T(8,128)(2,1)S(1)}, u32[]{:S(2)}, u32[]{:S(2)}) collective-permute-start(bf16[32,1920]{1,0:T(8,128)(2,1)S(1)} %collective-permute-done.3.refs_4_), channel_id=1, source_target_pairs={{0,2},{1,3},{2,0},{3,1},{4,6},{5,7},{6,4},{7,5},{8,10},{9,11},{10,... | collective-permute-start | bytes 368648 | tf_op jit(solution)/shard_map/ppermute | solution.py:194
  20.8 6.0 %collective-permute-start.11 = (bf16[32,1920]{1,0:T(8,128)(2,1)S(1)}, bf16[32,1920]{1,0:T(8,128)(2,1)S(1)}, u32[]{:S(2)}, u32[]{:S(2)}) collective-permute-start(bf16[32,1920]{1,0:T(8,128)(2,1)S(1)} %collective-permute-done.3.refs_4_), channel_id=1, source_target_pairs={{0,6},{1,7},{2,4},{3,5},{4,2},{5,3},{6,0},{7,1},{8,14},{9,15},{10,... | collective-permute-start | bytes 368648 | tf_op jit(solution)/shard_map/ppermute | solution.py:194
  21.2 6.2 %collective-permute-start.9 = (bf16[32,1920]{1,0:T(8,128)(2,1)S(1)}, bf16[32,1920]{1,0:T(8,128)(2,1)S(1)}, u32[]{:S(2)}, u32[]{:S(2)}) collective-permute-start(bf16[32,1920]{1,0:T(8,128)(2,1)S(1)} %collective-permute-done.3.refs_4_), channel_id=1, source_target_pairs={{0,4},{1,5},{2,6},{3,7},{4,0},{5,1},{6,2},{7,3},{8,12},{9,13},{10,... | collective-permute-start | bytes 368648 | tf_op jit(solution)/shard_map/ppermute | solution.py:194
  23.4 4.1 %collective-permute-start.4 = (bf16[32,1920]{1,0:T(8,128)(2,1)S(1)}, bf16[32,1920]{1,0:T(8,128)(2,1)S(1)}, u32[]{:S(2)}, u32[]{:S(2)}) collective-permute-start(bf16[32,1920]{1,0:T(8,128)(2,1)S(1)} %collective-permute-done.3.refs_4_), channel_id=1, source_target_pairs={{0,1},{1,0},{2,3},{3,2},{4,5},{5,4},{6,7},{7,6},{8,9},{9,8},{10,11... | collective-permute-start | bytes 368648 | tf_op jit(solution)/shard_map/ppermute | solution.py:194
  23.4 4.5 %collective-permute-start.2 = (bf16[32,1920]{1,0:T(8,128)(2,1)S(1)}, bf16[32,1920]{1,0:T(8,128)(2,1)S(1)}, u32[]{:S(2)}, u32[]{:S(2)}) collective-permute-start(bf16[32,1920]{1,0:T(8,128)(2,1)S(1)} %collective-permute-done.1.refs_2_), channel_id=1, source_target_pairs={{0,1},{1,0},{2,3},{3,2},{4,5},{5,4},{6,7},{7,6},{8,9},{9,8},{10,11... | collective-permute-start | bytes 368648 | tf_op jit(solution)/shard_map/ppermute | solution.py:194
  26.9 1.3 %collective-permute-start.8 = (bf16[32,1920]{1,0:T(8,128)(2,1)S(1)}, bf16[32,1920]{1,0:T(8,128)(2,1)S(1)}, u32[]{:S(2)}, u32[]{:S(2)}) collective-permute-start(bf16[32,1920]{1,0:T(8,128)(2,1)S(1)} %collective-permute-done.7.refs_8_), channel_id=1, source_target_pairs={{0,1},{1,0},{2,3},{3,2},{4,5},{5,4},{6,7},{7,6},{8,9},{9,8},{10,11... | collective-permute-start | bytes 368648 | tf_op jit(solution)/shard_map/ppermute | solution.py:194
  26.9 1.5 %collective-permute-start.14 = (bf16[32,1920]{1,0:T(8,128)(2,1)S(1)}, bf16[32,1920]{1,0:T(8,128)(2,1)S(1)}, u32[]{:S(2)}, u32[]{:S(2)}) collective-permute-start(bf16[32,1920]{1,0:T(8,128)(2,1)S(1)} %collective-permute-done.13.refs_14_), channel_id=1, source_target_pairs={{0,1},{1,0},{2,3},{3,2},{4,5},{5,4},{6,7},{7,6},{8,9},{9,8},{10,11... | collective-permute-start | bytes 368648 | tf_op jit(solution)/shard_map/ppermute | solution.py:194
  27.4 1.3 %collective-permute-start.12 = (bf16[32,1920]{1,0:T(8,128)(2,1)S(1)}, bf16[32,1920]{1,0:T(8,128)(2,1)S(1)}, u32[]{:S(2)}, u32[]{:S(2)}) collective-permute-start(bf16[32,1920]{1,0:T(8,128)(2,1)S(1)} %collective-permute-done.11.refs_12_), channel_id=1, source_target_pairs={{0,1},{1,0},{2,3},{3,2},{4,5},{5,4},{6,7},{7,6},{8,9},{9,8},{10,11... | collective-permute-start | bytes 368648 | tf_op jit(solution)/shard_map/ppermute | solution.py:194
  27.5 1.4 %collective-permute-start.10 = (bf16[32,1920]{1,0:T(8,128)(2,1)S(1)}, bf16[32,1920]{1,0:T(8,128)(2,1)S(1)}, u32[]{:S(2)}, u32[]{:S(2)}) collective-permute-start(bf16[32,1920]{1,0:T(8,128)(2,1)S(1)} %collective-permute-done.9.refs_10_), channel_id=1, source_target_pairs={{0,1},{1,0},{2,3},{3,2},{4,5},{5,4},{6,7},{7,6},{8,9},{9,8},{10,11... | collective-permute-start | bytes 368648 | tf_op jit(solution)/shard_map/ppermute | solution.py:194

commit v14 on v13

--- a/solution.py
+++ b/solution.py
@@ -11,10 +11,9 @@
 CHUNK = 32
 SUB = 16
 ROWS = 8
-ROLLS = 2
+ROLLS = 4
 TIED = 1
 HANDED = (0, 1, 2, 3, 8, 9, 4, 5, 6, 7, 12, 13, 14, 15, 10, 11)
-SUB = 16
 
 
 def correlate_kernel(*refs):
@@ -118,36 +117,34 @@
             ]
             height += size
 
-    def build_all(frames, chunk):
-        for section in range(sections):
-            build(frames[section // 2], section, chunk)
-
-    def accumulate_all(frames, chunk):
-        for group, part in zip(groups, frames):
-            accumulate(part, group, chunk)
-
-    build_all(even_refs, 0)
-    for copy in copies:
-        copy.wait()
-    accumulate_all(even_refs, 0)
-    build_all(odd_refs, 1)
-
-    def step(number, carry):
-        accumulate_all(odd_refs, 2 * number - 1)
-        build_all(even_refs, 2 * number)
-        accumulate_all(even_refs, 2 * number)
-        build_all(odd_refs, 2 * number + 1)
-        return carry
-
-    lax.fori_loop(1, chunks // 2, step, 0)
-    accumulate_all(odd_refs, chunks - 1)
-    for group, frames in zip(groups, even_refs):
-        active = [section for section in group if blocks[section] > 1]
-        if active:
-            tiles = max(blocks[section] for section in active) - 1
-            for section in active:
-                build(frames, section, chunks, tiles)
-            accumulate(frames, active, chunks, tiles)
+    stages = [(number, chunk, CHUNK) for chunk in range(chunks) for number in range(len(groups))]
+    for number, group in enumerate(groups):
+        tiles = max(blocks[section] for section in group) - 1
+        if tiles:
+            stages.append((number, chunks, tiles))
+
+    def buffer(stage):
+        number, chunk, _ = stages[stage]
+        return (even_refs, odd_refs)[chunk % 2][number]
+
+    def active(stage):
+        number, chunk, _ = stages[stage]
+        return [s for s in groups[number] if chunk < chunks or blocks[s] > 1]
+
+    def build_stage(stage):
+        for section in active(stage):
+            build(buffer(stage), section, *stages[stage][1:])
+
+    arrived = set()
+    build_stage(0)
+    for stage in range(len(stages)):
+        for section in active(stage):
+            if section not in arrived:
+                copies[section].wait()
+                arrived.add(section)
+        accumulate(buffer(stage), active(stage), *stages[stage][1:])
+        if stage + 1 < len(stages):
+            build_stage(stage + 1)
     place = 0
     for section in range(sections):
         for u in range(blocks[section]):

time: 43.4 us -> 43.3 us (level)
  no operation moved by 1% of the time
where the time goes in v14:
time: 43.3 us; the launch traced here: 43.1 us
  starting transfers between devices  14 us (32%)
  blocking collectives  11.7 us (27%)
  Pallas kernels  9.83 us (23%)
  waiting for transfers between devices  6.28 us (15%)
  between operations  0.69 us (2%)
  other arithmetic  0.61 us (1%)
    ppermute x15, starting transfers between devices, exchange(): return lax.ppermute(block, 'tmpl', [(i, i ^ distance) for i in range(size)])  14 us
    all_to_all x1, blocking collectives, maximum_over_group(): lax.all_to_all(copies, 'tmpl', split_axis=0, concat_axis=0, tiled=True)  11.7 us
    pallas_call x1, Pallas kernels, correlate(): pl.pallas_call(correlate_kernel, out_shape=pltpu.VMEM((padded, samples),...  7.13 us
    ppermute x15, waiting for transfers between devices, exchange(): return lax.ppermute(block, 'tmpl', [(i, i ^ distance) for i in range(size)])  6.28 us
    pallas_call x1, Pallas kernels, reconstruct(): pl.pallas_call(functools.partial(recon_kernel, order), out_shape=(jax.Sha...  1.98 us
  transfers between devices with their start and end apart: 15, of which 7 were waited for; matrix products, arithmetic and copies ran while one was open for 0% of the time, Pallas kernels for 2%

profile of v14, /device:TPU:0, one launch (start us, length us, event | category | flops | bytes accessed | tf_op | source)
XLA Modules:
  0.0 43.1 jit_solution(9104625963231916631)
XLA Ops:
  0.6 0.0 copy-start
  0.6 7.1 %correlate.1.refs_0_ = bf16[32,1920]{1,0:T(8,128)(2,1)S(1)} custom-call(bf16[72,128]{1,0:T(8,128)(2,1)} %bitcast.9, bf16[68,128]{1,0:T(8,128)(2,1)} %bitcast.10, bf16[66,128]{1,0:T(8,128)(2,1)} %bitcast.11, bf16[65,128]{1,0:T(8,128)(2,1)} %bitcast.12, bf16[4,32,8192]{2,1,0:T(8,128)(2,1)} %refs_4_.1), custom_call_target="tpu_custom_call" | custom-call | flops 1006632960 | bytes 2097152 | tf_op jit(solution)/shard_map/correlate/pallas_call | solution.py:165
  7.8 3.1 %collective-permute-start.5 = (bf16[32,1920]{1,0:T(8,128)(2,1)S(1)}, bf16[32,1920]{1,0:T(8,128)(2,1)S(1)}, u32[]{:S(2)}, u32[]{:S(2)}) collective-permute-start(bf16[32,1920]{1,0:T(8,128)(2,1)S(1)} %correlate.1.refs_0_), channel_id=1, source_target_pairs={{0,4},{1,5},{2,6},{3,7},{4,0},{5,1},{6,2},{7,3},{8,12},{9,13},{10,... | collective-permute-start | bytes 368648 | tf_op jit(solution)/shard_map/ppermute | solution.py:191
  10.9 2.6 %collective-permute-start.3 = (bf16[32,1920]{1,0:T(8,128)(2,1)S(1)}, bf16[32,1920]{1,0:T(8,128)(2,1)S(1)}, u32[]{:S(2)}, u32[]{:S(2)}) collective-permute-start(bf16[32,1920]{1,0:T(8,128)(2,1)S(1)} %correlate.1.refs_0_), channel_id=1, source_target_pairs={{0,8},{1,9},{2,10},{3,11},{4,12},{5,13},{6,14},{7,15},{8,0},{9,1},... | collective-permute-start | bytes 368648 | tf_op jit(solution)/shard_map/ppermute | solution.py:191
  13.5 1.5 %collective-permute-start.1 = (bf16[32,1920]{1,0:T(8,128)(2,1)S(1)}, bf16[32,1920]{1,0:T(8,128)(2,1)S(1)}, u32[]{:S(2)}, u32[]{:S(2)}) collective-permute-start(bf16[32,1920]{1,0:T(8,128)(2,1)S(1)} %correlate.1.refs_0_), channel_id=1, source_target_pairs={{0,2},{1,3},{2,0},{3,1},{4,6},{5,7},{6,4},{7,5},{8,10},{9,11},{10,... | collective-permute-start | bytes 368648 | tf_op jit(solution)/shard_map/ppermute | solution.py:191
  15.0 0.0 copy-done
  15.0 0.7 %arrange.1.coeffs_ref = bf16[4,256,512]{2,1,0:T(8,128)(2,1)S(1)} custom-call(s32[1]{0:T(128)} %bitcast.4.offset_ref, bf16[4,256,512]{2,1,0:T(8,128)(2,1)S(1)} %copy-done), custom_call_target="tpu_custom_call" | custom-call | flops 536870912 | bytes 2097152 | tf_op jit(solution)/shard_map/arrange/pallas_call | solution.py:236
  15.7 0.1 collective-permute-start
  15.8 0.0 collective-permute-done.5.refs_6_
  15.8 1.7 %collective-permute-start.7 = (bf16[32,1920]{1,0:T(8,128)(2,1)S(1)}, bf16[32,1920]{1,0:T(8,128)(2,1)S(1)}, u32[]{:S(2)}, u32[]{:S(2)}) collective-permute-start(bf16[32,1920]{1,0:T(8,128)(2,1)S(1)} %collective-permute-done.5.refs_6_), channel_id=1, source_target_pairs={{0,2},{1,3},{2,0},{3,1},{4,6},{5,7},{6,4},{7,5},{8,10},{9,11},{10,... | collective-permute-start | bytes 368648 | tf_op jit(solution)/shard_map/ppermute | solution.py:191
  17.5 0.0 collective-permute-start.6
  17.5 1.7 %collective-permute-done.3.refs_4_ = bf16[32,1920]{1,0:T(8,128)(2,1)S(1)} collective-permute-done((bf16[32,1920]{1,0:T(8,128)(2,1)S(1)}, bf16[32,1920]{1,0:T(8,128)(2,1)S(1)}, u32[]{:S(2)}, u32[]{:S(2)}) %collective-permute-start.3) | collective-permute-done | bytes 122912 | tf_op jit(solution)/shard_map/ppermute | solution.py:191
  19.2 1.5 %collective-permute-start.13 = (bf16[32,1920]{1,0:T(8,128)(2,1)S(1)}, bf16[32,1920]{1,0:T(8,128)(2,1)S(1)}, u32[]{:S(2)}, u32[]{:S(2)}) collective-permute-start(bf16[32,1920]{1,0:T(8,128)(2,1)S(1)} %collective-permute-done.3.refs_4_), channel_id=1, source_target_pairs={{0,2},{1,3},{2,0},{3,1},{4,6},{5,7},{6,4},{7,5},{8,10},{9,11},{10,... | collective-permute-start | bytes 368648 | tf_op jit(solution)/shard_map/ppermute | solution.py:191
  20.7 0.0 collective-permute-done.1.refs_2_
  20.8 0.4 collective-permute-start.11
  21.1 0.0 collective-permute-done.refs_1_
  21.1 1.6 %collective-permute-start.9 = (bf16[32,1920]{1,0:T(8,128)(2,1)S(1)}, bf16[32,1920]{1,0:T(8,128)(2,1)S(1)}, u32[]{:S(2)}, u32[]{:S(2)}) collective-permute-start(bf16[32,1920]{1,0:T(8,128)(2,1)S(1)} %collective-permute-done.3.refs_4_), channel_id=1, source_target_pairs={{0,4},{1,5},{2,6},{3,7},{4,0},{5,1},{6,2},{7,3},{8,12},{9,13},{10,... | collective-permute-start | bytes 368648 | tf_op jit(solution)/shard_map/ppermute | solution.py:191
  22.7 0.6 %collective-permute-done.7.refs_8_ = bf16[32,1920]{1,0:T(8,128)(2,1)S(1)} collective-permute-done((bf16[32,1920]{1,0:T(8,128)(2,1)S(1)}, bf16[32,1920]{1,0:T(8,128)(2,1)S(1)}, u32[]{:S(2)}, u32[]{:S(2)}) %collective-permute-start.7) | collective-permute-done | bytes 122912 | tf_op jit(solution)/shard_map/ppermute | solution.py:191
  23.3 0.0 collective-permute-start.4
  23.3 0.0 collective-permute-done.6.refs_7_
  23.3 0.5 %collective-permute-start.2 = (bf16[32,1920]{1,0:T(8,128)(2,1)S(1)}, bf16[32,1920]{1,0:T(8,128)(2,1)S(1)}, u32[]{:S(2)}, u32[]{:S(2)}) collective-permute-start(bf16[32,1920]{1,0:T(8,128)(2,1)S(1)} %collective-permute-done.1.refs_2_), channel_id=1, source_target_pairs={{0,1},{1,0},{2,3},{3,2},{4,5},{5,4},{6,7},{7,6},{8,9},{9,8},{10,11... | collective-permute-start | bytes 368648 | tf_op jit(solution)/shard_map/ppermute | solution.py:191
  23.8 3.0 %collective-permute-done.13.refs_14_ = bf16[32,1920]{1,0:T(8,128)(2,1)S(1)} collective-permute-done((bf16[32,1920]{1,0:T(8,128)(2,1)S(1)}, bf16[32,1920]{1,0:T(8,128)(2,1)S(1)}, u32[]{:S(2)}, u32[]{:S(2)}) %collective-permute-start.13) | collective-permute-done | bytes 122912 | tf_op jit(solution)/shard_map/ppermute | solution.py:191
  26.8 0.0 collective-permute-start.8
  26.8 0.0 collective-permute-done.11.refs_12_
  26.8 0.5 %collective-permute-start.14 = (bf16[32,1920]{1,0:T(8,128)(2,1)S(1)}, bf16[32,1920]{1,0:T(8,128)(2,1)S(1)}, u32[]{:S(2)}, u32[]{:S(2)}) collective-permute-start(bf16[32,1920]{1,0:T(8,128)(2,1)S(1)} %collective-permute-done.13.refs_14_), channel_id=1, source_target_pairs={{0,1},{1,0},{2,3},{3,2},{4,5},{5,4},{6,7},{7,6},{8,9},{9,8},{10,11... | collective-permute-start | bytes 368648 | tf_op jit(solution)/shard_map/ppermute | solution.py:191
  27.3 0.0 collective-permute-done.9.refs_10_
  27.3 0.1 collective-permute-start.12
  27.4 0.0 collective-permute-done.4.refs_5_
  27.4 0.4 %collective-permute-start.10 = (bf16[32,1920]{1,0:T(8,128)(2,1)S(1)}, bf16[32,1920]{1,0:T(8,128)(2,1)S(1)}, u32[]{:S(2)}, u32[]{:S(2)}) collective-permute-start(bf16[32,1920]{1,0:T(8,128)(2,1)S(1)} %collective-permute-done.9.refs_10_), channel_id=1, source_target_pairs={{0,1},{1,0},{2,3},{3,2},{4,5},{5,4},{6,7},{7,6},{8,9},{9,8},{10,11... | collective-permute-start | bytes 368648 | tf_op jit(solution)/shard_map/ppermute | solution.py:191
  27.8 0.0 collective-permute-done.2.refs_3_
  27.8 0.3 collective-permute-done.8.refs_9_
  28.1 0.2 collective-permute-done.14.refs_15_
  28.3 0.3 collective-permute-done.12.refs_13_
  28.7 0.2 collective-permute-done.10.refs_11_
  28.8 2.0 %reconstruct.1 = (bf16[256,1024]{1,0:T(8,128)(2,1)}, f32[1,1024]{1,0:T(1,128)S(1)}) custom-call(bf16[4,256,512]{2,1,0:T(8,128)(2,1)S(1)} %arrange.1.coeffs_ref, bf16[32,1920]{1,0:T(8,128)(2,1)S(1)} %correlate.1.refs_0_, bf16[32,1920]{1,0:T(8,128)(2,1)S(1)} %collective-permute-done.refs_1_, bf16[32,1920]{1,0:T(8,128)(2,1)S(1)} %collective-permute-done.1.refs_2_, ...), custom_call_target="tpu_custom_call" | custom-call | tf_op jit(solution)/shard_map/reconstruct/pallas_call | solution.py:295
  30.8 11.7 %all_to_all.5 = f32[16,8,128]{2,1,0:T(8,128)S(1)} all-to-all(f32[16,8,128]{2,1,0:T(8,128)S(1)} %broadcast_in_dim.8), channel_id=1, replica_groups=mesh['bank'=2,'tmpl'=16] {'tmpl'}, dimensions={0} | all-to-all | bytes 131072 | tf_op jit(solution)/shard_map/all_to_all | solution.py:220
  42.5 0.6 %reduce_max.9 = f32[8,128]{1,0:T(8,128)} reduce(f32[16,8,128]{2,1,0:T(8,128)S(1)} %all_to_all.5, f32[]{:T(128)} %constant.2.clone.1), dimensions={0}, to_apply=%region_0.0 | reduce | flops 15360 | bytes 69636 | tf_op jit(solution)/shard_map/reduce_max | solution.py:221
  (1 shorter events, 0.0 us)
Async XLA Ops:
  0.6 14.3 %copy-start = (bf16[4,256,512]{2,1,0:T(8,128)(2,1)S(1)}, bf16[4,256,512]{2,1,0:T(8,128)(2,1)}, u32[]{:S(2)}) copy-start(bf16[4,256,512]{2,1,0:T(8,128)(2,1)} %coeffs_ref.1) | copy-start | bytes 3145732
  7.8 8.0 %collective-permute-start.5 = (bf16[32,1920]{1,0:T(8,128)(2,1)S(1)}, bf16[32,1920]{1,0:T(8,128)(2,1)S(1)}, u32[]{:S(2)}, u32[]{:S(2)}) collective-permute-start(bf16[32,1920]{1,0:T(8,128)(2,1)S(1)} %correlate.1.refs_0_), channel_id=1, source_target_pairs={{0,4},{1,5},{2,6},{3,7},{4,0},{5,1},{6,2},{7,3},{8,12},{9,13},{10,... | collective-permute-start | bytes 368648 | tf_op jit(solution)/shard_map/ppermute | solution.py:191
  10.9 8.4 %collective-permute-start.3 = (bf16[32,1920]{1,0:T(8,128)(2,1)S(1)}, bf16[32,1920]{1,0:T(8,128)(2,1)S(1)}, u32[]{:S(2)}, u32[]{:S(2)}) collective-permute-start(bf16[32,1920]{1,0:T(8,128)(2,1)S(1)} %correlate.1.refs_0_), channel_id=1, source_target_pairs={{0,8},{1,9},{2,10},{3,11},{4,12},{5,13},{6,14},{7,15},{8,0},{9,1},... | collective-permute-start | bytes 368648 | tf_op jit(solution)/shard_map/ppermute | solution.py:191
  13.5 7.3 %collective-permute-start.1 = (bf16[32,1920]{1,0:T(8,128)(2,1)S(1)}, bf16[32,1920]{1,0:T(8,128)(2,1)S(1)}, u32[]{:S(2)}, u32[]{:S(2)}) collective-permute-start(bf16[32,1920]{1,0:T(8,128)(2,1)S(1)} %correlate.1.refs_0_), channel_id=1, source_target_pairs={{0,2},{1,3},{2,0},{3,1},{4,6},{5,7},{6,4},{7,5},{8,10},{9,11},{10,... | collective-permute-start | bytes 368648 | tf_op jit(solution)/shard_map/ppermute | solution.py:191
  15.7 5.4 %collective-permute-start = (bf16[32,1920]{1,0:T(8,128)(2,1)S(1)}, bf16[32,1920]{1,0:T(8,128)(2,1)S(1)}, u32[]{:S(2)}, u32[]{:S(2)}) collective-permute-start(bf16[32,1920]{1,0:T(8,128)(2,1)S(1)} %correlate.1.refs_0_), channel_id=1, source_target_pairs={{0,1},{1,0},{2,3},{3,2},{4,5},{5,4},{6,7},{7,6},{8,9},{9,8},{10,11... | collective-permute-start | bytes 368648 | tf_op jit(solution)/shard_map/ppermute | solution.py:191
  15.8 7.5 %collective-permute-start.7 = (bf16[32,1920]{1,0:T(8,128)(2,1)S(1)}, bf16[32,1920]{1,0:T(8,128)(2,1)S(1)}, u32[]{:S(2)}, u32[]{:S(2)}) collective-permute-start(bf16[32,1920]{1,0:T(8,128)(2,1)S(1)} %collective-permute-done.5.refs_6_), channel_id=1, source_target_pairs={{0,2},{1,3},{2,0},{3,1},{4,6},{5,7},{6,4},{7,5},{8,10},{9,11},{10,... | collective-permute-start | bytes 368648 | tf_op jit(solution)/shard_map/ppermute | solution.py:191
  17.5 5.8 %collective-permute-start.6 = (bf16[32,1920]{1,0:T(8,128)(2,1)S(1)}, bf16[32,1920]{1,0:T(8,128)(2,1)S(1)}, u32[]{:S(2)}, u32[]{:S(2)}) collective-permute-start(bf16[32,1920]{1,0:T(8,128)(2,1)S(1)} %collective-permute-done.5.refs_6_), channel_id=1, source_target_pairs={{0,1},{1,0},{2,3},{3,2},{4,5},{5,4},{6,7},{7,6},{8,9},{9,8},{10,11... | collective-permute-start | bytes 368648 | tf_op jit(solution)/shard_map/ppermute | solution.py:191
  19.2 7.6 %collective-permute-start.13 = (bf16[32,1920]{1,0:T(8,128)(2,1)S(1)}, bf16[32,1920]{1,0:T(8,128)(2,1)S(1)}, u32[]{:S(2)}, u32[]{:S(2)}) collective-permute-start(bf16[32,1920]{1,0:T(8,128)(2,1)S(1)} %collective-permute-done.3.refs_4_), channel_id=1, source_target_pairs={{0,2},{1,3},{2,0},{3,1},{4,6},{5,7},{6,4},{7,5},{8,10},{9,11},{10,... | collective-permute-start | bytes 368648 | tf_op jit(solution)/shard_map/ppermute | solution.py:191
  20.8 6.1 %collective-permute-start.11 = (bf16[32,1920]{1,0:T(8,128)(2,1)S(1)}, bf16[32,1920]{1,0:T(8,128)(2,1)S(1)}, u32[]{:S(2)}, u32[]{:S(2)}) collective-permute-start(bf16[32,1920]{1,0:T(8,128)(2,1)S(1)} %collective-permute-done.3.refs_4_), channel_id=1, source_target_pairs={{0,6},{1,7},{2,4},{3,5},{4,2},{5,3},{6,0},{7,1},{8,14},{9,15},{10,... | collective-permute-start | bytes 368648 | tf_op jit(solution)/shard_map/ppermute | solution.py:191
  21.1 6.2 %collective-permute-start.9 = (bf16[32,1920]{1,0:T(8,128)(2,1)S(1)}, bf16[32,1920]{1,0:T(8,128)(2,1)S(1)}, u32[]{:S(2)}, u32[]{:S(2)}) collective-permute-start(bf16[32,1920]{1,0:T(8,128)(2,1)S(1)} %collective-permute-done.3.refs_4_), channel_id=1, source_target_pairs={{0,4},{1,5},{2,6},{3,7},{4,0},{5,1},{6,2},{7,3},{8,12},{9,13},{10,... | collective-permute-start | bytes 368648 | tf_op jit(solution)/shard_map/ppermute | solution.py:191
  23.3 4.1 %collective-permute-start.4 = (bf16[32,1920]{1,0:T(8,128)(2,1)S(1)}, bf16[32,1920]{1,0:T(8,128)(2,1)S(1)}, u32[]{:S(2)}, u32[]{:S(2)}) collective-permute-start(bf16[32,1920]{1,0:T(8,128)(2,1)S(1)} %collective-permute-done.3.refs_4_), channel_id=1, source_target_pairs={{0,1},{1,0},{2,3},{3,2},{4,5},{5,4},{6,7},{7,6},{8,9},{9,8},{10,11... | collective-permute-start | bytes 368648 | tf_op jit(solution)/shard_map/ppermute | solution.py:191
  23.3 4.5 %collective-permute-start.2 = (bf16[32,1920]{1,0:T(8,128)(2,1)S(1)}, bf16[32,1920]{1,0:T(8,128)(2,1)S(1)}, u32[]{:S(2)}, u32[]{:S(2)}) collective-permute-start(bf16[32,1920]{1,0:T(8,128)(2,1)S(1)} %collective-permute-done.1.refs_2_), channel_id=1, source_target_pairs={{0,1},{1,0},{2,3},{3,2},{4,5},{5,4},{6,7},{7,6},{8,9},{9,8},{10,11... | collective-permute-start | bytes 368648 | tf_op jit(solution)/shard_map/ppermute | solution.py:191
  26.8 1.3 %collective-permute-start.8 = (bf16[32,1920]{1,0:T(8,128)(2,1)S(1)}, bf16[32,1920]{1,0:T(8,128)(2,1)S(1)}, u32[]{:S(2)}, u32[]{:S(2)}) collective-permute-start(bf16[32,1920]{1,0:T(8,128)(2,1)S(1)} %collective-permute-done.7.refs_8_), channel_id=1, source_target_pairs={{0,1},{1,0},{2,3},{3,2},{4,5},{5,4},{6,7},{7,6},{8,9},{9,8},{10,11... | collective-permute-start | bytes 368648 | tf_op jit(solution)/shard_map/ppermute | solution.py:191
  26.8 1.5 %collective-permute-start.14 = (bf16[32,1920]{1,0:T(8,128)(2,1)S(1)}, bf16[32,1920]{1,0:T(8,128)(2,1)S(1)}, u32[]{:S(2)}, u32[]{:S(2)}) collective-permute-start(bf16[32,1920]{1,0:T(8,128)(2,1)S(1)} %collective-permute-done.13.refs_14_), channel_id=1, source_target_pairs={{0,1},{1,0},{2,3},{3,2},{4,5},{5,4},{6,7},{7,6},{8,9},{9,8},{10,11... | collective-permute-start | bytes 368648 | tf_op jit(solution)/shard_map/ppermute | solution.py:191
  27.3 1.3 %collective-permute-start.12 = (bf16[32,1920]{1,0:T(8,128)(2,1)S(1)}, bf16[32,1920]{1,0:T(8,128)(2,1)S(1)}, u32[]{:S(2)}, u32[]{:S(2)}) collective-permute-start(bf16[32,1920]{1,0:T(8,128)(2,1)S(1)} %collective-permute-done.11.refs_12_), channel_id=1, source_target_pairs={{0,1},{1,0},{2,3},{3,2},{4,5},{5,4},{6,7},{7,6},{8,9},{9,8},{10,11... | collective-permute-start | bytes 368648 | tf_op jit(solution)/shard_map/ppermute | solution.py:191
  27.4 1.4 %collective-permute-start.10 = (bf16[32,1920]{1,0:T(8,128)(2,1)S(1)}, bf16[32,1920]{1,0:T(8,128)(2,1)S(1)}, u32[]{:S(2)}, u32[]{:S(2)}) collective-permute-start(bf16[32,1920]{1,0:T(8,128)(2,1)S(1)} %collective-permute-done.9.refs_10_), channel_id=1, source_target_pairs={{0,1},{1,0},{2,3},{3,2},{4,5},{5,4},{6,7},{7,6},{8,9},{9,8},{10,11... | collective-permute-start | bytes 368648 | tf_op jit(solution)/shard_map/ppermute | solution.py:191

commit v15 on v14

--- a/solution.py
+++ b/solution.py
@@ -12,8 +12,8 @@
 SUB = 16
 ROWS = 8
 ROLLS = 4
-TIED = 1
-HANDED = (0, 1, 2, 3, 8, 9, 4, 5, 6, 7, 12, 13, 14, 15, 10, 11)
+TIED = 9
+HANDED = (12, 13, 4, 5, 0, 1, 6, 7, 14, 15, 10, 11, 2, 3, 8, 9)
 
 
 def correlate_kernel(*refs):
@@ -215,9 +215,13 @@
 
 def maximum_over_group(values):
     size = lax.axis_size("tmpl")
+    values = jnp.maximum(values, exchange(values, 1))
     tiles = values.reshape(1, -1, LANE)
-    copies = jnp.broadcast_to(tiles, (size,) + tiles.shape[1:])
-    others = lax.all_to_all(copies, "tmpl", split_axis=0, concat_axis=0, tiled=True)
+    copies = jnp.broadcast_to(tiles, (size // 2,) + tiles.shape[1:])
+    groups = [list(range(core, size, 2)) for core in range(2)]
+    others = lax.all_to_all(
+        copies, "tmpl", split_axis=0, concat_axis=0, axis_index_groups=groups, tiled=True
+    )
     return jnp.max(others, axis=0).reshape(values.shape)
 
 

time: 43.3 us -> 44.7 us (1.032)
  waiting for transfers between devices: 6.28 us -> 9.63 us
  starting transfers between devices: 14 us -> 12.5 us
    ppermute x15 -> x16, waiting for transfers between devices: 6.28 us -> 9.63 us  [exchange(): return lax.ppermute(block, 'tmpl', [(i, i ^ distance) for i in range(size)])]
    ppermute x15 -> x16, starting transfers between devices: 14 us -> 12.5 us  [exchange(): return lax.ppermute(block, 'tmpl', [(i, i ^ distance) for i in range(size)])]
  transfers between devices with their start and end apart: 15 -> 16, of which waited for: 7 -> 8; matrix products, arithmetic and copies ran while one was open for 0% -> 0% of each run, Pallas kernels for 2% -> 2%
where the time goes in v15:
time: 44.7 us; the launch traced here: 44.5 us
  starting transfers between devices  12.5 us (28%)
  blocking collectives  11.3 us (25%)
  Pallas kernels  9.82 us (22%)
  waiting for transfers between devices  9.63 us (22%)
  between operations  0.7 us (2%)
  other arithmetic  0.6 us (1%)
    ppermute x16, starting transfers between devices, exchange(): return lax.ppermute(block, 'tmpl', [(i, i ^ distance) for i in range(size)])  12.5 us
    all_to_all x1, blocking collectives, maximum_over_group(): lax.all_to_all(copies, 'tmpl', split_axis=0, concat_axis=0, axis_index_gr...  11.3 us
    ppermute x16, waiting for transfers between devices, exchange(): return lax.ppermute(block, 'tmpl', [(i, i ^ distance) for i in range(size)])  9.63 us
    pallas_call x1, Pallas kernels, correlate(): pl.pallas_call(correlate_kernel, out_shape=pltpu.VMEM((padded, samples),...  7.13 us
    pallas_call x1, Pallas kernels, reconstruct(): pl.pallas_call(functools.partial(recon_kernel, order), out_shape=(jax.Sha...  1.97 us
  transfers between devices with their start and end apart: 16, of which 8 were waited for; matrix products, arithmetic and copies ran while one was open for 0% of the time, Pallas kernels for 2%

profile of v15, /device:TPU:0, one launch (start us, length us, event | category | flops | bytes accessed | tf_op | source)
XLA Modules:
  0.0 44.5 jit_solution(10397329299890851817)
XLA Ops:
  0.6 0.0 copy-start
  0.6 7.1 %correlate.1.refs_4_ = bf16[32,1920]{1,0:T(8,128)(2,1)S(1)} custom-call(bf16[72,128]{1,0:T(8,128)(2,1)} %bitcast.12, bf16[68,128]{1,0:T(8,128)(2,1)} %bitcast.13, bf16[66,128]{1,0:T(8,128)(2,1)} %bitcast.14, bf16[65,128]{1,0:T(8,128)(2,1)} %bitcast.15, bf16[4,32,8192]{2,1,0:T(8,128)(2,1)} %refs_4_.1), custom_call_target="tpu_custom_call" | custom-call | flops 1006632960 | bytes 2097152 | tf_op jit(solution)/shard_map/correlate/pallas_call | solution.py:165
  7.8 3.0 %collective-permute-start.12 = (bf16[32,1920]{1,0:T(8,128)(2,1)S(1)}, bf16[32,1920]{1,0:T(8,128)(2,1)S(1)}, u32[]{:S(2)}, u32[]{:S(2)}) collective-permute-start(bf16[32,1920]{1,0:T(8,128)(2,1)S(1)} %correlate.1.refs_4_), channel_id=1, source_target_pairs={{0,2},{1,3},{2,0},{3,1},{4,6},{5,7},{6,4},{7,5},{8,10},{9,11},{10,... | collective-permute-start | bytes 368648 | tf_op jit(solution)/shard_map/ppermute | solution.py:191
  10.8 1.6 %collective-permute-start.3 = (bf16[32,1920]{1,0:T(8,128)(2,1)S(1)}, bf16[32,1920]{1,0:T(8,128)(2,1)S(1)}, u32[]{:S(2)}, u32[]{:S(2)}) collective-permute-start(bf16[32,1920]{1,0:T(8,128)(2,1)S(1)} %correlate.1.refs_4_), channel_id=1, source_target_pairs={{0,4},{1,5},{2,6},{3,7},{4,0},{5,1},{6,2},{7,3},{8,12},{9,13},{10,... | collective-permute-start | bytes 368648 | tf_op jit(solution)/shard_map/ppermute | solution.py:191
  12.4 2.6 %collective-permute-start = (bf16[32,1920]{1,0:T(8,128)(2,1)S(1)}, bf16[32,1920]{1,0:T(8,128)(2,1)S(1)}, u32[]{:S(2)}, u32[]{:S(2)}) collective-permute-start(bf16[32,1920]{1,0:T(8,128)(2,1)S(1)} %correlate.1.refs_4_), channel_id=1, source_target_pairs={{0,8},{1,9},{2,10},{3,11},{4,12},{5,13},{6,14},{7,15},{8,0},{9,1},... | collective-permute-start | bytes 368648 | tf_op jit(solution)/shard_map/ppermute | solution.py:191
  15.0 0.0 collective-permute-start.5
  15.0 0.0 collective-permute-done.12.refs_12_
  15.0 0.5 %collective-permute-start.13 = (bf16[32,1920]{1,0:T(8,128)(2,1)S(1)}, bf16[32,1920]{1,0:T(8,128)(2,1)S(1)}, u32[]{:S(2)}, u32[]{:S(2)}) collective-permute-start(bf16[32,1920]{1,0:T(8,128)(2,1)S(1)} %collective-permute-done.12.refs_12_), channel_id=1, source_target_pairs={{0,1},{1,0},{2,3},{3,2},{4,5},{5,4},{6,7},{7,6},{8,9},{9,8},{10,11... | collective-permute-start | bytes 368648 | tf_op jit(solution)/shard_map/ppermute | solution.py:191
  15.5 1.6 %collective-permute-done.3.refs_2_ = bf16[32,1920]{1,0:T(8,128)(2,1)S(1)} collective-permute-done((bf16[32,1920]{1,0:T(8,128)(2,1)S(1)}, bf16[32,1920]{1,0:T(8,128)(2,1)S(1)}, u32[]{:S(2)}, u32[]{:S(2)}) %collective-permute-start.3) | collective-permute-done | bytes 122912 | tf_op jit(solution)/shard_map/ppermute | solution.py:191
  17.1 0.0 collective-permute-start.6
  17.2 0.0 collective-permute-start.4
  17.2 3.3 %collective-permute-done.refs_14_ = bf16[32,1920]{1,0:T(8,128)(2,1)S(1)} collective-permute-done((bf16[32,1920]{1,0:T(8,128)(2,1)S(1)}, bf16[32,1920]{1,0:T(8,128)(2,1)S(1)}, u32[]{:S(2)}, u32[]{:S(2)}) %collective-permute-start) | collective-permute-done | bytes 122912 | tf_op jit(solution)/shard_map/ppermute | solution.py:191
  20.5 0.5 %collective-permute-start.10 = (bf16[32,1920]{1,0:T(8,128)(2,1)S(1)}, bf16[32,1920]{1,0:T(8,128)(2,1)S(1)}, u32[]{:S(2)}, u32[]{:S(2)}) collective-permute-start(bf16[32,1920]{1,0:T(8,128)(2,1)S(1)} %collective-permute-done.refs_14_), channel_id=1, source_target_pairs={{0,2},{1,3},{2,0},{3,1},{4,6},{5,7},{6,4},{7,5},{8,10},{9,11},{10,... | collective-permute-start | bytes 368648 | tf_op jit(solution)/shard_map/ppermute | solution.py:191
  21.0 0.0 collective-permute-done.5.refs_5_
  21.0 1.3 %collective-permute-start.8 = (bf16[32,1920]{1,0:T(8,128)(2,1)S(1)}, bf16[32,1920]{1,0:T(8,128)(2,1)S(1)}, u32[]{:S(2)}, u32[]{:S(2)}) collective-permute-start(bf16[32,1920]{1,0:T(8,128)(2,1)S(1)} %collective-permute-done.refs_14_), channel_id=1, source_target_pairs={{0,6},{1,7},{2,4},{3,5},{4,2},{5,3},{6,0},{7,1},{8,14},{9,15},{10,... | collective-permute-start | bytes 368648 | tf_op jit(solution)/shard_map/ppermute | solution.py:191
  22.3 0.0 collective-permute-done.13.refs_13_
  22.3 1.7 %collective-permute-start.1 = (bf16[32,1920]{1,0:T(8,128)(2,1)S(1)}, bf16[32,1920]{1,0:T(8,128)(2,1)S(1)}, u32[]{:S(2)}, u32[]{:S(2)}) collective-permute-start(bf16[32,1920]{1,0:T(8,128)(2,1)S(1)} %collective-permute-done.refs_14_), channel_id=1, source_target_pairs={{0,4},{1,5},{2,6},{3,7},{4,0},{5,1},{6,2},{7,3},{8,12},{9,13},{10,... | collective-permute-start | bytes 368648 | tf_op jit(solution)/shard_map/ppermute | solution.py:191
  24.0 0.0 copy-done
  24.0 0.7 %arrange.1.coeffs_ref = bf16[4,256,512]{2,1,0:T(8,128)(2,1)S(1)} custom-call(s32[1]{0:T(128)} %bitcast.4.offset_ref, bf16[4,256,512]{2,1,0:T(8,128)(2,1)S(1)} %copy-done), custom_call_target="tpu_custom_call" | custom-call | flops 536870912 | bytes 2097152 | tf_op jit(solution)/shard_map/arrange/pallas_call | solution.py:240
  24.7 0.0 collective-permute-done.6.refs_6_
  24.7 0.1 collective-permute-start.14
  24.8 0.0 collective-permute-done.4.refs_3_
  24.8 0.5 %collective-permute-start.7 = (bf16[32,1920]{1,0:T(8,128)(2,1)S(1)}, bf16[32,1920]{1,0:T(8,128)(2,1)S(1)}, u32[]{:S(2)}, u32[]{:S(2)}) collective-permute-start(bf16[32,1920]{1,0:T(8,128)(2,1)S(1)} %collective-permute-done.6.refs_6_), channel_id=1, source_target_pairs={{0,1},{1,0},{2,3},{3,2},{4,5},{5,4},{6,7},{7,6},{8,9},{9,8},{10,11... | collective-permute-start | bytes 368648 | tf_op jit(solution)/shard_map/ppermute | solution.py:191
  25.3 1.8 %collective-permute-done.10.refs_10_ = bf16[32,1920]{1,0:T(8,128)(2,1)S(1)} collective-permute-done((bf16[32,1920]{1,0:T(8,128)(2,1)S(1)}, bf16[32,1920]{1,0:T(8,128)(2,1)S(1)}, u32[]{:S(2)}, u32[]{:S(2)}) %collective-permute-start.10) | collective-permute-done | bytes 122912 | tf_op jit(solution)/shard_map/ppermute | solution.py:191
  27.1 0.0 collective-permute-start.11
  27.1 0.0 collective-permute-done.8.refs_8_
  27.1 0.5 %collective-permute-start.9 = (bf16[32,1920]{1,0:T(8,128)(2,1)S(1)}, bf16[32,1920]{1,0:T(8,128)(2,1)S(1)}, u32[]{:S(2)}, u32[]{:S(2)}) collective-permute-start(bf16[32,1920]{1,0:T(8,128)(2,1)S(1)} %collective-permute-done.8.refs_8_), channel_id=1, source_target_pairs={{0,1},{1,0},{2,3},{3,2},{4,5},{5,4},{6,7},{7,6},{8,9},{9,8},{10,11... | collective-permute-start | bytes 368648 | tf_op jit(solution)/shard_map/ppermute | solution.py:191
  27.6 0.5 %collective-permute-done.1.refs_0_ = bf16[32,1920]{1,0:T(8,128)(2,1)S(1)} collective-permute-done((bf16[32,1920]{1,0:T(8,128)(2,1)S(1)}, bf16[32,1920]{1,0:T(8,128)(2,1)S(1)}, u32[]{:S(2)}, u32[]{:S(2)}) %collective-permute-start.1) | collective-permute-done | bytes 122912 | tf_op jit(solution)/shard_map/ppermute | solution.py:191
  28.1 0.0 collective-permute-start.2
  28.1 0.0 collective-permute-done.14.refs_15_
  28.1 0.0 collective-permute-done.7.refs_7_
  28.1 0.3 collective-permute-done.11.refs_11_
  28.4 0.2 collective-permute-done.9.refs_9_
  28.6 0.9 %collective-permute-done.2.refs_1_ = bf16[32,1920]{1,0:T(8,128)(2,1)S(1)} collective-permute-done((bf16[32,1920]{1,0:T(8,128)(2,1)S(1)}, bf16[32,1920]{1,0:T(8,128)(2,1)S(1)}, u32[]{:S(2)}, u32[]{:S(2)}) %collective-permute-start.2) | collective-permute-done | bytes 122912 | tf_op jit(solution)/shard_map/ppermute | solution.py:191
  29.5 2.0 %reconstruct.1 = (bf16[256,1024]{1,0:T(8,128)(2,1)}, f32[1,1024]{1,0:T(1,128)S(1)}) custom-call(bf16[4,256,512]{2,1,0:T(8,128)(2,1)S(1)} %arrange.1.coeffs_ref, bf16[32,1920]{1,0:T(8,128)(2,1)S(1)} %collective-permute-done.1.refs_0_, bf16[32,1920]{1,0:T(8,128)(2,1)S(1)} %collective-permute-done.2.refs_1_, ...), custom_call_target="tpu_custom_call" | custom-call | tf_op jit(solution)/shard_map/reconstruct/pallas_call | solution.py:299
  31.4 0.2 collective-permute-start.15
  31.6 1.0 %collective-permute-done.15 = f32[1024]{0:T(1024)S(1)} collective-permute-done((f32[1024]{0:T(1024)S(1)}, f32[1024]{0:T(1024)S(1)}, u32[]{:S(2)}, u32[]{:S(2)}) %collective-permute-start.15) | collective-permute-done | bytes 4128 | tf_op jit(solution)/shard_map/ppermute | solution.py:191
  32.6 11.3 %all_to_all.5 = f32[8,8,128]{2,1,0:T(8,128)S(1)} all-to-all(f32[8,8,128]{2,1,0:T(8,128)S(1)} %broadcast_in_dim.8), channel_id=1, replica_groups={{0,2,4,6,8,10,12,14},{1,3,5,7,9,11,13,15},{16,18,20,22,24,26,28,30},{17..., dimensions={0} | all-to-all | bytes 65536 | tf_op jit(solution)/shard_map/all_to_all | solution.py:222
  43.9 0.6 %reduce_max.9 = f32[8,128]{1,0:T(8,128)} reduce(f32[8,8,128]{2,1,0:T(8,128)S(1)} %all_to_all.5, f32[]{:T(128)} %constant.2.clone.1), dimensions={0}, to_apply=%region_0.0 | reduce | flops 7168 | bytes 36868 | tf_op jit(solution)/shard_map/reduce_max | solution.py:225
  (2 shorter events, 0.0 us)
Async XLA Ops:
  0.6 23.3 %copy-start = (bf16[4,256,512]{2,1,0:T(8,128)(2,1)S(1)}, bf16[4,256,512]{2,1,0:T(8,128)(2,1)}, u32[]{:S(2)}) copy-start(bf16[4,256,512]{2,1,0:T(8,128)(2,1)} %coeffs_ref.1) | copy-start | bytes 3145732
  7.8 7.2 %collective-permute-start.12 = (bf16[32,1920]{1,0:T(8,128)(2,1)S(1)}, bf16[32,1920]{1,0:T(8,128)(2,1)S(1)}, u32[]{:S(2)}, u32[]{:S(2)}) collective-permute-start(bf16[32,1920]{1,0:T(8,128)(2,1)S(1)} %correlate.1.refs_4_), channel_id=1, source_target_pairs={{0,2},{1,3},{2,0},{3,1},{4,6},{5,7},{6,4},{7,5},{8,10},{9,11},{10,... | collective-permute-start | bytes 368648 | tf_op jit(solution)/shard_map/ppermute | solution.py:191
  10.8 6.3 %collective-permute-start.3 = (bf16[32,1920]{1,0:T(8,128)(2,1)S(1)}, bf16[32,1920]{1,0:T(8,128)(2,1)S(1)}, u32[]{:S(2)}, u32[]{:S(2)}) collective-permute-start(bf16[32,1920]{1,0:T(8,128)(2,1)S(1)} %correlate.1.refs_4_), channel_id=1, source_target_pairs={{0,4},{1,5},{2,6},{3,7},{4,0},{5,1},{6,2},{7,3},{8,12},{9,13},{10,... | collective-permute-start | bytes 368648 | tf_op jit(solution)/shard_map/ppermute | solution.py:191
  12.4 8.1 %collective-permute-start = (bf16[32,1920]{1,0:T(8,128)(2,1)S(1)}, bf16[32,1920]{1,0:T(8,128)(2,1)S(1)}, u32[]{:S(2)}, u32[]{:S(2)}) collective-permute-start(bf16[32,1920]{1,0:T(8,128)(2,1)S(1)} %correlate.1.refs_4_), channel_id=1, source_target_pairs={{0,8},{1,9},{2,10},{3,11},{4,12},{5,13},{6,14},{7,15},{8,0},{9,1},... | collective-permute-start | bytes 368648 | tf_op jit(solution)/shard_map/ppermute | solution.py:191
  15.0 6.0 %collective-permute-start.5 = (bf16[32,1920]{1,0:T(8,128)(2,1)S(1)}, bf16[32,1920]{1,0:T(8,128)(2,1)S(1)}, u32[]{:S(2)}, u32[]{:S(2)}) collective-permute-start(bf16[32,1920]{1,0:T(8,128)(2,1)S(1)} %correlate.1.refs_4_), channel_id=1, source_target_pairs={{0,1},{1,0},{2,3},{3,2},{4,5},{5,4},{6,7},{7,6},{8,9},{9,8},{10,11... | collective-permute-start | bytes 368648 | tf_op jit(solution)/shard_map/ppermute | solution.py:191
  15.0 7.3 %collective-permute-start.13 = (bf16[32,1920]{1,0:T(8,128)(2,1)S(1)}, bf16[32,1920]{1,0:T(8,128)(2,1)S(1)}, u32[]{:S(2)}, u32[]{:S(2)}) collective-permute-start(bf16[32,1920]{1,0:T(8,128)(2,1)S(1)} %collective-permute-done.12.refs_12_), channel_id=1, source_target_pairs={{0,1},{1,0},{2,3},{3,2},{4,5},{5,4},{6,7},{7,6},{8,9},{9,8},{10,11... | collective-permute-start | bytes 368648 | tf_op jit(solution)/shard_map/ppermute | solution.py:191
  17.1 7.6 %collective-permute-start.6 = (bf16[32,1920]{1,0:T(8,128)(2,1)S(1)}, bf16[32,1920]{1,0:T(8,128)(2,1)S(1)}, u32[]{:S(2)}, u32[]{:S(2)}) collective-permute-start(bf16[32,1920]{1,0:T(8,128)(2,1)S(1)} %collective-permute-done.3.refs_2_), channel_id=1, source_target_pairs={{0,2},{1,3},{2,0},{3,1},{4,6},{5,7},{6,4},{7,5},{8,10},{9,11},{10,... | collective-permute-start | bytes 368648 | tf_op jit(solution)/shard_map/ppermute | solution.py:191
  17.2 7.6 %collective-permute-start.4 = (bf16[32,1920]{1,0:T(8,128)(2,1)S(1)}, bf16[32,1920]{1,0:T(8,128)(2,1)S(1)}, u32[]{:S(2)}, u32[]{:S(2)}) collective-permute-start(bf16[32,1920]{1,0:T(8,128)(2,1)S(1)} %collective-permute-done.3.refs_2_), channel_id=1, source_target_pairs={{0,1},{1,0},{2,3},{3,2},{4,5},{5,4},{6,7},{7,6},{8,9},{9,8},{10,11... | collective-permute-start | bytes 368648 | tf_op jit(solution)/shard_map/ppermute | solution.py:191
  20.5 6.6 %collective-permute-start.10 = (bf16[32,1920]{1,0:T(8,128)(2,1)S(1)}, bf16[32,1920]{1,0:T(8,128)(2,1)S(1)}, u32[]{:S(2)}, u32[]{:S(2)}) collective-permute-start(bf16[32,1920]{1,0:T(8,128)(2,1)S(1)} %collective-permute-done.refs_14_), channel_id=1, source_target_pairs={{0,2},{1,3},{2,0},{3,1},{4,6},{5,7},{6,4},{7,5},{8,10},{9,11},{10,... | collective-permute-start | bytes 368648 | tf_op jit(solution)/shard_map/ppermute | solution.py:191
  21.0 6.1 %collective-permute-start.8 = (bf16[32,1920]{1,0:T(8,128)(2,1)S(1)}, bf16[32,1920]{1,0:T(8,128)(2,1)S(1)}, u32[]{:S(2)}, u32[]{:S(2)}) collective-permute-start(bf16[32,1920]{1,0:T(8,128)(2,1)S(1)} %collective-permute-done.refs_14_), channel_id=1, source_target_pairs={{0,6},{1,7},{2,4},{3,5},{4,2},{5,3},{6,0},{7,1},{8,14},{9,15},{10,... | collective-permute-start | bytes 368648 | tf_op jit(solution)/shard_map/ppermute | solution.py:191
  22.3 5.8 %collective-permute-start.1 = (bf16[32,1920]{1,0:T(8,128)(2,1)S(1)}, bf16[32,1920]{1,0:T(8,128)(2,1)S(1)}, u32[]{:S(2)}, u32[]{:S(2)}) collective-permute-start(bf16[32,1920]{1,0:T(8,128)(2,1)S(1)} %collective-permute-done.refs_14_), channel_id=1, source_target_pairs={{0,4},{1,5},{2,6},{3,7},{4,0},{5,1},{6,2},{7,3},{8,12},{9,13},{10,... | collective-permute-start | bytes 368648 | tf_op jit(solution)/shard_map/ppermute | solution.py:191
  24.7 3.4 %collective-permute-start.14 = (bf16[32,1920]{1,0:T(8,128)(2,1)S(1)}, bf16[32,1920]{1,0:T(8,128)(2,1)S(1)}, u32[]{:S(2)}, u32[]{:S(2)}) collective-permute-start(bf16[32,1920]{1,0:T(8,128)(2,1)S(1)} %collective-permute-done.refs_14_), channel_id=1, source_target_pairs={{0,1},{1,0},{2,3},{3,2},{4,5},{5,4},{6,7},{7,6},{8,9},{9,8},{10,11... | collective-permute-start | bytes 368648 | tf_op jit(solution)/shard_map/ppermute | solution.py:191
  24.8 3.3 %collective-permute-start.7 = (bf16[32,1920]{1,0:T(8,128)(2,1)S(1)}, bf16[32,1920]{1,0:T(8,128)(2,1)S(1)}, u32[]{:S(2)}, u32[]{:S(2)}) collective-permute-start(bf16[32,1920]{1,0:T(8,128)(2,1)S(1)} %collective-permute-done.6.refs_6_), channel_id=1, source_target_pairs={{0,1},{1,0},{2,3},{3,2},{4,5},{5,4},{6,7},{7,6},{8,9},{9,8},{10,11... | collective-permute-start | bytes 368648 | tf_op jit(solution)/shard_map/ppermute | solution.py:191
  27.1 1.3 %collective-permute-start.11 = (bf16[32,1920]{1,0:T(8,128)(2,1)S(1)}, bf16[32,1920]{1,0:T(8,128)(2,1)S(1)}, u32[]{:S(2)}, u32[]{:S(2)}) collective-permute-start(bf16[32,1920]{1,0:T(8,128)(2,1)S(1)} %collective-permute-done.10.refs_10_), channel_id=1, source_target_pairs={{0,1},{1,0},{2,3},{3,2},{4,5},{5,4},{6,7},{7,6},{8,9},{9,8},{10,11... | collective-permute-start | bytes 368648 | tf_op jit(solution)/shard_map/ppermute | solution.py:191
  27.1 1.5 %collective-permute-start.9 = (bf16[32,1920]{1,0:T(8,128)(2,1)S(1)}, bf16[32,1920]{1,0:T(8,128)(2,1)S(1)}, u32[]{:S(2)}, u32[]{:S(2)}) collective-permute-start(bf16[32,1920]{1,0:T(8,128)(2,1)S(1)} %collective-permute-done.8.refs_8_), channel_id=1, source_target_pairs={{0,1},{1,0},{2,3},{3,2},{4,5},{5,4},{6,7},{7,6},{8,9},{9,8},{10,11... | collective-permute-start | bytes 368648 | tf_op jit(solution)/shard_map/ppermute | solution.py:191
  28.1 1.3 %collective-permute-start.2 = (bf16[32,1920]{1,0:T(8,128)(2,1)S(1)}, bf16[32,1920]{1,0:T(8,128)(2,1)S(1)}, u32[]{:S(2)}, u32[]{:S(2)}) collective-permute-start(bf16[32,1920]{1,0:T(8,128)(2,1)S(1)} %collective-permute-done.1.refs_0_), channel_id=1, source_target_pairs={{0,1},{1,0},{2,3},{3,2},{4,5},{5,4},{6,7},{7,6},{8,9},{9,8},{10,11... | collective-permute-start | bytes 368648 | tf_op jit(solution)/shard_map/ppermute | solution.py:191
  31.4 1.2 %collective-permute-start.15 = (f32[1024]{0:T(1024)S(1)}, f32[1024]{0:T(1024)S(1)}, u32[]{:S(2)}, u32[]{:S(2)}) collective-permute-start(f32[1024]{0:T(1024)S(1)} %bitcast.9), channel_id=1, source_target_pairs={{0,1},{1,0},{2,3},{3,2},{4,5},{5,4},{6,7},{7,6},{8,9},{9,8},{10,11... | collective-permute-start | bytes 12296 | tf_op jit(solution)/shard_map/ppermute | solution.py:191

commit v16 on v14

--- a/solution.py
+++ b/solution.py
@@ -13,7 +13,8 @@
 ROWS = 8
 ROLLS = 4
 TIED = 1
-HANDED = (0, 1, 2, 3, 8, 9, 4, 5, 6, 7, 12, 13, 14, 15, 10, 11)
+FIRST = (0, 5, 3, 7, 6, 4, 1, 2)
+SECOND = (7, 1, 4, 5, 3, 0, 2, 6)
 
 
 def correlate_kernel(*refs):
@@ -221,20 +222,26 @@
     return jnp.max(others, axis=0).reshape(values.shape)
 
 
-def arrange_kernel(offset_ref, coeffs_ref, out_ref):
+def arrange_kernel(order, offset_ref, coeffs_ref, out_ref):
     bases = coeffs_ref.shape[2]
+    rows = bases // len(order)
     source = lax.broadcasted_iota(jnp.int32, (bases, bases), 0)
-    target = lax.broadcasted_iota(jnp.int32, (bases, bases), 1) ^ offset_ref[0]
-    select = jnp.where(source == target, 1.0, 0.0).astype(jnp.bfloat16)
+    column = lax.broadcasted_iota(jnp.int32, (1, bases), 1)
+    target = column
+    for group, place in enumerate(order):
+        if group != place:
+            inside = (column >= group * rows) & (column < (group + 1) * rows)
+            target = jnp.where(inside, column + (place - group) * rows, target)
+    select = jnp.where(source == (target ^ offset_ref[0]), 1.0, 0.0).astype(jnp.bfloat16)
     for section in range(coeffs_ref.shape[0]):
         out_ref[section] = jnp.dot(
             coeffs_ref[section], select, preferred_element_type=jnp.float32
         ).astype(out_ref.dtype)
 
 
-def arrange(coeffs, offset):
+def arrange(coeffs, offset, order):
     return pl.pallas_call(
-        arrange_kernel,
+        functools.partial(arrange_kernel, order),
         out_shape=jax.ShapeDtypeStruct(coeffs.shape, coeffs.dtype),
         in_specs=[
             pl.BlockSpec(memory_space=pltpu.SMEM),
@@ -251,10 +258,50 @@
     )(offset, coeffs)
 
 
-def recon_kernel(order, coeffs_ref, *refs):
+def section_product(coeffs_ref, pieces, samples, section, place, size, at):
+    first = sum(samples >> s for s in range(section)) + place
+    basis = jnp.concatenate([ref[:, first : first + size] for ref in pieces], axis=0)
+    left = coeffs_ref[section, :, at : at + basis.shape[0]]
+    return jnp.dot(left, basis, preferred_element_type=jnp.float32)
+
+
+def partial_kernel(order, samples, coeffs_ref, *refs):
+    pieces, out_ref = [refs[order.index(place)] for place in range(len(order))], refs[-1]
+    for section in range(coeffs_ref.shape[0]):
+        width = samples >> section
+        offset = sum(samples >> s for s in range(section))
+        for place in range(0, width, 2 * LANE):
+            size = min(2 * LANE, width)
+            out_ref[:, offset + place : offset + place + size] = section_product(
+                coeffs_ref, pieces, samples, section, place, size, 0
+            )
+
+
+def partial_sums(coeffs, blocks, samples):
+    order = FIRST if len(FIRST) == len(blocks) else tuple(range(len(blocks)))
+    rows, width = sum(block.shape[0] for block in blocks), blocks[0].shape[1]
+    return pl.pallas_call(
+        functools.partial(partial_kernel, order, samples),
+        out_shape=pltpu.VMEM((coeffs.shape[1], width), jnp.float32),
+        in_specs=[pl.BlockSpec(memory_space=pltpu.VMEM)] * (1 + len(blocks)),
+        out_specs=pl.BlockSpec(memory_space=pltpu.VMEM),
+        compiler_params=pltpu.CompilerParams(vmem_limit_bytes=16 * 2**20),
+        cost_estimate=pl.CostEstimate(
+            flops=2 * coeffs.shape[1] * rows * width,
+            bytes_accessed=4 * coeffs.shape[1] * width + 2 * rows * width,
+            transcendentals=0,
+        ),
+        name="partial_sums",
+    )(coeffs, *[blocks[place] for place in order])
+
+
+def recon_kernel(order, begun, *refs):
+    coeffs_ref, refs = refs[0], refs[1:]
+    first_ref, refs = (refs[0], refs[1:]) if begun else (None, refs)
     pieces = [refs[order.index(place)] for place in range(len(order))]
     snr_ref, peak_ref = refs[-2], refs[-1]
     samples = snr_ref.shape[1]
+    at = coeffs_ref.shape[2] - sum(piece.shape[0] for piece in pieces)
     source = lax.broadcasted_iota(jnp.int32, (2 * LANE, 2 * LANE), 0) % LANE
     target = lax.broadcasted_iota(jnp.int32, (2 * LANE, 2 * LANE), 1) // 2
     repeat = jnp.where(source == target, 1.0, 0.0).astype(jnp.bfloat16)
@@ -265,9 +312,9 @@
         summed = []
         for place in range(0, width, 2 * LANE):
             size = min(2 * LANE, width)
-            first = offset + place
-            basis = jnp.concatenate([ref[:, first : first + size] for ref in pieces], axis=0)
-            part = jnp.dot(coeffs_ref[section], basis, preferred_element_type=jnp.float32)
+            part = section_product(coeffs_ref, pieces, samples, section, place, size, at)
+            if begun:
+                part = part + first_ref[:, offset + place : offset + place + size]
             if running is not None:
                 coarse = running[place // (2 * LANE)]
                 high = coarse.astype(jnp.bfloat16)
@@ -280,7 +327,7 @@
             summed.append(part)
         running = []
         for part in summed:
-            running += [part[:, at : at + LANE] for at in range(0, part.shape[1], LANE)]
+            running += [part[:, at_ : at_ + LANE] for at_ in range(0, part.shape[1], LANE)]
         if section == 0:
             for number, part in enumerate(summed):
                 place = number * 2 * LANE
@@ -290,28 +337,37 @@
                 )
 
 
-def reconstruct(coeffs, blocks, samples):
-    order = HANDED if len(HANDED) == len(blocks) else tuple(range(len(blocks)))
+def reconstruct(coeffs, first, blocks, samples):
+    order = SECOND if len(SECOND) == len(blocks) else tuple(range(len(blocks)))
+    begun = () if first is None else (first,)
     return pl.pallas_call(
-        functools.partial(recon_kernel, order),
+        functools.partial(recon_kernel, order, bool(begun)),
         out_shape=(
             jax.ShapeDtypeStruct((coeffs.shape[1], samples), jnp.bfloat16),
             jax.ShapeDtypeStruct((1, samples), jnp.float32),
         ),
-        in_specs=[pl.BlockSpec(memory_space=pltpu.VMEM)] * (1 + len(blocks)),
+        in_specs=[pl.BlockSpec(memory_space=pltpu.VMEM)] * (1 + len(begun) + len(blocks)),
         out_specs=(pl.BlockSpec(memory_space=pltpu.VMEM),) * 2,
         compiler_params=pltpu.CompilerParams(vmem_limit_bytes=16 * 2**20),
         name="reconstruct",
-    )(coeffs, *[blocks[place] for place in order])
+    )(coeffs, *begun, *[blocks[place] for place in order])
 
 
 def per_device(strain_fast, strain_half, strain_quarter, strain_eighth, basis_taps, recon_coeffs):
     streams = (strain_fast, strain_half, strain_quarter, strain_eighth)
     samples = strain_fast.shape[0] - basis_taps.shape[2]
-    offset = (lax.axis_index("tmpl") * basis_taps.shape[1]).astype(jnp.int32).reshape(1)
-    coeffs = arrange(recon_coeffs, offset)
+    rows = basis_taps.shape[1]
+    places = tuple(range(lax.axis_size("tmpl")))
+    early = places[::2] if rows % SUB == 0 else ()
+    order = early + tuple(place for place in places if place not in early)
+    offset = (lax.axis_index("tmpl") * rows).astype(jnp.int32).reshape(1)
+    coeffs = arrange(recon_coeffs, offset, order)
     blocks, coeffs = gather_blocks(correlate(streams, basis_taps), coeffs)
-    snr_series, local_peak = reconstruct(coeffs, blocks, samples)
+    first = None
+    if early:
+        first = partial_sums(coeffs, blocks[::2], samples)
+        blocks = blocks[1::2]
+    snr_series, local_peak = reconstruct(coeffs, first, blocks, samples)
     peak_snr = maximum_over_group(local_peak.reshape(samples))
     return (snr_series, peak_snr)
 

time: 43.3 us -> 45.2 us (1.044)
  blocking collectives: 11.7 us -> 13.4 us
  waiting for transfers between devices: 6.28 us -> 6.89 us
  starting transfers between devices: 14 us -> 13.5 us
    all_to_all x1, blocking collectives: 11.7 us -> 13.4 us  [maximum_over_group(): lax.all_to_all(copies, 'tmpl', split_axis=0, concat_axis=0, tiled=True)]
    ppermute x15, waiting for transfers between devices: 6.28 us -> 6.89 us  [exchange(): return lax.ppermute(block, 'tmpl', [(i, i ^ distance) for i in range(size)])]
    ppermute x15, starting transfers between devices: 14 us -> 13.5 us  [exchange(): return lax.ppermute(block, 'tmpl', [(i, i ^ distance) for i in range(size)])]
    pallas_call x2 -> x3, Pallas kernels: 2.7 us -> 2.8 us  [the longest x1 1.63 us: reconstruct(): pl.pallas_call(functools.partial(recon_kernel, order, bool(begun)), out_s...]
  transfers between devices with their start and end apart: 15 -> 15, of which waited for: 7 -> 6; matrix products, arithmetic and copies ran while one was open for 0% -> 0% of each run, Pallas kernels for 2% -> 3%
where the time goes in v16:
time: 45.2 us; the launch traced here: 45 us
  starting transfers between devices  13.5 us (30%)
  blocking collectives  13.4 us (30%)
  Pallas kernels  9.93 us (22%)
  waiting for transfers between devices  6.89 us (15%)
  between operations  0.7 us (2%)
  other arithmetic  0.61 us (1%)
    ppermute x15, starting transfers between devices, exchange(): return lax.ppermute(block, 'tmpl', [(i, i ^ distance) for i in range(size)])  13.5 us
    all_to_all x1, blocking collectives, maximum_over_group(): lax.all_to_all(copies, 'tmpl', split_axis=0, concat_axis=0, tiled=True)  13.4 us
    pallas_call x1, Pallas kernels, correlate(): pl.pallas_call(correlate_kernel, out_shape=pltpu.VMEM((padded, samples),...  7.13 us
    ppermute x15, waiting for transfers between devices, exchange(): return lax.ppermute(block, 'tmpl', [(i, i ^ distance) for i in range(size)])  6.89 us
    pallas_call x1, Pallas kernels, reconstruct(): pl.pallas_call(functools.partial(recon_kernel, order, bool(begun)), out_s...  1.63 us
  transfers between devices with their start and end apart: 15, of which 6 were waited for; matrix products, arithmetic and copies ran while one was open for 0% of the time, Pallas kernels for 3%

profile of v16, /device:TPU:0, one launch (start us, length us, event | category | flops | bytes accessed | tf_op | source)
XLA Modules:
  0.0 45.0 jit_solution(12277701378642970411)
XLA Ops:
  0.6 0.0 copy-start
  0.6 7.1 %correlate.1.refs_0_ = bf16[32,1920]{1,0:T(8,128)(2,1)S(1)} custom-call(bf16[72,128]{1,0:T(8,128)(2,1)} %bitcast.9, bf16[68,128]{1,0:T(8,128)(2,1)} %bitcast.10, bf16[66,128]{1,0:T(8,128)(2,1)} %bitcast.11, bf16[65,128]{1,0:T(8,128)(2,1)} %bitcast.12, bf16[4,32,8192]{2,1,0:T(8,128)(2,1)} %refs_4_.1), custom_call_target="tpu_custom_call" | custom-call | flops 1006632960 | bytes 2097152 | tf_op jit(solution)/shard_map/correlate/pallas_call | solution.py:166
  7.8 4.1 %collective-permute-start = (bf16[32,1920]{1,0:T(8,128)(2,1)S(1)}, bf16[32,1920]{1,0:T(8,128)(2,1)S(1)}, u32[]{:S(2)}, u32[]{:S(2)}) collective-permute-start(bf16[32,1920]{1,0:T(8,128)(2,1)S(1)} %correlate.1.refs_0_), channel_id=1, source_target_pairs={{0,8},{1,9},{2,10},{3,11},{4,12},{5,13},{6,14},{7,15},{8,0},{9,1},... | collective-permute-start | bytes 368648 | tf_op jit(solution)/shard_map/ppermute | solution.py:192
  11.9 1.6 %collective-permute-start.2 = (bf16[32,1920]{1,0:T(8,128)(2,1)S(1)}, bf16[32,1920]{1,0:T(8,128)(2,1)S(1)}, u32[]{:S(2)}, u32[]{:S(2)}) collective-permute-start(bf16[32,1920]{1,0:T(8,128)(2,1)S(1)} %correlate.1.refs_0_), channel_id=1, source_target_pairs={{0,4},{1,5},{2,6},{3,7},{4,0},{5,1},{6,2},{7,3},{8,12},{9,13},{10,... | collective-permute-start | bytes 368648 | tf_op jit(solution)/shard_map/ppermute | solution.py:192
  13.5 1.5 %collective-permute-start.6 = (bf16[32,1920]{1,0:T(8,128)(2,1)S(1)}, bf16[32,1920]{1,0:T(8,128)(2,1)S(1)}, u32[]{:S(2)}, u32[]{:S(2)}) collective-permute-start(bf16[32,1920]{1,0:T(8,128)(2,1)S(1)} %correlate.1.refs_0_), channel_id=1, source_target_pairs={{0,2},{1,3},{2,0},{3,1},{4,6},{5,7},{6,4},{7,5},{8,10},{9,11},{10,... | collective-permute-start | bytes 368648 | tf_op jit(solution)/shard_map/ppermute | solution.py:192
  15.0 0.0 copy-done
  15.0 0.7 %arrange.1.coeffs_ref.refs_0_ = bf16[4,256,512]{2,1,0:T(8,128)(2,1)S(1)} custom-call(s32[1]{0:T(128)} %bitcast.4.offset_ref, bf16[4,256,512]{2,1,0:T(8,128)(2,1)S(1)} %copy-done), custom_call_target="tpu_custom_call" | custom-call | flops 536870912 | bytes 2097152 | tf_op jit(solution)/shard_map/arrange/pallas_call | solution.py:243
  15.7 0.1 collective-permute-start.12
  15.8 2.1 %collective-permute-done.refs_5_ = bf16[32,1920]{1,0:T(8,128)(2,1)S(1)} collective-permute-done((bf16[32,1920]{1,0:T(8,128)(2,1)S(1)}, bf16[32,1920]{1,0:T(8,128)(2,1)S(1)}, u32[]{:S(2)}, u32[]{:S(2)}) %collective-permute-start) | collective-permute-done | bytes 122912 | tf_op jit(solution)/shard_map/ppermute | solution.py:192
  17.9 1.6 %collective-permute-start.1 = (bf16[32,1920]{1,0:T(8,128)(2,1)S(1)}, bf16[32,1920]{1,0:T(8,128)(2,1)S(1)}, u32[]{:S(2)}, u32[]{:S(2)}) collective-permute-start(bf16[32,1920]{1,0:T(8,128)(2,1)S(1)} %collective-permute-done.refs_5_), channel_id=1, source_target_pairs={{0,2},{1,3},{2,0},{3,1},{4,6},{5,7},{6,4},{7,5},{8,10},{9,11},{10,... | collective-permute-start | bytes 368648 | tf_op jit(solution)/shard_map/ppermute | solution.py:192
  19.5 0.5 %collective-permute-start.4 = (bf16[32,1920]{1,0:T(8,128)(2,1)S(1)}, bf16[32,1920]{1,0:T(8,128)(2,1)S(1)}, u32[]{:S(2)}, u32[]{:S(2)}) collective-permute-start(bf16[32,1920]{1,0:T(8,128)(2,1)S(1)} %collective-permute-done.refs_5_), channel_id=1, source_target_pairs={{0,6},{1,7},{2,4},{3,5},{4,2},{5,3},{6,0},{7,1},{8,14},{9,15},{10,... | collective-permute-start | bytes 368648 | tf_op jit(solution)/shard_map/ppermute | solution.py:192
  20.0 0.0 collective-permute-done.2.refs_7_
  20.0 1.4 %collective-permute-start.5 = (bf16[32,1920]{1,0:T(8,128)(2,1)S(1)}, bf16[32,1920]{1,0:T(8,128)(2,1)S(1)}, u32[]{:S(2)}, u32[]{:S(2)}) collective-permute-start(bf16[32,1920]{1,0:T(8,128)(2,1)S(1)} %collective-permute-done.refs_5_), channel_id=1, source_target_pairs={{0,4},{1,5},{2,6},{3,7},{4,0},{5,1},{6,2},{7,3},{8,12},{9,13},{10,... | collective-permute-start | bytes 368648 | tf_op jit(solution)/shard_map/ppermute | solution.py:192
  21.4 0.0 collective-permute-done.6.refs_6_
  21.4 1.6 %collective-permute-start.3 = (bf16[32,1920]{1,0:T(8,128)(2,1)S(1)}, bf16[32,1920]{1,0:T(8,128)(2,1)S(1)}, u32[]{:S(2)}, u32[]{:S(2)}) collective-permute-start(bf16[32,1920]{1,0:T(8,128)(2,1)S(1)} %collective-permute-done.2.refs_7_), channel_id=1, source_target_pairs={{0,2},{1,3},{2,0},{3,1},{4,6},{5,7},{6,4},{7,5},{8,10},{9,11},{10,... | collective-permute-start | bytes 368648 | tf_op jit(solution)/shard_map/ppermute | solution.py:192
  23.0 0.0 collective-permute-done.12.refs_7_
  23.0 0.0 collective-permute-start.9
  23.0 3.1 %collective-permute-done.1.refs_1_ = bf16[32,1920]{1,0:T(8,128)(2,1)S(1)} collective-permute-done((bf16[32,1920]{1,0:T(8,128)(2,1)S(1)}, bf16[32,1920]{1,0:T(8,128)(2,1)S(1)}, u32[]{:S(2)}, u32[]{:S(2)}) %collective-permute-start.1) | collective-permute-done | bytes 122912 | tf_op jit(solution)/shard_map/ppermute | solution.py:192
  26.1 0.0 collective-permute-start.13
  26.1 0.0 collective-permute-done.4.refs_3_
  26.2 0.5 %collective-permute-start.8 = (bf16[32,1920]{1,0:T(8,128)(2,1)S(1)}, bf16[32,1920]{1,0:T(8,128)(2,1)S(1)}, u32[]{:S(2)}, u32[]{:S(2)}) collective-permute-start(bf16[32,1920]{1,0:T(8,128)(2,1)S(1)} %collective-permute-done.6.refs_6_), channel_id=1, source_target_pairs={{0,1},{1,0},{2,3},{3,2},{4,5},{5,4},{6,7},{7,6},{8,9},{9,8},{10,11... | collective-permute-start | bytes 368648 | tf_op jit(solution)/shard_map/ppermute | solution.py:192
  26.7 0.0 collective-permute-done.5.refs_4_
  26.7 0.1 collective-permute-start.10
  26.7 0.8 %collective-permute-done.3.refs_2_ = bf16[32,1920]{1,0:T(8,128)(2,1)S(1)} collective-permute-done((bf16[32,1920]{1,0:T(8,128)(2,1)S(1)}, bf16[32,1920]{1,0:T(8,128)(2,1)S(1)}, u32[]{:S(2)}, u32[]{:S(2)}) %collective-permute-start.3) | collective-permute-done | bytes 122912 | tf_op jit(solution)/shard_map/ppermute | solution.py:192
  27.5 0.0 collective-permute-start.14
  27.5 0.0 collective-permute-done.9.refs_4_
  27.5 0.5 %collective-permute-start.7 = (bf16[32,1920]{1,0:T(8,128)(2,1)S(1)}, bf16[32,1920]{1,0:T(8,128)(2,1)S(1)}, u32[]{:S(2)}, u32[]{:S(2)}) collective-permute-start(bf16[32,1920]{1,0:T(8,128)(2,1)S(1)} %collective-permute-done.4.refs_3_), channel_id=1, source_target_pairs={{0,1},{1,0},{2,3},{3,2},{4,5},{5,4},{6,7},{7,6},{8,9},{9,8},{10,11... | collective-permute-start | bytes 368648 | tf_op jit(solution)/shard_map/ppermute | solution.py:192
  28.0 0.0 collective-permute-done.13.refs_8_
  28.0 0.1 collective-permute-start.11
  28.1 0.4 partial_sums.1.refs_1_
  28.6 0.0 collective-permute-done.8.refs_3_
  28.6 0.0 collective-permute-done.10.refs_5_
  28.6 0.3 collective-permute-done.14.refs_9_
  28.9 0.2 collective-permute-done.7.refs_2_
  29.0 0.3 collective-permute-done.11.refs_6_
  29.4 1.6 %reconstruct.1 = (bf16[256,1024]{1,0:T(8,128)(2,1)}, f32[1,1024]{1,0:T(1,128)S(1)}) custom-call(bf16[4,256,512]{2,1,0:T(8,128)(2,1)S(1)} %arrange.1.coeffs_ref.refs_0_, f32[256,1920]{1,0:T(8,128)S(1)} %partial_sums.1.refs_1_, bf16[32,1920]{1,0:T(8,128)(2,1)S(1)} %collective-permute-done.7.refs_2_, bf16[32,1920]{1,0:T(8,128)(2,1)S(1)} %collective-permute-done.8.refs_3_, ...), custom_call_target="tpu_custom_call" | custom-call | tf_op jit(solution)/shard_map/reconstruct/pallas_call | solution.py:343
  31.0 13.4 %all_to_all.5 = f32[16,8,128]{2,1,0:T(8,128)S(1)} all-to-all(f32[16,8,128]{2,1,0:T(8,128)S(1)} %broadcast_in_dim.8), channel_id=1, replica_groups=mesh['bank'=2,'tmpl'=16] {'tmpl'}, dimensions={0} | all-to-all | bytes 131072 | tf_op jit(solution)/shard_map/all_to_all | solution.py:221
  44.4 0.6 %reduce_max.9 = f32[8,128]{1,0:T(8,128)} reduce(f32[16,8,128]{2,1,0:T(8,128)S(1)} %all_to_all.5, f32[]{:T(128)} %constant.2.clone.1), dimensions={0}, to_apply=%region_0.0 | reduce | flops 15360 | bytes 69636 | tf_op jit(solution)/shard_map/reduce_max | solution.py:222
  (1 shorter events, 0.0 us)
Async XLA Ops:
  0.6 14.3 %copy-start = (bf16[4,256,512]{2,1,0:T(8,128)(2,1)S(1)}, bf16[4,256,512]{2,1,0:T(8,128)(2,1)}, u32[]{:S(2)}) copy-start(bf16[4,256,512]{2,1,0:T(8,128)(2,1)} %coeffs_ref.1) | copy-start | bytes 3145732
  7.8 10.2 %collective-permute-start = (bf16[32,1920]{1,0:T(8,128)(2,1)S(1)}, bf16[32,1920]{1,0:T(8,128)(2,1)S(1)}, u32[]{:S(2)}, u32[]{:S(2)}) collective-permute-start(bf16[32,1920]{1,0:T(8,128)(2,1)S(1)} %correlate.1.refs_0_), channel_id=1, source_target_pairs={{0,8},{1,9},{2,10},{3,11},{4,12},{5,13},{6,14},{7,15},{8,0},{9,1},... | collective-permute-start | bytes 368648 | tf_op jit(solution)/shard_map/ppermute | solution.py:192
  11.9 8.1 %collective-permute-start.2 = (bf16[32,1920]{1,0:T(8,128)(2,1)S(1)}, bf16[32,1920]{1,0:T(8,128)(2,1)S(1)}, u32[]{:S(2)}, u32[]{:S(2)}) collective-permute-start(bf16[32,1920]{1,0:T(8,128)(2,1)S(1)} %correlate.1.refs_0_), channel_id=1, source_target_pairs={{0,4},{1,5},{2,6},{3,7},{4,0},{5,1},{6,2},{7,3},{8,12},{9,13},{10,... | collective-permute-start | bytes 368648 | tf_op jit(solution)/shard_map/ppermute | solution.py:192
  13.5 8.0 %collective-permute-start.6 = (bf16[32,1920]{1,0:T(8,128)(2,1)S(1)}, bf16[32,1920]{1,0:T(8,128)(2,1)S(1)}, u32[]{:S(2)}, u32[]{:S(2)}) collective-permute-start(bf16[32,1920]{1,0:T(8,128)(2,1)S(1)} %correlate.1.refs_0_), channel_id=1, source_target_pairs={{0,2},{1,3},{2,0},{3,1},{4,6},{5,7},{6,4},{7,5},{8,10},{9,11},{10,... | collective-permute-start | bytes 368648 | tf_op jit(solution)/shard_map/ppermute | solution.py:192
  15.7 7.3 %collective-permute-start.12 = (bf16[32,1920]{1,0:T(8,128)(2,1)S(1)}, bf16[32,1920]{1,0:T(8,128)(2,1)S(1)}, u32[]{:S(2)}, u32[]{:S(2)}) collective-permute-start(bf16[32,1920]{1,0:T(8,128)(2,1)S(1)} %correlate.1.refs_0_), channel_id=1, source_target_pairs={{0,1},{1,0},{2,3},{3,2},{4,5},{5,4},{6,7},{7,6},{8,9},{9,8},{10,11... | collective-permute-start | bytes 368648 | tf_op jit(solution)/shard_map/ppermute | solution.py:192
  17.9 8.2 %collective-permute-start.1 = (bf16[32,1920]{1,0:T(8,128)(2,1)S(1)}, bf16[32,1920]{1,0:T(8,128)(2,1)S(1)}, u32[]{:S(2)}, u32[]{:S(2)}) collective-permute-start(bf16[32,1920]{1,0:T(8,128)(2,1)S(1)} %collective-permute-done.refs_5_), channel_id=1, source_target_pairs={{0,2},{1,3},{2,0},{3,1},{4,6},{5,7},{6,4},{7,5},{8,10},{9,11},{10,... | collective-permute-start | bytes 368648 | tf_op jit(solution)/shard_map/ppermute | solution.py:192
  19.5 6.6 %collective-permute-start.4 = (bf16[32,1920]{1,0:T(8,128)(2,1)S(1)}, bf16[32,1920]{1,0:T(8,128)(2,1)S(1)}, u32[]{:S(2)}, u32[]{:S(2)}) collective-permute-start(bf16[32,1920]{1,0:T(8,128)(2,1)S(1)} %collective-permute-done.refs_5_), channel_id=1, source_target_pairs={{0,6},{1,7},{2,4},{3,5},{4,2},{5,3},{6,0},{7,1},{8,14},{9,15},{10,... | collective-permute-start | bytes 368648 | tf_op jit(solution)/shard_map/ppermute | solution.py:192
  20.0 6.6 %collective-permute-start.5 = (bf16[32,1920]{1,0:T(8,128)(2,1)S(1)}, bf16[32,1920]{1,0:T(8,128)(2,1)S(1)}, u32[]{:S(2)}, u32[]{:S(2)}) collective-permute-start(bf16[32,1920]{1,0:T(8,128)(2,1)S(1)} %collective-permute-done.refs_5_), channel_id=1, source_target_pairs={{0,4},{1,5},{2,6},{3,7},{4,0},{5,1},{6,2},{7,3},{8,12},{9,13},{10,... | collective-permute-start | bytes 368648 | tf_op jit(solution)/shard_map/ppermute | solution.py:192
  21.4 6.1 %collective-permute-start.3 = (bf16[32,1920]{1,0:T(8,128)(2,1)S(1)}, bf16[32,1920]{1,0:T(8,128)(2,1)S(1)}, u32[]{:S(2)}, u32[]{:S(2)}) collective-permute-start(bf16[32,1920]{1,0:T(8,128)(2,1)S(1)} %collective-permute-done.2.refs_7_), channel_id=1, source_target_pairs={{0,2},{1,3},{2,0},{3,1},{4,6},{5,7},{6,4},{7,5},{8,10},{9,11},{10,... | collective-permute-start | bytes 368648 | tf_op jit(solution)/shard_map/ppermute | solution.py:192
  23.0 4.5 %collective-permute-start.9 = (bf16[32,1920]{1,0:T(8,128)(2,1)S(1)}, bf16[32,1920]{1,0:T(8,128)(2,1)S(1)}, u32[]{:S(2)}, u32[]{:S(2)}) collective-permute-start(bf16[32,1920]{1,0:T(8,128)(2,1)S(1)} %collective-permute-done.refs_5_), channel_id=1, source_target_pairs={{0,1},{1,0},{2,3},{3,2},{4,5},{5,4},{6,7},{7,6},{8,9},{9,8},{10,11... | collective-permute-start | bytes 368648 | tf_op jit(solution)/shard_map/ppermute | solution.py:192
  26.1 1.9 %collective-permute-start.13 = (bf16[32,1920]{1,0:T(8,128)(2,1)S(1)}, bf16[32,1920]{1,0:T(8,128)(2,1)S(1)}, u32[]{:S(2)}, u32[]{:S(2)}) collective-permute-start(bf16[32,1920]{1,0:T(8,128)(2,1)S(1)} %collective-permute-done.2.refs_7_), channel_id=1, source_target_pairs={{0,1},{1,0},{2,3},{3,2},{4,5},{5,4},{6,7},{7,6},{8,9},{9,8},{10,11... | collective-permute-start | bytes 368648 | tf_op jit(solution)/shard_map/ppermute | solution.py:192
  26.2 2.4 %collective-permute-start.8 = (bf16[32,1920]{1,0:T(8,128)(2,1)S(1)}, bf16[32,1920]{1,0:T(8,128)(2,1)S(1)}, u32[]{:S(2)}, u32[]{:S(2)}) collective-permute-start(bf16[32,1920]{1,0:T(8,128)(2,1)S(1)} %collective-permute-done.6.refs_6_), channel_id=1, source_target_pairs={{0,1},{1,0},{2,3},{3,2},{4,5},{5,4},{6,7},{7,6},{8,9},{9,8},{10,11... | collective-permute-start | bytes 368648 | tf_op jit(solution)/shard_map/ppermute | solution.py:192
  26.7 1.9 %collective-permute-start.10 = (bf16[32,1920]{1,0:T(8,128)(2,1)S(1)}, bf16[32,1920]{1,0:T(8,128)(2,1)S(1)}, u32[]{:S(2)}, u32[]{:S(2)}) collective-permute-start(bf16[32,1920]{1,0:T(8,128)(2,1)S(1)} %collective-permute-done.1.refs_1_), channel_id=1, source_target_pairs={{0,1},{1,0},{2,3},{3,2},{4,5},{5,4},{6,7},{7,6},{8,9},{9,8},{10,11... | collective-permute-start | bytes 368648 | tf_op jit(solution)/shard_map/ppermute | solution.py:192
  27.5 1.3 %collective-permute-start.14 = (bf16[32,1920]{1,0:T(8,128)(2,1)S(1)}, bf16[32,1920]{1,0:T(8,128)(2,1)S(1)}, u32[]{:S(2)}, u32[]{:S(2)}) collective-permute-start(bf16[32,1920]{1,0:T(8,128)(2,1)S(1)} %collective-permute-done.5.refs_4_), channel_id=1, source_target_pairs={{0,1},{1,0},{2,3},{3,2},{4,5},{5,4},{6,7},{7,6},{8,9},{9,8},{10,11... | collective-permute-start | bytes 368648 | tf_op jit(solution)/shard_map/ppermute | solution.py:192
  27.5 1.5 %collective-permute-start.7 = (bf16[32,1920]{1,0:T(8,128)(2,1)S(1)}, bf16[32,1920]{1,0:T(8,128)(2,1)S(1)}, u32[]{:S(2)}, u32[]{:S(2)}) collective-permute-start(bf16[32,1920]{1,0:T(8,128)(2,1)S(1)} %collective-permute-done.4.refs_3_), channel_id=1, source_target_pairs={{0,1},{1,0},{2,3},{3,2},{4,5},{5,4},{6,7},{7,6},{8,9},{9,8},{10,11... | collective-permute-start | bytes 368648 | tf_op jit(solution)/shard_map/ppermute | solution.py:192
  28.0 1.3 %collective-permute-start.11 = (bf16[32,1920]{1,0:T(8,128)(2,1)S(1)}, bf16[32,1920]{1,0:T(8,128)(2,1)S(1)}, u32[]{:S(2)}, u32[]{:S(2)}) collective-permute-start(bf16[32,1920]{1,0:T(8,128)(2,1)S(1)} %collective-permute-done.3.refs_2_), channel_id=1, source_target_pairs={{0,1},{1,0},{2,3},{3,2},{4,5},{5,4},{6,7},{7,6},{8,9},{9,8},{10,11... | collective-permute-start | bytes 368648 | tf_op jit(solution)/shard_map/ppermute | solution.py:192

commit v17 on v14

--- a/solution.py
+++ b/solution.py
@@ -13,7 +13,7 @@
 ROWS = 8
 ROLLS = 4
 TIED = 1
-HANDED = (0, 1, 2, 3, 8, 9, 4, 5, 6, 7, 12, 13, 14, 15, 10, 11)
+HANDED = (6, 7, 2, 3, 0, 1, 12, 13, 8, 9, 10, 11, 4, 5, 14, 15)
 
 
 def correlate_kernel(*refs):
@@ -204,9 +204,14 @@
     held = {0: block}
     for place in range(2, size, 2):
         high = 1 << (place.bit_length() - 1)
-        held[place] = exchange(held[place ^ high and high], place ^ high or place)
+        if place in (high, size - 2):
+            held[place] = exchange(block, place)
+        else:
+            held[place] = exchange(held[high], place ^ high)
     for place in range(1, size, 2):
         source = held[place ^ 1]
+        if place == size - 1:
+            source, held[place - 9] = lax.optimization_barrier((source, held[place - 9]))
         if place == TIED:
             source, ready = lax.optimization_barrier((source, ready))
         held[place] = exchange(source, 1)

time: 43.3 us -> 45.2 us (1.044)
  waiting for transfers between devices: 6.28 us -> 8.87 us
  blocking collectives: 11.7 us -> 11 us
    ppermute x15, waiting for transfers between devices: 6.28 us -> 8.87 us  [exchange(): return lax.ppermute(block, 'tmpl', [(i, i ^ distance) for i in range(size)])]
    all_to_all x1, blocking collectives: 11.7 us -> 11 us  [maximum_over_group(): lax.all_to_all(copies, 'tmpl', split_axis=0, concat_axis=0, tiled=True)]
  transfers between devices with their start and end apart: 15 -> 15, of which waited for: 7 -> 6; matrix products, arithmetic and copies ran while one was open for 0% -> 0% of each run, Pallas kernels for 2% -> 2%
where the time goes in v17:
time: 45.2 us; the launch traced here: 45 us
  starting transfers between devices  14 us (31%)
  blocking collectives  11 us (24%)
  Pallas kernels  9.82 us (22%)
  waiting for transfers between devices  8.87 us (20%)
  between operations  0.69 us (2%)
  other arithmetic  0.61 us (1%)
    ppermute x15, starting transfers between devices, exchange(): return lax.ppermute(block, 'tmpl', [(i, i ^ distance) for i in range(size)])  14 us
    all_to_all x1, blocking collectives, maximum_over_group(): lax.all_to_all(copies, 'tmpl', split_axis=0, concat_axis=0, tiled=True)  11 us
    ppermute x15, waiting for transfers between devices, exchange(): return lax.ppermute(block, 'tmpl', [(i, i ^ distance) for i in range(size)])  8.87 us
    pallas_call x1, Pallas kernels, correlate(): pl.pallas_call(correlate_kernel, out_shape=pltpu.VMEM((padded, samples),...  7.13 us
    pallas_call x1, Pallas kernels, reconstruct(): pl.pallas_call(functools.partial(recon_kernel, order), out_shape=(jax.Sha...  1.98 us
  transfers between devices with their start and end apart: 15, of which 6 were waited for; matrix products, arithmetic and copies ran while one was open for 0% of the time, Pallas kernels for 2%

profile of v17, /device:TPU:0, one launch (start us, length us, event | category | flops | bytes accessed | tf_op | source)
XLA Modules:
  0.0 45.0 jit_solution(14310879942037943920)
XLA Ops:
  0.6 0.0 copy-start
  0.6 7.1 %correlate.1.refs_4_ = bf16[32,1920]{1,0:T(8,128)(2,1)S(1)} custom-call(bf16[72,128]{1,0:T(8,128)(2,1)} %bitcast.9, bf16[68,128]{1,0:T(8,128)(2,1)} %bitcast.10, bf16[66,128]{1,0:T(8,128)(2,1)} %bitcast.11, bf16[65,128]{1,0:T(8,128)(2,1)} %bitcast.12, bf16[4,32,8192]{2,1,0:T(8,128)(2,1)} %refs_4_.1), custom_call_target="tpu_custom_call" | custom-call | flops 1006632960 | bytes 2097152 | tf_op jit(solution)/shard_map/correlate/pallas_call | solution.py:165
  7.8 3.1 %collective-permute-start.1 = (bf16[32,1920]{1,0:T(8,128)(2,1)S(1)}, bf16[32,1920]{1,0:T(8,128)(2,1)S(1)}, u32[]{:S(2)}, u32[]{:S(2)}) collective-permute-start(bf16[32,1920]{1,0:T(8,128)(2,1)S(1)} %correlate.1.refs_4_), channel_id=1, source_target_pairs={{0,4},{1,5},{2,6},{3,7},{4,0},{5,1},{6,2},{7,3},{8,12},{9,13},{10,... | collective-permute-start | bytes 368648 | tf_op jit(solution)/shard_map/ppermute | solution.py:191
  10.9 2.6 %collective-permute-start.7 = (bf16[32,1920]{1,0:T(8,128)(2,1)S(1)}, bf16[32,1920]{1,0:T(8,128)(2,1)S(1)}, u32[]{:S(2)}, u32[]{:S(2)}) collective-permute-start(bf16[32,1920]{1,0:T(8,128)(2,1)S(1)} %correlate.1.refs_4_), channel_id=1, source_target_pairs={{0,8},{1,9},{2,10},{3,11},{4,12},{5,13},{6,14},{7,15},{8,0},{9,1},... | collective-permute-start | bytes 368648 | tf_op jit(solution)/shard_map/ppermute | solution.py:191
  13.5 1.5 %collective-permute-start.4 = (bf16[32,1920]{1,0:T(8,128)(2,1)S(1)}, bf16[32,1920]{1,0:T(8,128)(2,1)S(1)}, u32[]{:S(2)}, u32[]{:S(2)}) collective-permute-start(bf16[32,1920]{1,0:T(8,128)(2,1)S(1)} %correlate.1.refs_4_), channel_id=1, source_target_pairs={{0,2},{1,3},{2,0},{3,1},{4,6},{5,7},{6,4},{7,5},{8,10},{9,11},{10,... | collective-permute-start | bytes 368648 | tf_op jit(solution)/shard_map/ppermute | solution.py:191
  15.0 0.0 collective-permute-start
  15.0 0.7 %collective-permute-done.1.refs_12_ = bf16[32,1920]{1,0:T(8,128)(2,1)S(1)} collective-permute-done((bf16[32,1920]{1,0:T(8,128)(2,1)S(1)}, bf16[32,1920]{1,0:T(8,128)(2,1)S(1)}, u32[]{:S(2)}, u32[]{:S(2)}) %collective-permute-start.1) | collective-permute-done | bytes 122912 | tf_op jit(solution)/shard_map/ppermute | solution.py:191
  15.7 1.8 %collective-permute-start.2 = (bf16[32,1920]{1,0:T(8,128)(2,1)S(1)}, bf16[32,1920]{1,0:T(8,128)(2,1)S(1)}, u32[]{:S(2)}, u32[]{:S(2)}) collective-permute-start(bf16[32,1920]{1,0:T(8,128)(2,1)S(1)} %collective-permute-done.1.refs_12_), channel_id=1, source_target_pairs={{0,2},{1,3},{2,0},{3,1},{4,6},{5,7},{6,4},{7,5},{8,10},{9,11},{10,... | collective-permute-start | bytes 368648 | tf_op jit(solution)/shard_map/ppermute | solution.py:191
  17.5 0.0 copy-done
  17.5 0.7 %arrange.1.coeffs_ref = bf16[4,256,512]{2,1,0:T(8,128)(2,1)S(1)} custom-call(s32[1]{0:T(128)} %bitcast.4.offset_ref, bf16[4,256,512]{2,1,0:T(8,128)(2,1)S(1)} %copy-done), custom_call_target="tpu_custom_call" | custom-call | flops 536870912 | bytes 2097152 | tf_op jit(solution)/shard_map/arrange/pallas_call | solution.py:241
  18.3 0.1 collective-permute-start.6
  18.3 4.3 %collective-permute-done.7.refs_8_ = bf16[32,1920]{1,0:T(8,128)(2,1)S(1)} collective-permute-done((bf16[32,1920]{1,0:T(8,128)(2,1)S(1)}, bf16[32,1920]{1,0:T(8,128)(2,1)S(1)}, u32[]{:S(2)}, u32[]{:S(2)}) %collective-permute-start.7) | collective-permute-done | bytes 122912 | tf_op jit(solution)/shard_map/ppermute | solution.py:191
  22.6 1.5 %collective-permute-start.11 = (bf16[32,1920]{1,0:T(8,128)(2,1)S(1)}, bf16[32,1920]{1,0:T(8,128)(2,1)S(1)}, u32[]{:S(2)}, u32[]{:S(2)}) collective-permute-start(bf16[32,1920]{1,0:T(8,128)(2,1)S(1)} %collective-permute-done.7.refs_8_), channel_id=1, source_target_pairs={{0,2},{1,3},{2,0},{3,1},{4,6},{5,7},{6,4},{7,5},{8,10},{9,11},{10,... | collective-permute-start | bytes 368648 | tf_op jit(solution)/shard_map/ppermute | solution.py:191
  24.2 0.0 collective-permute-done.4.refs_2_
  24.2 0.0 collective-permute-start.10
  24.2 0.0 collective-permute-done.refs_14_
  24.2 1.8 %collective-permute-start.8 = (bf16[32,1920]{1,0:T(8,128)(2,1)S(1)}, bf16[32,1920]{1,0:T(8,128)(2,1)S(1)}, u32[]{:S(2)}, u32[]{:S(2)}) collective-permute-start(bf16[32,1920]{1,0:T(8,128)(2,1)S(1)} %collective-permute-done.7.refs_8_), channel_id=1, source_target_pairs={{0,4},{1,5},{2,6},{3,7},{4,0},{5,1},{6,2},{7,3},{8,12},{9,13},{10,... | collective-permute-start | bytes 368648 | tf_op jit(solution)/shard_map/ppermute | solution.py:191
  26.0 0.0 collective-permute-done.2.refs_0_
  26.0 0.0 collective-permute-start.5
  26.0 0.0 collective-permute-done.6.refs_5_
  26.0 0.5 %collective-permute-start.13 = (bf16[32,1920]{1,0:T(8,128)(2,1)S(1)}, bf16[32,1920]{1,0:T(8,128)(2,1)S(1)}, u32[]{:S(2)}, u32[]{:S(2)}) collective-permute-start(bf16[32,1920]{1,0:T(8,128)(2,1)S(1)} %collective-permute-done.1.refs_12_), channel_id=1, source_target_pairs={{0,1},{1,0},{2,3},{3,2},{4,5},{5,4},{6,7},{7,6},{8,9},{9,8},{10,11... | collective-permute-start | bytes 368648 | tf_op jit(solution)/shard_map/ppermute | solution.py:191
  26.5 1.0 %collective-permute-done.11.refs_10_ = bf16[32,1920]{1,0:T(8,128)(2,1)S(1)} collective-permute-done((bf16[32,1920]{1,0:T(8,128)(2,1)S(1)}, bf16[32,1920]{1,0:T(8,128)(2,1)S(1)}, u32[]{:S(2)}, u32[]{:S(2)}) %collective-permute-start.11) | collective-permute-done | bytes 122912 | tf_op jit(solution)/shard_map/ppermute | solution.py:191
  27.5 0.0 collective-permute-start.3
  27.5 0.0 collective-permute-done.10.refs_9_
  27.5 0.5 %collective-permute-start.12 = (bf16[32,1920]{1,0:T(8,128)(2,1)S(1)}, bf16[32,1920]{1,0:T(8,128)(2,1)S(1)}, u32[]{:S(2)}, u32[]{:S(2)}) collective-permute-start(bf16[32,1920]{1,0:T(8,128)(2,1)S(1)} %collective-permute-done.11.refs_10_), channel_id=1, source_target_pairs={{0,1},{1,0},{2,3},{3,2},{4,5},{5,4},{6,7},{7,6},{8,9},{9,8},{10,11... | collective-permute-start | bytes 368648 | tf_op jit(solution)/shard_map/ppermute | solution.py:191
  28.0 1.9 %collective-permute-done.8.refs_6_ = bf16[32,1920]{1,0:T(8,128)(2,1)S(1)} collective-permute-done((bf16[32,1920]{1,0:T(8,128)(2,1)S(1)}, bf16[32,1920]{1,0:T(8,128)(2,1)S(1)}, u32[]{:S(2)}, u32[]{:S(2)}) %collective-permute-start.8) | collective-permute-done | bytes 122912 | tf_op jit(solution)/shard_map/ppermute | solution.py:191
  29.9 0.0 collective-permute-start.9
  29.9 0.0 collective-permute-done.5.refs_3_
  29.9 0.5 %collective-permute-start.14 = (bf16[32,1920]{1,0:T(8,128)(2,1)S(1)}, bf16[32,1920]{1,0:T(8,128)(2,1)S(1)}, u32[]{:S(2)}, u32[]{:S(2)}) collective-permute-start(bf16[32,1920]{1,0:T(8,128)(2,1)S(1)} %collective-permute-done.refs_14_), channel_id=1, source_target_pairs={{0,1},{1,0},{2,3},{3,2},{4,5},{5,4},{6,7},{7,6},{8,9},{9,8},{10,11... | collective-permute-start | bytes 368648 | tf_op jit(solution)/shard_map/ppermute | solution.py:191
  30.4 0.0 collective-permute-done.13.refs_13_
  30.4 0.0 collective-permute-done.12.refs_11_
  30.4 0.8 %collective-permute-done.9.refs_7_ = bf16[32,1920]{1,0:T(8,128)(2,1)S(1)} collective-permute-done((bf16[32,1920]{1,0:T(8,128)(2,1)S(1)}, bf16[32,1920]{1,0:T(8,128)(2,1)S(1)}, u32[]{:S(2)}, u32[]{:S(2)}) %collective-permute-start.9) | collective-permute-done | bytes 122912 | tf_op jit(solution)/shard_map/ppermute | solution.py:191
  31.2 0.0 collective-permute-done.3.refs_1_
  31.2 0.2 collective-permute-done.14.refs_15_
  31.4 2.0 %reconstruct.1 = (bf16[256,1024]{1,0:T(8,128)(2,1)}, f32[1,1024]{1,0:T(1,128)S(1)}) custom-call(bf16[4,256,512]{2,1,0:T(8,128)(2,1)S(1)} %arrange.1.coeffs_ref, bf16[32,1920]{1,0:T(8,128)(2,1)S(1)} %collective-permute-done.2.refs_0_, bf16[32,1920]{1,0:T(8,128)(2,1)S(1)} %collective-permute-done.3.refs_1_, ...), custom_call_target="tpu_custom_call" | custom-call | tf_op jit(solution)/shard_map/reconstruct/pallas_call | solution.py:300
  33.4 11.0 %all_to_all.5 = f32[16,8,128]{2,1,0:T(8,128)S(1)} all-to-all(f32[16,8,128]{2,1,0:T(8,128)S(1)} %broadcast_in_dim.8), channel_id=1, replica_groups=mesh['bank'=2,'tmpl'=16] {'tmpl'}, dimensions={0} | all-to-all | bytes 131072 | tf_op jit(solution)/shard_map/all_to_all | solution.py:225
  44.4 0.6 %reduce_max.9 = f32[8,128]{1,0:T(8,128)} reduce(f32[16,8,128]{2,1,0:T(8,128)S(1)} %all_to_all.5, f32[]{:T(128)} %constant.2.clone.1), dimensions={0}, to_apply=%region_0.0 | reduce | flops 15360 | bytes 69636 | tf_op jit(solution)/shard_map/reduce_max | solution.py:226
  (1 shorter events, 0.0 us)
Async XLA Ops:
  0.6 16.9 %copy-start = (bf16[4,256,512]{2,1,0:T(8,128)(2,1)S(1)}, bf16[4,256,512]{2,1,0:T(8,128)(2,1)}, u32[]{:S(2)}) copy-start(bf16[4,256,512]{2,1,0:T(8,128)(2,1)} %coeffs_ref.1) | copy-start | bytes 3145732
  7.8 7.9 %collective-permute-start.1 = (bf16[32,1920]{1,0:T(8,128)(2,1)S(1)}, bf16[32,1920]{1,0:T(8,128)(2,1)S(1)}, u32[]{:S(2)}, u32[]{:S(2)}) collective-permute-start(bf16[32,1920]{1,0:T(8,128)(2,1)S(1)} %correlate.1.refs_4_), channel_id=1, source_target_pairs={{0,4},{1,5},{2,6},{3,7},{4,0},{5,1},{6,2},{7,3},{8,12},{9,13},{10,... | collective-permute-start | bytes 368648 | tf_op jit(solution)/shard_map/ppermute | solution.py:191
  10.9 11.8 %collective-permute-start.7 = (bf16[32,1920]{1,0:T(8,128)(2,1)S(1)}, bf16[32,1920]{1,0:T(8,128)(2,1)S(1)}, u32[]{:S(2)}, u32[]{:S(2)}) collective-permute-start(bf16[32,1920]{1,0:T(8,128)(2,1)S(1)} %correlate.1.refs_4_), channel_id=1, source_target_pairs={{0,8},{1,9},{2,10},{3,11},{4,12},{5,13},{6,14},{7,15},{8,0},{9,1},... | collective-permute-start | bytes 368648 | tf_op jit(solution)/shard_map/ppermute | solution.py:191
  13.5 10.7 %collective-permute-start.4 = (bf16[32,1920]{1,0:T(8,128)(2,1)S(1)}, bf16[32,1920]{1,0:T(8,128)(2,1)S(1)}, u32[]{:S(2)}, u32[]{:S(2)}) collective-permute-start(bf16[32,1920]{1,0:T(8,128)(2,1)S(1)} %correlate.1.refs_4_), channel_id=1, source_target_pairs={{0,2},{1,3},{2,0},{3,1},{4,6},{5,7},{6,4},{7,5},{8,10},{9,11},{10,... | collective-permute-start | bytes 368648 | tf_op jit(solution)/shard_map/ppermute | solution.py:191
  15.0 9.2 %collective-permute-start = (bf16[32,1920]{1,0:T(8,128)(2,1)S(1)}, bf16[32,1920]{1,0:T(8,128)(2,1)S(1)}, u32[]{:S(2)}, u32[]{:S(2)}) collective-permute-start(bf16[32,1920]{1,0:T(8,128)(2,1)S(1)} %correlate.1.refs_4_), channel_id=1, source_target_pairs={{0,14},{1,15},{2,12},{3,13},{4,10},{5,11},{6,8},{7,9},{8,6},{9,7},... | collective-permute-start | bytes 368648 | tf_op jit(solution)/shard_map/ppermute | solution.py:191
  15.7 10.3 %collective-permute-start.2 = (bf16[32,1920]{1,0:T(8,128)(2,1)S(1)}, bf16[32,1920]{1,0:T(8,128)(2,1)S(1)}, u32[]{:S(2)}, u32[]{:S(2)}) collective-permute-start(bf16[32,1920]{1,0:T(8,128)(2,1)S(1)} %collective-permute-done.1.refs_12_), channel_id=1, source_target_pairs={{0,2},{1,3},{2,0},{3,1},{4,6},{5,7},{6,4},{7,5},{8,10},{9,11},{10,... | collective-permute-start | bytes 368648 | tf_op jit(solution)/shard_map/ppermute | solution.py:191
  18.3 7.8 %collective-permute-start.6 = (bf16[32,1920]{1,0:T(8,128)(2,1)S(1)}, bf16[32,1920]{1,0:T(8,128)(2,1)S(1)}, u32[]{:S(2)}, u32[]{:S(2)}) collective-permute-start(bf16[32,1920]{1,0:T(8,128)(2,1)S(1)} %correlate.1.refs_4_), channel_id=1, source_target_pairs={{0,1},{1,0},{2,3},{3,2},{4,5},{5,4},{6,7},{7,6},{8,9},{9,8},{10,11... | collective-permute-start | bytes 368648 | tf_op jit(solution)/shard_map/ppermute | solution.py:191
  22.6 4.9 %collective-permute-start.11 = (bf16[32,1920]{1,0:T(8,128)(2,1)S(1)}, bf16[32,1920]{1,0:T(8,128)(2,1)S(1)}, u32[]{:S(2)}, u32[]{:S(2)}) collective-permute-start(bf16[32,1920]{1,0:T(8,128)(2,1)S(1)} %collective-permute-done.7.refs_8_), channel_id=1, source_target_pairs={{0,2},{1,3},{2,0},{3,1},{4,6},{5,7},{6,4},{7,5},{8,10},{9,11},{10,... | collective-permute-start | bytes 368648 | tf_op jit(solution)/shard_map/ppermute | solution.py:191
  24.2 3.4 %collective-permute-start.10 = (bf16[32,1920]{1,0:T(8,128)(2,1)S(1)}, bf16[32,1920]{1,0:T(8,128)(2,1)S(1)}, u32[]{:S(2)}, u32[]{:S(2)}) collective-permute-start(bf16[32,1920]{1,0:T(8,128)(2,1)S(1)} %collective-permute-done.7.refs_8_), channel_id=1, source_target_pairs={{0,1},{1,0},{2,3},{3,2},{4,5},{5,4},{6,7},{7,6},{8,9},{9,8},{10,11... | collective-permute-start | bytes 368648 | tf_op jit(solution)/shard_map/ppermute | solution.py:191
  24.2 5.7 %collective-permute-start.8 = (bf16[32,1920]{1,0:T(8,128)(2,1)S(1)}, bf16[32,1920]{1,0:T(8,128)(2,1)S(1)}, u32[]{:S(2)}, u32[]{:S(2)}) collective-permute-start(bf16[32,1920]{1,0:T(8,128)(2,1)S(1)} %collective-permute-done.7.refs_8_), channel_id=1, source_target_pairs={{0,4},{1,5},{2,6},{3,7},{4,0},{5,1},{6,2},{7,3},{8,12},{9,13},{10,... | collective-permute-start | bytes 368648 | tf_op jit(solution)/shard_map/ppermute | solution.py:191
  26.0 3.9 %collective-permute-start.5 = (bf16[32,1920]{1,0:T(8,128)(2,1)S(1)}, bf16[32,1920]{1,0:T(8,128)(2,1)S(1)}, u32[]{:S(2)}, u32[]{:S(2)}) collective-permute-start(bf16[32,1920]{1,0:T(8,128)(2,1)S(1)} %collective-permute-done.4.refs_2_), channel_id=1, source_target_pairs={{0,1},{1,0},{2,3},{3,2},{4,5},{5,4},{6,7},{7,6},{8,9},{9,8},{10,11... | collective-permute-start | bytes 368648 | tf_op jit(solution)/shard_map/ppermute | solution.py:191
  26.0 4.4 %collective-permute-start.13 = (bf16[32,1920]{1,0:T(8,128)(2,1)S(1)}, bf16[32,1920]{1,0:T(8,128)(2,1)S(1)}, u32[]{:S(2)}, u32[]{:S(2)}) collective-permute-start(bf16[32,1920]{1,0:T(8,128)(2,1)S(1)} %collective-permute-done.1.refs_12_), channel_id=1, source_target_pairs={{0,1},{1,0},{2,3},{3,2},{4,5},{5,4},{6,7},{7,6},{8,9},{9,8},{10,11... | collective-permute-start | bytes 368648 | tf_op jit(solution)/shard_map/ppermute | solution.py:191
  27.5 3.7 %collective-permute-start.3 = (bf16[32,1920]{1,0:T(8,128)(2,1)S(1)}, bf16[32,1920]{1,0:T(8,128)(2,1)S(1)}, u32[]{:S(2)}, u32[]{:S(2)}) collective-permute-start(bf16[32,1920]{1,0:T(8,128)(2,1)S(1)} %collective-permute-done.2.refs_0_), channel_id=1, source_target_pairs={{0,1},{1,0},{2,3},{3,2},{4,5},{5,4},{6,7},{7,6},{8,9},{9,8},{10,11... | collective-permute-start | bytes 368648 | tf_op jit(solution)/shard_map/ppermute | solution.py:191
  27.5 2.9 %collective-permute-start.12 = (bf16[32,1920]{1,0:T(8,128)(2,1)S(1)}, bf16[32,1920]{1,0:T(8,128)(2,1)S(1)}, u32[]{:S(2)}, u32[]{:S(2)}) collective-permute-start(bf16[32,1920]{1,0:T(8,128)(2,1)S(1)} %collective-permute-done.11.refs_10_), channel_id=1, source_target_pairs={{0,1},{1,0},{2,3},{3,2},{4,5},{5,4},{6,7},{7,6},{8,9},{9,8},{10,11... | collective-permute-start | bytes 368648 | tf_op jit(solution)/shard_map/ppermute | solution.py:191
  29.9 1.3 %collective-permute-start.9 = (bf16[32,1920]{1,0:T(8,128)(2,1)S(1)}, bf16[32,1920]{1,0:T(8,128)(2,1)S(1)}, u32[]{:S(2)}, u32[]{:S(2)}) collective-permute-start(bf16[32,1920]{1,0:T(8,128)(2,1)S(1)} %collective-permute-done.8.refs_6_), channel_id=1, source_target_pairs={{0,1},{1,0},{2,3},{3,2},{4,5},{5,4},{6,7},{7,6},{8,9},{9,8},{10,11... | collective-permute-start | bytes 368648 | tf_op jit(solution)/shard_map/ppermute | solution.py:191
  29.9 1.5 %collective-permute-start.14 = (bf16[32,1920]{1,0:T(8,128)(2,1)S(1)}, bf16[32,1920]{1,0:T(8,128)(2,1)S(1)}, u32[]{:S(2)}, u32[]{:S(2)}) collective-permute-start(bf16[32,1920]{1,0:T(8,128)(2,1)S(1)} %collective-permute-done.refs_14_), channel_id=1, source_target_pairs={{0,1},{1,0},{2,3},{3,2},{4,5},{5,4},{6,7},{7,6},{8,9},{9,8},{10,11... | collective-permute-start | bytes 368648 | tf_op jit(solution)/shard_map/ppermute | solution.py:191

commit v18 on v13

--- a/solution.py
+++ b/solution.py
@@ -11,10 +11,9 @@
 CHUNK = 32
 SUB = 16
 ROWS = 8
-ROLLS = 2
+ROLLS = 4
 TIED = 1
 HANDED = (0, 1, 2, 3, 8, 9, 4, 5, 6, 7, 12, 13, 14, 15, 10, 11)
-SUB = 16
 
 
 def correlate_kernel(*refs):
@@ -258,39 +257,39 @@
     pieces = [refs[order.index(place)] for place in range(len(order))]
     snr_ref, peak_ref = refs[-2], refs[-1]
     samples = snr_ref.shape[1]
-    source = lax.broadcasted_iota(jnp.int32, (2 * LANE, 2 * LANE), 0) % LANE
-    target = lax.broadcasted_iota(jnp.int32, (2 * LANE, 2 * LANE), 1) // 2
-    repeat = jnp.where(source == target, 1.0, 0.0).astype(jnp.bfloat16)
-    running = None
-    for section in (3, 2, 1, 0):
-        width = samples >> section
-        offset = sum(samples >> s for s in range(section))
-        summed = []
-        for place in range(0, width, 2 * LANE):
-            size = min(2 * LANE, width)
-            first = offset + place
-            basis = jnp.concatenate([ref[:, first : first + size] for ref in pieces], axis=0)
-            part = jnp.dot(coeffs_ref[section], basis, preferred_element_type=jnp.float32)
-            if running is not None:
-                coarse = running[place // (2 * LANE)]
-                high = coarse.astype(jnp.bfloat16)
-                low = (coarse - high.astype(jnp.float32)).astype(jnp.bfloat16)
-                part = part + jnp.dot(
-                    jnp.concatenate([high, low], axis=1),
-                    repeat,
-                    preferred_element_type=jnp.float32,
-                )
-            summed.append(part)
-        running = []
-        for part in summed:
-            running += [part[:, at : at + LANE] for at in range(0, part.shape[1], LANE)]
-        if section == 0:
-            for number, part in enumerate(summed):
-                place = number * 2 * LANE
-                snr_ref[:, place : place + 2 * LANE] = part.astype(snr_ref.dtype)
-                peak_ref[:, place : place + 2 * LANE] = jnp.max(
-                    jnp.abs(part), axis=0, keepdims=True
-                )
+    wide = 2 * LANE
+
+    def product(section, place, size):
+        first = sum(samples >> s for s in range(section)) + place
+        basis = jnp.concatenate([ref[:, first : first + size] for ref in pieces], axis=0)
+        return jnp.dot(coeffs_ref[section], basis, preferred_element_type=jnp.float32)
+
+    slow = {}
+    for section in (3, 2, 1):
+        for place in range(0, samples >> section, wide):
+            size = min(wide, samples >> section)
+            part = product(section, place, size)
+            high = part.astype(jnp.bfloat16)
+            low = (part - high.astype(jnp.float32)).astype(jnp.bfloat16)
+            for at in range(0, size, LANE):
+                slow[section, (place + at) // LANE] = [high[:, at : at + LANE], low[:, at : at + LANE]]
+    source = lax.broadcasted_iota(jnp.int32, (wide, wide), 0) % LANE
+    target = lax.broadcasted_iota(jnp.int32, (wide, wide), 1)
+
+    for place in range(0, samples, wide):
+        left, right = [], []
+        for section in (1, 2, 3):
+            column = place >> section
+            left += slow[section, column // LANE]
+            match = source == (target >> section) + column % LANE
+            right.append(jnp.where(match, 1.0, 0.0).astype(jnp.bfloat16))
+        total = product(0, place, wide) + jnp.dot(
+            jnp.concatenate(left, axis=1),
+            jnp.concatenate(right, axis=0),
+            preferred_element_type=jnp.float32,
+        )
+        snr_ref[:, place : place + wide] = total.astype(snr_ref.dtype)
+        peak_ref[:, place : place + wide] = jnp.max(jnp.abs(total), axis=0, keepdims=True)
 
 
 def reconstruct(coeffs, blocks, samples):

time: 43.4 us -> 43.1 us (level)
  no operation moved by 1% of the time
where the time goes in v18:
time: 43.1 us; the launch traced here: 43 us
  starting transfers between devices  14 us (32%)
  blocking collectives  11.7 us (27%)
  Pallas kernels  9.65 us (22%)
  waiting for transfers between devices  6.27 us (15%)
  between operations  0.69 us (2%)
  other arithmetic  0.61 us (1%)
    ppermute x15, starting transfers between devices, exchange(): return lax.ppermute(block, 'tmpl', [(i, i ^ distance) for i in range(size)])  14 us
    all_to_all x1, blocking collectives, maximum_over_group(): lax.all_to_all(copies, 'tmpl', split_axis=0, concat_axis=0, tiled=True)  11.7 us
    pallas_call x1, Pallas kernels, correlate(): pl.pallas_call(correlate_kernel, out_shape=pltpu.VMEM((padded, samples),...  6.91 us
    ppermute x15, waiting for transfers between devices, exchange(): return lax.ppermute(block, 'tmpl', [(i, i ^ distance) for i in range(size)])  6.27 us
    pallas_call x1, Pallas kernels, reconstruct(): pl.pallas_call(functools.partial(recon_kernel, order), out_shape=(jax.Sha...  2.02 us
  transfers between devices with their start and end apart: 15, of which 7 were waited for; matrix products, arithmetic and copies ran while one was open for 0% of the time, Pallas kernels for 2%

profile of v18, /device:TPU:0, one launch (start us, length us, event | category | flops | bytes accessed | tf_op | source)
XLA Modules:
  0.0 43.0 jit_solution(14388031349695156538)
XLA Ops:
  0.6 0.0 copy-start
  0.6 6.9 %correlate.1.refs_0_ = bf16[32,1920]{1,0:T(8,128)(2,1)S(1)} custom-call(bf16[72,128]{1,0:T(8,128)(2,1)} %bitcast.9, bf16[68,128]{1,0:T(8,128)(2,1)} %bitcast.10, bf16[66,128]{1,0:T(8,128)(2,1)} %bitcast.11, bf16[65,128]{1,0:T(8,128)(2,1)} %bitcast.12, bf16[4,32,8192]{2,1,0:T(8,128)(2,1)} %refs_4_.1), custom_call_target="tpu_custom_call" | custom-call | flops 1006632960 | bytes 2097152 | tf_op jit(solution)/shard_map/correlate/pallas_call | solution.py:167
  7.6 3.1 %collective-permute-start.5 = (bf16[32,1920]{1,0:T(8,128)(2,1)S(1)}, bf16[32,1920]{1,0:T(8,128)(2,1)S(1)}, u32[]{:S(2)}, u32[]{:S(2)}) collective-permute-start(bf16[32,1920]{1,0:T(8,128)(2,1)S(1)} %correlate.1.refs_0_), channel_id=1, source_target_pairs={{0,4},{1,5},{2,6},{3,7},{4,0},{5,1},{6,2},{7,3},{8,12},{9,13},{10,... | collective-permute-start | bytes 368648 | tf_op jit(solution)/shard_map/ppermute | solution.py:193
  10.6 2.6 %collective-permute-start.3 = (bf16[32,1920]{1,0:T(8,128)(2,1)S(1)}, bf16[32,1920]{1,0:T(8,128)(2,1)S(1)}, u32[]{:S(2)}, u32[]{:S(2)}) collective-permute-start(bf16[32,1920]{1,0:T(8,128)(2,1)S(1)} %correlate.1.refs_0_), channel_id=1, source_target_pairs={{0,8},{1,9},{2,10},{3,11},{4,12},{5,13},{6,14},{7,15},{8,0},{9,1},... | collective-permute-start | bytes 368648 | tf_op jit(solution)/shard_map/ppermute | solution.py:193
  13.2 1.5 %collective-permute-start.1 = (bf16[32,1920]{1,0:T(8,128)(2,1)S(1)}, bf16[32,1920]{1,0:T(8,128)(2,1)S(1)}, u32[]{:S(2)}, u32[]{:S(2)}) collective-permute-start(bf16[32,1920]{1,0:T(8,128)(2,1)S(1)} %correlate.1.refs_0_), channel_id=1, source_target_pairs={{0,2},{1,3},{2,0},{3,1},{4,6},{5,7},{6,4},{7,5},{8,10},{9,11},{10,... | collective-permute-start | bytes 368648 | tf_op jit(solution)/shard_map/ppermute | solution.py:193
  14.8 0.0 copy-done
  14.8 0.7 %arrange.1.coeffs_ref = bf16[4,256,512]{2,1,0:T(8,128)(2,1)S(1)} custom-call(s32[1]{0:T(128)} %bitcast.4.offset_ref, bf16[4,256,512]{2,1,0:T(8,128)(2,1)S(1)} %copy-done), custom_call_target="tpu_custom_call" | custom-call | flops 536870912 | bytes 2097152 | tf_op jit(solution)/shard_map/arrange/pallas_call | solution.py:238
  15.5 0.1 collective-permute-start
  15.6 0.0 collective-permute-done.5.refs_6_
  15.6 1.7 %collective-permute-start.7 = (bf16[32,1920]{1,0:T(8,128)(2,1)S(1)}, bf16[32,1920]{1,0:T(8,128)(2,1)S(1)}, u32[]{:S(2)}, u32[]{:S(2)}) collective-permute-start(bf16[32,1920]{1,0:T(8,128)(2,1)S(1)} %collective-permute-done.5.refs_6_), channel_id=1, source_target_pairs={{0,2},{1,3},{2,0},{3,1},{4,6},{5,7},{6,4},{7,5},{8,10},{9,11},{10,... | collective-permute-start | bytes 368648 | tf_op jit(solution)/shard_map/ppermute | solution.py:193
  17.3 0.0 collective-permute-start.6
  17.3 1.7 %collective-permute-done.3.refs_4_ = bf16[32,1920]{1,0:T(8,128)(2,1)S(1)} collective-permute-done((bf16[32,1920]{1,0:T(8,128)(2,1)S(1)}, bf16[32,1920]{1,0:T(8,128)(2,1)S(1)}, u32[]{:S(2)}, u32[]{:S(2)}) %collective-permute-start.3) | collective-permute-done | bytes 122912 | tf_op jit(solution)/shard_map/ppermute | solution.py:193
  19.0 1.5 %collective-permute-start.13 = (bf16[32,1920]{1,0:T(8,128)(2,1)S(1)}, bf16[32,1920]{1,0:T(8,128)(2,1)S(1)}, u32[]{:S(2)}, u32[]{:S(2)}) collective-permute-start(bf16[32,1920]{1,0:T(8,128)(2,1)S(1)} %collective-permute-done.3.refs_4_), channel_id=1, source_target_pairs={{0,2},{1,3},{2,0},{3,1},{4,6},{5,7},{6,4},{7,5},{8,10},{9,11},{10,... | collective-permute-start | bytes 368648 | tf_op jit(solution)/shard_map/ppermute | solution.py:193
  20.5 0.0 collective-permute-done.1.refs_2_
  20.5 0.4 collective-permute-start.11
  20.9 0.0 collective-permute-done.refs_1_
  20.9 1.6 %collective-permute-start.9 = (bf16[32,1920]{1,0:T(8,128)(2,1)S(1)}, bf16[32,1920]{1,0:T(8,128)(2,1)S(1)}, u32[]{:S(2)}, u32[]{:S(2)}) collective-permute-start(bf16[32,1920]{1,0:T(8,128)(2,1)S(1)} %collective-permute-done.3.refs_4_), channel_id=1, source_target_pairs={{0,4},{1,5},{2,6},{3,7},{4,0},{5,1},{6,2},{7,3},{8,12},{9,13},{10,... | collective-permute-start | bytes 368648 | tf_op jit(solution)/shard_map/ppermute | solution.py:193
  22.5 0.6 %collective-permute-done.7.refs_8_ = bf16[32,1920]{1,0:T(8,128)(2,1)S(1)} collective-permute-done((bf16[32,1920]{1,0:T(8,128)(2,1)S(1)}, bf16[32,1920]{1,0:T(8,128)(2,1)S(1)}, u32[]{:S(2)}, u32[]{:S(2)}) %collective-permute-start.7) | collective-permute-done | bytes 122912 | tf_op jit(solution)/shard_map/ppermute | solution.py:193
  23.1 0.0 collective-permute-start.4
  23.1 0.0 collective-permute-done.6.refs_7_
  23.1 0.5 %collective-permute-start.2 = (bf16[32,1920]{1,0:T(8,128)(2,1)S(1)}, bf16[32,1920]{1,0:T(8,128)(2,1)S(1)}, u32[]{:S(2)}, u32[]{:S(2)}) collective-permute-start(bf16[32,1920]{1,0:T(8,128)(2,1)S(1)} %collective-permute-done.1.refs_2_), channel_id=1, source_target_pairs={{0,1},{1,0},{2,3},{3,2},{4,5},{5,4},{6,7},{7,6},{8,9},{9,8},{10,11... | collective-permute-start | bytes 368648 | tf_op jit(solution)/shard_map/ppermute | solution.py:193
  23.6 3.0 %collective-permute-done.13.refs_14_ = bf16[32,1920]{1,0:T(8,128)(2,1)S(1)} collective-permute-done((bf16[32,1920]{1,0:T(8,128)(2,1)S(1)}, bf16[32,1920]{1,0:T(8,128)(2,1)S(1)}, u32[]{:S(2)}, u32[]{:S(2)}) %collective-permute-start.13) | collective-permute-done | bytes 122912 | tf_op jit(solution)/shard_map/ppermute | solution.py:193
  26.6 0.0 collective-permute-start.8
  26.6 0.0 collective-permute-done.11.refs_12_
  26.6 0.5 %collective-permute-start.14 = (bf16[32,1920]{1,0:T(8,128)(2,1)S(1)}, bf16[32,1920]{1,0:T(8,128)(2,1)S(1)}, u32[]{:S(2)}, u32[]{:S(2)}) collective-permute-start(bf16[32,1920]{1,0:T(8,128)(2,1)S(1)} %collective-permute-done.13.refs_14_), channel_id=1, source_target_pairs={{0,1},{1,0},{2,3},{3,2},{4,5},{5,4},{6,7},{7,6},{8,9},{9,8},{10,11... | collective-permute-start | bytes 368648 | tf_op jit(solution)/shard_map/ppermute | solution.py:193
  27.1 0.0 collective-permute-done.9.refs_10_
  27.1 0.1 collective-permute-start.12
  27.2 0.0 collective-permute-done.4.refs_5_
  27.2 0.4 %collective-permute-start.10 = (bf16[32,1920]{1,0:T(8,128)(2,1)S(1)}, bf16[32,1920]{1,0:T(8,128)(2,1)S(1)}, u32[]{:S(2)}, u32[]{:S(2)}) collective-permute-start(bf16[32,1920]{1,0:T(8,128)(2,1)S(1)} %collective-permute-done.9.refs_10_), channel_id=1, source_target_pairs={{0,1},{1,0},{2,3},{3,2},{4,5},{5,4},{6,7},{7,6},{8,9},{9,8},{10,11... | collective-permute-start | bytes 368648 | tf_op jit(solution)/shard_map/ppermute | solution.py:193
  27.6 0.0 collective-permute-done.2.refs_3_
  27.6 0.3 collective-permute-done.8.refs_9_
  27.9 0.2 collective-permute-done.14.refs_15_
  28.1 0.3 collective-permute-done.12.refs_13_
  28.4 0.2 collective-permute-done.10.refs_11_
  28.6 2.0 %reconstruct.1 = (bf16[256,1024]{1,0:T(8,128)(2,1)}, f32[1,1024]{1,0:T(1,128)S(1)}) custom-call(bf16[4,256,512]{2,1,0:T(8,128)(2,1)S(1)} %arrange.1.coeffs_ref, bf16[32,1920]{1,0:T(8,128)(2,1)S(1)} %correlate.1.refs_0_, bf16[32,1920]{1,0:T(8,128)(2,1)S(1)} %collective-permute-done.refs_1_, bf16[32,1920]{1,0:T(8,128)(2,1)S(1)} %collective-permute-done.1.refs_2_, ...), custom_call_target="tpu_custom_call" | custom-call | tf_op jit(solution)/shard_map/reconstruct/pallas_call | solution.py:297
  30.6 11.7 %all_to_all.5 = f32[16,8,128]{2,1,0:T(8,128)S(1)} all-to-all(f32[16,8,128]{2,1,0:T(8,128)S(1)} %broadcast_in_dim.8), channel_id=1, replica_groups=mesh['bank'=2,'tmpl'=16] {'tmpl'}, dimensions={0} | all-to-all | bytes 131072 | tf_op jit(solution)/shard_map/all_to_all | solution.py:222
  42.4 0.6 %reduce_max.9 = f32[8,128]{1,0:T(8,128)} reduce(f32[16,8,128]{2,1,0:T(8,128)S(1)} %all_to_all.5, f32[]{:T(128)} %constant.2.clone.1), dimensions={0}, to_apply=%region_0.0 | reduce | flops 15360 | bytes 69636 | tf_op jit(solution)/shard_map/reduce_max | solution.py:223
  (1 shorter events, 0.0 us)
Async XLA Ops:
  0.6 14.1 %copy-start = (bf16[4,256,512]{2,1,0:T(8,128)(2,1)S(1)}, bf16[4,256,512]{2,1,0:T(8,128)(2,1)}, u32[]{:S(2)}) copy-start(bf16[4,256,512]{2,1,0:T(8,128)(2,1)} %coeffs_ref.1) | copy-start | bytes 3145732
  7.6 8.0 %collective-permute-start.5 = (bf16[32,1920]{1,0:T(8,128)(2,1)S(1)}, bf16[32,1920]{1,0:T(8,128)(2,1)S(1)}, u32[]{:S(2)}, u32[]{:S(2)}) collective-permute-start(bf16[32,1920]{1,0:T(8,128)(2,1)S(1)} %correlate.1.refs_0_), channel_id=1, source_target_pairs={{0,4},{1,5},{2,6},{3,7},{4,0},{5,1},{6,2},{7,3},{8,12},{9,13},{10,... | collective-permute-start | bytes 368648 | tf_op jit(solution)/shard_map/ppermute | solution.py:193
  10.6 8.4 %collective-permute-start.3 = (bf16[32,1920]{1,0:T(8,128)(2,1)S(1)}, bf16[32,1920]{1,0:T(8,128)(2,1)S(1)}, u32[]{:S(2)}, u32[]{:S(2)}) collective-permute-start(bf16[32,1920]{1,0:T(8,128)(2,1)S(1)} %correlate.1.refs_0_), channel_id=1, source_target_pairs={{0,8},{1,9},{2,10},{3,11},{4,12},{5,13},{6,14},{7,15},{8,0},{9,1},... | collective-permute-start | bytes 368648 | tf_op jit(solution)/shard_map/ppermute | solution.py:193
  13.2 7.3 %collective-permute-start.1 = (bf16[32,1920]{1,0:T(8,128)(2,1)S(1)}, bf16[32,1920]{1,0:T(8,128)(2,1)S(1)}, u32[]{:S(2)}, u32[]{:S(2)}) collective-permute-start(bf16[32,1920]{1,0:T(8,128)(2,1)S(1)} %correlate.1.refs_0_), channel_id=1, source_target_pairs={{0,2},{1,3},{2,0},{3,1},{4,6},{5,7},{6,4},{7,5},{8,10},{9,11},{10,... | collective-permute-start | bytes 368648 | tf_op jit(solution)/shard_map/ppermute | solution.py:193
  15.5 5.4 %collective-permute-start = (bf16[32,1920]{1,0:T(8,128)(2,1)S(1)}, bf16[32,1920]{1,0:T(8,128)(2,1)S(1)}, u32[]{:S(2)}, u32[]{:S(2)}) collective-permute-start(bf16[32,1920]{1,0:T(8,128)(2,1)S(1)} %correlate.1.refs_0_), channel_id=1, source_target_pairs={{0,1},{1,0},{2,3},{3,2},{4,5},{5,4},{6,7},{7,6},{8,9},{9,8},{10,11... | collective-permute-start | bytes 368648 | tf_op jit(solution)/shard_map/ppermute | solution.py:193
  15.6 7.5 %collective-permute-start.7 = (bf16[32,1920]{1,0:T(8,128)(2,1)S(1)}, bf16[32,1920]{1,0:T(8,128)(2,1)S(1)}, u32[]{:S(2)}, u32[]{:S(2)}) collective-permute-start(bf16[32,1920]{1,0:T(8,128)(2,1)S(1)} %collective-permute-done.5.refs_6_), channel_id=1, source_target_pairs={{0,2},{1,3},{2,0},{3,1},{4,6},{5,7},{6,4},{7,5},{8,10},{9,11},{10,... | collective-permute-start | bytes 368648 | tf_op jit(solution)/shard_map/ppermute | solution.py:193
  17.3 5.8 %collective-permute-start.6 = (bf16[32,1920]{1,0:T(8,128)(2,1)S(1)}, bf16[32,1920]{1,0:T(8,128)(2,1)S(1)}, u32[]{:S(2)}, u32[]{:S(2)}) collective-permute-start(bf16[32,1920]{1,0:T(8,128)(2,1)S(1)} %collective-permute-done.5.refs_6_), channel_id=1, source_target_pairs={{0,1},{1,0},{2,3},{3,2},{4,5},{5,4},{6,7},{7,6},{8,9},{9,8},{10,11... | collective-permute-start | bytes 368648 | tf_op jit(solution)/shard_map/ppermute | solution.py:193
  19.0 7.6 %collective-permute-start.13 = (bf16[32,1920]{1,0:T(8,128)(2,1)S(1)}, bf16[32,1920]{1,0:T(8,128)(2,1)S(1)}, u32[]{:S(2)}, u32[]{:S(2)}) collective-permute-start(bf16[32,1920]{1,0:T(8,128)(2,1)S(1)} %collective-permute-done.3.refs_4_), channel_id=1, source_target_pairs={{0,2},{1,3},{2,0},{3,1},{4,6},{5,7},{6,4},{7,5},{8,10},{9,11},{10,... | collective-permute-start | bytes 368648 | tf_op jit(solution)/shard_map/ppermute | solution.py:193
  20.5 6.0 %collective-permute-start.11 = (bf16[32,1920]{1,0:T(8,128)(2,1)S(1)}, bf16[32,1920]{1,0:T(8,128)(2,1)S(1)}, u32[]{:S(2)}, u32[]{:S(2)}) collective-permute-start(bf16[32,1920]{1,0:T(8,128)(2,1)S(1)} %collective-permute-done.3.refs_4_), channel_id=1, source_target_pairs={{0,6},{1,7},{2,4},{3,5},{4,2},{5,3},{6,0},{7,1},{8,14},{9,15},{10,... | collective-permute-start | bytes 368648 | tf_op jit(solution)/shard_map/ppermute | solution.py:193
  20.9 6.2 %collective-permute-start.9 = (bf16[32,1920]{1,0:T(8,128)(2,1)S(1)}, bf16[32,1920]{1,0:T(8,128)(2,1)S(1)}, u32[]{:S(2)}, u32[]{:S(2)}) collective-permute-start(bf16[32,1920]{1,0:T(8,128)(2,1)S(1)} %collective-permute-done.3.refs_4_), channel_id=1, source_target_pairs={{0,4},{1,5},{2,6},{3,7},{4,0},{5,1},{6,2},{7,3},{8,12},{9,13},{10,... | collective-permute-start | bytes 368648 | tf_op jit(solution)/shard_map/ppermute | solution.py:193
  23.1 4.1 %collective-permute-start.4 = (bf16[32,1920]{1,0:T(8,128)(2,1)S(1)}, bf16[32,1920]{1,0:T(8,128)(2,1)S(1)}, u32[]{:S(2)}, u32[]{:S(2)}) collective-permute-start(bf16[32,1920]{1,0:T(8,128)(2,1)S(1)} %collective-permute-done.3.refs_4_), channel_id=1, source_target_pairs={{0,1},{1,0},{2,3},{3,2},{4,5},{5,4},{6,7},{7,6},{8,9},{9,8},{10,11... | collective-permute-start | bytes 368648 | tf_op jit(solution)/shard_map/ppermute | solution.py:193
  23.1 4.5 %collective-permute-start.2 = (bf16[32,1920]{1,0:T(8,128)(2,1)S(1)}, bf16[32,1920]{1,0:T(8,128)(2,1)S(1)}, u32[]{:S(2)}, u32[]{:S(2)}) collective-permute-start(bf16[32,1920]{1,0:T(8,128)(2,1)S(1)} %collective-permute-done.1.refs_2_), channel_id=1, source_target_pairs={{0,1},{1,0},{2,3},{3,2},{4,5},{5,4},{6,7},{7,6},{8,9},{9,8},{10,11... | collective-permute-start | bytes 368648 | tf_op jit(solution)/shard_map/ppermute | solution.py:193
  26.6 1.3 %collective-permute-start.8 = (bf16[32,1920]{1,0:T(8,128)(2,1)S(1)}, bf16[32,1920]{1,0:T(8,128)(2,1)S(1)}, u32[]{:S(2)}, u32[]{:S(2)}) collective-permute-start(bf16[32,1920]{1,0:T(8,128)(2,1)S(1)} %collective-permute-done.7.refs_8_), channel_id=1, source_target_pairs={{0,1},{1,0},{2,3},{3,2},{4,5},{5,4},{6,7},{7,6},{8,9},{9,8},{10,11... | collective-permute-start | bytes 368648 | tf_op jit(solution)/shard_map/ppermute | solution.py:193
  26.6 1.5 %collective-permute-start.14 = (bf16[32,1920]{1,0:T(8,128)(2,1)S(1)}, bf16[32,1920]{1,0:T(8,128)(2,1)S(1)}, u32[]{:S(2)}, u32[]{:S(2)}) collective-permute-start(bf16[32,1920]{1,0:T(8,128)(2,1)S(1)} %collective-permute-done.13.refs_14_), channel_id=1, source_target_pairs={{0,1},{1,0},{2,3},{3,2},{4,5},{5,4},{6,7},{7,6},{8,9},{9,8},{10,11... | collective-permute-start | bytes 368648 | tf_op jit(solution)/shard_map/ppermute | solution.py:193
  27.1 1.3 %collective-permute-start.12 = (bf16[32,1920]{1,0:T(8,128)(2,1)S(1)}, bf16[32,1920]{1,0:T(8,128)(2,1)S(1)}, u32[]{:S(2)}, u32[]{:S(2)}) collective-permute-start(bf16[32,1920]{1,0:T(8,128)(2,1)S(1)} %collective-permute-done.11.refs_12_), channel_id=1, source_target_pairs={{0,1},{1,0},{2,3},{3,2},{4,5},{5,4},{6,7},{7,6},{8,9},{9,8},{10,11... | collective-permute-start | bytes 368648 | tf_op jit(solution)/shard_map/ppermute | solution.py:193
  27.2 1.4 %collective-permute-start.10 = (bf16[32,1920]{1,0:T(8,128)(2,1)S(1)}, bf16[32,1920]{1,0:T(8,128)(2,1)S(1)}, u32[]{:S(2)}, u32[]{:S(2)}) collective-permute-start(bf16[32,1920]{1,0:T(8,128)(2,1)S(1)} %collective-permute-done.9.refs_10_), channel_id=1, source_target_pairs={{0,1},{1,0},{2,3},{3,2},{4,5},{5,4},{6,7},{7,6},{8,9},{9,8},{10,11... | collective-permute-start | bytes 368648 | tf_op jit(solution)/shard_map/ppermute | solution.py:193

commit v19 on v18

--- a/solution.py
+++ b/solution.py
@@ -12,8 +12,8 @@
 SUB = 16
 ROWS = 8
 ROLLS = 4
-TIED = 1
-HANDED = (0, 1, 2, 3, 8, 9, 4, 5, 6, 7, 12, 13, 14, 15, 10, 11)
+TIED = 10
+HANDED = (0, 8, 1, 4, 10, 2, 3, 9, 6, 12, 7, 13, 5, 11)
 
 
 def correlate_kernel(*refs):
@@ -193,7 +193,7 @@
     return lax.ppermute(block, "tmpl", [(i, i ^ distance) for i in range(size)])
 
 
-def gather_blocks(block, ready):
+def gather_blocks(block, ready, groups):
     size = lax.axis_size("tmpl")
     if block.shape[0] % SUB:
         stride = 1
@@ -207,12 +207,24 @@
     for place in range(2, size, 2):
         high = 1 << (place.bit_length() - 1)
         held[place] = exchange(held[place ^ high and high], place ^ high or place)
-    for place in range(1, size, 2):
-        source = held[place ^ 1]
-        if place == TIED:
+    blocks = []
+    for places in groups:
+        if places[0] & 1 == 0:
+            blocks += [held[place] for place in places]
+            continue
+        sources = [held[place ^ 1] for place in places]
+        source = sources[0] if len(sources) == 1 else jnp.concatenate(sources, axis=0)
+        if places == groups[TIED]:
             source, ready = lax.optimization_barrier((source, ready))
-        held[place] = exchange(source, 1)
-    return [held[place] for place in range(size)], ready
+        blocks.append(exchange(source, 1))
+    return blocks, ready
+
+
+def block_groups(size):
+    first = [place for place in range(1, size, 2) if (place ^ 1) & ((place ^ 1) - 1) == 0][:-1]
+    rest = [place for place in range(1, size, 2) if place not in first]
+    alone = [(place,) for place in list(range(0, size, 2))]
+    return alone + [tuple(first)] + [(place,) for place in rest]
 
 
 def maximum_over_group(values):
@@ -223,20 +235,26 @@
     return jnp.max(others, axis=0).reshape(values.shape)
 
 
-def arrange_kernel(offset_ref, coeffs_ref, out_ref):
+def arrange_kernel(order, offset_ref, coeffs_ref, out_ref):
     bases = coeffs_ref.shape[2]
+    rows = bases // len(order)
     source = lax.broadcasted_iota(jnp.int32, (bases, bases), 0)
-    target = lax.broadcasted_iota(jnp.int32, (bases, bases), 1) ^ offset_ref[0]
-    select = jnp.where(source == target, 1.0, 0.0).astype(jnp.bfloat16)
+    column = lax.broadcasted_iota(jnp.int32, (1, bases), 1)
+    target = column
+    for group, place in enumerate(order):
+        if group != place:
+            inside = (column >= group * rows) & (column < (group + 1) * rows)
+            target = jnp.where(inside, column + (place - group) * rows, target)
+    select = jnp.where(source == (target ^ offset_ref[0]), 1.0, 0.0).astype(jnp.bfloat16)
     for section in range(coeffs_ref.shape[0]):
         out_ref[section] = jnp.dot(
             coeffs_ref[section], select, preferred_element_type=jnp.float32
         ).astype(out_ref.dtype)
 
 
-def arrange(coeffs, offset):
+def arrange(coeffs, offset, order):
     return pl.pallas_call(
-        arrange_kernel,
+        functools.partial(arrange_kernel, order),
         out_shape=jax.ShapeDtypeStruct(coeffs.shape, coeffs.dtype),
         in_specs=[
             pl.BlockSpec(memory_space=pltpu.SMEM),
@@ -255,9 +273,10 @@
 
 def recon_kernel(order, coeffs_ref, *refs):
     pieces = [refs[order.index(place)] for place in range(len(order))]
-    snr_ref, peak_ref = refs[-2], refs[-1]
+    out_ref, peak_ref, snr_ref, sems = refs[-4:]
     samples = snr_ref.shape[1]
     wide = 2 * LANE
+    copies = []
 
     def product(section, place, size):
         first = sum(samples >> s for s in range(section)) + place
@@ -289,7 +308,17 @@
             preferred_element_type=jnp.float32,
         )
         snr_ref[:, place : place + wide] = total.astype(snr_ref.dtype)
+        copies.append(
+            pltpu.make_async_copy(
+                snr_ref.at[:, pl.ds(place, wide)],
+                out_ref.at[:, pl.ds(place, wide)],
+                sems.at[place // wide],
+            )
+        )
+        copies[-1].start()
         peak_ref[:, place : place + wide] = jnp.max(jnp.abs(total), axis=0, keepdims=True)
+    for copy in copies:
+        copy.wait()
 
 
 def reconstruct(coeffs, blocks, samples):
@@ -301,7 +330,14 @@
             jax.ShapeDtypeStruct((1, samples), jnp.float32),
         ),
         in_specs=[pl.BlockSpec(memory_space=pltpu.VMEM)] * (1 + len(blocks)),
-        out_specs=(pl.BlockSpec(memory_space=pltpu.VMEM),) * 2,
+        out_specs=(
+            pl.BlockSpec(memory_space=pltpu.HBM),
+            pl.BlockSpec(memory_space=pltpu.VMEM),
+        ),
+        scratch_shapes=[
+            pltpu.VMEM((coeffs.shape[1], samples), jnp.bfloat16),
+            pltpu.SemaphoreType.DMA((samples // (2 * LANE),)),
+        ],
         compiler_params=pltpu.CompilerParams(vmem_limit_bytes=16 * 2**20),
         name="reconstruct",
     )(coeffs, *[blocks[place] for place in order])
@@ -310,9 +346,12 @@
 def per_device(strain_fast, strain_half, strain_quarter, strain_eighth, basis_taps, recon_coeffs):
     streams = (strain_fast, strain_half, strain_quarter, strain_eighth)
     samples = strain_fast.shape[0] - basis_taps.shape[2]
-    offset = (lax.axis_index("tmpl") * basis_taps.shape[1]).astype(jnp.int32).reshape(1)
-    coeffs = arrange(recon_coeffs, offset)
-    blocks, coeffs = gather_blocks(correlate(streams, basis_taps), coeffs)
+    size, rows = lax.axis_size("tmpl"), basis_taps.shape[1]
+    groups = block_groups(size) if rows % SUB == 0 else [tuple(range(size))]
+    order = tuple(place for places in groups for place in places)
+    offset = (lax.axis_index("tmpl") * rows).astype(jnp.int32).reshape(1)
+    coeffs = arrange(recon_coeffs, offset, order)
+    blocks, coeffs = gather_blocks(correlate(streams, basis_taps), coeffs, groups)
     snr_series, local_peak = reconstruct(coeffs, blocks, samples)
     peak_snr = maximum_over_group(local_peak.reshape(samples))
     return (snr_series, peak_snr)

time: 43.1 us -> 43.3 us (level)
  waiting for transfers between devices: 6.27 us -> 7.73 us
  blocking collectives: 11.7 us -> 10.5 us
    ppermute x15 -> x13, waiting for transfers between devices: 6.27 us -> 7.73 us  [exchange(): return lax.ppermute(block, 'tmpl', [(i, i ^ distance) for i in range(size)])]
    all_to_all x1, blocking collectives: 11.7 us -> 10.5 us  [maximum_over_group(): lax.all_to_all(copies, 'tmpl', split_axis=0, concat_axis=0, tiled=True)]
    ppermute x15 -> x13, starting transfers between devices: 14 us -> 13.9 us  [exchange(): return lax.ppermute(block, 'tmpl', [(i, i ^ distance) for i in range(size)])]
  transfers between devices with their start and end apart: 15 -> 13, of which waited for: 7 -> 5; matrix products, arithmetic and copies ran while one was open for 0% -> 0% of each run, Pallas kernels for 2% -> 2%
where the time goes in v19:
time: 43.3 us; the launch traced here: 43.2 us
  starting transfers between devices  13.9 us (32%)
  blocking collectives  10.5 us (24%)
  Pallas kernels  9.64 us (22%)
  waiting for transfers between devices  7.73 us (18%)
  between operations  0.71 us (2%)
  other arithmetic  0.64 us (1%)
    ppermute x13, starting transfers between devices, exchange(): return lax.ppermute(block, 'tmpl', [(i, i ^ distance) for i in range(size)])  13.9 us
    all_to_all x1, blocking collectives, maximum_over_group(): lax.all_to_all(copies, 'tmpl', split_axis=0, concat_axis=0, tiled=True)  10.5 us
    ppermute x13, waiting for transfers between devices, exchange(): return lax.ppermute(block, 'tmpl', [(i, i ^ distance) for i in range(size)])  7.73 us
    pallas_call x1, Pallas kernels, correlate(): pl.pallas_call(correlate_kernel, out_shape=pltpu.VMEM((padded, samples),...  6.91 us
    pallas_call x1, Pallas kernels, reconstruct(): pl.pallas_call(functools.partial(recon_kernel, order), out_shape=(jax.Sha...  2 us
  transfers between devices with their start and end apart: 13, of which 5 were waited for; matrix products, arithmetic and copies ran while one was open for 0% of the time, Pallas kernels for 2%

profile of v19, /device:TPU:0, one launch (start us, length us, event | category | flops | bytes accessed | tf_op | source)
XLA Modules:
  0.0 43.2 jit_solution(1220234817389204472)
XLA Ops:
  0.6 0.0 copy-start
  0.6 6.9 %correlate.1.refs_0_ = bf16[32,1920]{1,0:T(8,128)(2,1)S(1)} custom-call(bf16[72,128]{1,0:T(8,128)(2,1)} %bitcast.9, bf16[68,128]{1,0:T(8,128)(2,1)} %bitcast.10, bf16[66,128]{1,0:T(8,128)(2,1)} %bitcast.11, bf16[65,128]{1,0:T(8,128)(2,1)} %bitcast.12, bf16[4,32,8192]{2,1,0:T(8,128)(2,1)} %refs_4_.1), custom_call_target="tpu_custom_call" | custom-call | flops 1006632960 | bytes 2097152 | tf_op jit(solution)/shard_map/correlate/pallas_call | solution.py:167
  7.6 3.1 %collective-permute-start.2 = (bf16[32,1920]{1,0:T(8,128)(2,1)S(1)}, bf16[32,1920]{1,0:T(8,128)(2,1)S(1)}, u32[]{:S(2)}, u32[]{:S(2)}) collective-permute-start(bf16[32,1920]{1,0:T(8,128)(2,1)S(1)} %correlate.1.refs_0_), channel_id=1, source_target_pairs={{0,4},{1,5},{2,6},{3,7},{4,0},{5,1},{6,2},{7,3},{8,12},{9,13},{10,... | collective-permute-start | bytes 368648 | tf_op jit(solution)/shard_map/ppermute | solution.py:193
  10.6 1.5 %collective-permute-start.1 = (bf16[32,1920]{1,0:T(8,128)(2,1)S(1)}, bf16[32,1920]{1,0:T(8,128)(2,1)S(1)}, u32[]{:S(2)}, u32[]{:S(2)}) collective-permute-start(bf16[32,1920]{1,0:T(8,128)(2,1)S(1)} %correlate.1.refs_0_), channel_id=1, source_target_pairs={{0,2},{1,3},{2,0},{3,1},{4,6},{5,7},{6,4},{7,5},{8,10},{9,11},{10,... | collective-permute-start | bytes 368648 | tf_op jit(solution)/shard_map/ppermute | solution.py:193
  12.2 2.6 %collective-permute-start = (bf16[32,1920]{1,0:T(8,128)(2,1)S(1)}, bf16[32,1920]{1,0:T(8,128)(2,1)S(1)}, u32[]{:S(2)}, u32[]{:S(2)}) collective-permute-start(bf16[32,1920]{1,0:T(8,128)(2,1)S(1)} %correlate.1.refs_0_), channel_id=1, source_target_pairs={{0,8},{1,9},{2,10},{3,11},{4,12},{5,13},{6,14},{7,15},{8,0},{9,1},... | collective-permute-start | bytes 368648 | tf_op jit(solution)/shard_map/ppermute | solution.py:193
  14.8 0.0 collective-permute-done.2.refs_5_
  14.8 2.1 %collective-permute-start.5 = (bf16[32,1920]{1,0:T(8,128)(2,1)S(1)}, bf16[32,1920]{1,0:T(8,128)(2,1)S(1)}, u32[]{:S(2)}, u32[]{:S(2)}) collective-permute-start(bf16[32,1920]{1,0:T(8,128)(2,1)S(1)} %collective-permute-done.2.refs_5_), channel_id=1, source_target_pairs={{0,2},{1,3},{2,0},{3,1},{4,6},{5,7},{6,4},{7,5},{8,10},{9,11},{10,... | collective-permute-start | bytes 368648 | tf_op jit(solution)/shard_map/ppermute | solution.py:193
  16.9 0.0 collective-permute-done.1.refs_2_
  16.9 0.1 collective-permute-start.3
  17.0 0.0 copy-done
  17.0 0.7 %arrange.1.coeffs_ref = bf16[4,256,512]{2,1,0:T(8,128)(2,1)S(1)} custom-call(s32[1]{0:T(128)} %bitcast.4.offset_ref, bf16[4,256,512]{2,1,0:T(8,128)(2,1)S(1)} %copy-done), custom_call_target="tpu_custom_call" | custom-call | flops 536870912 | bytes 2097152 | tf_op jit(solution)/shard_map/arrange/pallas_call | solution.py:256
  17.7 2.5 %collective-permute-done.refs_3_ = bf16[32,1920]{1,0:T(8,128)(2,1)S(1)} collective-permute-done((bf16[32,1920]{1,0:T(8,128)(2,1)S(1)}, bf16[32,1920]{1,0:T(8,128)(2,1)S(1)}, u32[]{:S(2)}, u32[]{:S(2)}) %collective-permute-start) | collective-permute-done | bytes 122912 | tf_op jit(solution)/shard_map/ppermute | solution.py:193
  20.2 0.6 %collective-permute-start.11 = (bf16[32,1920]{1,0:T(8,128)(2,1)S(1)}, bf16[32,1920]{1,0:T(8,128)(2,1)S(1)}, u32[]{:S(2)}, u32[]{:S(2)}) collective-permute-start(bf16[32,1920]{1,0:T(8,128)(2,1)S(1)} %collective-permute-done.refs_3_), channel_id=1, source_target_pairs={{0,2},{1,3},{2,0},{3,1},{4,6},{5,7},{6,4},{7,5},{8,10},{9,11},{10,... | collective-permute-start | bytes 368648 | tf_op jit(solution)/shard_map/ppermute | solution.py:193
  20.8 0.6 %collective-permute-start.9 = (bf16[32,1920]{1,0:T(8,128)(2,1)S(1)}, bf16[32,1920]{1,0:T(8,128)(2,1)S(1)}, u32[]{:S(2)}, u32[]{:S(2)}) collective-permute-start(bf16[32,1920]{1,0:T(8,128)(2,1)S(1)} %collective-permute-done.refs_3_), channel_id=1, source_target_pairs={{0,6},{1,7},{2,4},{3,5},{4,2},{5,3},{6,0},{7,1},{8,14},{9,15},{10,... | collective-permute-start | bytes 368648 | tf_op jit(solution)/shard_map/ppermute | solution.py:193
  21.4 2.3 %collective-permute-start.7 = (bf16[32,1920]{1,0:T(8,128)(2,1)S(1)}, bf16[32,1920]{1,0:T(8,128)(2,1)S(1)}, u32[]{:S(2)}, u32[]{:S(2)}) collective-permute-start(bf16[32,1920]{1,0:T(8,128)(2,1)S(1)} %collective-permute-done.refs_3_), channel_id=1, source_target_pairs={{0,4},{1,5},{2,6},{3,7},{4,0},{5,1},{6,2},{7,3},{8,12},{9,13},{10,... | collective-permute-start | bytes 368648 | tf_op jit(solution)/shard_map/ppermute | solution.py:193
  23.7 0.0 collective-permute-done.5.refs_6_
  23.7 0.0 collective-permute-start.4
  23.7 3.5 %collective-permute-done.11.refs_12_ = bf16[32,1920]{1,0:T(8,128)(2,1)S(1)} collective-permute-done((bf16[32,1920]{1,0:T(8,128)(2,1)S(1)}, bf16[32,1920]{1,0:T(8,128)(2,1)S(1)}, u32[]{:S(2)}, u32[]{:S(2)}) %collective-permute-start.11) | collective-permute-done | bytes 122912 | tf_op jit(solution)/shard_map/ppermute | solution.py:193
  27.2 0.0 collective-permute-start.6
  27.2 0.0 collective-permute-done.9.refs_10_
  27.2 0.5 %collective-permute-start.12 = (bf16[32,1920]{1,0:T(8,128)(2,1)S(1)}, bf16[32,1920]{1,0:T(8,128)(2,1)S(1)}, u32[]{:S(2)}, u32[]{:S(2)}) collective-permute-start(bf16[32,1920]{1,0:T(8,128)(2,1)S(1)} %collective-permute-done.11.refs_12_), channel_id=1, source_target_pairs={{0,1},{1,0},{2,3},{3,2},{4,5},{5,4},{6,7},{7,6},{8,9},{9,8},{10,11... | collective-permute-start | bytes 368648 | tf_op jit(solution)/shard_map/ppermute | solution.py:193
  27.7 0.7 %collective-permute-done.7.refs_8_ = bf16[32,1920]{1,0:T(8,128)(2,1)S(1)} collective-permute-done((bf16[32,1920]{1,0:T(8,128)(2,1)S(1)}, bf16[32,1920]{1,0:T(8,128)(2,1)S(1)}, u32[]{:S(2)}, u32[]{:S(2)}) %collective-permute-start.7) | collective-permute-done | bytes 122912 | tf_op jit(solution)/shard_map/ppermute | solution.py:193
  28.5 0.0 collective-permute-start.10
  28.5 0.0 collective-permute-done.4.refs_4_
  28.5 0.5 %collective-permute-start.8 = (bf16[32,1920]{1,0:T(8,128)(2,1)S(1)}, bf16[32,1920]{1,0:T(8,128)(2,1)S(1)}, u32[]{:S(2)}, u32[]{:S(2)}) collective-permute-start(bf16[32,1920]{1,0:T(8,128)(2,1)S(1)} %collective-permute-done.7.refs_8_), channel_id=1, source_target_pairs={{0,1},{1,0},{2,3},{3,2},{4,5},{5,4},{6,7},{7,6},{8,9},{9,8},{10,11... | collective-permute-start | bytes 368648 | tf_op jit(solution)/shard_map/ppermute | solution.py:193
  29.0 0.0 collective-permute-done.6.refs_7_
  29.0 0.0 collective-permute-done.12.refs_13_
  29.0 0.8 %collective-permute-done.10.refs_11_ = bf16[32,1920]{1,0:T(8,128)(2,1)S(1)} collective-permute-done((bf16[32,1920]{1,0:T(8,128)(2,1)S(1)}, bf16[32,1920]{1,0:T(8,128)(2,1)S(1)}, u32[]{:S(2)}, u32[]{:S(2)}) %collective-permute-start.10) | collective-permute-done | bytes 122912 | tf_op jit(solution)/shard_map/ppermute | solution.py:193
  29.8 0.2 collective-permute-done.8.refs_9_
  30.0 0.0 collective-permute-done.3.refs_1_
  30.0 2.0 %reconstruct.1 = (bf16[256,1024]{1,0:T(8,128)(2,1)}, f32[1,1024]{1,0:T(1,128)S(1)}) custom-call(bf16[4,256,512]{2,1,0:T(8,128)(2,1)S(1)} %arrange.1.coeffs_ref, bf16[32,1920]{1,0:T(8,128)(2,1)S(1)} %correlate.1.refs_0_, bf16[96,1920]{1,0:T(8,128)(2,1)S(1)} %collective-permute-done.3.refs_1_, bf16[32,1920]{1,0:T(8,128)(2,1)S(1)} %collective-permute-done.1.refs_2_, ...), custom_call_target="tpu_custom_call" | custom-call | tf_op jit(solution)/shard_map/reconstruct/pallas_call | solution.py:326
  32.0 10.5 %all_to_all.5 = f32[16,8,128]{2,1,0:T(8,128)S(1)} all-to-all(f32[16,8,128]{2,1,0:T(8,128)S(1)} %broadcast_in_dim.8), channel_id=1, replica_groups=mesh['bank'=2,'tmpl'=16] {'tmpl'}, dimensions={0} | all-to-all | bytes 131072 | tf_op jit(solution)/shard_map/all_to_all | solution.py:234
  42.5 0.6 %reduce_max.9 = f32[8,128]{1,0:T(8,128)} reduce(f32[16,8,128]{2,1,0:T(8,128)S(1)} %all_to_all.5, f32[]{:T(128)} %constant.2.clone.1), dimensions={0}, to_apply=%region_0.0 | reduce | flops 15360 | bytes 69636 | tf_op jit(solution)/shard_map/reduce_max | solution.py:235
  (2 shorter events, 0.0 us)
Async XLA Ops:
  0.6 16.4 %copy-start = (bf16[4,256,512]{2,1,0:T(8,128)(2,1)S(1)}, bf16[4,256,512]{2,1,0:T(8,128)(2,1)}, u32[]{:S(2)}) copy-start(bf16[4,256,512]{2,1,0:T(8,128)(2,1)} %coeffs_ref.1) | copy-start | bytes 3145732
  7.6 7.2 %collective-permute-start.2 = (bf16[32,1920]{1,0:T(8,128)(2,1)S(1)}, bf16[32,1920]{1,0:T(8,128)(2,1)S(1)}, u32[]{:S(2)}, u32[]{:S(2)}) collective-permute-start(bf16[32,1920]{1,0:T(8,128)(2,1)S(1)} %correlate.1.refs_0_), channel_id=1, source_target_pairs={{0,4},{1,5},{2,6},{3,7},{4,0},{5,1},{6,2},{7,3},{8,12},{9,13},{10,... | collective-permute-start | bytes 368648 | tf_op jit(solution)/shard_map/ppermute | solution.py:193
  10.6 6.2 %collective-permute-start.1 = (bf16[32,1920]{1,0:T(8,128)(2,1)S(1)}, bf16[32,1920]{1,0:T(8,128)(2,1)S(1)}, u32[]{:S(2)}, u32[]{:S(2)}) collective-permute-start(bf16[32,1920]{1,0:T(8,128)(2,1)S(1)} %correlate.1.refs_0_), channel_id=1, source_target_pairs={{0,2},{1,3},{2,0},{3,1},{4,6},{5,7},{6,4},{7,5},{8,10},{9,11},{10,... | collective-permute-start | bytes 368648 | tf_op jit(solution)/shard_map/ppermute | solution.py:193
  12.2 8.0 %collective-permute-start = (bf16[32,1920]{1,0:T(8,128)(2,1)S(1)}, bf16[32,1920]{1,0:T(8,128)(2,1)S(1)}, u32[]{:S(2)}, u32[]{:S(2)}) collective-permute-start(bf16[32,1920]{1,0:T(8,128)(2,1)S(1)} %correlate.1.refs_0_), channel_id=1, source_target_pairs={{0,8},{1,9},{2,10},{3,11},{4,12},{5,13},{6,14},{7,15},{8,0},{9,1},... | collective-permute-start | bytes 368648 | tf_op jit(solution)/shard_map/ppermute | solution.py:193
  14.8 8.9 %collective-permute-start.5 = (bf16[32,1920]{1,0:T(8,128)(2,1)S(1)}, bf16[32,1920]{1,0:T(8,128)(2,1)S(1)}, u32[]{:S(2)}, u32[]{:S(2)}) collective-permute-start(bf16[32,1920]{1,0:T(8,128)(2,1)S(1)} %collective-permute-done.2.refs_5_), channel_id=1, source_target_pairs={{0,2},{1,3},{2,0},{3,1},{4,6},{5,7},{6,4},{7,5},{8,10},{9,11},{10,... | collective-permute-start | bytes 368648 | tf_op jit(solution)/shard_map/ppermute | solution.py:193
  16.9 13.1 %collective-permute-start.3 = (bf16[96,1920]{1,0:T(8,128)(2,1)S(1)}, bf16[96,1920]{1,0:T(8,128)(2,1)S(1)}, u32[]{:S(2)}, u32[]{:S(2)}) collective-permute-start(bf16[96,1920]{1,0:T(8,128)(2,1)S(1)} %pad_maximum_fusion), channel_id=1, source_target_pairs={{0,1},{1,0},{2,3},{3,2},{4,5},{5,4},{6,7},{7,6},{8,9},{9,8},{10,11... | collective-permute-start | bytes 1105928 | tf_op jit(solution)/shard_map/ppermute | solution.py:193
  20.2 7.0 %collective-permute-start.11 = (bf16[32,1920]{1,0:T(8,128)(2,1)S(1)}, bf16[32,1920]{1,0:T(8,128)(2,1)S(1)}, u32[]{:S(2)}, u32[]{:S(2)}) collective-permute-start(bf16[32,1920]{1,0:T(8,128)(2,1)S(1)} %collective-permute-done.refs_3_), channel_id=1, source_target_pairs={{0,2},{1,3},{2,0},{3,1},{4,6},{5,7},{6,4},{7,5},{8,10},{9,11},{10,... | collective-permute-start | bytes 368648 | tf_op jit(solution)/shard_map/ppermute | solution.py:193
  20.8 6.5 %collective-permute-start.9 = (bf16[32,1920]{1,0:T(8,128)(2,1)S(1)}, bf16[32,1920]{1,0:T(8,128)(2,1)S(1)}, u32[]{:S(2)}, u32[]{:S(2)}) collective-permute-start(bf16[32,1920]{1,0:T(8,128)(2,1)S(1)} %collective-permute-done.refs_3_), channel_id=1, source_target_pairs={{0,6},{1,7},{2,4},{3,5},{4,2},{5,3},{6,0},{7,1},{8,14},{9,15},{10,... | collective-permute-start | bytes 368648 | tf_op jit(solution)/shard_map/ppermute | solution.py:193
  21.4 7.1 %collective-permute-start.7 = (bf16[32,1920]{1,0:T(8,128)(2,1)S(1)}, bf16[32,1920]{1,0:T(8,128)(2,1)S(1)}, u32[]{:S(2)}, u32[]{:S(2)}) collective-permute-start(bf16[32,1920]{1,0:T(8,128)(2,1)S(1)} %collective-permute-done.refs_3_), channel_id=1, source_target_pairs={{0,4},{1,5},{2,6},{3,7},{4,0},{5,1},{6,2},{7,3},{8,12},{9,13},{10,... | collective-permute-start | bytes 368648 | tf_op jit(solution)/shard_map/ppermute | solution.py:193
  23.7 4.8 %collective-permute-start.4 = (bf16[32,1920]{1,0:T(8,128)(2,1)S(1)}, bf16[32,1920]{1,0:T(8,128)(2,1)S(1)}, u32[]{:S(2)}, u32[]{:S(2)}) collective-permute-start(bf16[32,1920]{1,0:T(8,128)(2,1)S(1)} %collective-permute-done.refs_3_), channel_id=1, source_target_pairs={{0,1},{1,0},{2,3},{3,2},{4,5},{5,4},{6,7},{7,6},{8,9},{9,8},{10,11... | collective-permute-start | bytes 368648 | tf_op jit(solution)/shard_map/ppermute | solution.py:193
  27.2 1.7 %collective-permute-start.6 = (bf16[32,1920]{1,0:T(8,128)(2,1)S(1)}, bf16[32,1920]{1,0:T(8,128)(2,1)S(1)}, u32[]{:S(2)}, u32[]{:S(2)}) collective-permute-start(bf16[32,1920]{1,0:T(8,128)(2,1)S(1)} %collective-permute-done.5.refs_6_), channel_id=1, source_target_pairs={{0,1},{1,0},{2,3},{3,2},{4,5},{5,4},{6,7},{7,6},{8,9},{9,8},{10,11... | collective-permute-start | bytes 368648 | tf_op jit(solution)/shard_map/ppermute | solution.py:193
  27.2 1.7 %collective-permute-start.12 = (bf16[32,1920]{1,0:T(8,128)(2,1)S(1)}, bf16[32,1920]{1,0:T(8,128)(2,1)S(1)}, u32[]{:S(2)}, u32[]{:S(2)}) collective-permute-start(bf16[32,1920]{1,0:T(8,128)(2,1)S(1)} %collective-permute-done.11.refs_12_), channel_id=1, source_target_pairs={{0,1},{1,0},{2,3},{3,2},{4,5},{5,4},{6,7},{7,6},{8,9},{9,8},{10,11... | collective-permute-start | bytes 368648 | tf_op jit(solution)/shard_map/ppermute | solution.py:193
  28.5 1.3 %collective-permute-start.10 = (bf16[32,1920]{1,0:T(8,128)(2,1)S(1)}, bf16[32,1920]{1,0:T(8,128)(2,1)S(1)}, u32[]{:S(2)}, u32[]{:S(2)}) collective-permute-start(bf16[32,1920]{1,0:T(8,128)(2,1)S(1)} %collective-permute-done.9.refs_10_), channel_id=1, source_target_pairs={{0,1},{1,0},{2,3},{3,2},{4,5},{5,4},{6,7},{7,6},{8,9},{9,8},{10,11... | collective-permute-start | bytes 368648 | tf_op jit(solution)/shard_map/ppermute | solution.py:193
  28.5 1.5 %collective-permute-start.8 = (bf16[32,1920]{1,0:T(8,128)(2,1)S(1)}, bf16[32,1920]{1,0:T(8,128)(2,1)S(1)}, u32[]{:S(2)}, u32[]{:S(2)}) collective-permute-start(bf16[32,1920]{1,0:T(8,128)(2,1)S(1)} %collective-permute-done.7.refs_8_), channel_id=1, source_target_pairs={{0,1},{1,0},{2,3},{3,2},{4,5},{5,4},{6,7},{7,6},{8,9},{9,8},{10,11... | collective-permute-start | bytes 368648 | tf_op jit(solution)/shard_map/ppermute | solution.py:193

commit v20 on v18

--- a/solution.py
+++ b/solution.py
@@ -12,7 +12,7 @@
 SUB = 16
 ROWS = 8
 ROLLS = 4
-TIED = 1
+TIED = 7
 HANDED = (0, 1, 2, 3, 8, 9, 4, 5, 6, 7, 12, 13, 14, 15, 10, 11)
 
 
@@ -206,7 +206,10 @@
     held = {0: block}
     for place in range(2, size, 2):
         high = 1 << (place.bit_length() - 1)
-        held[place] = exchange(held[place ^ high and high], place ^ high or place)
+        if place <= size // 2:
+            held[place] = exchange(block, place)
+        else:
+            held[place] = exchange(held[high], place ^ high)
     for place in range(1, size, 2):
         source = held[place ^ 1]
         if place == TIED:

time: 43.1 us -> 43.2 us (level)
  blocking collectives: 11.7 us -> 9.49 us
  waiting for transfers between devices: 6.27 us -> 8.1 us
    all_to_all x1, blocking collectives: 11.7 us -> 9.49 us  [maximum_over_group(): lax.all_to_all(copies, 'tmpl', split_axis=0, concat_axis=0, tiled=True)]
    ppermute x15, waiting for transfers between devices: 6.27 us -> 8.1 us  [exchange(): return lax.ppermute(block, 'tmpl', [(i, i ^ distance) for i in range(size)])]
where the time goes in v20:
time: 43.2 us; the launch traced here: 43 us
  starting transfers between devices  14.4 us (33%)
  Pallas kernels  9.66 us (22%)
  blocking collectives  9.49 us (22%)
  waiting for transfers between devices  8.1 us (19%)
  between operations  0.69 us (2%)
  other arithmetic  0.61 us (1%)
    ppermute x15, starting transfers between devices, exchange(): return lax.ppermute(block, 'tmpl', [(i, i ^ distance) for i in range(size)])  14.4 us
    all_to_all x1, blocking collectives, maximum_over_group(): lax.all_to_all(copies, 'tmpl', split_axis=0, concat_axis=0, tiled=True)  9.49 us
    ppermute x15, waiting for transfers between devices, exchange(): return lax.ppermute(block, 'tmpl', [(i, i ^ distance) for i in range(size)])  8.1 us
    pallas_call x1, Pallas kernels, correlate(): pl.pallas_call(correlate_kernel, out_shape=pltpu.VMEM((padded, samples),...  6.91 us
    pallas_call x1, Pallas kernels, reconstruct(): pl.pallas_call(functools.partial(recon_kernel, order), out_shape=(jax.Sha...  2.03 us
  transfers between devices with their start and end apart: 15, of which 7 were waited for; matrix products, arithmetic and copies ran while one was open for 0% of the time, Pallas kernels for 2%

profile of v20, /device:TPU:0, one launch (start us, length us, event | category | flops | bytes accessed | tf_op | source)
XLA Modules:
  0.0 43.0 jit_solution(1897511007852104738)
XLA Ops:
  0.6 0.0 copy-start
  0.6 6.9 %correlate.1.refs_0_ = bf16[32,1920]{1,0:T(8,128)(2,1)S(1)} custom-call(bf16[72,128]{1,0:T(8,128)(2,1)} %bitcast.9, bf16[68,128]{1,0:T(8,128)(2,1)} %bitcast.10, bf16[66,128]{1,0:T(8,128)(2,1)} %bitcast.11, bf16[65,128]{1,0:T(8,128)(2,1)} %bitcast.12, bf16[4,32,8192]{2,1,0:T(8,128)(2,1)} %refs_4_.1), custom_call_target="tpu_custom_call" | custom-call | flops 1006632960 | bytes 2097152 | tf_op jit(solution)/shard_map/correlate/pallas_call | solution.py:167
  7.6 3.1 %collective-permute-start.6 = (bf16[32,1920]{1,0:T(8,128)(2,1)S(1)}, bf16[32,1920]{1,0:T(8,128)(2,1)S(1)}, u32[]{:S(2)}, u32[]{:S(2)}) collective-permute-start(bf16[32,1920]{1,0:T(8,128)(2,1)S(1)} %correlate.1.refs_0_), channel_id=1, source_target_pairs={{0,4},{1,5},{2,6},{3,7},{4,0},{5,1},{6,2},{7,3},{8,12},{9,13},{10,... | collective-permute-start | bytes 368648 | tf_op jit(solution)/shard_map/ppermute | solution.py:193
  10.6 2.6 %collective-permute-start.4 = (bf16[32,1920]{1,0:T(8,128)(2,1)S(1)}, bf16[32,1920]{1,0:T(8,128)(2,1)S(1)}, u32[]{:S(2)}, u32[]{:S(2)}) collective-permute-start(bf16[32,1920]{1,0:T(8,128)(2,1)S(1)} %correlate.1.refs_0_), channel_id=1, source_target_pairs={{0,8},{1,9},{2,10},{3,11},{4,12},{5,13},{6,14},{7,15},{8,0},{9,1},... | collective-permute-start | bytes 368648 | tf_op jit(solution)/shard_map/ppermute | solution.py:193
  13.2 1.5 %collective-permute-start.2 = (bf16[32,1920]{1,0:T(8,128)(2,1)S(1)}, bf16[32,1920]{1,0:T(8,128)(2,1)S(1)}, u32[]{:S(2)}, u32[]{:S(2)}) collective-permute-start(bf16[32,1920]{1,0:T(8,128)(2,1)S(1)} %correlate.1.refs_0_), channel_id=1, source_target_pairs={{0,2},{1,3},{2,0},{3,1},{4,6},{5,7},{6,4},{7,5},{8,10},{9,11},{10,... | collective-permute-start | bytes 368648 | tf_op jit(solution)/shard_map/ppermute | solution.py:193
  14.8 0.0 collective-permute-start.1
  14.8 0.4 collective-permute-start
  15.2 0.3 collective-permute-done.6.refs_6_
  15.5 0.0 collective-permute-start.7
  15.5 2.6 %collective-permute-done.4.refs_4_ = bf16[32,1920]{1,0:T(8,128)(2,1)S(1)} collective-permute-done((bf16[32,1920]{1,0:T(8,128)(2,1)S(1)}, bf16[32,1920]{1,0:T(8,128)(2,1)S(1)}, u32[]{:S(2)}, u32[]{:S(2)}) %collective-permute-start.4) | collective-permute-done | bytes 122912 | tf_op jit(solution)/shard_map/ppermute | solution.py:193
  18.1 1.5 %collective-permute-start.13 = (bf16[32,1920]{1,0:T(8,128)(2,1)S(1)}, bf16[32,1920]{1,0:T(8,128)(2,1)S(1)}, u32[]{:S(2)}, u32[]{:S(2)}) collective-permute-start(bf16[32,1920]{1,0:T(8,128)(2,1)S(1)} %collective-permute-done.4.refs_4_), channel_id=1, source_target_pairs={{0,2},{1,3},{2,0},{3,1},{4,6},{5,7},{6,4},{7,5},{8,10},{9,11},{10,... | collective-permute-start | bytes 368648 | tf_op jit(solution)/shard_map/ppermute | solution.py:193
  19.6 1.5 %collective-permute-done.2.refs_2_ = bf16[32,1920]{1,0:T(8,128)(2,1)S(1)} collective-permute-done((bf16[32,1920]{1,0:T(8,128)(2,1)S(1)}, bf16[32,1920]{1,0:T(8,128)(2,1)S(1)}, u32[]{:S(2)}, u32[]{:S(2)}) %collective-permute-start.2) | collective-permute-done | bytes 122912 | tf_op jit(solution)/shard_map/ppermute | solution.py:193
  21.1 1.1 %collective-permute-start.11 = (bf16[32,1920]{1,0:T(8,128)(2,1)S(1)}, bf16[32,1920]{1,0:T(8,128)(2,1)S(1)}, u32[]{:S(2)}, u32[]{:S(2)}) collective-permute-start(bf16[32,1920]{1,0:T(8,128)(2,1)S(1)} %collective-permute-done.4.refs_4_), channel_id=1, source_target_pairs={{0,6},{1,7},{2,4},{3,5},{4,2},{5,3},{6,0},{7,1},{8,14},{9,15},{10,... | collective-permute-start | bytes 368648 | tf_op jit(solution)/shard_map/ppermute | solution.py:193
  22.2 0.0 collective-permute-done.1.refs_1_
  22.2 3.0 %collective-permute-start.9 = (bf16[32,1920]{1,0:T(8,128)(2,1)S(1)}, bf16[32,1920]{1,0:T(8,128)(2,1)S(1)}, u32[]{:S(2)}, u32[]{:S(2)}) collective-permute-start(bf16[32,1920]{1,0:T(8,128)(2,1)S(1)} %collective-permute-done.4.refs_4_), channel_id=1, source_target_pairs={{0,4},{1,5},{2,6},{3,7},{4,0},{5,1},{6,2},{7,3},{8,12},{9,13},{10,... | collective-permute-start | bytes 368648 | tf_op jit(solution)/shard_map/ppermute | solution.py:193
  25.2 0.0 collective-permute-done.refs_8_
  25.2 0.0 collective-permute-start.5
  25.2 0.0 copy-done
  25.2 0.7 %arrange.1.coeffs_ref = bf16[4,256,512]{2,1,0:T(8,128)(2,1)S(1)} custom-call(s32[1]{0:T(128)} %bitcast.4.offset_ref, bf16[4,256,512]{2,1,0:T(8,128)(2,1)S(1)} %copy-done), custom_call_target="tpu_custom_call" | custom-call | flops 536870912 | bytes 2097152 | tf_op jit(solution)/shard_map/arrange/pallas_call | solution.py:241
  25.9 0.0 collective-permute-done.7.refs_7_
  25.9 0.6 %collective-permute-start.8 = (bf16[32,1920]{1,0:T(8,128)(2,1)S(1)}, bf16[32,1920]{1,0:T(8,128)(2,1)S(1)}, u32[]{:S(2)}, u32[]{:S(2)}) collective-permute-start(bf16[32,1920]{1,0:T(8,128)(2,1)S(1)} %collective-permute-done.refs_8_), channel_id=1, source_target_pairs={{0,1},{1,0},{2,3},{3,2},{4,5},{5,4},{6,7},{7,6},{8,9},{9,8},{10,11... | collective-permute-start | bytes 368648 | tf_op jit(solution)/shard_map/ppermute | solution.py:193
  26.5 0.0 collective-permute-done.13.refs_14_
  26.5 0.1 collective-permute-start.3
  26.6 0.3 collective-permute-done.11.refs_12_
  26.9 0.1 collective-permute-start.14
  27.0 2.3 %collective-permute-done.9.refs_10_ = bf16[32,1920]{1,0:T(8,128)(2,1)S(1)} collective-permute-done((bf16[32,1920]{1,0:T(8,128)(2,1)S(1)}, bf16[32,1920]{1,0:T(8,128)(2,1)S(1)}, u32[]{:S(2)}, u32[]{:S(2)}) %collective-permute-start.9) | collective-permute-done | bytes 122912 | tf_op jit(solution)/shard_map/ppermute | solution.py:193
  29.4 0.0 collective-permute-start.12
  29.4 0.0 collective-permute-done.5.refs_5_
  29.4 0.5 %collective-permute-start.10 = (bf16[32,1920]{1,0:T(8,128)(2,1)S(1)}, bf16[32,1920]{1,0:T(8,128)(2,1)S(1)}, u32[]{:S(2)}, u32[]{:S(2)}) collective-permute-start(bf16[32,1920]{1,0:T(8,128)(2,1)S(1)} %collective-permute-done.9.refs_10_), channel_id=1, source_target_pairs={{0,1},{1,0},{2,3},{3,2},{4,5},{5,4},{6,7},{7,6},{8,9},{9,8},{10,11... | collective-permute-start | bytes 368648 | tf_op jit(solution)/shard_map/ppermute | solution.py:193
  29.9 0.0 collective-permute-done.3.refs_3_
  29.9 0.0 collective-permute-done.8.refs_9_
  29.9 0.0 collective-permute-done.14.refs_15_
  29.9 0.8 %collective-permute-done.12.refs_13_ = bf16[32,1920]{1,0:T(8,128)(2,1)S(1)} collective-permute-done((bf16[32,1920]{1,0:T(8,128)(2,1)S(1)}, bf16[32,1920]{1,0:T(8,128)(2,1)S(1)}, u32[]{:S(2)}, u32[]{:S(2)}) %collective-permute-start.12) | collective-permute-done | bytes 122912 | tf_op jit(solution)/shard_map/ppermute | solution.py:193
  30.7 0.2 collective-permute-done.10.refs_11_
  30.9 2.0 %reconstruct.1 = (bf16[256,1024]{1,0:T(8,128)(2,1)}, f32[1,1024]{1,0:T(1,128)S(1)}) custom-call(bf16[4,256,512]{2,1,0:T(8,128)(2,1)S(1)} %arrange.1.coeffs_ref, bf16[32,1920]{1,0:T(8,128)(2,1)S(1)} %correlate.1.refs_0_, bf16[32,1920]{1,0:T(8,128)(2,1)S(1)} %collective-permute-done.1.refs_1_, bf16[32,1920]{1,0:T(8,128)(2,1)S(1)} %collective-permute-done.2.refs_2_, ...), custom_call_target="tpu_custom_call" | custom-call | tf_op jit(solution)/shard_map/reconstruct/pallas_call | solution.py:300
  32.9 9.5 %all_to_all.5 = f32[16,8,128]{2,1,0:T(8,128)S(1)} all-to-all(f32[16,8,128]{2,1,0:T(8,128)S(1)} %broadcast_in_dim.8), channel_id=1, replica_groups=mesh['bank'=2,'tmpl'=16] {'tmpl'}, dimensions={0} | all-to-all | bytes 131072 | tf_op jit(solution)/shard_map/all_to_all | solution.py:225
  42.4 0.6 %reduce_max.9 = f32[8,128]{1,0:T(8,128)} reduce(f32[16,8,128]{2,1,0:T(8,128)S(1)} %all_to_all.5, f32[]{:T(128)} %constant.2.clone.1), dimensions={0}, to_apply=%region_0.0 | reduce | flops 15360 | bytes 69636 | tf_op jit(solution)/shard_map/reduce_max | solution.py:226
  (1 shorter events, 0.0 us)
Async XLA Ops:
  0.6 24.6 %copy-start = (bf16[4,256,512]{2,1,0:T(8,128)(2,1)S(1)}, bf16[4,256,512]{2,1,0:T(8,128)(2,1)}, u32[]{:S(2)}) copy-start(bf16[4,256,512]{2,1,0:T(8,128)(2,1)} %coeffs_ref.1) | copy-start | bytes 3145732
  7.6 7.9 %collective-permute-start.6 = (bf16[32,1920]{1,0:T(8,128)(2,1)S(1)}, bf16[32,1920]{1,0:T(8,128)(2,1)S(1)}, u32[]{:S(2)}, u32[]{:S(2)}) collective-permute-start(bf16[32,1920]{1,0:T(8,128)(2,1)S(1)} %correlate.1.refs_0_), channel_id=1, source_target_pairs={{0,4},{1,5},{2,6},{3,7},{4,0},{5,1},{6,2},{7,3},{8,12},{9,13},{10,... | collective-permute-start | bytes 368648 | tf_op jit(solution)/shard_map/ppermute | solution.py:193
  10.6 7.4 %collective-permute-start.4 = (bf16[32,1920]{1,0:T(8,128)(2,1)S(1)}, bf16[32,1920]{1,0:T(8,128)(2,1)S(1)}, u32[]{:S(2)}, u32[]{:S(2)}) collective-permute-start(bf16[32,1920]{1,0:T(8,128)(2,1)S(1)} %correlate.1.refs_0_), channel_id=1, source_target_pairs={{0,8},{1,9},{2,10},{3,11},{4,12},{5,13},{6,14},{7,15},{8,0},{9,1},... | collective-permute-start | bytes 368648 | tf_op jit(solution)/shard_map/ppermute | solution.py:193
  13.2 7.9 %collective-permute-start.2 = (bf16[32,1920]{1,0:T(8,128)(2,1)S(1)}, bf16[32,1920]{1,0:T(8,128)(2,1)S(1)}, u32[]{:S(2)}, u32[]{:S(2)}) collective-permute-start(bf16[32,1920]{1,0:T(8,128)(2,1)S(1)} %correlate.1.refs_0_), channel_id=1, source_target_pairs={{0,2},{1,3},{2,0},{3,1},{4,6},{5,7},{6,4},{7,5},{8,10},{9,11},{10,... | collective-permute-start | bytes 368648 | tf_op jit(solution)/shard_map/ppermute | solution.py:193
  14.8 7.5 %collective-permute-start.1 = (bf16[32,1920]{1,0:T(8,128)(2,1)S(1)}, bf16[32,1920]{1,0:T(8,128)(2,1)S(1)}, u32[]{:S(2)}, u32[]{:S(2)}) collective-permute-start(bf16[32,1920]{1,0:T(8,128)(2,1)S(1)} %correlate.1.refs_0_), channel_id=1, source_target_pairs={{0,1},{1,0},{2,3},{3,2},{4,5},{5,4},{6,7},{7,6},{8,9},{9,8},{10,11... | collective-permute-start | bytes 368648 | tf_op jit(solution)/shard_map/ppermute | solution.py:193
  14.8 10.4 %collective-permute-start = (bf16[32,1920]{1,0:T(8,128)(2,1)S(1)}, bf16[32,1920]{1,0:T(8,128)(2,1)S(1)}, u32[]{:S(2)}, u32[]{:S(2)}) collective-permute-start(bf16[32,1920]{1,0:T(8,128)(2,1)S(1)} %correlate.1.refs_0_), channel_id=1, source_target_pairs={{0,6},{1,7},{2,4},{3,5},{4,2},{5,3},{6,0},{7,1},{8,14},{9,15},{10,... | collective-permute-start | bytes 368648 | tf_op jit(solution)/shard_map/ppermute | solution.py:193
  15.5 10.5 %collective-permute-start.7 = (bf16[32,1920]{1,0:T(8,128)(2,1)S(1)}, bf16[32,1920]{1,0:T(8,128)(2,1)S(1)}, u32[]{:S(2)}, u32[]{:S(2)}) collective-permute-start(bf16[32,1920]{1,0:T(8,128)(2,1)S(1)} %collective-permute-done.6.refs_6_), channel_id=1, source_target_pairs={{0,1},{1,0},{2,3},{3,2},{4,5},{5,4},{6,7},{7,6},{8,9},{9,8},{10,11... | collective-permute-start | bytes 368648 | tf_op jit(solution)/shard_map/ppermute | solution.py:193
  18.1 8.4 %collective-permute-start.13 = (bf16[32,1920]{1,0:T(8,128)(2,1)S(1)}, bf16[32,1920]{1,0:T(8,128)(2,1)S(1)}, u32[]{:S(2)}, u32[]{:S(2)}) collective-permute-start(bf16[32,1920]{1,0:T(8,128)(2,1)S(1)} %collective-permute-done.4.refs_4_), channel_id=1, source_target_pairs={{0,2},{1,3},{2,0},{3,1},{4,6},{5,7},{6,4},{7,5},{8,10},{9,11},{10,... | collective-permute-start | bytes 368648 | tf_op jit(solution)/shard_map/ppermute | solution.py:193
  21.1 5.8 %collective-permute-start.11 = (bf16[32,1920]{1,0:T(8,128)(2,1)S(1)}, bf16[32,1920]{1,0:T(8,128)(2,1)S(1)}, u32[]{:S(2)}, u32[]{:S(2)}) collective-permute-start(bf16[32,1920]{1,0:T(8,128)(2,1)S(1)} %collective-permute-done.4.refs_4_), channel_id=1, source_target_pairs={{0,6},{1,7},{2,4},{3,5},{4,2},{5,3},{6,0},{7,1},{8,14},{9,15},{10,... | collective-permute-start | bytes 368648 | tf_op jit(solution)/shard_map/ppermute | solution.py:193
  22.2 7.1 %collective-permute-start.9 = (bf16[32,1920]{1,0:T(8,128)(2,1)S(1)}, bf16[32,1920]{1,0:T(8,128)(2,1)S(1)}, u32[]{:S(2)}, u32[]{:S(2)}) collective-permute-start(bf16[32,1920]{1,0:T(8,128)(2,1)S(1)} %collective-permute-done.4.refs_4_), channel_id=1, source_target_pairs={{0,4},{1,5},{2,6},{3,7},{4,0},{5,1},{6,2},{7,3},{8,12},{9,13},{10,... | collective-permute-start | bytes 368648 | tf_op jit(solution)/shard_map/ppermute | solution.py:193
  25.2 4.2 %collective-permute-start.5 = (bf16[32,1920]{1,0:T(8,128)(2,1)S(1)}, bf16[32,1920]{1,0:T(8,128)(2,1)S(1)}, u32[]{:S(2)}, u32[]{:S(2)}) collective-permute-start(bf16[32,1920]{1,0:T(8,128)(2,1)S(1)} %collective-permute-done.4.refs_4_), channel_id=1, source_target_pairs={{0,1},{1,0},{2,3},{3,2},{4,5},{5,4},{6,7},{7,6},{8,9},{9,8},{10,11... | collective-permute-start | bytes 368648 | tf_op jit(solution)/shard_map/ppermute | solution.py:193
  25.9 3.9 %collective-permute-start.8 = (bf16[32,1920]{1,0:T(8,128)(2,1)S(1)}, bf16[32,1920]{1,0:T(8,128)(2,1)S(1)}, u32[]{:S(2)}, u32[]{:S(2)}) collective-permute-start(bf16[32,1920]{1,0:T(8,128)(2,1)S(1)} %collective-permute-done.refs_8_), channel_id=1, source_target_pairs={{0,1},{1,0},{2,3},{3,2},{4,5},{5,4},{6,7},{7,6},{8,9},{9,8},{10,11... | collective-permute-start | bytes 368648 | tf_op jit(solution)/shard_map/ppermute | solution.py:193
  26.5 3.4 %collective-permute-start.3 = (bf16[32,1920]{1,0:T(8,128)(2,1)S(1)}, bf16[32,1920]{1,0:T(8,128)(2,1)S(1)}, u32[]{:S(2)}, u32[]{:S(2)}) collective-permute-start(bf16[32,1920]{1,0:T(8,128)(2,1)S(1)} %collective-permute-done.2.refs_2_), channel_id=1, source_target_pairs={{0,1},{1,0},{2,3},{3,2},{4,5},{5,4},{6,7},{7,6},{8,9},{9,8},{10,11... | collective-permute-start | bytes 368648 | tf_op jit(solution)/shard_map/ppermute | solution.py:193
  26.9 3.0 %collective-permute-start.14 = (bf16[32,1920]{1,0:T(8,128)(2,1)S(1)}, bf16[32,1920]{1,0:T(8,128)(2,1)S(1)}, u32[]{:S(2)}, u32[]{:S(2)}) collective-permute-start(bf16[32,1920]{1,0:T(8,128)(2,1)S(1)} %collective-permute-done.13.refs_14_), channel_id=1, source_target_pairs={{0,1},{1,0},{2,3},{3,2},{4,5},{5,4},{6,7},{7,6},{8,9},{9,8},{10,11... | collective-permute-start | bytes 368648 | tf_op jit(solution)/shard_map/ppermute | solution.py:193
  29.4 1.3 %collective-permute-start.12 = (bf16[32,1920]{1,0:T(8,128)(2,1)S(1)}, bf16[32,1920]{1,0:T(8,128)(2,1)S(1)}, u32[]{:S(2)}, u32[]{:S(2)}) collective-permute-start(bf16[32,1920]{1,0:T(8,128)(2,1)S(1)} %collective-permute-done.11.refs_12_), channel_id=1, source_target_pairs={{0,1},{1,0},{2,3},{3,2},{4,5},{5,4},{6,7},{7,6},{8,9},{9,8},{10,11... | collective-permute-start | bytes 368648 | tf_op jit(solution)/shard_map/ppermute | solution.py:193
  29.4 1.5 %collective-permute-start.10 = (bf16[32,1920]{1,0:T(8,128)(2,1)S(1)}, bf16[32,1920]{1,0:T(8,128)(2,1)S(1)}, u32[]{:S(2)}, u32[]{:S(2)}) collective-permute-start(bf16[32,1920]{1,0:T(8,128)(2,1)S(1)} %collective-permute-done.9.refs_10_), channel_id=1, source_target_pairs={{0,1},{1,0},{2,3},{3,2},{4,5},{5,4},{6,7},{7,6},{8,9},{9,8},{10,11... | collective-permute-start | bytes 368648 | tf_op jit(solution)/shard_map/ppermute | solution.py:193

commit v21 on v19

--- a/solution.py
+++ b/solution.py
@@ -12,8 +12,8 @@
 SUB = 16
 ROWS = 8
 ROLLS = 4
-TIED = 10
-HANDED = (0, 8, 1, 4, 10, 2, 3, 9, 6, 12, 7, 13, 5, 11)
+TIED = 8
+HANDED = (0, 1, 8, 4, 2, 3, 6, 7, 5, 9)
 
 
 def correlate_kernel(*refs):
@@ -206,7 +206,10 @@
     held = {0: block}
     for place in range(2, size, 2):
         high = 1 << (place.bit_length() - 1)
-        held[place] = exchange(held[place ^ high and high], place ^ high or place)
+        if place <= size // 2:
+            held[place] = exchange(block, place)
+        else:
+            held[place] = exchange(held[high], place ^ high)
     blocks = []
     for places in groups:
         if places[0] & 1 == 0:
@@ -221,10 +224,12 @@
 
 
 def block_groups(size):
-    first = [place for place in range(1, size, 2) if (place ^ 1) & ((place ^ 1) - 1) == 0][:-1]
-    rest = [place for place in range(1, size, 2) if place not in first]
-    alone = [(place,) for place in list(range(0, size, 2))]
-    return alone + [tuple(first)] + [(place,) for place in rest]
+    middle = size // 2 + 1
+    alone = [(place,) for place in range(0, size, 2)]
+    return alone + [
+        tuple(range(1, middle + 1, 2)),
+        tuple(range(middle + 2, size, 2)),
+    ]
 
 
 def maximum_over_group(values):

time: 43.3 us -> 45.3 us (1.046)
  waiting for transfers between devices: 7.73 us -> 10.4 us
  starting transfers between devices: 13.9 us -> 12.6 us
  blocking collectives: 10.5 us -> 11 us
    ppermute x13 -> x9, waiting for transfers between devices: 7.73 us -> 10.4 us  [exchange(): return lax.ppermute(block, 'tmpl', [(i, i ^ distance) for i in range(size)])]
    ppermute x13 -> x9, starting transfers between devices: 13.9 us -> 12.6 us  [exchange(): return lax.ppermute(block, 'tmpl', [(i, i ^ distance) for i in range(size)])]
  transfers between devices with their start and end apart: 13 -> 9, of which waited for: 5 -> 5; matrix products, arithmetic and copies ran while one was open for 0% -> 0% of each run, Pallas kernels for 2% -> 2%
where the time goes in v21:
time: 45.3 us; the launch traced here: 45.2 us
  starting transfers between devices  12.6 us (28%)
  blocking collectives  11 us (24%)
  waiting for transfers between devices  10.4 us (23%)
  Pallas kernels  9.64 us (21%)
  between operations  0.74 us (2%)
  other arithmetic  0.64 us (1%)
    ppermute x9, starting transfers between devices, exchange(): return lax.ppermute(block, 'tmpl', [(i, i ^ distance) for i in range(size)])  12.6 us
    all_to_all x1, blocking collectives, maximum_over_group(): lax.all_to_all(copies, 'tmpl', split_axis=0, concat_axis=0, tiled=True)  11 us
    ppermute x9, waiting for transfers between devices, exchange(): return lax.ppermute(block, 'tmpl', [(i, i ^ distance) for i in range(size)])  10.4 us
    pallas_call x1, Pallas kernels, correlate(): pl.pallas_call(correlate_kernel, out_shape=pltpu.VMEM((padded, samples),...  6.91 us
    pallas_call x1, Pallas kernels, reconstruct(): pl.pallas_call(functools.partial(recon_kernel, order), out_shape=(jax.Sha...  2.01 us
  transfers between devices with their start and end apart: 9, of which 5 were waited for; matrix products, arithmetic and copies ran while one was open for 0% of the time, Pallas kernels for 2%

profile of v21, /device:TPU:0, one launch (start us, length us, event | category | flops | bytes accessed | tf_op | source)
XLA Modules:
  0.0 45.2 jit_solution(17723853199671941903)
XLA Ops:
  0.6 0.0 copy-start
  0.6 6.9 %correlate.1.refs_0_ = bf16[32,1920]{1,0:T(8,128)(2,1)S(1)} custom-call(bf16[72,128]{1,0:T(8,128)(2,1)} %bitcast.9, bf16[68,128]{1,0:T(8,128)(2,1)} %bitcast.10, bf16[66,128]{1,0:T(8,128)(2,1)} %bitcast.11, bf16[65,128]{1,0:T(8,128)(2,1)} %bitcast.12, bf16[4,32,8192]{2,1,0:T(8,128)(2,1)} %refs_4_.1), custom_call_target="tpu_custom_call" | custom-call | flops 1006632960 | bytes 2097152 | tf_op jit(solution)/shard_map/correlate/pallas_call | solution.py:167
  7.6 3.0 %collective-permute-start = (bf16[32,1920]{1,0:T(8,128)(2,1)S(1)}, bf16[32,1920]{1,0:T(8,128)(2,1)S(1)}, u32[]{:S(2)}, u32[]{:S(2)}) collective-permute-start(bf16[32,1920]{1,0:T(8,128)(2,1)S(1)} %correlate.1.refs_0_), channel_id=1, source_target_pairs={{0,2},{1,3},{2,0},{3,1},{4,6},{5,7},{6,4},{7,5},{8,10},{9,11},{10,... | collective-permute-start | bytes 368648 | tf_op jit(solution)/shard_map/ppermute | solution.py:193
  10.6 1.6 %collective-permute-start.1 = (bf16[32,1920]{1,0:T(8,128)(2,1)S(1)}, bf16[32,1920]{1,0:T(8,128)(2,1)S(1)}, u32[]{:S(2)}, u32[]{:S(2)}) collective-permute-start(bf16[32,1920]{1,0:T(8,128)(2,1)S(1)} %correlate.1.refs_0_), channel_id=1, source_target_pairs={{0,4},{1,5},{2,6},{3,7},{4,0},{5,1},{6,2},{7,3},{8,12},{9,13},{10,... | collective-permute-start | bytes 368648 | tf_op jit(solution)/shard_map/ppermute | solution.py:193
  12.2 0.0 collective-permute-start.2
  12.2 3.0 %collective-permute-start.3 = (bf16[32,1920]{1,0:T(8,128)(2,1)S(1)}, bf16[32,1920]{1,0:T(8,128)(2,1)S(1)}, u32[]{:S(2)}, u32[]{:S(2)}) collective-permute-start(bf16[32,1920]{1,0:T(8,128)(2,1)S(1)} %correlate.1.refs_0_), channel_id=1, source_target_pairs={{0,8},{1,9},{2,10},{3,11},{4,12},{5,13},{6,14},{7,15},{8,0},{9,1},... | collective-permute-start | bytes 368648 | tf_op jit(solution)/shard_map/ppermute | solution.py:193
  15.2 0.0 copy-done
  15.2 0.7 %arrange.1.coeffs_ref = bf16[4,256,512]{2,1,0:T(8,128)(2,1)S(1)} custom-call(s32[1]{0:T(128)} %bitcast.4.offset_ref, bf16[4,256,512]{2,1,0:T(8,128)(2,1)S(1)} %copy-done), custom_call_target="tpu_custom_call" | custom-call | flops 536870912 | bytes 2097152 | tf_op jit(solution)/shard_map/arrange/pallas_call | solution.py:261
  15.9 3.9 %collective-permute-done.3.refs_3_ = bf16[32,1920]{1,0:T(8,128)(2,1)S(1)} collective-permute-done((bf16[32,1920]{1,0:T(8,128)(2,1)S(1)}, bf16[32,1920]{1,0:T(8,128)(2,1)S(1)}, u32[]{:S(2)}, u32[]{:S(2)}) %collective-permute-start.3) | collective-permute-done | bytes 122912 | tf_op jit(solution)/shard_map/ppermute | solution.py:193
  19.8 3.4 %collective-permute-start.5 = (bf16[32,1920]{1,0:T(8,128)(2,1)S(1)}, bf16[32,1920]{1,0:T(8,128)(2,1)S(1)}, u32[]{:S(2)}, u32[]{:S(2)}) collective-permute-start(bf16[32,1920]{1,0:T(8,128)(2,1)S(1)} %collective-permute-done.3.refs_3_), channel_id=1, source_target_pairs={{0,4},{1,5},{2,6},{3,7},{4,0},{5,1},{6,2},{7,3},{8,12},{9,13},{10,... | collective-permute-start | bytes 368648 | tf_op jit(solution)/shard_map/ppermute | solution.py:193
  23.2 0.0 collective-permute-start.6
  23.3 0.0 collective-permute-done.refs_1_
  23.3 1.4 %collective-permute-start.7 = (bf16[32,1920]{1,0:T(8,128)(2,1)S(1)}, bf16[32,1920]{1,0:T(8,128)(2,1)S(1)}, u32[]{:S(2)}, u32[]{:S(2)}) collective-permute-start(bf16[32,1920]{1,0:T(8,128)(2,1)S(1)} %collective-permute-done.3.refs_3_), channel_id=1, source_target_pairs={{0,2},{1,3},{2,0},{3,1},{4,6},{5,7},{6,4},{7,5},{8,10},{9,11},{10,... | collective-permute-start | bytes 368648 | tf_op jit(solution)/shard_map/ppermute | solution.py:193
  24.7 0.0 collective-permute-done.1.refs_4_
  24.7 0.0 collective-permute-done.2.refs_5_
  24.8 0.1 collective-permute-start.4
  24.9 2.2 %collective-permute-done.5.refs_6_ = bf16[32,1920]{1,0:T(8,128)(2,1)S(1)} collective-permute-done((bf16[32,1920]{1,0:T(8,128)(2,1)S(1)}, bf16[32,1920]{1,0:T(8,128)(2,1)S(1)}, u32[]{:S(2)}, u32[]{:S(2)}) %collective-permute-start.5) | collective-permute-done | bytes 122912 | tf_op jit(solution)/shard_map/ppermute | solution.py:193
  27.1 2.0 %collective-permute-done.6.refs_7_ = bf16[32,1920]{1,0:T(8,128)(2,1)S(1)} collective-permute-done((bf16[32,1920]{1,0:T(8,128)(2,1)S(1)}, bf16[32,1920]{1,0:T(8,128)(2,1)S(1)}, u32[]{:S(2)}, u32[]{:S(2)}) %collective-permute-start.6) | collective-permute-done | bytes 122912 | tf_op jit(solution)/shard_map/ppermute | solution.py:193
  29.1 0.7 %collective-permute-done.7.refs_8_ = bf16[32,1920]{1,0:T(8,128)(2,1)S(1)} collective-permute-done((bf16[32,1920]{1,0:T(8,128)(2,1)S(1)}, bf16[32,1920]{1,0:T(8,128)(2,1)S(1)}, u32[]{:S(2)}, u32[]{:S(2)}) %collective-permute-start.7) | collective-permute-done | bytes 122912 | tf_op jit(solution)/shard_map/ppermute | solution.py:193
  29.8 0.1 collective-permute-start.8
  29.9 1.7 %collective-permute-done.8.refs_9_ = bf16[96,1920]{1,0:T(8,128)(2,1)S(1)} collective-permute-done((bf16[96,1920]{1,0:T(8,128)(2,1)S(1)}, bf16[96,1920]{1,0:T(8,128)(2,1)S(1)}, u32[]{:S(2)}, u32[]{:S(2)}) %collective-permute-start.8) | collective-permute-done | bytes 368672 | tf_op jit(solution)/shard_map/ppermute | solution.py:193
  31.5 0.0 collective-permute-done.4.refs_2_
  31.6 2.0 %reconstruct.1 = (bf16[256,1024]{1,0:T(8,128)(2,1)}, f32[1,1024]{1,0:T(1,128)S(1)}) custom-call(bf16[4,256,512]{2,1,0:T(8,128)(2,1)S(1)} %arrange.1.coeffs_ref, bf16[32,1920]{1,0:T(8,128)(2,1)S(1)} %correlate.1.refs_0_, bf16[32,1920]{1,0:T(8,128)(2,1)S(1)} %collective-permute-done.refs_1_, bf16[160,1920]{1,0:T(8,128)(2,1)S(1)} %collective-permute-done.4.refs_2_, ...), custom_call_target="tpu_custom_call" | custom-call | tf_op jit(solution)/shard_map/reconstruct/pallas_call | solution.py:331
  33.6 11.0 %all_to_all.5 = f32[16,8,128]{2,1,0:T(8,128)S(1)} all-to-all(f32[16,8,128]{2,1,0:T(8,128)S(1)} %broadcast_in_dim.8), channel_id=1, replica_groups=mesh['bank'=2,'tmpl'=16] {'tmpl'}, dimensions={0} | all-to-all | bytes 131072 | tf_op jit(solution)/shard_map/all_to_all | solution.py:239
  44.6 0.6 %reduce_max.9 = f32[8,128]{1,0:T(8,128)} reduce(f32[16,8,128]{2,1,0:T(8,128)S(1)} %all_to_all.5, f32[]{:T(128)} %constant.2.clone.1), dimensions={0}, to_apply=%region_0.0 | reduce | flops 15360 | bytes 69636 | tf_op jit(solution)/shard_map/reduce_max | solution.py:240
  (7 shorter events, 0.1 us)
Async XLA Ops:
  0.6 14.5 %copy-start = (bf16[4,256,512]{2,1,0:T(8,128)(2,1)S(1)}, bf16[4,256,512]{2,1,0:T(8,128)(2,1)}, u32[]{:S(2)}) copy-start(bf16[4,256,512]{2,1,0:T(8,128)(2,1)} %coeffs_ref.1) | copy-start | bytes 3145732
  7.6 15.7 %collective-permute-start = (bf16[32,1920]{1,0:T(8,128)(2,1)S(1)}, bf16[32,1920]{1,0:T(8,128)(2,1)S(1)}, u32[]{:S(2)}, u32[]{:S(2)}) collective-permute-start(bf16[32,1920]{1,0:T(8,128)(2,1)S(1)} %correlate.1.refs_0_), channel_id=1, source_target_pairs={{0,2},{1,3},{2,0},{3,1},{4,6},{5,7},{6,4},{7,5},{8,10},{9,11},{10,... | collective-permute-start | bytes 368648 | tf_op jit(solution)/shard_map/ppermute | solution.py:193
  10.6 14.1 %collective-permute-start.1 = (bf16[32,1920]{1,0:T(8,128)(2,1)S(1)}, bf16[32,1920]{1,0:T(8,128)(2,1)S(1)}, u32[]{:S(2)}, u32[]{:S(2)}) collective-permute-start(bf16[32,1920]{1,0:T(8,128)(2,1)S(1)} %correlate.1.refs_0_), channel_id=1, source_target_pairs={{0,4},{1,5},{2,6},{3,7},{4,0},{5,1},{6,2},{7,3},{8,12},{9,13},{10,... | collective-permute-start | bytes 368648 | tf_op jit(solution)/shard_map/ppermute | solution.py:193
  12.2 12.6 %collective-permute-start.2 = (bf16[32,1920]{1,0:T(8,128)(2,1)S(1)}, bf16[32,1920]{1,0:T(8,128)(2,1)S(1)}, u32[]{:S(2)}, u32[]{:S(2)}) collective-permute-start(bf16[32,1920]{1,0:T(8,128)(2,1)S(1)} %correlate.1.refs_0_), channel_id=1, source_target_pairs={{0,6},{1,7},{2,4},{3,5},{4,2},{5,3},{6,0},{7,1},{8,14},{9,15},{10,... | collective-permute-start | bytes 368648 | tf_op jit(solution)/shard_map/ppermute | solution.py:193
  12.2 7.6 %collective-permute-start.3 = (bf16[32,1920]{1,0:T(8,128)(2,1)S(1)}, bf16[32,1920]{1,0:T(8,128)(2,1)S(1)}, u32[]{:S(2)}, u32[]{:S(2)}) collective-permute-start(bf16[32,1920]{1,0:T(8,128)(2,1)S(1)} %correlate.1.refs_0_), channel_id=1, source_target_pairs={{0,8},{1,9},{2,10},{3,11},{4,12},{5,13},{6,14},{7,15},{8,0},{9,1},... | collective-permute-start | bytes 368648 | tf_op jit(solution)/shard_map/ppermute | solution.py:193
  19.8 7.3 %collective-permute-start.5 = (bf16[32,1920]{1,0:T(8,128)(2,1)S(1)}, bf16[32,1920]{1,0:T(8,128)(2,1)S(1)}, u32[]{:S(2)}, u32[]{:S(2)}) collective-permute-start(bf16[32,1920]{1,0:T(8,128)(2,1)S(1)} %collective-permute-done.3.refs_3_), channel_id=1, source_target_pairs={{0,4},{1,5},{2,6},{3,7},{4,0},{5,1},{6,2},{7,3},{8,12},{9,13},{10,... | collective-permute-start | bytes 368648 | tf_op jit(solution)/shard_map/ppermute | solution.py:193
  23.2 5.8 %collective-permute-start.6 = (bf16[32,1920]{1,0:T(8,128)(2,1)S(1)}, bf16[32,1920]{1,0:T(8,128)(2,1)S(1)}, u32[]{:S(2)}, u32[]{:S(2)}) collective-permute-start(bf16[32,1920]{1,0:T(8,128)(2,1)S(1)} %collective-permute-done.3.refs_3_), channel_id=1, source_target_pairs={{0,6},{1,7},{2,4},{3,5},{4,2},{5,3},{6,0},{7,1},{8,14},{9,15},{10,... | collective-permute-start | bytes 368648 | tf_op jit(solution)/shard_map/ppermute | solution.py:193
  23.3 6.5 %collective-permute-start.7 = (bf16[32,1920]{1,0:T(8,128)(2,1)S(1)}, bf16[32,1920]{1,0:T(8,128)(2,1)S(1)}, u32[]{:S(2)}, u32[]{:S(2)}) collective-permute-start(bf16[32,1920]{1,0:T(8,128)(2,1)S(1)} %collective-permute-done.3.refs_3_), channel_id=1, source_target_pairs={{0,2},{1,3},{2,0},{3,1},{4,6},{5,7},{6,4},{7,5},{8,10},{9,11},{10,... | collective-permute-start | bytes 368648 | tf_op jit(solution)/shard_map/ppermute | solution.py:193
  24.8 6.7 %collective-permute-start.4 = (bf16[160,1920]{1,0:T(8,128)(2,1)S(1)}, bf16[160,1920]{1,0:T(8,128)(2,1)S(1)}, u32[]{:S(2)}, u32[]{:S(2)}) collective-permute-start(bf16[160,1920]{1,0:T(8,128)(2,1)S(1)} %constant_dynamic-update-slice_fusion), channel_id=1, source_target_pairs={{0,1},{1,0},{2,3},{3,2},{4,5},{5,4},{6,7},{7,6},{8,9},{9,8},{10,11... | collective-permute-start | bytes 1843208 | tf_op jit(solution)/shard_map/ppermute | solution.py:193
  29.8 1.8 %collective-permute-start.8 = (bf16[96,1920]{1,0:T(8,128)(2,1)S(1)}, bf16[96,1920]{1,0:T(8,128)(2,1)S(1)}, u32[]{:S(2)}, u32[]{:S(2)}) collective-permute-start(bf16[96,1920]{1,0:T(8,128)(2,1)S(1)} %pad_maximum_fusion), channel_id=1, source_target_pairs={{0,1},{1,0},{2,3},{3,2},{4,5},{5,4},{6,7},{7,6},{8,9},{9,8},{10,11... | collective-permute-start | bytes 1105928 | tf_op jit(solution)/shard_map/ppermute | solution.py:193

commit v22 on v20

--- a/solution.py
+++ b/solution.py
@@ -12,8 +12,8 @@
 SUB = 16
 ROWS = 8
 ROLLS = 4
-TIED = 7
-HANDED = (0, 1, 2, 3, 8, 9, 4, 5, 6, 7, 12, 13, 14, 15, 10, 11)
+TIED = 3
+HANDED = (0, 1, 6, 7, 2, 3, 4, 5, 8, 9, 12, 13, 14, 15, 10, 11)
 
 
 def correlate_kernel(*refs):

time: 43.2 us -> 44 us (1.019)
  blocking collectives: 9.49 us -> 11 us
  starting transfers between devices: 14.4 us -> 13.1 us
  waiting for transfers between devices: 8.1 us -> 8.83 us
    all_to_all x1, blocking collectives: 9.49 us -> 11 us  [maximum_over_group(): lax.all_to_all(copies, 'tmpl', split_axis=0, concat_axis=0, tiled=True)]
    ppermute x15, starting transfers between devices: 14.4 us -> 13.1 us  [exchange(): return lax.ppermute(block, 'tmpl', [(i, i ^ distance) for i in range(size)])]
    ppermute x15, waiting for transfers between devices: 8.1 us -> 8.83 us  [exchange(): return lax.ppermute(block, 'tmpl', [(i, i ^ distance) for i in range(size)])]
  transfers between devices with their start and end apart: 15 -> 15, of which waited for: 7 -> 8; matrix products, arithmetic and copies ran while one was open for 0% -> 0% of each run, Pallas kernels for 2% -> 2%
where the time goes in v22:
time: 44 us; the launch traced here: 43.8 us
  starting transfers between devices  13.1 us (30%)
  blocking collectives  11 us (25%)
  Pallas kernels  9.65 us (22%)
  waiting for transfers between devices  8.83 us (20%)
  between operations  0.67 us (2%)
  other arithmetic  0.61 us (1%)
    ppermute x15, starting transfers between devices, exchange(): return lax.ppermute(block, 'tmpl', [(i, i ^ distance) for i in range(size)])  13.1 us
    all_to_all x1, blocking collectives, maximum_over_group(): lax.all_to_all(copies, 'tmpl', split_axis=0, concat_axis=0, tiled=True)  11 us
    ppermute x15, waiting for transfers between devices, exchange(): return lax.ppermute(block, 'tmpl', [(i, i ^ distance) for i in range(size)])  8.83 us
    pallas_call x1, Pallas kernels, correlate(): pl.pallas_call(correlate_kernel, out_shape=pltpu.VMEM((padded, samples),...  6.91 us
    pallas_call x1, Pallas kernels, reconstruct(): pl.pallas_call(functools.partial(recon_kernel, order), out_shape=(jax.Sha...  2.02 us
  transfers between devices with their start and end apart: 15, of which 8 were waited for; matrix products, arithmetic and copies ran while one was open for 0% of the time, Pallas kernels for 2%

profile of v22, /device:TPU:0, one launch (start us, length us, event | category | flops | bytes accessed | tf_op | source)
XLA Modules:
  0.0 43.8 jit_solution(12146048230671256881)
XLA Ops:
  0.6 0.0 copy-start
  0.6 6.9 %correlate.1.refs_0_ = bf16[32,1920]{1,0:T(8,128)(2,1)S(1)} custom-call(bf16[72,128]{1,0:T(8,128)(2,1)} %bitcast.9, bf16[68,128]{1,0:T(8,128)(2,1)} %bitcast.10, bf16[66,128]{1,0:T(8,128)(2,1)} %bitcast.11, bf16[65,128]{1,0:T(8,128)(2,1)} %bitcast.12, bf16[4,32,8192]{2,1,0:T(8,128)(2,1)} %refs_4_.1), custom_call_target="tpu_custom_call" | custom-call | flops 1006632960 | bytes 2097152 | tf_op jit(solution)/shard_map/correlate/pallas_call | solution.py:167
  7.6 4.1 %collective-permute-start.7 = (bf16[32,1920]{1,0:T(8,128)(2,1)S(1)}, bf16[32,1920]{1,0:T(8,128)(2,1)S(1)}, u32[]{:S(2)}, u32[]{:S(2)}) collective-permute-start(bf16[32,1920]{1,0:T(8,128)(2,1)S(1)} %correlate.1.refs_0_), channel_id=1, source_target_pairs={{0,8},{1,9},{2,10},{3,11},{4,12},{5,13},{6,14},{7,15},{8,0},{9,1},... | collective-permute-start | bytes 368648 | tf_op jit(solution)/shard_map/ppermute | solution.py:193
  11.7 1.6 %collective-permute-start.5 = (bf16[32,1920]{1,0:T(8,128)(2,1)S(1)}, bf16[32,1920]{1,0:T(8,128)(2,1)S(1)}, u32[]{:S(2)}, u32[]{:S(2)}) collective-permute-start(bf16[32,1920]{1,0:T(8,128)(2,1)S(1)} %correlate.1.refs_0_), channel_id=1, source_target_pairs={{0,4},{1,5},{2,6},{3,7},{4,0},{5,1},{6,2},{7,3},{8,12},{9,13},{10,... | collective-permute-start | bytes 368648 | tf_op jit(solution)/shard_map/ppermute | solution.py:193
  13.2 1.4 %collective-permute-start.2 = (bf16[32,1920]{1,0:T(8,128)(2,1)S(1)}, bf16[32,1920]{1,0:T(8,128)(2,1)S(1)}, u32[]{:S(2)}, u32[]{:S(2)}) collective-permute-start(bf16[32,1920]{1,0:T(8,128)(2,1)S(1)} %correlate.1.refs_0_), channel_id=1, source_target_pairs={{0,6},{1,7},{2,4},{3,5},{4,2},{5,3},{6,0},{7,1},{8,14},{9,15},{10,... | collective-permute-start | bytes 368648 | tf_op jit(solution)/shard_map/ppermute | solution.py:193
  14.6 0.0 collective-permute-start.1
  14.6 0.5 %collective-permute-start = (bf16[32,1920]{1,0:T(8,128)(2,1)S(1)}, bf16[32,1920]{1,0:T(8,128)(2,1)S(1)}, u32[]{:S(2)}, u32[]{:S(2)}) collective-permute-start(bf16[32,1920]{1,0:T(8,128)(2,1)S(1)} %correlate.1.refs_0_), channel_id=1, source_target_pairs={{0,2},{1,3},{2,0},{3,1},{4,6},{5,7},{6,4},{7,5},{8,10},{9,11},{10,... | collective-permute-start | bytes 368648 | tf_op jit(solution)/shard_map/ppermute | solution.py:193
  15.2 2.6 %collective-permute-done.7.refs_8_ = bf16[32,1920]{1,0:T(8,128)(2,1)S(1)} collective-permute-done((bf16[32,1920]{1,0:T(8,128)(2,1)S(1)}, bf16[32,1920]{1,0:T(8,128)(2,1)S(1)}, u32[]{:S(2)}, u32[]{:S(2)}) %collective-permute-start.7) | collective-permute-done | bytes 122912 | tf_op jit(solution)/shard_map/ppermute | solution.py:193
  17.7 1.6 %collective-permute-start.13 = (bf16[32,1920]{1,0:T(8,128)(2,1)S(1)}, bf16[32,1920]{1,0:T(8,128)(2,1)S(1)}, u32[]{:S(2)}, u32[]{:S(2)}) collective-permute-start(bf16[32,1920]{1,0:T(8,128)(2,1)S(1)} %collective-permute-done.7.refs_8_), channel_id=1, source_target_pairs={{0,2},{1,3},{2,0},{3,1},{4,6},{5,7},{6,4},{7,5},{8,10},{9,11},{10,... | collective-permute-start | bytes 368648 | tf_op jit(solution)/shard_map/ppermute | solution.py:193
  19.3 0.0 collective-permute-done.5.refs_6_
  19.3 2.2 %collective-permute-start.11 = (bf16[32,1920]{1,0:T(8,128)(2,1)S(1)}, bf16[32,1920]{1,0:T(8,128)(2,1)S(1)}, u32[]{:S(2)}, u32[]{:S(2)}) collective-permute-start(bf16[32,1920]{1,0:T(8,128)(2,1)S(1)} %collective-permute-done.7.refs_8_), channel_id=1, source_target_pairs={{0,6},{1,7},{2,4},{3,5},{4,2},{5,3},{6,0},{7,1},{8,14},{9,15},{10,... | collective-permute-start | bytes 368648 | tf_op jit(solution)/shard_map/ppermute | solution.py:193
  21.5 1.0 %collective-permute-done.2.refs_2_ = bf16[32,1920]{1,0:T(8,128)(2,1)S(1)} collective-permute-done((bf16[32,1920]{1,0:T(8,128)(2,1)S(1)}, bf16[32,1920]{1,0:T(8,128)(2,1)S(1)}, u32[]{:S(2)}, u32[]{:S(2)}) %collective-permute-start.2) | collective-permute-done | bytes 122912 | tf_op jit(solution)/shard_map/ppermute | solution.py:193
  22.4 0.6 %collective-permute-start.9 = (bf16[32,1920]{1,0:T(8,128)(2,1)S(1)}, bf16[32,1920]{1,0:T(8,128)(2,1)S(1)}, u32[]{:S(2)}, u32[]{:S(2)}) collective-permute-start(bf16[32,1920]{1,0:T(8,128)(2,1)S(1)} %collective-permute-done.7.refs_8_), channel_id=1, source_target_pairs={{0,4},{1,5},{2,6},{3,7},{4,0},{5,1},{6,2},{7,3},{8,12},{9,13},{10,... | collective-permute-start | bytes 368648 | tf_op jit(solution)/shard_map/ppermute | solution.py:193
  23.1 0.0 collective-permute-done.1.refs_1_
  23.1 0.0 collective-permute-start.8
  23.1 1.7 %collective-permute-done.refs_4_ = bf16[32,1920]{1,0:T(8,128)(2,1)S(1)} collective-permute-done((bf16[32,1920]{1,0:T(8,128)(2,1)S(1)}, bf16[32,1920]{1,0:T(8,128)(2,1)S(1)}, u32[]{:S(2)}, u32[]{:S(2)}) %collective-permute-start) | collective-permute-done | bytes 122912 | tf_op jit(solution)/shard_map/ppermute | solution.py:193
  24.7 0.0 collective-permute-start.6
  24.7 0.0 copy-done
  24.7 0.7 %arrange.1.coeffs_ref = bf16[4,256,512]{2,1,0:T(8,128)(2,1)S(1)} custom-call(s32[1]{0:T(128)} %bitcast.4.offset_ref, bf16[4,256,512]{2,1,0:T(8,128)(2,1)S(1)} %copy-done), custom_call_target="tpu_custom_call" | custom-call | flops 536870912 | bytes 2097152 | tf_op jit(solution)/shard_map/arrange/pallas_call | solution.py:241
  25.5 2.4 %collective-permute-done.13.refs_14_ = bf16[32,1920]{1,0:T(8,128)(2,1)S(1)} collective-permute-done((bf16[32,1920]{1,0:T(8,128)(2,1)S(1)}, bf16[32,1920]{1,0:T(8,128)(2,1)S(1)}, u32[]{:S(2)}, u32[]{:S(2)}) %collective-permute-start.13) | collective-permute-done | bytes 122912 | tf_op jit(solution)/shard_map/ppermute | solution.py:193
  27.8 0.0 collective-permute-start.4
  27.8 0.0 collective-permute-done.11.refs_12_
  27.8 0.5 %collective-permute-start.3 = (bf16[32,1920]{1,0:T(8,128)(2,1)S(1)}, bf16[32,1920]{1,0:T(8,128)(2,1)S(1)}, u32[]{:S(2)}, u32[]{:S(2)}) collective-permute-start(bf16[32,1920]{1,0:T(8,128)(2,1)S(1)} %collective-permute-done.2.refs_2_), channel_id=1, source_target_pairs={{0,1},{1,0},{2,3},{3,2},{4,5},{5,4},{6,7},{7,6},{8,9},{9,8},{10,11... | collective-permute-start | bytes 368648 | tf_op jit(solution)/shard_map/ppermute | solution.py:193
  28.3 0.0 collective-permute-done.9.refs_10_
  28.4 0.1 collective-permute-start.14
  28.4 0.0 collective-permute-done.8.refs_9_
  28.4 0.4 %collective-permute-start.12 = (bf16[32,1920]{1,0:T(8,128)(2,1)S(1)}, bf16[32,1920]{1,0:T(8,128)(2,1)S(1)}, u32[]{:S(2)}, u32[]{:S(2)}) collective-permute-start(bf16[32,1920]{1,0:T(8,128)(2,1)S(1)} %collective-permute-done.11.refs_12_), channel_id=1, source_target_pairs={{0,1},{1,0},{2,3},{3,2},{4,5},{5,4},{6,7},{7,6},{8,9},{9,8},{10,11... | collective-permute-start | bytes 368648 | tf_op jit(solution)/shard_map/ppermute | solution.py:193
  28.9 0.0 collective-permute-done.6.refs_7_
  28.9 0.1 collective-permute-start.10
  28.9 0.4 collective-permute-done.3.refs_3_
  29.3 0.0 collective-permute-done.4.refs_5_
  29.3 0.3 collective-permute-done.14.refs_15_
  29.7 0.2 collective-permute-done.12.refs_13_
  29.9 0.3 collective-permute-done.10.refs_11_
  30.2 2.0 %reconstruct.1 = (bf16[256,1024]{1,0:T(8,128)(2,1)}, f32[1,1024]{1,0:T(1,128)S(1)}) custom-call(bf16[4,256,512]{2,1,0:T(8,128)(2,1)S(1)} %arrange.1.coeffs_ref, bf16[32,1920]{1,0:T(8,128)(2,1)S(1)} %correlate.1.refs_0_, bf16[32,1920]{1,0:T(8,128)(2,1)S(1)} %collective-permute-done.1.refs_1_, bf16[32,1920]{1,0:T(8,128)(2,1)S(1)} %collective-permute-done.2.refs_2_, ...), custom_call_target="tpu_custom_call" | custom-call | tf_op jit(solution)/shard_map/reconstruct/pallas_call | solution.py:300
  32.2 11.0 %all_to_all.5 = f32[16,8,128]{2,1,0:T(8,128)S(1)} all-to-all(f32[16,8,128]{2,1,0:T(8,128)S(1)} %broadcast_in_dim.8), channel_id=1, replica_groups=mesh['bank'=2,'tmpl'=16] {'tmpl'}, dimensions={0} | all-to-all | bytes 131072 | tf_op jit(solution)/shard_map/all_to_all | solution.py:225
  43.2 0.6 %reduce_max.9 = f32[8,128]{1,0:T(8,128)} reduce(f32[16,8,128]{2,1,0:T(8,128)S(1)} %all_to_all.5, f32[]{:T(128)} %constant.2.clone.1), dimensions={0}, to_apply=%region_0.0 | reduce | flops 15360 | bytes 69636 | tf_op jit(solution)/shard_map/reduce_max | solution.py:226
  (1 shorter events, 0.0 us)
Async XLA Ops:
  0.6 24.1 %copy-start = (bf16[4,256,512]{2,1,0:T(8,128)(2,1)S(1)}, bf16[4,256,512]{2,1,0:T(8,128)(2,1)}, u32[]{:S(2)}) copy-start(bf16[4,256,512]{2,1,0:T(8,128)(2,1)} %coeffs_ref.1) | copy-start | bytes 3145732
  7.6 10.2 %collective-permute-start.7 = (bf16[32,1920]{1,0:T(8,128)(2,1)S(1)}, bf16[32,1920]{1,0:T(8,128)(2,1)S(1)}, u32[]{:S(2)}, u32[]{:S(2)}) collective-permute-start(bf16[32,1920]{1,0:T(8,128)(2,1)S(1)} %correlate.1.refs_0_), channel_id=1, source_target_pairs={{0,8},{1,9},{2,10},{3,11},{4,12},{5,13},{6,14},{7,15},{8,0},{9,1},... | collective-permute-start | bytes 368648 | tf_op jit(solution)/shard_map/ppermute | solution.py:193
  11.7 7.6 %collective-permute-start.5 = (bf16[32,1920]{1,0:T(8,128)(2,1)S(1)}, bf16[32,1920]{1,0:T(8,128)(2,1)S(1)}, u32[]{:S(2)}, u32[]{:S(2)}) collective-permute-start(bf16[32,1920]{1,0:T(8,128)(2,1)S(1)} %correlate.1.refs_0_), channel_id=1, source_target_pairs={{0,4},{1,5},{2,6},{3,7},{4,0},{5,1},{6,2},{7,3},{8,12},{9,13},{10,... | collective-permute-start | bytes 368648 | tf_op jit(solution)/shard_map/ppermute | solution.py:193
  13.2 9.2 %collective-permute-start.2 = (bf16[32,1920]{1,0:T(8,128)(2,1)S(1)}, bf16[32,1920]{1,0:T(8,128)(2,1)S(1)}, u32[]{:S(2)}, u32[]{:S(2)}) collective-permute-start(bf16[32,1920]{1,0:T(8,128)(2,1)S(1)} %correlate.1.refs_0_), channel_id=1, source_target_pairs={{0,6},{1,7},{2,4},{3,5},{4,2},{5,3},{6,0},{7,1},{8,14},{9,15},{10,... | collective-permute-start | bytes 368648 | tf_op jit(solution)/shard_map/ppermute | solution.py:193
  14.6 8.4 %collective-permute-start.1 = (bf16[32,1920]{1,0:T(8,128)(2,1)S(1)}, bf16[32,1920]{1,0:T(8,128)(2,1)S(1)}, u32[]{:S(2)}, u32[]{:S(2)}) collective-permute-start(bf16[32,1920]{1,0:T(8,128)(2,1)S(1)} %correlate.1.refs_0_), channel_id=1, source_target_pairs={{0,1},{1,0},{2,3},{3,2},{4,5},{5,4},{6,7},{7,6},{8,9},{9,8},{10,11... | collective-permute-start | bytes 368648 | tf_op jit(solution)/shard_map/ppermute | solution.py:193
  14.6 10.1 %collective-permute-start = (bf16[32,1920]{1,0:T(8,128)(2,1)S(1)}, bf16[32,1920]{1,0:T(8,128)(2,1)S(1)}, u32[]{:S(2)}, u32[]{:S(2)}) collective-permute-start(bf16[32,1920]{1,0:T(8,128)(2,1)S(1)} %correlate.1.refs_0_), channel_id=1, source_target_pairs={{0,2},{1,3},{2,0},{3,1},{4,6},{5,7},{6,4},{7,5},{8,10},{9,11},{10,... | collective-permute-start | bytes 368648 | tf_op jit(solution)/shard_map/ppermute | solution.py:193
  17.7 10.1 %collective-permute-start.13 = (bf16[32,1920]{1,0:T(8,128)(2,1)S(1)}, bf16[32,1920]{1,0:T(8,128)(2,1)S(1)}, u32[]{:S(2)}, u32[]{:S(2)}) collective-permute-start(bf16[32,1920]{1,0:T(8,128)(2,1)S(1)} %collective-permute-done.7.refs_8_), channel_id=1, source_target_pairs={{0,2},{1,3},{2,0},{3,1},{4,6},{5,7},{6,4},{7,5},{8,10},{9,11},{10,... | collective-permute-start | bytes 368648 | tf_op jit(solution)/shard_map/ppermute | solution.py:193
  19.3 8.5 %collective-permute-start.11 = (bf16[32,1920]{1,0:T(8,128)(2,1)S(1)}, bf16[32,1920]{1,0:T(8,128)(2,1)S(1)}, u32[]{:S(2)}, u32[]{:S(2)}) collective-permute-start(bf16[32,1920]{1,0:T(8,128)(2,1)S(1)} %collective-permute-done.7.refs_8_), channel_id=1, source_target_pairs={{0,6},{1,7},{2,4},{3,5},{4,2},{5,3},{6,0},{7,1},{8,14},{9,15},{10,... | collective-permute-start | bytes 368648 | tf_op jit(solution)/shard_map/ppermute | solution.py:193
  22.4 5.9 %collective-permute-start.9 = (bf16[32,1920]{1,0:T(8,128)(2,1)S(1)}, bf16[32,1920]{1,0:T(8,128)(2,1)S(1)}, u32[]{:S(2)}, u32[]{:S(2)}) collective-permute-start(bf16[32,1920]{1,0:T(8,128)(2,1)S(1)} %collective-permute-done.7.refs_8_), channel_id=1, source_target_pairs={{0,4},{1,5},{2,6},{3,7},{4,0},{5,1},{6,2},{7,3},{8,12},{9,13},{10,... | collective-permute-start | bytes 368648 | tf_op jit(solution)/shard_map/ppermute | solution.py:193
  23.1 5.4 %collective-permute-start.8 = (bf16[32,1920]{1,0:T(8,128)(2,1)S(1)}, bf16[32,1920]{1,0:T(8,128)(2,1)S(1)}, u32[]{:S(2)}, u32[]{:S(2)}) collective-permute-start(bf16[32,1920]{1,0:T(8,128)(2,1)S(1)} %collective-permute-done.7.refs_8_), channel_id=1, source_target_pairs={{0,1},{1,0},{2,3},{3,2},{4,5},{5,4},{6,7},{7,6},{8,9},{9,8},{10,11... | collective-permute-start | bytes 368648 | tf_op jit(solution)/shard_map/ppermute | solution.py:193
  24.7 4.1 %collective-permute-start.6 = (bf16[32,1920]{1,0:T(8,128)(2,1)S(1)}, bf16[32,1920]{1,0:T(8,128)(2,1)S(1)}, u32[]{:S(2)}, u32[]{:S(2)}) collective-permute-start(bf16[32,1920]{1,0:T(8,128)(2,1)S(1)} %collective-permute-done.5.refs_6_), channel_id=1, source_target_pairs={{0,1},{1,0},{2,3},{3,2},{4,5},{5,4},{6,7},{7,6},{8,9},{9,8},{10,11... | collective-permute-start | bytes 368648 | tf_op jit(solution)/shard_map/ppermute | solution.py:193
  27.8 1.5 %collective-permute-start.4 = (bf16[32,1920]{1,0:T(8,128)(2,1)S(1)}, bf16[32,1920]{1,0:T(8,128)(2,1)S(1)}, u32[]{:S(2)}, u32[]{:S(2)}) collective-permute-start(bf16[32,1920]{1,0:T(8,128)(2,1)S(1)} %collective-permute-done.refs_4_), channel_id=1, source_target_pairs={{0,1},{1,0},{2,3},{3,2},{4,5},{5,4},{6,7},{7,6},{8,9},{9,8},{10,11... | collective-permute-start | bytes 368648 | tf_op jit(solution)/shard_map/ppermute | solution.py:193
  27.8 1.5 %collective-permute-start.3 = (bf16[32,1920]{1,0:T(8,128)(2,1)S(1)}, bf16[32,1920]{1,0:T(8,128)(2,1)S(1)}, u32[]{:S(2)}, u32[]{:S(2)}) collective-permute-start(bf16[32,1920]{1,0:T(8,128)(2,1)S(1)} %collective-permute-done.2.refs_2_), channel_id=1, source_target_pairs={{0,1},{1,0},{2,3},{3,2},{4,5},{5,4},{6,7},{7,6},{8,9},{9,8},{10,11... | collective-permute-start | bytes 368648 | tf_op jit(solution)/shard_map/ppermute | solution.py:193
  28.4 1.3 %collective-permute-start.14 = (bf16[32,1920]{1,0:T(8,128)(2,1)S(1)}, bf16[32,1920]{1,0:T(8,128)(2,1)S(1)}, u32[]{:S(2)}, u32[]{:S(2)}) collective-permute-start(bf16[32,1920]{1,0:T(8,128)(2,1)S(1)} %collective-permute-done.13.refs_14_), channel_id=1, source_target_pairs={{0,1},{1,0},{2,3},{3,2},{4,5},{5,4},{6,7},{7,6},{8,9},{9,8},{10,11... | collective-permute-start | bytes 368648 | tf_op jit(solution)/shard_map/ppermute | solution.py:193
  28.4 1.4 %collective-permute-start.12 = (bf16[32,1920]{1,0:T(8,128)(2,1)S(1)}, bf16[32,1920]{1,0:T(8,128)(2,1)S(1)}, u32[]{:S(2)}, u32[]{:S(2)}) collective-permute-start(bf16[32,1920]{1,0:T(8,128)(2,1)S(1)} %collective-permute-done.11.refs_12_), channel_id=1, source_target_pairs={{0,1},{1,0},{2,3},{3,2},{4,5},{5,4},{6,7},{7,6},{8,9},{9,8},{10,11... | collective-permute-start | bytes 368648 | tf_op jit(solution)/shard_map/ppermute | solution.py:193
  28.9 1.3 %collective-permute-start.10 = (bf16[32,1920]{1,0:T(8,128)(2,1)S(1)}, bf16[32,1920]{1,0:T(8,128)(2,1)S(1)}, u32[]{:S(2)}, u32[]{:S(2)}) collective-permute-start(bf16[32,1920]{1,0:T(8,128)(2,1)S(1)} %collective-permute-done.9.refs_10_), channel_id=1, source_target_pairs={{0,1},{1,0},{2,3},{3,2},{4,5},{5,4},{6,7},{7,6},{8,9},{9,8},{10,11... | collective-permute-start | bytes 368648 | tf_op jit(solution)/shard_map/ppermute | solution.py:193
